TPU v7x, 32 devices: a whole 2x2x4 slice. The times are simulated.
32 devices in a mesh: groups: 2 (over y), key: 4 (over z), shard: 2 (over x), lane: 2 (over core).
Axes of the slice: x: 2, y: 2, z: 4, core: 2. Of those that a mesh axis runs over, the one named last changes fastest.
Arguments:
- events: bfloat16 [8192, 256], P(('groups', 'key', 'shard'), 'lane'), parts along dimension 0, may hold values from -6 to 6
- event_weight: float32 [8192], P(('groups', 'key', 'shard')), parts along dimension 0, may hold values from 0.25 to 4
- route: int32 [8192, 1], P(('groups', 'key', 'shard')), parts along dimension 0, may hold values from 0 to 7; in each aligned block of 512 rows (0 to 511, 512 to 1023, ...) at most 128 rows name the same one
- bucket: int32 [8192], P(('groups', 'key', 'shard')), parts along dimension 0, may hold values from 0 to 4095
- segment: int32 [65536], P(('groups', 'key', 'shard')), parts along dimension 0, may hold values from 0 to 63, never falling along the last dimension, each value on 1 to 2048 neighbouring positions
- decay_rate: float32 [8], P('lane'), may hold values from 0.000390625 to 0.0029296875
Outputs:
- table: bfloat16 [65536, 256], P(('groups', 'key', 'shard'), 'lane'), parts along dimension 0
- event_features: bfloat16 [8192, 256], P(('groups', 'key', 'shard'), 'lane'), parts along dimension 0
There are 2 independent parts, one for each index of `groups`. A program takes and returns all parts, laid end to end along the dimension named above; an argument that names none is the same for every part. Nothing has to cross between parts.
Inputs may be any that keep to these rules, and one draw needn't show every extreme that they name: `route`: among the rows of one device at most 128 name the same owner, a bound that some block reaches. `segment`: never falling along the slots; each user holds 1 to 2048 slots in a row, one exactly 2048.
All inputs are finite; a program needn't handle non-finite values.
Results may differ from a plain program's by a relative error of at most 0.0056.
Values may be sent and summed in bfloat16 or wider, within the bound.
No kernel may reach another device: no remote copies, remote signals or barrier semaphores. Data moves between devices by JAX's collectives and lax.ppermute only.
A program may use at most 64 MiB of HBM per device.

v0:
```python
import jax
import jax.numpy as jnp
from jax import lax
from jax.sharding import PartitionSpec as P


def from_behind(block, axis, distance):
    devices = range(lax.axis_size(axis))
    route = [(i - distance, i) for i in devices if i - distance in devices]
    return lax.ppermute(block, axis, route)


def owner_places(route, owners, capacity):
    target = route[:, 0]
    marks = (target[:, None] == jnp.arange(owners, dtype=jnp.int32)[None, :]).astype(jnp.int32)
    before = jnp.cumsum(marks, axis=0) - marks
    rank = jnp.sum(before * marks, axis=1)
    return target * capacity + rank


def on_device(events, event_weight, route, bucket, segment, decay_rate):
    rows, width = events.shape
    key_count = lax.axis_size("key")
    shard_count = lax.axis_size("shard")
    owners = key_count * shard_count
    capacity = 2 * rows // owners
    slots = segment.shape[0]
    window = slots // 4
    place = owner_places(route, owners, capacity)
    weighted = (event_weight[:, None] * events.astype(jnp.float32)).astype(jnp.bfloat16)
    outgoing = jnp.zeros((owners * capacity, width), jnp.bfloat16).at[place].set(weighted)
    high_part = (
        jnp.zeros((owners * capacity,), jnp.bfloat16)
        .at[place]
        .set((bucket // 128).astype(jnp.bfloat16))
    )
    low_part = (
        jnp.zeros((owners * capacity,), jnp.bfloat16)
        .at[place]
        .set((bucket % 128).astype(jnp.bfloat16))
    )
    arrived, high_in, low_in = (
        lax.all_to_all(
            outgoing.reshape(owners, capacity, width),
            ("key", "shard"),
            split_axis=0,
            concat_axis=0,
            tiled=True,
        ),
        lax.all_to_all(
            high_part.reshape(owners, capacity),
            ("key", "shard"),
            split_axis=0,
            concat_axis=0,
            tiled=True,
        ),
        lax.all_to_all(
            low_part.reshape(owners, capacity),
            ("key", "shard"),
            split_axis=0,
            concat_axis=0,
            tiled=True,
        ),
    )
    received = arrived.reshape(owners * capacity, width)
    arrival = (high_in.astype(jnp.int32) * 128 + low_in.astype(jnp.int32)).reshape(
        owners * capacity
    )
    block_rows = 256
    count_blocks = owners * capacity // block_rows
    slot_index = jnp.arange(slots, dtype=jnp.int32)

    def add_block(total, pair):
        values, index = pair
        hot_table = (slot_index[:, None] == index[None, :]).astype(jnp.bfloat16)
        return (total + jnp.dot(hot_table, values, preferred_element_type=jnp.float32), None)

    summed, _ = lax.scan(
        add_block,
        jnp.zeros((slots, width), jnp.float32),
        (
            received.reshape(count_blocks, block_rows, width),
            arrival.reshape(count_blocks, block_rows),
        ),
    )
    summed_round = summed.astype(jnp.bfloat16)
    user_mark = segment + 1
    mark_high = (user_mark // 128).astype(jnp.bfloat16)
    mark_low = (user_mark % 128).astype(jnp.bfloat16)
    tail_sums, tail_high, tail_low = from_behind(
        (summed_round[slots - window :], mark_high[slots - window :], mark_low[slots - window :]),
        ("key", "shard"),
        1,
    )
    tail_marks = tail_high.astype(jnp.int32) * 128 + tail_low.astype(jnp.int32)
    extended = jnp.concatenate([tail_sums, summed_round], axis=0)
    marks_ext = jnp.concatenate([tail_marks, user_mark])
    block = min(512, slots)
    span = block + window
    groups = decay_rate.shape[0]
    group_cols = width // groups
    gap = (
        jnp.arange(block, dtype=jnp.int32)[:, None]
        + window
        - jnp.arange(span, dtype=jnp.int32)[None, :]
    )
    inside = (gap >= 0) & (gap <= window)
    gap_float = gap.astype(jnp.float32)
    decay_table = jnp.exp(-decay_rate[:, None, None] * gap_float[None])
    pieces = []
    for start in range(0, slots, block):
        source = extended[start : start + span]
        source_marks = marks_ext[start : start + span]
        query_marks = marks_ext[window + start : window + start + block]
        keep = inside & (query_marks[:, None] == source_marks[None, :])
        count = jnp.sum(keep.astype(jnp.float32), axis=1)
        factor = jnp.where(keep[None], decay_table, jnp.float32(0.0)).astype(jnp.bfloat16)
        mixed = jnp.einsum(
            "gim,mgc->igc",
            factor,
            source.reshape(span, groups, group_cols),
            preferred_element_type=jnp.float32,
        )
        pieces.append(
            (mixed.reshape(block, width) * lax.rsqrt(count)[:, None]).astype(jnp.bfloat16)
        )
    table = jnp.concatenate(pieces, axis=0)

    def fetch(index):
        hot_table = (index[:, None] == slot_index[None, :]).astype(jnp.bfloat16)
        return jnp.dot(hot_table, table, preferred_element_type=jnp.float32).astype(jnp.bfloat16)

    answered = lax.map(fetch, arrival.reshape(count_blocks, block_rows))
    returned = lax.all_to_all(
        answered.reshape(owners, capacity, width),
        ("key", "shard"),
        split_axis=0,
        concat_axis=0,
        tiled=True,
    )
    event_features = returned.reshape(owners * capacity, width)[place]
    return (table, event_features)


def solution(mesh):
    placed = (
        P(("groups", "key", "shard"), "lane"),
        P(("groups", "key", "shard")),
        P(("groups", "key", "shard"), None),
        P(("groups", "key", "shard")),
        P(("groups", "key", "shard")),
        P("lane"),
    )
    return jax.shard_map(
        on_device,
        mesh=mesh,
        in_specs=placed,
        out_specs=(P(("groups", "key", "shard"), "lane"), P(("groups", "key", "shard"), "lane")),
        check_vma=False,
    )
```

profile of v0, /device:TPU:0, one launch (start us, length us, event | category | flops | bytes accessed | tf_op | source)
XLA Modules:
  0.0 147.6 jit_solution(7340855356768285098)
XLA Ops:
  2.2 4.8 %collective-permute-start.1 = (bf16[1024]{0:T(1024)(128)(2,1)S(1)}, bf16[1024]{0:T(1024)(128)(2,1)S(1)}, u32[]{:S(2)}, u32[]{:S(2)}) collective-permute-start(bf16[1024]{0:T(1024)(128)(2,1)S(1)} %get-tuple-element.140), channel_id=1, source_target_pairs={{0,2},{2,4},{4,6},{6,8},{8,10},{10,12},{12,14},{1,3},{3,5},{5,7},{... | collective-permute-start | bytes 6152 | tf_op jit(solution)/shard_map/ppermute | solution.py:10
  7.0 3.5 %collective-permute-start.2 = (bf16[1024]{0:T(1024)(128)(2,1)S(1)}, bf16[1024]{0:T(1024)(128)(2,1)S(1)}, u32[]{:S(2)}, u32[]{:S(2)}) collective-permute-start(bf16[1024]{0:T(1024)(128)(2,1)S(1)} %get-tuple-element.141), channel_id=1, source_target_pairs={{0,2},{2,4},{4,6},{6,8},{8,10},{10,12},{12,14},{1,3},{3,5},{5,7},{... | collective-permute-start | bytes 6152 | tf_op jit(solution)/shard_map/ppermute | solution.py:10
  14.7 3.8 %scatter_custom_fusion = bf16[1024]{0:T(1024)(128)(2,1)S(1)} fusion(s32[512]{0:T(512)S(1)} %bitcast.100, bf16[512]{0:T(512)(128)(2,1)S(1)} %get-tuple-element.150, bf16[]{:T(256)} %constant.77.clone.1), kind=kCustom, calls=%fused_computation.128 | custom fusion | bytes 2050 | tf_op jit(solution)/shard_map/scatter | solution.py:35
  19.1 4.8 %all-to-all-start = ((bf16[8,1,128]{2,1,0:T(2,128)(2,1)}), bf16[8,1,128]{2,1,0:T(2,128)(2,1)S(1)}, u32[]{:S(2)}, u32[]{:S(2)}) async-start(bf16[8,1,128]{2,1,0:T(2,128)(2,1)} %copy.56), calls=%async_computation | async-start | bytes 8192 | tf_op jit(solution)/shard_map/all_to_all | solution.py:50
  25.8 3.8 %scatter_custom_fusion.1 = bf16[1024]{0:T(1024)(128)(2,1)S(1)} fusion(s32[512]{0:T(512)S(1)} %bitcast.101, bf16[512]{0:T(512)(128)(2,1)S(1)} %get-tuple-element.151, bf16[]{:T(256)} %constant.77.clone.1), kind=kCustom, calls=%fused_computation.126 | custom fusion | bytes 2050 | tf_op jit(solution)/shard_map/scatter | solution.py:40
  33.4 6.0 %all-to-all-start.1 = ((bf16[8,1,128]{2,1,0:T(2,128)(2,1)}), bf16[8,1,128]{2,1,0:T(2,128)(2,1)S(1)}, u32[]{:S(2)}, u32[]{:S(2)}) async-start(bf16[8,1,128]{2,1,0:T(2,128)(2,1)} %copy.57), calls=%async_computation.1 | async-start | bytes 8192 | tf_op jit(solution)/shard_map/all_to_all | solution.py:57
  39.4 6.4 %all-to-all-done.1 = bf16[8,1,128]{2,1,0:T(2,128)(2,1)S(1)} async-done(((bf16[8,1,128]{2,1,0:T(2,128)(2,1)}), bf16[8,1,128]{2,1,0:T(2,128)(2,1)S(1)}, u32[]{:S(2)}, u32[]{:S(2)}) %all-to-all-start.1) | async-done | bytes 2080 | tf_op jit(solution)/shard_map/all_to_all | solution.py:57
  45.8 3.6 %all-to-all-start.2 = ((bf16[8,128,128]{2,1,0:T(8,128)(2,1)}), bf16[8,128,128]{2,1,0:T(8,128)(2,1)S(1)}, u32[]{:S(2)}, u32[]{:S(2)}) async-start(bf16[8,128,128]{2,1,0:T(8,128)(2,1)} %bitcast.8), calls=%async_computation.2 | async-start | bytes 524288 | tf_op jit(solution)/shard_map/all_to_all | solution.py:43
  49.4 6.0 %compare_and_fusion = (pred[512,1536]{1,0:T(8,128)(4,1)}, pred[512,1536]{1,0:T(8,128)(4,1)}, pred[512,1536]{1,0:T(8,128)(4,1)}, pred[512,1536]{1,0:T(8,128)(4,1)...) fusion(s32[1536]{0:T(1024)S(1)} %get-tuple-element.138, ...), kind=kLoop, calls=%fused_computation.58 | loop fusion | flops 15728640 | bytes 6359040 | tf_op jit(solution)/shard_map/and | solution.py:115
  57.4 5.6 %while.23 = (s32[]{:T(128)}, f32[4096,128]{1,0:T(8,128)S(1)}, s32[4,256]{1,0:T(4,128)S(1)}, bf16[4,256,128]{2,1,0:T(8,128)(2,1)S(1)}, s32[]{:T(128)}, /*index=5*/s32[]{:T(128)}) while((s32[]{:T(128)}, f32[4096,128]{1,0:T(8,128)S(1)}, s32[4,256]{1,0:T(4,128)S(1)}, bf16[4,256,128]{2,1,0:T(8,128)(2,1)S(1)}, s32[]{:T(128)}, ...), condition=%wide.region_7.8_spmd.clone, body=%wide.region_6.7_spmd.clone.sunk | while | flops 270532608 | bytes 4262999 | solution.py:78
  65.0 5.5 %convert_reduce_fusion = (f32[512]{0:T(512)S(1)}, f32[512]{0:T(512)S(1)}, f32[512]{0:T(512)S(1)}, f32[512]{0:T(512)S(1)}, f32[512]{0:T(512)S(1)}, /*index=5*/f32[512]{0:T(512)S(1)}, f32[512]{0:T(512)S(1)}, f32[512]{0:T(512)S(1)}) fusion(s32[1536]{0:T(1024)S(1)} %get-tuple-element.138, s32[512]{0:T(512)S(1)} %get-tuple-element.131, s32[512]{0:T(512)S(1)} %iota_add_fusion, ...), kind=kLoop, calls=%fused_computation.45 | loop fusion | flops 28307456 | bytes 83968 | tf_op jit(solution)/shard_map/reduce_sum | solution.py:116
  73.7 4.6 %fusion.15 = f32[4,32,512]{2,1,0:T(8,128)} fusion(bf16[1536,4,32]{0,2,1:T(8,128)(2,1)S(1)} %bitcast.81, f32[512,1536]{1,0:T(8,128)} %fusion.29, f32[4]{0:T(128)} %neg.4, pred[512,1536]{1,0:T(8,128)(4,1)} %get-tuple-element.144), kind=kOutput, calls=%fused_computation.31 | convolution fusion | flops 210763776 | bytes 4587536 | tf_op jit(solution)/shard_map/gim,mgc->igc/dot_general | solution.py:118
  79.6 4.6 %fusion.14 = f32[4,32,512]{2,1,0:T(8,128)} fusion(bf16[1536,4,32]{0,2,1:T(8,128)(2,1)S(1)} %bitcast.82, f32[512,1536]{1,0:T(8,128)} %fusion.29, f32[4]{0:T(128)} %neg.4, pred[512,1536]{1,0:T(8,128)(4,1)} %get-tuple-element.143), kind=kOutput, calls=%fused_computation.30 | convolution fusion | flops 210763776 | bytes 4587536 | tf_op jit(solution)/shard_map/gim,mgc->igc/dot_general | solution.py:118
  85.5 4.6 %fusion.13 = f32[4,32,512]{2,1,0:T(8,128)} fusion(bf16[1536,4,32]{0,2,1:T(8,128)(2,1)S(1)} %bitcast.83, f32[512,1536]{1,0:T(8,128)} %fusion.29, f32[4]{0:T(128)S(1)} %copy-done.11, pred[512,1536]{1,0:T(8,128)(4,1)} %get-tuple-element.149), kind=kOutput, calls=%fused_computation.29 | convolution fusion | flops 210763776 | bytes 4587536 | tf_op jit(solution)/shard_map/gim,mgc->igc/dot_general | solution.py:118
  91.3 4.6 %fusion.16 = f32[4,32,512]{2,1,0:T(8,128)} fusion(bf16[1536,4,32]{0,2,1:T(8,128)(2,1)S(1)} %bitcast.84, f32[512,1536]{1,0:T(8,128)} %fusion.29, f32[4]{0:T(128)S(1)} %copy-done.11, pred[512,1536]{1,0:T(8,128)(4,1)} %get-tuple-element.145), kind=kOutput, calls=%fused_computation.32 | convolution fusion | flops 210763776 | bytes 4587536 | tf_op jit(solution)/shard_map/gim,mgc->igc/dot_general | solution.py:118
  97.1 4.5 %fusion.17 = f32[4,32,512]{2,1,0:T(8,128)} fusion(bf16[1536,4,32]{0,2,1:T(8,128)(2,1)S(1)} %bitcast.85, f32[512,1536]{1,0:T(8,128)} %fusion.29, f32[4]{0:T(128)S(1)} %copy-done.11, pred[512,1536]{1,0:T(8,128)(4,1)} %get-tuple-element.146), kind=kOutput, calls=%fused_computation.33 | convolution fusion | flops 210763776 | bytes 4587536 | tf_op jit(solution)/shard_map/gim,mgc->igc/dot_general | solution.py:118
  103.0 4.6 %fusion.18 = f32[4,32,512]{2,1,0:T(8,128)} fusion(bf16[1536,4,32]{0,2,1:T(8,128)(2,1)S(1)} %bitcast.86, f32[512,1536]{1,0:T(8,128)} %fusion.29, f32[4]{0:T(128)S(1)} %copy-done.11, pred[512,1536]{1,0:T(8,128)(4,1)} %get-tuple-element.147), kind=kOutput, calls=%fused_computation.34 | convolution fusion | flops 210763776 | bytes 4587536 | tf_op jit(solution)/shard_map/gim,mgc->igc/dot_general | solution.py:118
  108.8 4.6 %fusion.19 = f32[4,32,512]{2,1,0:T(8,128)} fusion(bf16[1536,4,32]{0,2,1:T(8,128)(2,1)S(1)} %bitcast.87, f32[512,1536]{1,0:T(8,128)} %fusion.29, f32[4]{0:T(128)S(1)} %copy-done.11, pred[512,1536]{1,0:T(8,128)(4,1)} %get-tuple-element.148), kind=kOutput, calls=%fused_computation.35 | convolution fusion | flops 210763776 | bytes 4587536 | tf_op jit(solution)/shard_map/gim,mgc->igc/dot_general | solution.py:118
  114.7 4.5 %fusion.20 = f32[4,32,512]{2,1,0:T(8,128)} fusion(bf16[1536,4,32]{0,2,1:T(8,128)(2,1)S(1)} %bitcast.80, f32[512,1536]{1,0:T(8,128)} %fusion.29, f32[4]{0:T(128)S(1)} %copy-done.11, pred[512,1536]{1,0:T(8,128)(4,1)} %get-tuple-element.142), kind=kOutput, calls=%fused_computation.36 | convolution fusion | flops 210763776 | bytes 4587536 | tf_op jit(solution)/shard_map/gim,mgc->igc/dot_general | solution.py:118
  122.6 10.4 %while.22 = (s32[]{:T(128)}, bf16[4,256,128]{2,1,0:T(8,128)(2,1)}, s32[4,256]{1,0:T(4,128)S(1)}, bf16[4096,128]{1,0:T(8,128)(2,1)}, s32[]{:T(128)}) while((s32[]{:T(128)}, bf16[4,256,128]{2,1,0:T(8,128)(2,1)}, s32[4,256]{1,0:T(4,128)S(1)}, bf16[4096,128]{1,0:T(8,128)(2,1)}, s32[]{:T(128)}) %tuple.91), condition=%wide.region_17.18_spmd.clone, body=%wide.region_16.17_spmd.clone.sunk | while | flops 269516800 | bytes 1117761 | solution.py:133
  122.6 2.6 %fusion.81 = bf16[4,256,128]{2,1,0:T(8,128)(2,1)} fusion(bf16[4,256,128]{2,1,0:T(8,128)(2,1)} %get-tuple-element.226, s32[]{:T(128)} %get-tuple-element.225, bf16[4096,128]{1,0:T(8,128)(2,1)} %get-tuple-element.233, s32[256]{0:T(256)S(1)} %bitcast.97), kind=kOutput, calls=%fused_computation.11.clone.1 | convolution fusion | flops 269516800 | bytes 1115648 | tf_op jit(solution)/shard_map/while/body/eval_jaxpr/dot_general | solution.py:131
  127.9 2.6 %fusion.81 = bf16[4,256,128]{2,1,0:T(8,128)(2,1)} fusion(bf16[4,256,128]{2,1,0:T(8,128)(2,1)} %get-tuple-element.226, s32[]{:T(128)} %get-tuple-element.225, bf16[4096,128]{1,0:T(8,128)(2,1)} %get-tuple-element.233, s32[256]{0:T(256)S(1)} %bitcast.97), kind=kOutput, calls=%fused_computation.11.clone.1 | convolution fusion | flops 269516800 | bytes 1115648 | tf_op jit(solution)/shard_map/while/body/eval_jaxpr/dot_general | solution.py:131
  133.1 4.4 %all-to-all-start.3 = ((bf16[8,128,128]{2,1,0:T(8,128)(2,1)}), bf16[8,128,128]{2,1,0:T(8,128)(2,1)S(1)}, u32[]{:S(2)}, u32[]{:S(2)}) async-start(bf16[8,128,128]{2,1,0:T(8,128)(2,1)} %bitcast.34), calls=%async_computation.3 | async-start | bytes 524288 | tf_op jit(solution)/shard_map/all_to_all | solution.py:134
  137.5 8.2 %all-to-all-done.3 = bf16[8,128,128]{2,1,0:T(8,128)(2,1)S(1)} async-done(((bf16[8,128,128]{2,1,0:T(8,128)(2,1)}), bf16[8,128,128]{2,1,0:T(8,128)(2,1)S(1)}, u32[]{:S(2)}, u32[]{:S(2)}) %all-to-all-start.3) | async-done | bytes 262176 | tf_op jit(solution)/shard_map/all_to_all | solution.py:134
  (105 shorter events, 43.9 us)
Async XLA Ops:
  0.6 29.6 %copy-start.10 = (f32[4]{0:T(128)S(1)}, f32[4]{0:T(128)}, u32[]{:S(2)}) copy-start(f32[4]{0:T(128)} %param.15) | copy-start | bytes 52
  0.6 30.2 %copy-start = (bf16[512,128]{1,0:T(8,128)(2,1)S(1)}, bf16[512,128]{1,0:T(8,128)(2,1)}, u32[]{:S(2)}) copy-start(bf16[512,128]{1,0:T(8,128)(2,1)} %param.10) | copy-start | bytes 393220
  0.6 30.2 %copy-start.9 = (f32[512]{0:T(512)S(1)}, f32[512]{0:T(512)}, u32[]{:S(2)}) copy-start(f32[512]{0:T(512)} %param.11) | copy-start | bytes 6148
  2.2 31.2 %collective-permute-start.1 = (bf16[1024]{0:T(1024)(128)(2,1)S(1)}, bf16[1024]{0:T(1024)(128)(2,1)S(1)}, u32[]{:S(2)}, u32[]{:S(2)}) collective-permute-start(bf16[1024]{0:T(1024)(128)(2,1)S(1)} %get-tuple-element.140), channel_id=1, source_target_pairs={{0,2},{2,4},{4,6},{6,8},{8,10},{10,12},{12,14},{1,3},{3,5},{5,7},{... | collective-permute-start | bytes 6152 | tf_op jit(solution)/shard_map/ppermute | solution.py:10
  7.0 26.4 %collective-permute-start.2 = (bf16[1024]{0:T(1024)(128)(2,1)S(1)}, bf16[1024]{0:T(1024)(128)(2,1)S(1)}, u32[]{:S(2)}, u32[]{:S(2)}) collective-permute-start(bf16[1024]{0:T(1024)(128)(2,1)S(1)} %get-tuple-element.141), channel_id=1, source_target_pairs={{0,2},{2,4},{4,6},{6,8},{8,10},{10,12},{12,14},{1,3},{3,5},{5,7},{... | collective-permute-start | bytes 6152 | tf_op jit(solution)/shard_map/ppermute | solution.py:10
  14.0 19.4 %copy-start.7 = (s32[512,1]{0,1:T(1,128)}, s32[512,1]{0,1:T(1,128)S(1)}, u32[]{:S(2)}) copy-start(s32[512,1]{0,1:T(1,128)S(1)} %compare_select_fusion) | copy-start | bytes 6148
  19.1 14.3 %all-to-all-start = ((bf16[8,1,128]{2,1,0:T(2,128)(2,1)}), bf16[8,1,128]{2,1,0:T(2,128)(2,1)S(1)}, u32[]{:S(2)}, u32[]{:S(2)}) async-start(bf16[8,1,128]{2,1,0:T(2,128)(2,1)} %copy.56), calls=%async_computation | async-start | bytes 8192 | tf_op jit(solution)/shard_map/all_to_all | solution.py:50
  33.4 12.4 %all-to-all-start.1 = ((bf16[8,1,128]{2,1,0:T(2,128)(2,1)}), bf16[8,1,128]{2,1,0:T(2,128)(2,1)S(1)}, u32[]{:S(2)}, u32[]{:S(2)}) async-start(bf16[8,1,128]{2,1,0:T(2,128)(2,1)} %copy.57), calls=%async_computation.1 | async-start | bytes 8192 | tf_op jit(solution)/shard_map/all_to_all | solution.py:57
  45.8 11.6 %all-to-all-start.2 = ((bf16[8,128,128]{2,1,0:T(8,128)(2,1)}), bf16[8,128,128]{2,1,0:T(8,128)(2,1)S(1)}, u32[]{:S(2)}, u32[]{:S(2)}) async-start(bf16[8,128,128]{2,1,0:T(8,128)(2,1)} %bitcast.8), calls=%async_computation.2 | async-start | bytes 524288 | tf_op jit(solution)/shard_map/all_to_all | solution.py:43
  63.1 10.2 %collective-permute-start = (bf16[1024,128]{1,0:T(8,128)(2,1)S(1)}, bf16[1024,128]{1,0:T(8,128)(2,1)S(1)}, u32[]{:S(2)}, u32[]{:S(2)}) collective-permute-start(bf16[1024,128]{1,0:T(8,128)(2,1)S(1)} %slice.119), channel_id=1, source_target_pairs={{0,2},{2,4},{4,6},{6,8},{8,10},{10,12},{12,14},{1,3},{3,5},{5,7},{... | collective-permute-start | bytes 786440 | tf_op jit(solution)/shard_map/ppermute | solution.py:10
  79.6 5.9 %copy-start.11 = (f32[4]{0:T(128)S(1)}, f32[4]{0:T(128)}, u32[]{:S(2)}) copy-start(f32[4]{0:T(128)} %neg.4) | copy-start | bytes 52
  114.6 5.7 %copy-start.6 = (f32[512]{0:T(512)S(1)}, f32[512]{0:T(512)}, u32[]{:S(2)}) copy-start(f32[512]{0:T(512)} %rsqrt.56) | copy-start | bytes 6148
  114.6 5.8 %copy-start.5 = (f32[512]{0:T(512)S(1)}, f32[512]{0:T(512)}, u32[]{:S(2)}) copy-start(f32[512]{0:T(512)} %rsqrt.57) | copy-start | bytes 6148
  114.6 6.0 %copy-start.4 = (f32[512]{0:T(512)S(1)}, f32[512]{0:T(512)}, u32[]{:S(2)}) copy-start(f32[512]{0:T(512)} %rsqrt.58) | copy-start | bytes 6148
  114.6 6.2 %copy-start.3 = (f32[512]{0:T(512)S(1)}, f32[512]{0:T(512)}, u32[]{:S(2)}) copy-start(f32[512]{0:T(512)} %rsqrt.59) | copy-start | bytes 6148
  114.7 6.3 %copy-start.2 = (f32[512]{0:T(512)S(1)}, f32[512]{0:T(512)}, u32[]{:S(2)}) copy-start(f32[512]{0:T(512)} %rsqrt.60) | copy-start | bytes 6148
  121.7 1.0 copy-start.1
  122.6 14.8 %copy-start.8 = (s32[512,1]{0,1:T(1,128)S(1)}, s32[512,1]{0,1:T(1,128)}, u32[]{:S(2)}) copy-start(s32[512,1]{0,1:T(1,128)} %copy-done.7) | copy-start | bytes 6148
  133.1 12.6 %all-to-all-start.3 = ((bf16[8,128,128]{2,1,0:T(8,128)(2,1)}), bf16[8,128,128]{2,1,0:T(8,128)(2,1)S(1)}, u32[]{:S(2)}, u32[]{:S(2)}) async-start(bf16[8,128,128]{2,1,0:T(8,128)(2,1)} %bitcast.34), calls=%async_computation.3 | async-start | bytes 524288 | tf_op jit(solution)/shard_map/all_to_all | solution.py:134
where the time goes:
time: 149 us; the launch traced here: 148 us
  matrix products  52.3 us (35%)
  starting transfers between devices  29 us (19%)
  local copies, waits for them, and re-layouts  24.8 us (17%)
  other arithmetic  23.8 us (16%)
  waiting for transfers between devices  16.5 us (11%)
    dot_general x8, matrix products, on_device(): jnp.einsum('gim,mgc->igc', factor, source.reshape(span, groups, group_col...  36.5 us
    dot_general x4, matrix products, fetch(): jnp.dot(hot_table, table, preferred_element_type=jnp.float32)  10.4 us
    ppermute x3, starting transfers between devices, from_behind(): return lax.ppermute(block, axis, route)  10.2 us
    reshape x8, local copies, waits for them, and re-layouts, on_device(): mixed.reshape(block, width) * lax.rsqrt(count)[:, None]  8.56 us
    all_to_all x1, waiting for transfers between devices, on_device(): lax.all_to_all(answered.reshape(owners, capacity, width), ('key', 'shard'...  8.2 us
    all_to_all x1, waiting for transfers between devices, on_device(): lax.all_to_all(low_part.reshape(owners, capacity), ('key', 'shard'), spli...  6.38 us
    and x1, other arithmetic, on_device(): keep = inside & (query_marks[:, None] == source_marks[None, :])  6.03 us
    all_to_all x1, starting transfers between devices, on_device(): lax.all_to_all(low_part.reshape(owners, capacity), ('key', 'shard'), spli...  6.01 us
  transfers between devices with their start and end apart: 7, of which 3 were waited for; matrix products, arithmetic and copies ran while one was open for 22% of the time, Pallas kernels for 0%

commit v1 on v0

v1 whole, which is shorter than its diff:
```python
import functools
import jax
import jax.numpy as jnp
from jax import lax
from jax.experimental import pallas as pl
from jax.experimental.pallas import tpu as pltpu
from jax.sharding import PartitionSpec as P

LANES = 128
LOW = 7
MASK = 127
F32 = jnp.float32
BF16 = jnp.bfloat16
I32 = jnp.int32
FAR = 1e9
NT = (((1,), (1,)), ((), ()))


def dims(owners, rows, slots):
    chunks = rows // LANES
    users = 8 * owners
    user_rows = -(-users // LANES)
    code_rows = -(-(3 * chunks + 2 * user_rows) // 16) * 16
    span = min(owners, 8)
    return chunks, user_rows, code_rows, span


def iota(shape, axis):
    return lax.broadcasted_iota(I32, shape, axis)


def rate_row(rate_ref):
    groups = rate_ref.shape[0]
    lane = iota((1, LANES), 1)
    row = jnp.full((1, LANES), rate_ref[0], F32)
    for g in range(1, groups):
        row = jnp.where(lane >= g * (LANES // groups), rate_ref[g], row)
    return row


def send_kernel(owners, slots, rate_ref, events_ref, weight_ref, route_ref, bucket_ref, segment_ref, out_ref):
    rows = events_ref.shape[0]
    chunks, user_rows, code_rows, span = dims(owners, rows, slots)
    rate = rate_row(rate_ref)
    route = route_ref[...]
    bucket = bucket_ref[...]
    spot = (route & (span - 1)) * slots + bucket - span * slots // 2
    columns = jnp.concatenate([weight_ref[...], spot.astype(F32)], axis=0).T
    for r in range(chunks):
        part = pl.ds(r * LANES, LANES)
        weighted = (columns[:, r : r + 1] * events_ref[part, :].astype(F32)).astype(BF16)
        grown = weighted.astype(F32) * jnp.exp(columns[:, chunks + r : chunks + r + 1] * rate)
        out_ref[part, :] = grown.astype(BF16)
    ones = jnp.ones((8, LANES), BF16)
    high, low = [], []
    for u in range(user_rows):
        user = iota((LANES, LANES), 0) + u * LANES
        below = jnp.zeros((LANES, LANES), F32)
        for r in range(slots // LANES):
            below += jnp.where(segment_ref[r : r + 1, :] < user, F32(1), F32(0))
        count = lax.dot_general(ones, below.astype(BF16), NT, preferred_element_type=F32)[0:1].astype(I32)
        high.append(count >> LOW)
        low.append(count & MASK)
    spare = code_rows - 3 * chunks - 2 * user_rows
    pad = [jnp.zeros((spare, LANES), I32)] if spare else []
    codes = jnp.concatenate([route, bucket >> LOW, bucket & MASK] + high + low + pad, axis=0)
    out_ref[pl.ds(rows, code_rows), :] = codes.astype(F32).astype(BF16)


def each(count, body):
    if count <= 8:
        for i in range(count):
            body(i)
    else:
        lax.fori_loop(0, count, lambda i, c: (body(i), c)[1], 0)


def gather_kernel(
    owners, rows, slots, me_ref, rate_ref, route_ref, bucket_ref, all_ref,
    table_ref, feature_ref,
    place_ref, until_ref, own_ref, tail_ref, codes_ref, rows_ref, from_ref, last_ref, total_ref,
):
    chunks, user_rows, code_rows, span = dims(owners, rows, slots)
    window = slots // 4
    block_rows = rows + code_rows
    capacity = 2 * rows // owners
    per_group = LANES // capacity
    groups = owners // per_group
    me = me_ref[0]
    base = (me * slots).astype(F32)
    rate = rate_row(rate_ref)

    starts = []
    for u in range(user_rows):
        def add(s, total):
            tile = all_ref[pl.ds(pl.multiple_of(s * block_rows + rows, 16), code_rows), :].astype(F32)
            at = 3 * chunks + u
            return total + F32(LANES) * tile[at : at + 1] + tile[at + user_rows : at + user_rows + 1]

        starts.append(lax.fori_loop(0, owners, add, jnp.zeros((1, LANES), F32), unroll=owners <= 8))
    start_columns = [jnp.broadcast_to(row, (8, LANES)).T[:, 0:1] for row in starts]
    steps = []
    for u in range(user_rows):
        before = pltpu.roll(starts[u], 1, 1)
        first = starts[u - 1][:, LANES - 1 : LANES] if u else jnp.zeros((1, 1), F32)
        step = (starts[u] - jnp.where(iota((1, LANES), 1) == 0, first, before)).astype(I32)
        pair = jnp.concatenate([jnp.broadcast_to(step >> LOW, (LANES, LANES)), jnp.broadcast_to(step & MASK, (LANES, LANES))], axis=0)
        steps.append(pair.astype(F32).astype(BF16))

    def run_start(position):
        total = jnp.zeros((position.shape[0], 2 * LANES), F32)
        for u in range(user_rows):
            reached = jnp.where(starts[u] <= position, F32(1), F32(0)).astype(BF16)
            total += lax.dot_general(reached, steps[u], NT, preferred_element_type=F32)
        return F32(LANES) * total[:, :LANES] + total[:, LANES:]

    def root(position):
        return lax.rsqrt(jnp.minimum(position - run_start(position), F32(window)) + F32(1))

    def decode(s):
        tile = all_ref[pl.ds(pl.multiple_of(s * block_rows + rows, 16), code_rows), :].astype(F32)
        route = tile[0:chunks]
        bucket = F32(LANES) * tile[chunks : 2 * chunks] + tile[2 * chunks : 3 * chunks]
        place = route * F32(slots) + bucket
        until = []
        for r in range(chunks):
            row = place[r : r + 1]
            after = jnp.full((1, LANES), FAR, F32)
            for column in start_columns:
                later = jnp.where(column > row, column, F32(FAR))
                after = jnp.minimum(after, jnp.min(later, axis=0, keepdims=True))
            until.append(jnp.minimum(row + F32(window), after - F32(1)))
        until = jnp.concatenate(until, axis=0)
        local = place - base
        end = until - base
        near = (local.astype(I32), end.astype(I32))
        codes = jnp.concatenate([near[0] >> LOW, near[0] & MASK, near[1] >> LOW, near[1] & MASK], axis=0)
        spare = jnp.full((8 - chunks, LANES), -1, F32)
        place_ref[s] = jnp.concatenate([place, spare], axis=0)
        until_ref[s] = jnp.concatenate([until, spare], axis=0)
        codes_ref[s] = codes.astype(F32)
        own = (local >= 0) & (local < F32(slots))
        tail = (local >= F32(-window)) & (local < 0)
        spare = jnp.zeros((8 - chunks, LANES), F32)
        own_ref[s] = jnp.concatenate([jnp.where(own, F32(1), F32(0)), spare], axis=0)
        tail_ref[s] = jnp.concatenate([jnp.where(tail, F32(1), F32(0)), spare], axis=0)

    each(owners, decode)

    upper = jnp.where(iota((LANES, LANES), 0) < iota((LANES, LANES), 1), F32(1), F32(0)).astype(BF16)
    full = jnp.ones((LANES, LANES), BF16)
    lines = owners * 8
    at, by = iota((lines, lines), 0), iota((lines, lines), 1)
    earlier = jnp.where(((at >> 3) == (by >> 3)) & (by < at), F32(1), F32(0)).astype(BF16)
    for ref in (own_ref, tail_ref):
        marked = ref[...].reshape(lines, LANES)
        mark = marked.astype(BF16)
        inner = jnp.dot(mark, upper, preferred_element_type=F32)
        sums = jnp.dot(mark, full, preferred_element_type=F32).astype(BF16)
        rank = inner + jnp.dot(earlier, sums, preferred_element_type=F32)
        source = iota((lines, LANES), 0) >> 3
        rank += ((source & (per_group - 1)) * capacity).astype(F32)
        ref[...] = jnp.where(marked > 0, rank, F32(-1)).reshape(owners, 8, LANES)

    spots = iota((LANES, LANES), 0).astype(F32)
    code_line = iota((4 * chunks, LANES), 0) & (chunks - 1)

    def pack(kind, ref, g):
        def add(i, carry):
            values, places = carry
            s = g * per_group + i
            ranks = ref[s]
            codes = codes_ref[s]
            hot = jnp.concatenate(
                [jnp.where(spots == ranks[r : r + 1], F32(1), F32(0)).astype(BF16) for r in range(chunks)], axis=1
            )
            wide = jnp.concatenate(
                [jnp.where(code_line == r, codes, F32(0)).astype(BF16) for r in range(chunks)], axis=1
            )
            block = all_ref[pl.ds(pl.multiple_of(s * block_rows, 16), rows), :]
            values += jnp.dot(hot, block, preferred_element_type=F32)
            places += lax.dot_general(wide, hot, NT, preferred_element_type=F32)
            return values, places

        zero = (jnp.zeros((LANES, LANES), F32), jnp.zeros((4 * chunks, LANES), F32))
        values, places = lax.fori_loop(0, per_group, add, zero, unroll=per_group == 1)
        line = kind * groups + g
        rows_ref[line * LANES : (line + 1) * LANES, :] = values.astype(BF16)
        part = [jnp.sum(places[k * chunks : (k + 1) * chunks], axis=0, keepdims=True) for k in range(4)]
        from_ref[line : line + 1, :] = F32(LANES) * part[0] + part[1]
        last_ref[line : line + 1, :] = F32(LANES) * part[2] + part[3]

    for kind, ref in enumerate((own_ref, tail_ref)):
        for g in range(groups):
            pack(kind, ref, g)

    block = 256
    own_offset = ((me & (span - 1)) * slots - span * slots // 2).astype(F32)
    tail_offset = (((me - 1) & (span - 1)) * slots + slots - span * slots // 2).astype(F32)
    inner = iota((block, LANES), 0)

    def summed(position, kind):
        masks = []
        for g in range(groups):
            line = kind * groups + g
            held = (position >= from_ref[line : line + 1, :]) & (position <= last_ref[line : line + 1, :])
            masks.append(jnp.where(held, F32(1), F32(0)).astype(BF16))
        held = jnp.concatenate(masks, axis=1)
        events = rows_ref[kind * groups * LANES : (kind + 1) * groups * LANES, :]
        return jnp.dot(held, events, preferred_element_type=F32)

    def table_block(b, with_tail):
        position = (inner + b * block).astype(F32)
        value = summed(position, 0) * jnp.exp(-rate * (position + own_offset))
        if with_tail:
            value += summed(position, 1) * jnp.exp(-rate * (position + tail_offset))
        value *= root(position + base)
        table_ref[pl.ds(pl.multiple_of(b * block, block), block), :] = value.astype(BF16)

    lax.fori_loop(0, window // block, lambda b, c: (table_block(b, True), c)[1], 0)
    lax.fori_loop(window // block, slots // block, lambda b, c: (table_block(b, False), c)[1], 0)

    route = route_ref[...]
    place = route * slots + bucket_ref[...]
    first = (route >> (span.bit_length() - 1)) * (span * slots)
    columns = jnp.concatenate([place, first], axis=0).astype(F32).T
    position = jnp.concatenate(
        [jnp.broadcast_to(columns[:, r : r + 1], (LANES, LANES)) for r in range(chunks)], axis=0
    )
    first = jnp.concatenate(
        [jnp.broadcast_to(columns[:, chunks + r : chunks + r + 1], (LANES, LANES)) for r in range(chunks)], axis=0
    )
    scale = root(position)
    value = jnp.zeros((rows, LANES), F32)
    for shift in (0,) if owners <= span else (0, 1):
        total_ref[...] = jnp.zeros((rows, LANES), F32)

        def add(s):
            begin, end = place_ref[s], until_ref[s]
            masks = []
            for r in range(chunks):
                held = (position >= begin[r : r + 1]) & (position <= end[r : r + 1])
                if owners > span:
                    inside = begin[r : r + 1] >= first
                    held &= inside if shift == 0 else jnp.logical_not(inside)
                masks.append(jnp.where(held, F32(1), F32(0)).astype(BF16))
            events = all_ref[pl.ds(pl.multiple_of(s * block_rows, 16), rows), :]
            total_ref[...] += jnp.dot(jnp.concatenate(masks, axis=1), events, preferred_element_type=F32)

        each(owners, add)
        center = first + F32(span * slots // 2 - shift * span * slots)
        value += total_ref[...] * jnp.exp(-rate * (position - center))
    feature_ref[...] = (value * scale).astype(BF16)


def on_device(events, event_weight, route, bucket, segment, decay_rate):
    rows, width = events.shape
    shard_count = lax.axis_size("shard")
    owners = lax.axis_size("key") * shard_count
    slots = segment.shape[0]
    chunks, user_rows, code_rows, span = dims(owners, rows, slots)
    block_rows = rows + code_rows
    smem = pl.BlockSpec(memory_space=pltpu.SMEM)
    vmem = pl.BlockSpec(memory_space=pltpu.VMEM)
    route = route.reshape(chunks, LANES)
    bucket = bucket.reshape(chunks, LANES)
    block = pl.pallas_call(
        functools.partial(send_kernel, owners, slots),
        out_shape=jax.ShapeDtypeStruct((block_rows, width), BF16),
        in_specs=[smem] + [vmem] * 5,
        out_specs=vmem,
        name="weigh",
    )(decay_rate, events, event_weight.reshape(chunks, LANES), route, bucket, segment.reshape(slots // LANES, LANES))
    gathered = lax.all_gather(block, ("key", "shard"), axis=0, tiled=True)
    me = (lax.axis_index("key") * shard_count + lax.axis_index("shard")).astype(I32).reshape(1)
    lines = 2 * rows // LANES * 2
    return pl.pallas_call(
        functools.partial(gather_kernel, owners, rows, slots),
        out_shape=(
            jax.ShapeDtypeStruct((slots, width), BF16),
            jax.ShapeDtypeStruct((rows, width), BF16),
        ),
        in_specs=[smem, smem] + [vmem] * 3,
        out_specs=(vmem, vmem),
        scratch_shapes=[
            pltpu.VMEM((owners, 8, LANES), F32),
            pltpu.VMEM((owners, 8, LANES), F32),
            pltpu.VMEM((owners, 8, LANES), F32),
            pltpu.VMEM((owners, 8, LANES), F32),
            pltpu.VMEM((owners, 4 * chunks, LANES), F32),
            pltpu.VMEM((lines * LANES, LANES), BF16),
            pltpu.VMEM((lines, LANES), F32),
            pltpu.VMEM((lines, LANES), F32),
            pltpu.VMEM((rows, LANES), F32),
        ],
        compiler_params=pltpu.CompilerParams(vmem_limit_bytes=56 * 1024 * 1024),
        name="aggregate",
    )(me, decay_rate, route, bucket, gathered)


def solution(mesh):
    placed = (
        P(("groups", "key", "shard"), "lane"),
        P(("groups", "key", "shard")),
        P(("groups", "key", "shard"), None),
        P(("groups", "key", "shard")),
        P(("groups", "key", "shard")),
        P("lane"),
    )
    return jax.shard_map(
        on_device,
        mesh=mesh,
        in_specs=placed,
        out_specs=(P(("groups", "key", "shard"), "lane"), P(("groups", "key", "shard"), "lane")),
        check_vma=False,
    )
```

time: 149 us -> 72.5 us (0.49)
  matrix products: 52.3 us -> 0 us
  starting transfers between devices: 29 us -> 0.04 us
  waiting for transfers between devices: 16.5 us -> 44.5 us
  local copies, waits for them, and re-layouts: 24.8 us -> 0 us
  other arithmetic: 23.8 us -> 0 us
  Pallas kernels: 0 us -> 13.8 us
  between operations: 1.1 us -> 14 us
    dot_general x16 -> x0, matrix products: 52.3 us -> none  [the longest x8 36.5 us: on_device(): jnp.einsum('gim,mgc->igc', factor, source.reshape(span, groups, group_col...]
    all_gather x0 -> x1, waiting for transfers between devices: none -> 44.5 us  [on_device(): gathered = lax.all_gather(block, ('key', 'shard'), axis=0, tiled=True)]
    all_to_all x4 -> x0, starting transfers between devices: 18.8 us -> none  [the longest x1 6.01 us: on_device(): lax.all_to_all(low_part.reshape(owners, capacity), ('key', 'shard'), spli...]
    all_to_all x4 -> x0, waiting for transfers between devices: 16.5 us -> none  [the longest x1 8.2 us: on_device(): lax.all_to_all(answered.reshape(owners, capacity, width), ('key', 'shard'...]
    pallas_call x0 -> x2, Pallas kernels: none -> 13.8 us  [the longest x1 11.7 us: on_device(): pl.pallas_call(functools.partial(gather_kernel, owners, rows, slots), out...]
    ppermute x3 -> x0, starting transfers between devices: 10.2 us -> none  [from_behind(): return lax.ppermute(block, axis, route)]
    reshape x8 -> x0, local copies, waits for them, and re-layouts: 8.56 us -> none  [on_device(): mixed.reshape(block, width) * lax.rsqrt(count)[:, None]]
    scatter x2 -> x0, local copies, waits for them, and re-layouts: 7.53 us -> none  [the longest x1 3.77 us: on_device(): low_part = jnp.zeros((owners * capacity,), jnp.bfloat16).at[place].set((b...]
  transfers between devices with their start and end apart: 7 -> 1, of which waited for: 3 -> 1; matrix products, arithmetic and copies ran while one was open for 22% -> 0% of each run, Pallas kernels for 0% -> 0%
where the time goes in v1:
time: 72.5 us; the launch traced here: 72.3 us
  waiting for transfers between devices  44.5 us (61%)
  between operations  14 us (19%)
  Pallas kernels  13.8 us (19%)
    all_gather x1, waiting for transfers between devices, on_device(): gathered = lax.all_gather(block, ('key', 'shard'), axis=0, tiled=True)  44.5 us
    pallas_call x1, Pallas kernels, on_device(): pl.pallas_call(functools.partial(gather_kernel, owners, rows, slots), out...  11.7 us
    pallas_call x1, Pallas kernels, on_device(): pl.pallas_call(functools.partial(send_kernel, owners, slots), out_shape=j...  2.07 us
  transfers between devices with their start and end apart: 1, of which 1 were waited for; matrix products, arithmetic and copies ran while one was open for 0% of the time, Pallas kernels for 0%

profile of v1, /device:TPU:0, one launch (start us, length us, event | category | flops | bytes accessed | tf_op | source)
XLA Modules:
  0.0 72.3 jit_solution(2708915486079632192)
XLA Ops:
  7.2 0.0 all-gather.2.cloned.1.call-start
  7.2 2.1 %weigh.1 = bf16[528,128]{1,0:T(8,128)(2,1)} custom-call(f32[4]{0:T(128)} %rate_ref.3, bf16[512,128]{1,0:T(8,128)(2,1)} %events_ref.1, f32[4,128]{1,0:T(4,128)} %bitcast.10, s32[4,128]{1,0:T(4,128)} %bitcast.6, s32[4,128]{1,0:T(4,128)} %bitcast.8, s32[32,128]{1,0:T(8,128)} %bitcast.5), custom_call_target="tpu_custom_call" | custom-call | tf_op jit(solution)/shard_map/weigh/pallas_call | solution.py:267
  9.3 0.0 all-gather.2.cloned.1.call-update
  9.3 44.5 %all-gather.2.cloned.1.call-done.all_ref = bf16[4224,128]{1,0:T(8,128)(2,1)} async-done(((bf16[528,128]{1,0:T(8,128)(2,1)}), bf16[4224,128]{1,0:T(8,128)(2,1)}) %all-gather.2.cloned.1.call-update) | async-done | bytes 1081360 | tf_op jit(solution)/shard_map/all_gather | solution.py:274
  53.8 11.7 %aggregate.1 = (bf16[4096,128]{1,0:T(8,128)(2,1)}, bf16[512,128]{1,0:T(8,128)(2,1)}) custom-call(s32[1]{0:T(128)} %bitcast.me_ref, f32[4]{0:T(128)} %rate_ref.3, s32[4,128]{1,0:T(4,128)} %bitcast.7, s32[4,128]{1,0:T(4,128)} %bitcast.9, bf16[4224,128]{1,0:T(8,128)(2,1)} %all-gather.2.cloned.1.call-done.all_ref), custom_call_target="tpu_custom_call" | custom-call | tf_op jit(solution)/shard_map/aggregate/pallas_call | solution.py:277
Async XLA Ops:
  7.2 46.6 %all-gather.2.cloned.1.call-start = ((), (), s32[]{:S(2)}) async-start(), calls=%async_computation | async-start | bytes 1216512 | tf_op jit(solution)/shard_map/all_gather | solution.py:274
Sparse Core Ops, SparseCore 0:
  10.7 42.9 all-gather.1

commit v2 on v1

--- a/solution.py
+++ b/solution.py
@@ -20,7 +20,7 @@
     chunks = rows // LANES
     users = 8 * owners
     user_rows = -(-users // LANES)
-    code_rows = -(-(3 * chunks + 2 * user_rows) // 16) * 16
+    code_rows = -(-(3 * chunks + 2 * user_rows + 1) // 16) * 16
     span = min(owners, 8)
     return chunks, user_rows, code_rows, span
 
@@ -38,19 +38,28 @@
     return row
 
 
-def send_kernel(owners, slots, rate_ref, events_ref, weight_ref, route_ref, bucket_ref, segment_ref, out_ref):
+def send_kernel(owners, slots, events_ref, weight_ref, route_ref, bucket_ref, segment_ref, out_ref):
     rows = events_ref.shape[0]
     chunks, user_rows, code_rows, span = dims(owners, rows, slots)
-    rate = rate_row(rate_ref)
     route = route_ref[...]
     bucket = bucket_ref[...]
-    spot = (route & (span - 1)) * slots + bucket - span * slots // 2
-    columns = jnp.concatenate([weight_ref[...], spot.astype(F32)], axis=0).T
+    columns = jnp.concatenate([weight_ref[...], jnp.zeros((8 - chunks, LANES), F32)], axis=0).T
+    weighted = []
+    largest = jnp.zeros((LANES, LANES), F32)
     for r in range(chunks):
         part = pl.ds(r * LANES, LANES)
-        weighted = (columns[:, r : r + 1] * events_ref[part, :].astype(F32)).astype(BF16)
-        grown = weighted.astype(F32) * jnp.exp(columns[:, chunks + r : chunks + r + 1] * rate)
-        out_ref[part, :] = grown.astype(BF16)
+        weighted.append((columns[:, r : r + 1] * events_ref[part, :].astype(F32)).astype(BF16).astype(F32))
+        largest = jnp.maximum(largest, jnp.abs(weighted[-1]))
+    largest = jnp.max(jnp.max(largest, axis=0, keepdims=True), axis=1, keepdims=True)
+    power = jnp.zeros((1, 1), F32)
+    factor = jnp.ones((1, 1), F32)
+    for bits in (64, 32, 16, 8, 4, 2, 1):
+        more = factor * F32(2.0**bits)
+        fits = largest * more <= F32(32768)
+        factor = jnp.where(fits, more, factor)
+        power = jnp.where(fits, power + F32(bits), power)
+    for r in range(chunks):
+        out_ref[pl.ds(r * LANES, LANES), :] = (weighted[r] * factor).astype(BF16)
     ones = jnp.ones((8, LANES), BF16)
     high, low = [], []
     for u in range(user_rows):
@@ -62,7 +71,7 @@
         high.append(count >> LOW)
         low.append(count & MASK)
     spare = code_rows - 3 * chunks - 2 * user_rows
-    pad = [jnp.zeros((spare, LANES), I32)] if spare else []
+    pad = [jnp.broadcast_to(power, (spare, LANES)).astype(I32)]
     codes = jnp.concatenate([route, bucket >> LOW, bucket & MASK] + high + low + pad, axis=0)
     out_ref[pl.ds(rows, code_rows), :] = codes.astype(F32).astype(BF16)
 
@@ -78,11 +87,12 @@
 def gather_kernel(
     owners, rows, slots, me_ref, rate_ref, route_ref, bucket_ref, all_ref,
     table_ref, feature_ref,
-    place_ref, until_ref, own_ref, tail_ref, codes_ref, rows_ref, from_ref, last_ref, total_ref,
+    grown_ref, place_ref, until_ref, own_ref, tail_ref, codes_ref, rows_ref, from_ref, last_ref, total_ref,
 ):
     chunks, user_rows, code_rows, span = dims(owners, rows, slots)
     window = slots // 4
     block_rows = rows + code_rows
+    power_row = 3 * chunks + 2 * user_rows
     capacity = 2 * rows // owners
     per_group = LANES // capacity
     groups = owners // per_group
@@ -122,6 +132,14 @@
         route = tile[0:chunks]
         bucket = F32(LANES) * tile[chunks : 2 * chunks] + tile[2 * chunks : 3 * chunks]
         place = route * F32(slots) + bucket
+        spot = ((route.astype(I32) & (span - 1)) * slots - span * slots // 2).astype(F32) + bucket
+        shrink = jnp.broadcast_to(tile[power_row : power_row + 1] * F32(-0.6931471805599453), (8 - chunks, LANES))
+        columns = jnp.concatenate([spot, shrink], axis=0).T
+        for r in range(chunks):
+            events = all_ref[pl.ds(pl.multiple_of(s * block_rows + r * LANES, 16), LANES), :].astype(F32)
+            growth = jnp.exp(columns[:, r : r + 1] * rate + columns[:, chunks : chunks + 1])
+            part = pl.ds(pl.multiple_of(s * rows + r * LANES, LANES), LANES)
+            grown_ref[part, :] = (events * growth).astype(BF16)
         until = []
         for r in range(chunks):
             row = place[r : r + 1]
@@ -177,7 +195,7 @@
             wide = jnp.concatenate(
                 [jnp.where(code_line == r, codes, F32(0)).astype(BF16) for r in range(chunks)], axis=1
             )
-            block = all_ref[pl.ds(pl.multiple_of(s * block_rows, 16), rows), :]
+            block = grown_ref[pl.ds(pl.multiple_of(s * rows, LANES), rows), :]
             values += jnp.dot(hot, block, preferred_element_type=F32)
             places += lax.dot_general(wide, hot, NT, preferred_element_type=F32)
             return values, places
@@ -244,7 +262,7 @@
                     inside = begin[r : r + 1] >= first
                     held &= inside if shift == 0 else jnp.logical_not(inside)
                 masks.append(jnp.where(held, F32(1), F32(0)).astype(BF16))
-            events = all_ref[pl.ds(pl.multiple_of(s * block_rows, 16), rows), :]
+            events = grown_ref[pl.ds(pl.multiple_of(s * rows, LANES), rows), :]
             total_ref[...] += jnp.dot(jnp.concatenate(masks, axis=1), events, preferred_element_type=F32)
 
         each(owners, add)
@@ -267,11 +285,11 @@
     block = pl.pallas_call(
         functools.partial(send_kernel, owners, slots),
         out_shape=jax.ShapeDtypeStruct((block_rows, width), BF16),
-        in_specs=[smem] + [vmem] * 5,
+        in_specs=[vmem] * 5,
         out_specs=vmem,
         name="weigh",
-    )(decay_rate, events, event_weight.reshape(chunks, LANES), route, bucket, segment.reshape(slots // LANES, LANES))
-    gathered = lax.all_gather(block, ("key", "shard"), axis=0, tiled=True)
+    )(events, event_weight.reshape(chunks, LANES), route, bucket, segment.reshape(slots // LANES, LANES))
+    gathered = lax.all_gather(block.astype(jnp.float16), ("key", "shard"), axis=0, tiled=True).astype(BF16)
     me = (lax.axis_index("key") * shard_count + lax.axis_index("shard")).astype(I32).reshape(1)
     lines = 2 * rows // LANES * 2
     return pl.pallas_call(
@@ -283,6 +301,7 @@
         in_specs=[smem, smem] + [vmem] * 3,
         out_specs=(vmem, vmem),
         scratch_shapes=[
+            pltpu.VMEM((owners * rows, LANES), BF16),
             pltpu.VMEM((owners, 8, LANES), F32),
             pltpu.VMEM((owners, 8, LANES), F32),
             pltpu.VMEM((owners, 8, LANES), F32),

time: 72.5 us -> 52.2 us (0.72)
  waiting for transfers between devices: 44.5 us -> 0 us
  blocking collectives: 0 us -> 34.8 us
  between operations: 14 us -> 0.64 us
  other arithmetic: 0 us -> 2.04 us
  Pallas kernels: 13.8 us -> 14.6 us
    all_gather x1 -> x0, waiting for transfers between devices: 44.5 us -> none  [on_device(): gathered = lax.all_gather(block, ('key', 'shard'), axis=0, tiled=True)]
    all_gather x0 -> x1, blocking collectives: none -> 34.8 us  [on_device(): lax.all_gather(block.astype(jnp.float16), ('key', 'shard'), axis=0, tiled...]
    convert_element_type x0 -> x2, other arithmetic: none -> 2.04 us  [the longest x1 1.11 us: on_device(): lax.all_gather(block.astype(jnp.float16), ('key', 'shard'), axis=0, tiled...]
  transfers between devices with their start and end apart: 1 -> 0, of which waited for: 1 -> 0; matrix products, arithmetic and copies ran while one was open for 0% -> 0% of each run, Pallas kernels for 0% -> 0%
where the time goes in v2:
time: 52.2 us; the launch traced here: 52 us
  blocking collectives  34.8 us (67%)
  Pallas kernels  14.6 us (28%)
  other arithmetic  2.04 us (4%)
  between operations  0.64 us (1%)
    all_gather x1, blocking collectives, on_device(): lax.all_gather(block.astype(jnp.float16), ('key', 'shard'), axis=0, tiled...  34.8 us
    pallas_call x1, Pallas kernels, on_device(): pl.pallas_call(functools.partial(gather_kernel, owners, rows, slots), out...  12.4 us
    pallas_call x1, Pallas kernels, on_device(): pl.pallas_call(functools.partial(send_kernel, owners, slots), out_shape=j...  2.12 us
    convert_element_type x1, other arithmetic, on_device(): lax.all_gather(block.astype(jnp.float16), ('key', 'shard'), axis=0, tiled...  1.11 us

profile of v2, /device:TPU:0, one launch (start us, length us, event | category | flops | bytes accessed | tf_op | source)
XLA Modules:
  0.0 52.0 jit_solution(11336775247796384001)
XLA Ops:
  0.6 2.1 %weigh.1 = bf16[528,128]{1,0:T(8,128)(2,1)} custom-call(bf16[512,128]{1,0:T(8,128)(2,1)} %events_ref.1, f32[4,128]{1,0:T(4,128)} %bitcast.10, s32[4,128]{1,0:T(4,128)} %bitcast.6, s32[4,128]{1,0:T(4,128)} %bitcast.8, s32[32,128]{1,0:T(8,128)} %bitcast.5), custom_call_target="tpu_custom_call" | custom-call | tf_op jit(solution)/shard_map/weigh/pallas_call | solution.py:285
  2.8 0.9 %convert_element_type.6 = f16[528,128]{1,0:T(8,128)(2,1)S(1)} convert(bf16[528,128]{1,0:T(8,128)(2,1)} %weigh.1) | non-fusion elementwise | flops 67584 | bytes 270336 | tf_op jit(solution)/shard_map/convert_element_type | solution.py:292
  3.7 34.8 %all-gather.1 = f16[4224,128]{1,0:T(8,128)(2,1)S(1)} all-gather(f16[528,128]{1,0:T(8,128)(2,1)S(1)} %convert_element_type.6), channel_id=1, replica_groups=mesh['groups'=2,'key'=4,'shard'=2,'lane'=2] {'key','shard'}, dimensions={0}, use_global_device_ids=true | all-gather | bytes 1216512 | tf_op jit(solution)/shard_map/all_gather | solution.py:292
  38.5 1.1 %convert_element_type.7.all_ref = bf16[4224,128]{1,0:T(8,128)(2,1)} convert(f16[4224,128]{1,0:T(8,128)(2,1)S(1)} %all-gather.1) | non-fusion elementwise | flops 540672 | bytes 2162688 | tf_op jit(solution)/shard_map/convert_element_type | solution.py:292
  39.6 12.4 %aggregate.1 = (bf16[4096,128]{1,0:T(8,128)(2,1)}, bf16[512,128]{1,0:T(8,128)(2,1)}) custom-call(s32[1]{0:T(128)} %bitcast.me_ref, f32[4]{0:T(128)} %rate_ref.1, s32[4,128]{1,0:T(4,128)} %bitcast.7, s32[4,128]{1,0:T(4,128)} %bitcast.9, bf16[4224,128]{1,0:T(8,128)(2,1)} %convert_element_type.7.all_ref), custom_call_target="tpu_custom_call" | custom-call | tf_op jit(solution)/shard_map/aggregate/pallas_call | solution.py:295

commit v3 on v1

--- a/solution.py
+++ b/solution.py
@@ -50,7 +50,9 @@
         part = pl.ds(r * LANES, LANES)
         weighted = (columns[:, r : r + 1] * events_ref[part, :].astype(F32)).astype(BF16)
         grown = weighted.astype(F32) * jnp.exp(columns[:, chunks + r : chunks + r + 1] * rate)
-        out_ref[part, :] = grown.astype(BF16)
+        grown = grown.astype(BF16)
+        for o in range(owners):
+            out_ref[o, part, :] = grown
     ones = jnp.ones((8, LANES), BF16)
     high, low = [], []
     for u in range(user_rows):
@@ -64,7 +66,9 @@
     spare = code_rows - 3 * chunks - 2 * user_rows
     pad = [jnp.zeros((spare, LANES), I32)] if spare else []
     codes = jnp.concatenate([route, bucket >> LOW, bucket & MASK] + high + low + pad, axis=0)
-    out_ref[pl.ds(rows, code_rows), :] = codes.astype(F32).astype(BF16)
+    codes = codes.astype(F32).astype(BF16)
+    for o in range(owners):
+        out_ref[o, pl.ds(rows, code_rows), :] = codes
 
 
 def each(count, body):
@@ -266,12 +270,14 @@
     bucket = bucket.reshape(chunks, LANES)
     block = pl.pallas_call(
         functools.partial(send_kernel, owners, slots),
-        out_shape=jax.ShapeDtypeStruct((block_rows, width), BF16),
+        out_shape=jax.ShapeDtypeStruct((owners, block_rows, width), BF16),
         in_specs=[smem] + [vmem] * 5,
         out_specs=vmem,
+        compiler_params=pltpu.CompilerParams(vmem_limit_bytes=56 * 1024 * 1024),
         name="weigh",
     )(decay_rate, events, event_weight.reshape(chunks, LANES), route, bucket, segment.reshape(slots // LANES, LANES))
-    gathered = lax.all_gather(block, ("key", "shard"), axis=0, tiled=True)
+    gathered = lax.all_to_all(block, ("key", "shard"), split_axis=0, concat_axis=0, tiled=True)
+    gathered = gathered.reshape(owners * block_rows, width)
     me = (lax.axis_index("key") * shard_count + lax.axis_index("shard")).astype(I32).reshape(1)
     lines = 2 * rows // LANES * 2
     return pl.pallas_call(

time: 72.5 us -> 49.7 us (0.69)
  waiting for transfers between devices: 44.5 us -> 26.5 us
  between operations: 14 us -> 0.63 us
  starting transfers between devices: 0.04 us -> 7.25 us
  local copies, waits for them, and re-layouts: 0 us -> 0.97 us
    all_gather x1 -> x0, waiting for transfers between devices: 44.5 us -> none  [on_device(): gathered = lax.all_gather(block, ('key', 'shard'), axis=0, tiled=True)]
    all_to_all x0 -> x1, waiting for transfers between devices: none -> 26.5 us  [on_device(): lax.all_to_all(block, ('key', 'shard'), split_axis=0, concat_axis=0, tile...]
    all_to_all x0 -> x1, starting transfers between devices: none -> 7.25 us  [on_device(): lax.all_to_all(block, ('key', 'shard'), split_axis=0, concat_axis=0, tile...]
    unnamed x0 -> x2, local copies, waits for them, and re-layouts: none -> 0.97 us
where the time goes in v3:
time: 49.7 us; the launch traced here: 49.4 us
  waiting for transfers between devices  26.5 us (53%)
  Pallas kernels  14.1 us (28%)
  starting transfers between devices  7.25 us (15%)
  local copies, waits for them, and re-layouts  0.97 us (2%)
  between operations  0.63 us (1%)
    all_to_all x1, waiting for transfers between devices, on_device(): lax.all_to_all(block, ('key', 'shard'), split_axis=0, concat_axis=0, tile...  26.5 us
    pallas_call x1, Pallas kernels, on_device(): pl.pallas_call(functools.partial(gather_kernel, owners, rows, slots), out...  11.7 us
    all_to_all x1, starting transfers between devices, on_device(): lax.all_to_all(block, ('key', 'shard'), split_axis=0, concat_axis=0, tile...  7.25 us
    pallas_call x1, Pallas kernels, on_device(): pl.pallas_call(functools.partial(send_kernel, owners, slots), out_shape=j...  2.39 us
  transfers between devices with their start and end apart: 1, of which 1 were waited for; matrix products, arithmetic and copies ran while one was open for 0% of the time, Pallas kernels for 0%

profile of v3, /device:TPU:0, one launch (start us, length us, event | category | flops | bytes accessed | tf_op | source)
XLA Modules:
  0.0 49.4 jit_solution(15675689265964268438)
XLA Ops:
  0.6 2.4 %weigh.1 = bf16[8,528,128]{2,1,0:T(8,128)(2,1)} custom-call(f32[4]{0:T(128)} %rate_ref.3, bf16[512,128]{1,0:T(8,128)(2,1)} %events_ref.1, f32[4,128]{1,0:T(4,128)} %bitcast.12, s32[4,128]{1,0:T(4,128)} %bitcast.8, s32[4,128]{1,0:T(4,128)} %bitcast.10, s32[32,128]{1,0:T(8,128)} %bitcast.7), custom_call_target="tpu_custom_call" | custom-call | tf_op jit(solution)/shard_map/weigh/pallas_call | solution.py:271
  3.0 7.3 %all-to-all-start = ((bf16[8,528,128]{2,1,0:T(8,128)(2,1)}), bf16[8,528,128]{2,1,0:T(8,128)(2,1)S(1)}, u32[]{:S(2)}, u32[]{:S(2)}) async-start(bf16[8,528,128]{2,1,0:T(8,128)(2,1)} %weigh.1), calls=%async_computation | async-start | bytes 2162688 | tf_op jit(solution)/shard_map/all_to_all | solution.py:279
  10.3 26.5 %all-to-all-done = bf16[8,528,128]{2,1,0:T(8,128)(2,1)S(1)} async-done(((bf16[8,528,128]{2,1,0:T(8,128)(2,1)}), bf16[8,528,128]{2,1,0:T(8,128)(2,1)S(1)}, u32[]{:S(2)}, u32[]{:S(2)}) %all-to-all-start) | async-done | bytes 1081376 | tf_op jit(solution)/shard_map/all_to_all | solution.py:279
  36.7 0.0 copy-start
  36.7 1.0 %copy-done = bf16[8,528,128]{2,1,0:T(8,128)(2,1)} copy-done((bf16[8,528,128]{2,1,0:T(8,128)(2,1)}, bf16[8,528,128]{2,1,0:T(8,128)(2,1)S(1)}, u32[]{:S(2)}) %copy-start) | copy-done | bytes 1081368
  37.7 11.7 %aggregate.1 = (bf16[4096,128]{1,0:T(8,128)(2,1)}, bf16[512,128]{1,0:T(8,128)(2,1)}) custom-call(s32[1]{0:T(128)} %bitcast.me_ref, f32[4]{0:T(128)} %rate_ref.3, s32[4,128]{1,0:T(4,128)} %bitcast.9, s32[4,128]{1,0:T(4,128)} %bitcast.11, bf16[4224,128]{1,0:T(8,128)(2,1)} %bitcast.6), custom_call_target="tpu_custom_call" | custom-call | tf_op jit(solution)/shard_map/aggregate/pallas_call | solution.py:283
Async XLA Ops:
  3.0 33.7 %all-to-all-start = ((bf16[8,528,128]{2,1,0:T(8,128)(2,1)}), bf16[8,528,128]{2,1,0:T(8,128)(2,1)S(1)}, u32[]{:S(2)}, u32[]{:S(2)}) async-start(bf16[8,528,128]{2,1,0:T(8,128)(2,1)} %weigh.1), calls=%async_computation | async-start | bytes 2162688 | tf_op jit(solution)/shard_map/all_to_all | solution.py:279
  36.7 1.0 %copy-start = (bf16[8,528,128]{2,1,0:T(8,128)(2,1)}, bf16[8,528,128]{2,1,0:T(8,128)(2,1)S(1)}, u32[]{:S(2)}) copy-start(bf16[8,528,128]{2,1,0:T(8,128)(2,1)S(1)} %all-to-all-done) | copy-start | bytes 3244036

commit v4 on v1

v4 whole, which is shorter than its diff:
```python
import functools
import jax
import jax.numpy as jnp
from jax import lax
from jax.experimental import pallas as pl
from jax.experimental.pallas import tpu as pltpu
from jax.sharding import PartitionSpec as P

LANES = 128
LOW = 7
MASK = 127
F32 = jnp.float32
BF16 = jnp.bfloat16
I32 = jnp.int32
FAR = 1e9
NT = (((1,), (1,)), ((), ()))
BLOCK = 256


class Sizes:
    def __init__(self, owners, rows, slots):
        self.owners, self.rows, self.slots = owners, rows, slots
        self.window = slots // 4
        self.chunks = rows // LANES
        self.user_rows = -(-8 * owners // LANES)
        self.code_rows = -(-(3 * self.chunks + 2 * self.user_rows) // 16) * 16
        self.span = min(owners, 8)
        self.shifts = 1 if owners <= self.span else 2
        self.capacity = 2 * rows // owners
        self.per_group = LANES // self.capacity
        self.groups = owners // self.per_group


def iota(shape, axis):
    return lax.broadcasted_iota(I32, shape, axis)


def ones_where(condition):
    return jnp.where(condition, F32(1), F32(0)).astype(BF16)


def dot(a, b):
    return jnp.dot(a, b, preferred_element_type=F32)


def loop(count, body, carry):
    if count <= 8:
        for i in range(count):
            carry = body(i, carry)
        return carry
    return lax.fori_loop(0, count, body, carry)


def block_of(pieces, s):
    return (pieces[s], 0) if len(pieces) > 1 else (pieces[0], s)


def send_kernel(z, me_ref, rate_ref, events_ref, weight_ref, route_ref, bucket_ref, segment_ref, block_ref, own_ref):
    groups = rate_ref.shape[0]
    lane = iota((1, LANES), 1)
    rate = jnp.full((1, LANES), rate_ref[0], F32)
    for g in range(1, groups):
        rate = jnp.where(lane >= g * (LANES // groups), rate_ref[g], rate)
    route = route_ref[...]
    bucket = bucket_ref[...]
    place = (route * z.slots + bucket).astype(F32)
    first = ((route >> (z.span.bit_length() - 1)) * (z.span * z.slots)).astype(F32)
    me = jnp.full((8 - 1, LANES), me_ref[0], I32).astype(F32)
    own_ref[...] = jnp.concatenate([place, first, rate, me], axis=0)
    spot = place - first - F32(z.span * z.slots // 2)
    columns = jnp.concatenate([weight_ref[...], spot], axis=0).T
    for r in range(z.chunks):
        part = slice(r * LANES, (r + 1) * LANES)
        weighted = (columns[:, r : r + 1] * events_ref[part, :].astype(F32)).astype(BF16)
        grown = weighted.astype(F32) * jnp.exp(columns[:, z.chunks + r : z.chunks + r + 1] * rate)
        block_ref[part, :] = grown.astype(BF16)
    ones = jnp.ones((8, LANES), BF16)
    high, low = [], []
    for u in range(z.user_rows):
        user = iota((LANES, LANES), 0) + u * LANES
        below = jnp.zeros((LANES, LANES), F32)
        for r in range(z.slots // LANES):
            below += jnp.where(segment_ref[r : r + 1, :] < user, F32(1), F32(0))
        count = lax.dot_general(ones, below.astype(BF16), NT, preferred_element_type=F32)[0:1].astype(I32)
        high.append(count >> LOW)
        low.append(count & MASK)
    spare = z.code_rows - 3 * z.chunks - 2 * z.user_rows
    pad = [jnp.zeros((spare, LANES), I32)] if spare else []
    codes = jnp.concatenate([route, bucket >> LOW, bucket & MASK] + high + low + pad, axis=0)
    block_ref[z.rows : z.rows + z.code_rows, :] = codes.astype(F32).astype(BF16)


def gather_kernel(z, count, *refs):
    own_ref = refs[0]
    pieces = refs[1 : 1 + count]
    (
        table_ref, feature_ref,
        place_ref, until_ref, rank_ref, tail_ref, codes_ref, rows_ref, from_ref, last_ref,
    ) = refs[1 + count :]
    rate = own_ref[8:9, :]
    me = own_ref[9:10, :]
    base = me * F32(z.slots)

    def code_tile(s):
        ref, i = block_of(pieces, s)
        return ref[i, z.rows : z.rows + z.code_rows, :].astype(F32)

    def row_block(s):
        ref, i = block_of(pieces, s)
        return ref[i, 0 : z.rows, :]

    starts = []
    for u in range(z.user_rows):
        def add(s, total):
            tile = code_tile(s)
            at = 3 * z.chunks + u
            return total + F32(LANES) * tile[at : at + 1] + tile[at + z.user_rows : at + z.user_rows + 1]

        starts.append(loop(z.owners, add, jnp.zeros((1, LANES), F32)))
    start_columns = [jnp.broadcast_to(row, (8, LANES)).T[:, 0:1] for row in starts]
    steps = []
    for u in range(z.user_rows):
        before = pltpu.roll(starts[u], 1, 1)
        first = starts[u - 1][:, LANES - 1 : LANES] if u else jnp.zeros((1, 1), F32)
        step = (starts[u] - jnp.where(iota((1, LANES), 1) == 0, first, before)).astype(I32)
        pair = [jnp.broadcast_to(step >> LOW, (LANES, LANES)), jnp.broadcast_to(step & MASK, (LANES, LANES))]
        steps.append(jnp.concatenate(pair, axis=0).astype(F32).astype(BF16))

    def root(position):
        total = jnp.zeros((position.shape[0], 2 * LANES), F32)
        for u in range(z.user_rows):
            total += lax.dot_general(ones_where(starts[u] <= position), steps[u], NT, preferred_element_type=F32)
        start = F32(LANES) * total[:, :LANES] + total[:, LANES:]
        return lax.rsqrt(jnp.minimum(position - start, F32(z.window)) + F32(1))

    def decode(s, carry):
        tile = code_tile(s)
        bucket = F32(LANES) * tile[z.chunks : 2 * z.chunks] + tile[2 * z.chunks : 3 * z.chunks]
        place = tile[0 : z.chunks] * F32(z.slots) + bucket
        until = []
        for r in range(z.chunks):
            row = place[r : r + 1]
            after = jnp.full((1, LANES), FAR, F32)
            for column in start_columns:
                users = column[: min(LANES, 8 * z.owners)]
                later = jnp.where(users > row, users, F32(FAR))
                after = jnp.minimum(after, jnp.min(later, axis=0, keepdims=True))
            until.append(jnp.minimum(row + F32(z.window), after - F32(1)))
        until = jnp.concatenate(until, axis=0)
        local = place - base
        near, far = local.astype(I32), (until - base).astype(I32)
        codes = jnp.concatenate([near >> LOW, near & MASK, far >> LOW, far & MASK], axis=0)
        codes_ref[s] = codes.astype(F32)
        spare = jnp.zeros((8 - z.chunks, LANES), F32)
        place_ref[s] = jnp.concatenate([place, spare], axis=0)
        until_ref[s] = jnp.concatenate([until, spare], axis=0)
        own = (local >= 0) & (local < F32(z.slots))
        tail = (local >= F32(-z.window)) & (local < 0)
        rank_ref[s] = jnp.concatenate([jnp.where(own, F32(1), F32(0)), spare], axis=0)
        tail_ref[s] = jnp.concatenate([jnp.where(tail, F32(1), F32(0)), spare], axis=0)
        return carry

    loop(z.owners, decode, 0)

    upper = ones_where(iota((LANES, LANES), 0) < iota((LANES, LANES), 1))
    full = jnp.ones((LANES, LANES), BF16)
    lines = z.owners * 8
    at, by = iota((lines, lines), 0), iota((lines, lines), 1)
    earlier = ones_where(((at >> 3) == (by >> 3)) & (by < at))
    source = iota((lines, LANES), 0) >> 3
    offset = ((source & (z.per_group - 1)) * z.capacity).astype(F32)
    for ref in (rank_ref, tail_ref):
        marked = ref[...].reshape(lines, LANES)
        mark = marked.astype(BF16)
        rank = dot(mark, upper) + dot(earlier, dot(mark, full).astype(BF16)) + offset
        ref[...] = jnp.where(marked > 0, rank, F32(-1)).reshape(z.owners, 8, LANES)

    spots = iota((LANES, LANES), 0).astype(F32)
    code_line = iota((4 * z.chunks, LANES), 0) & (z.chunks - 1)

    def pack(kind, ref, g):
        def add(i, carry):
            values, places = carry
            s = g * z.per_group + i
            ranks = ref[s]
            codes = codes_ref[s]
            hot = jnp.concatenate([ones_where(spots == ranks[r : r + 1]) for r in range(z.chunks)], axis=1)
            wide = [jnp.where(code_line == r, codes, F32(0)).astype(BF16) for r in range(z.chunks)]
            values += dot(hot, row_block(s))
            places += lax.dot_general(jnp.concatenate(wide, axis=1), hot, NT, preferred_element_type=F32)
            return values, places

        zero = (jnp.zeros((LANES, LANES), F32), jnp.zeros((4 * z.chunks, LANES), F32))
        values, places = loop(z.per_group, add, zero)
        line = kind * z.groups + g
        rows_ref[line * LANES : (line + 1) * LANES, :] = values.astype(BF16)
        part = [jnp.sum(places[k * z.chunks : (k + 1) * z.chunks], axis=0, keepdims=True) for k in range(4)]
        from_ref[line : line + 1, :] = F32(LANES) * part[0] + part[1]
        last_ref[line : line + 1, :] = F32(LANES) * part[2] + part[3]

    for kind, ref in enumerate((rank_ref, tail_ref)):
        for g in range(z.groups):
            pack(kind, ref, g)

    middle = F32(z.span * z.slots // 2)
    span_of = lambda owner: (owner.astype(I32) >> (z.span.bit_length() - 1)).astype(F32) * F32(z.span)
    own_offset = (me - span_of(me)) * F32(z.slots) - middle
    tail_offset = (me - span_of(me - F32(1))) * F32(z.slots) - middle
    inner = iota((BLOCK, LANES), 0).astype(F32)
    fall = jnp.exp(-rate * inner)

    def summed(b, kinds):
        masks = []
        for line in range(kinds.start * z.groups, kinds.stop * z.groups):
            begin, end = from_ref[line : line + 1, :], last_ref[line : line + 1, :]
            masks.append(ones_where((inner >= begin - F32(b * BLOCK)) & (inner <= end - F32(b * BLOCK))))
        events = rows_ref[kinds.start * z.groups * LANES : kinds.stop * z.groups * LANES, :]
        return dot(jnp.concatenate(masks, axis=1), events)

    for b in range(z.slots // BLOCK):
        start = F32(b * BLOCK)
        tailed = b * BLOCK < z.window
        value = summed(b, range(0, 2 if tailed and z.shifts == 1 else 1)) * jnp.exp(-rate * (start + own_offset))
        if tailed and z.shifts > 1:
            value += summed(b, range(1, 2)) * jnp.exp(-rate * (start + tail_offset))
        value = value * fall * root(inner + (start + base))
        table_ref[b * BLOCK : (b + 1) * BLOCK, :] = value.astype(BF16)

    columns = own_ref[0:8, :].T
    wide_column = lambda at: jnp.broadcast_to(columns[:, at : at + 1], (LANES, LANES))
    for t in range(z.rows // BLOCK):
        at = t * (BLOCK // LANES)
        position = jnp.concatenate([wide_column(at + k) for k in range(BLOCK // LANES)], axis=0)
        first = jnp.concatenate([wide_column(z.chunks + at + k) for k in range(BLOCK // LANES)], axis=0)
        total = jnp.zeros((BLOCK, LANES), F32)
        for shift in range(z.shifts):
            def add(s, value):
                begin, end = place_ref[s], until_ref[s]
                masks = []
                for r in range(z.chunks):
                    held = (position >= begin[r : r + 1]) & (position <= end[r : r + 1])
                    if z.shifts > 1:
                        inside = begin[r : r + 1] >= first
                        held &= inside if shift == 0 else jnp.logical_not(inside)
                    masks.append(ones_where(held))
                return value + dot(jnp.concatenate(masks, axis=1), row_block(s))

            value = loop(z.owners, add, jnp.zeros((BLOCK, LANES), F32))
            center = first + F32(z.span * z.slots // 2 - shift * z.span * z.slots)
            total += value * jnp.exp(-rate * (position - center))
        feature_ref[t * BLOCK : (t + 1) * BLOCK, :] = (total * root(position)).astype(BF16)


def spread(blocks, axis):
    distance = lax.axis_size(axis) // 2
    while distance:
        pairs = [(i, i ^ distance) for i in range(lax.axis_size(axis))]
        blocks = blocks + [lax.ppermute(block, axis, pairs) for block in blocks]
        distance //= 2
    return blocks


def on_device(events, event_weight, route, bucket, segment, decay_rate):
    rows, width = events.shape
    shard_count = lax.axis_size("shard")
    owners = lax.axis_size("key") * shard_count
    slots = segment.shape[0]
    z = Sizes(owners, rows, slots)
    block_rows = rows + z.code_rows
    smem = pl.BlockSpec(memory_space=pltpu.SMEM)
    vmem = pl.BlockSpec(memory_space=pltpu.VMEM)
    shape = jax.ShapeDtypeStruct
    me = (lax.axis_index("key") * shard_count + lax.axis_index("shard")).astype(I32).reshape(1)
    block, own = pl.pallas_call(
        functools.partial(send_kernel, z),
        out_shape=(shape((block_rows, width), BF16), shape((16, LANES), F32)),
        in_specs=[smem, smem] + [vmem] * 5,
        out_specs=(vmem, vmem),
        compiler_params=pltpu.CompilerParams(vmem_limit_bytes=56 * 1024 * 1024),
        name="weigh",
    )(
        me, decay_rate, events, event_weight.reshape(z.chunks, LANES), route.reshape(z.chunks, LANES),
        bucket.reshape(z.chunks, LANES), segment.reshape(slots // LANES, LANES),
    )
    blocks = spread(spread([block], "key"), "shard")
    if owners > 8:
        blocks = [jnp.concatenate(blocks, axis=0)]
    blocks = [b.reshape(-1, block_rows, width) for b in blocks]
    lines = 2 * z.groups
    return pl.pallas_call(
        functools.partial(gather_kernel, z, len(blocks)),
        out_shape=(shape((slots, width), BF16), shape((rows, width), BF16)),
        in_specs=[vmem] * (1 + len(blocks)),
        out_specs=(vmem, vmem),
        scratch_shapes=[
            pltpu.VMEM((owners, 8, LANES), F32),
            pltpu.VMEM((owners, 8, LANES), F32),
            pltpu.VMEM((owners, 8, LANES), F32),
            pltpu.VMEM((owners, 8, LANES), F32),
            pltpu.VMEM((owners, 4 * z.chunks, LANES), F32),
            pltpu.VMEM((lines * LANES, LANES), BF16),
            pltpu.VMEM((lines, LANES), F32),
            pltpu.VMEM((lines, LANES), F32),
        ],
        compiler_params=pltpu.CompilerParams(vmem_limit_bytes=(16 if owners <= 8 else 48) * 1024 * 1024),
        name="aggregate",
    )(own, *blocks)


def solution(mesh):
    placed = (
        P(("groups", "key", "shard"), "lane"),
        P(("groups", "key", "shard")),
        P(("groups", "key", "shard"), None),
        P(("groups", "key", "shard")),
        P(("groups", "key", "shard")),
        P("lane"),
    )
    return jax.shard_map(
        on_device,
        mesh=mesh,
        in_specs=placed,
        out_specs=(P(("groups", "key", "shard"), "lane"), P(("groups", "key", "shard"), "lane")),
        check_vma=False,
    )
```

time: 72.5 us -> 37.8 us (0.52)
  waiting for transfers between devices: 44.5 us -> 14.3 us
  between operations: 14 us -> 0.65 us
  starting transfers between devices: 0.04 us -> 11.4 us
  Pallas kernels: 13.8 us -> 9.66 us
  local copies, waits for them, and re-layouts: 0 us -> 1.6 us
    all_gather x1 -> x0, waiting for transfers between devices: 44.5 us -> none  [on_device(): gathered = lax.all_gather(block, ('key', 'shard'), axis=0, tiled=True)]
    ppermute x0 -> x7, waiting for transfers between devices: none -> 14.3 us  [spread(): blocks = blocks + [lax.ppermute(block, axis, pairs) for block in blocks]]
    ppermute x0 -> x7, starting transfers between devices: none -> 11.4 us  [spread(): blocks = blocks + [lax.ppermute(block, axis, pairs) for block in blocks]]
    pallas_call x2, Pallas kernels: 13.8 us -> 9.66 us  [the longest x1 7.58 us: on_device(): pl.pallas_call(functools.partial(gather_kernel, z, len(blocks)), out_shap...]
    unnamed x0 -> x4, local copies, waits for them, and re-layouts: none -> 1.6 us
  transfers between devices with their start and end apart: 1 -> 7, of which waited for: 1 -> 5; matrix products, arithmetic and copies ran while one was open for 0% -> 0% of each run, Pallas kernels for 0% -> 0%
where the time goes in v4:
time: 37.8 us; the launch traced here: 37.6 us
  waiting for transfers between devices  14.3 us (38%)
  starting transfers between devices  11.4 us (30%)
  Pallas kernels  9.66 us (26%)
  local copies, waits for them, and re-layouts  1.6 us (4%)
  between operations  0.65 us (2%)
    ppermute x7, waiting for transfers between devices, spread(): blocks = blocks + [lax.ppermute(block, axis, pairs) for block in blocks]  14.3 us
    ppermute x7, starting transfers between devices, spread(): blocks = blocks + [lax.ppermute(block, axis, pairs) for block in blocks]  11.4 us
    pallas_call x1, Pallas kernels, on_device(): pl.pallas_call(functools.partial(gather_kernel, z, len(blocks)), out_shap...  7.58 us
    pallas_call x1, Pallas kernels, on_device(): pl.pallas_call(functools.partial(send_kernel, z), out_shape=(shape((block...  2.08 us
    unnamed x4, local copies, waits for them, and re-layouts  1.6 us
  transfers between devices with their start and end apart: 7, of which 5 were waited for; matrix products, arithmetic and copies ran while one was open for 0% of the time, Pallas kernels for 0%

profile of v4, /device:TPU:0, one launch (start us, length us, event | category | flops | bytes accessed | tf_op | source)
XLA Modules:
  0.0 37.6 jit_solution(2579448276787917228)
XLA Ops:
  0.6 2.1 %weigh.1 = (bf16[528,128]{1,0:T(8,128)(2,1)}, f32[16,128]{1,0:T(8,128)}) custom-call(s32[1]{0:T(128)} %bitcast.me_ref, f32[4]{0:T(128)} %rate_ref.1, bf16[512,128]{1,0:T(8,128)(2,1)} %events_ref.1, f32[4,128]{1,0:T(4,128)} %bitcast.22, s32[4,128]{1,0:T(4,128)} %bitcast.23, s32[4,128]{1,0:T(4,128)} %bitcast.24, s32[32,128]{1,0:T(8,128)} %bitcast.21), custom_call_target="tpu_custom_call" | custom-call | tf_op jit(solution)/shard_map/weigh/pallas_call | solution.py:274
  2.7 4.0 %collective-permute-start = (bf16[528,128]{1,0:T(8,128)(2,1)}, bf16[528,128]{1,0:T(8,128)(2,1)S(1)}, u32[]{:S(2)}, u32[]{:S(2)}) collective-permute-start(bf16[528,128]{1,0:T(8,128)(2,1)} %get-tuple-element.5), channel_id=1, source_target_pairs={{0,8},{4,12},{8,0},{12,4},{1,9},{5,13},{9,1},{13,5},{2,10},{6,14},... | collective-permute-start | bytes 405512 | tf_op jit(solution)/shard_map/ppermute | solution.py:258
  6.8 1.6 %collective-permute-start.1 = (bf16[528,128]{1,0:T(8,128)(2,1)}, bf16[528,128]{1,0:T(8,128)(2,1)S(1)}, u32[]{:S(2)}, u32[]{:S(2)}) collective-permute-start(bf16[528,128]{1,0:T(8,128)(2,1)} %get-tuple-element.5), channel_id=1, source_target_pairs={{0,4},{4,0},{8,12},{12,8},{1,5},{5,1},{9,13},{13,9},{2,6},{6,2},{1... | collective-permute-start | bytes 405512 | tf_op jit(solution)/shard_map/ppermute | solution.py:258
  8.3 5.2 %collective-permute-done = bf16[528,128]{1,0:T(8,128)(2,1)S(1)} collective-permute-done((bf16[528,128]{1,0:T(8,128)(2,1)}, bf16[528,128]{1,0:T(8,128)(2,1)S(1)}, u32[]{:S(2)}, u32[]{:S(2)}) %collective-permute-start) | collective-permute-done | bytes 135200 | tf_op jit(solution)/shard_map/ppermute | solution.py:258
  13.5 0.7 %collective-permute-start.2 = (bf16[528,128]{1,0:T(8,128)(2,1)S(1)}, bf16[528,128]{1,0:T(8,128)(2,1)S(1)}, u32[]{:S(2)}, u32[]{:S(2)}) collective-permute-start(bf16[528,128]{1,0:T(8,128)(2,1)S(1)} %collective-permute-done), channel_id=1, source_target_pairs={{0,4},{4,0},{8,12},{12,8},{1,5},{5,1},{9,13},{13,9},{2,6},{6,2},{1... | collective-permute-start | bytes 405512 | tf_op jit(solution)/shard_map/ppermute | solution.py:258
  14.3 1.5 %collective-permute-start.3 = (bf16[528,128]{1,0:T(8,128)(2,1)}, bf16[528,128]{1,0:T(8,128)(2,1)S(1)}, u32[]{:S(2)}, u32[]{:S(2)}) collective-permute-start(bf16[528,128]{1,0:T(8,128)(2,1)} %get-tuple-element.5), channel_id=1, source_target_pairs={{0,2},{2,0},{1,3},{3,1},{4,6},{6,4},{5,7},{7,5},{8,10},{10,8},{9,1... | collective-permute-start | bytes 405512 | tf_op jit(solution)/shard_map/ppermute | solution.py:258
  15.8 0.5 %collective-permute-start.4 = (bf16[528,128]{1,0:T(8,128)(2,1)S(1)}, bf16[528,128]{1,0:T(8,128)(2,1)S(1)}, u32[]{:S(2)}, u32[]{:S(2)}) collective-permute-start(bf16[528,128]{1,0:T(8,128)(2,1)S(1)} %collective-permute-done), channel_id=1, source_target_pairs={{0,2},{2,0},{1,3},{3,1},{4,6},{6,4},{5,7},{7,5},{8,10},{10,8},{9,1... | collective-permute-start | bytes 405512 | tf_op jit(solution)/shard_map/ppermute | solution.py:258
  16.3 0.0 collective-permute-done.1
  16.3 1.5 %collective-permute-start.5 = (bf16[528,128]{1,0:T(8,128)(2,1)S(1)}, bf16[528,128]{1,0:T(8,128)(2,1)S(1)}, u32[]{:S(2)}, u32[]{:S(2)}) collective-permute-start(bf16[528,128]{1,0:T(8,128)(2,1)S(1)} %collective-permute-done.1), channel_id=1, source_target_pairs={{0,2},{2,0},{1,3},{3,1},{4,6},{6,4},{5,7},{7,5},{8,10},{10,8},{9,1... | collective-permute-start | bytes 405512 | tf_op jit(solution)/shard_map/ppermute | solution.py:258
  17.8 0.8 %collective-permute-done.2 = bf16[528,128]{1,0:T(8,128)(2,1)S(1)} collective-permute-done((bf16[528,128]{1,0:T(8,128)(2,1)S(1)}, bf16[528,128]{1,0:T(8,128)(2,1)S(1)}, u32[]{:S(2)}, u32[]{:S(2)}) %collective-permute-start.2) | collective-permute-done | bytes 135200 | tf_op jit(solution)/shard_map/ppermute | solution.py:258
  18.6 1.5 %collective-permute-start.6 = (bf16[528,128]{1,0:T(8,128)(2,1)S(1)}, bf16[528,128]{1,0:T(8,128)(2,1)S(1)}, u32[]{:S(2)}, u32[]{:S(2)}) collective-permute-start(bf16[528,128]{1,0:T(8,128)(2,1)S(1)} %collective-permute-done.2), channel_id=1, source_target_pairs={{0,2},{2,0},{1,3},{3,1},{4,6},{6,4},{5,7},{7,5},{8,10},{10,8},{9,1... | collective-permute-start | bytes 405512 | tf_op jit(solution)/shard_map/ppermute | solution.py:258
  20.1 0.9 %collective-permute-done.3 = bf16[528,128]{1,0:T(8,128)(2,1)S(1)} collective-permute-done((bf16[528,128]{1,0:T(8,128)(2,1)}, bf16[528,128]{1,0:T(8,128)(2,1)S(1)}, u32[]{:S(2)}, u32[]{:S(2)}) %collective-permute-start.3) | collective-permute-done | bytes 135200 | tf_op jit(solution)/shard_map/ppermute | solution.py:258
  21.0 5.8 %collective-permute-done.5 = bf16[528,128]{1,0:T(8,128)(2,1)S(1)} collective-permute-done((bf16[528,128]{1,0:T(8,128)(2,1)S(1)}, bf16[528,128]{1,0:T(8,128)(2,1)S(1)}, u32[]{:S(2)}, u32[]{:S(2)}) %collective-permute-start.5) | collective-permute-done | bytes 135200 | tf_op jit(solution)/shard_map/ppermute | solution.py:258
  26.8 0.0 collective-permute-done.4
  26.8 1.6 %collective-permute-done.6 = bf16[528,128]{1,0:T(8,128)(2,1)S(1)} collective-permute-done((bf16[528,128]{1,0:T(8,128)(2,1)S(1)}, bf16[528,128]{1,0:T(8,128)(2,1)S(1)}, u32[]{:S(2)}, u32[]{:S(2)}) %collective-permute-start.6) | collective-permute-done | bytes 135200 | tf_op jit(solution)/shard_map/ppermute | solution.py:258
  28.4 0.0 copy-start.1
  28.4 0.7 %copy-done.1 = f32[16,128]{1,0:T(8,128)S(1)} copy-done((f32[16,128]{1,0:T(8,128)S(1)}, f32[16,128]{1,0:T(8,128)}, u32[]{:S(2)}) %copy-start.1) | copy-done | bytes 8216
  29.1 0.0 copy-start
  29.1 0.9 %copy-done = bf16[528,128]{1,0:T(8,128)(2,1)S(1)} copy-done((bf16[528,128]{1,0:T(8,128)(2,1)S(1)}, bf16[528,128]{1,0:T(8,128)(2,1)}, u32[]{:S(2)}) %copy-start) | copy-done | bytes 135192
  30.0 7.6 %aggregate.1 = (bf16[4096,128]{1,0:T(8,128)(2,1)}, bf16[512,128]{1,0:T(8,128)(2,1)}) custom-call(f32[16,128]{1,0:T(8,128)S(1)} %copy-done.1, bf16[1,528,128]{2,1,0:T(8,128)(2,1)S(1)} %bitcast.13, bf16[1,528,128]{2,1,0:T(8,128)(2,1)S(1)} %bitcast.14, bf16[1,528,128]{2,1,0:T(8,128)(2,1)S(1)} %bitcast.15, bf16[1,528,128]{2,1,0:T(8,128)(2,1)S(1)} %bitcast.16, ...), custom_call_target="tpu_custom_call" | custom-call | tf_op jit(solution)/shard_map/aggregate/pallas_call | solution.py:290
Async XLA Ops:
  2.7 10.8 %collective-permute-start = (bf16[528,128]{1,0:T(8,128)(2,1)}, bf16[528,128]{1,0:T(8,128)(2,1)S(1)}, u32[]{:S(2)}, u32[]{:S(2)}) collective-permute-start(bf16[528,128]{1,0:T(8,128)(2,1)} %get-tuple-element.5), channel_id=1, source_target_pairs={{0,8},{4,12},{8,0},{12,4},{1,9},{5,13},{9,1},{13,5},{2,10},{6,14},... | collective-permute-start | bytes 405512 | tf_op jit(solution)/shard_map/ppermute | solution.py:258
  6.8 9.5 %collective-permute-start.1 = (bf16[528,128]{1,0:T(8,128)(2,1)}, bf16[528,128]{1,0:T(8,128)(2,1)S(1)}, u32[]{:S(2)}, u32[]{:S(2)}) collective-permute-start(bf16[528,128]{1,0:T(8,128)(2,1)} %get-tuple-element.5), channel_id=1, source_target_pairs={{0,4},{4,0},{8,12},{12,8},{1,5},{5,1},{9,13},{13,9},{2,6},{6,2},{1... | collective-permute-start | bytes 405512 | tf_op jit(solution)/shard_map/ppermute | solution.py:258
  13.5 5.0 %collective-permute-start.2 = (bf16[528,128]{1,0:T(8,128)(2,1)S(1)}, bf16[528,128]{1,0:T(8,128)(2,1)S(1)}, u32[]{:S(2)}, u32[]{:S(2)}) collective-permute-start(bf16[528,128]{1,0:T(8,128)(2,1)S(1)} %collective-permute-done), channel_id=1, source_target_pairs={{0,4},{4,0},{8,12},{12,8},{1,5},{5,1},{9,13},{13,9},{2,6},{6,2},{1... | collective-permute-start | bytes 405512 | tf_op jit(solution)/shard_map/ppermute | solution.py:258
  14.3 6.7 %collective-permute-start.3 = (bf16[528,128]{1,0:T(8,128)(2,1)}, bf16[528,128]{1,0:T(8,128)(2,1)S(1)}, u32[]{:S(2)}, u32[]{:S(2)}) collective-permute-start(bf16[528,128]{1,0:T(8,128)(2,1)} %get-tuple-element.5), channel_id=1, source_target_pairs={{0,2},{2,0},{1,3},{3,1},{4,6},{6,4},{5,7},{7,5},{8,10},{10,8},{9,1... | collective-permute-start | bytes 405512 | tf_op jit(solution)/shard_map/ppermute | solution.py:258
  15.8 11.0 %collective-permute-start.4 = (bf16[528,128]{1,0:T(8,128)(2,1)S(1)}, bf16[528,128]{1,0:T(8,128)(2,1)S(1)}, u32[]{:S(2)}, u32[]{:S(2)}) collective-permute-start(bf16[528,128]{1,0:T(8,128)(2,1)S(1)} %collective-permute-done), channel_id=1, source_target_pairs={{0,2},{2,0},{1,3},{3,1},{4,6},{6,4},{5,7},{7,5},{8,10},{10,8},{9,1... | collective-permute-start | bytes 405512 | tf_op jit(solution)/shard_map/ppermute | solution.py:258
  16.3 10.5 %collective-permute-start.5 = (bf16[528,128]{1,0:T(8,128)(2,1)S(1)}, bf16[528,128]{1,0:T(8,128)(2,1)S(1)}, u32[]{:S(2)}, u32[]{:S(2)}) collective-permute-start(bf16[528,128]{1,0:T(8,128)(2,1)S(1)} %collective-permute-done.1), channel_id=1, source_target_pairs={{0,2},{2,0},{1,3},{3,1},{4,6},{6,4},{5,7},{7,5},{8,10},{10,8},{9,1... | collective-permute-start | bytes 405512 | tf_op jit(solution)/shard_map/ppermute | solution.py:258
  18.6 9.8 %collective-permute-start.6 = (bf16[528,128]{1,0:T(8,128)(2,1)S(1)}, bf16[528,128]{1,0:T(8,128)(2,1)S(1)}, u32[]{:S(2)}, u32[]{:S(2)}) collective-permute-start(bf16[528,128]{1,0:T(8,128)(2,1)S(1)} %collective-permute-done.2), channel_id=1, source_target_pairs={{0,2},{2,0},{1,3},{3,1},{4,6},{6,4},{5,7},{7,5},{8,10},{10,8},{9,1... | collective-permute-start | bytes 405512 | tf_op jit(solution)/shard_map/ppermute | solution.py:258
  28.4 0.7 %copy-start.1 = (f32[16,128]{1,0:T(8,128)S(1)}, f32[16,128]{1,0:T(8,128)}, u32[]{:S(2)}) copy-start(f32[16,128]{1,0:T(8,128)} %get-tuple-element.4.refs_0_) | copy-start | bytes 24580
  29.1 0.9 %copy-start = (bf16[528,128]{1,0:T(8,128)(2,1)S(1)}, bf16[528,128]{1,0:T(8,128)(2,1)}, u32[]{:S(2)}) copy-start(bf16[528,128]{1,0:T(8,128)(2,1)} %get-tuple-element.5) | copy-start | bytes 405508

commit v5 on v4

v5 whole, which is shorter than its diff:
```python
import functools
import jax
import jax.numpy as jnp
from jax import lax
from jax.experimental import pallas as pl
from jax.experimental.pallas import tpu as pltpu
from jax.sharding import PartitionSpec as P

LANES = 128
LOW = 7
MASK = 127
F32 = jnp.float32
BF16 = jnp.bfloat16
I32 = jnp.int32
I16 = jnp.int16
FAR = 1e9
NT = (((1,), (1,)), ((), ()))
BLOCK = 256


class Sizes:
    def __init__(self, owners, rows, slots):
        self.owners, self.rows, self.slots = owners, rows, slots
        self.window = slots // 4
        self.chunks = rows // LANES
        self.user_rows = -(-8 * owners // LANES)
        self.code_rows = -(-(3 * self.chunks + 2 * self.user_rows) // 16) * 16
        self.span = min(owners, 8)
        self.shifts = 1 if owners <= self.span else 2
        self.capacity = 2 * rows // owners
        self.per_group = LANES // self.capacity
        self.groups = owners // self.per_group


def iota(shape, axis):
    return lax.broadcasted_iota(I32, shape, axis)


def ones_where(condition):
    return jnp.where(condition, F32(1), F32(0)).astype(BF16)


def dot(a, b):
    return jnp.dot(a, b, preferred_element_type=F32)


def loop(count, body, carry):
    if count <= 8:
        for i in range(count):
            carry = body(i, carry)
        return carry
    return lax.fori_loop(0, count, body, carry)


def send_kernel(z, me_ref, rate_ref, events_ref, weight_ref, route_ref, bucket_ref, segment_ref, block_ref, own_ref):
    groups = rate_ref.shape[0]
    lane = iota((1, LANES), 1)
    rate = jnp.full((1, LANES), rate_ref[0], F32)
    for g in range(1, groups):
        rate = jnp.where(lane >= g * (LANES // groups), rate_ref[g], rate)
    route = route_ref[...]
    bucket = bucket_ref[...]
    place = (route * z.slots + bucket).astype(F32)
    first = ((route >> (z.span.bit_length() - 1)) * (z.span * z.slots)).astype(F32)
    me = jnp.full((8 - 1, LANES), me_ref[0], I32).astype(F32)
    own_ref[0:16, :] = jnp.concatenate([place, first, rate, me], axis=0)
    spot = place - first - F32(z.span * z.slots // 2)
    columns = jnp.concatenate([weight_ref[...], spot], axis=0).T
    for r in range(z.chunks):
        part = slice(r * LANES, (r + 1) * LANES)
        weighted = (columns[:, r : r + 1] * events_ref[part, :].astype(F32)).astype(BF16)
        grown = weighted.astype(F32) * jnp.exp(columns[:, z.chunks + r : z.chunks + r + 1] * rate)
        block_ref[part, :] = grown.astype(BF16)
    ones = jnp.ones((8, LANES), BF16)
    high, low = [], []
    for u in range(z.user_rows):
        user = iota((LANES, LANES), 0) + u * LANES
        below = jnp.zeros((LANES, LANES), F32)
        for r in range(z.slots // LANES):
            below += jnp.where(segment_ref[r : r + 1, :] < user, F32(1), F32(0))
        count = lax.dot_general(ones, below.astype(BF16), NT, preferred_element_type=F32)[0:1]
        own_ref[16 + u : 17 + u, :] = count
        count = count.astype(I32)
        high.append(count >> LOW)
        low.append(count & MASK)
    spare = z.code_rows - 3 * z.chunks - 2 * z.user_rows
    pad = [jnp.zeros((spare, LANES), I32)] if spare else []
    codes = jnp.concatenate([route, bucket >> LOW, bucket & MASK] + high + low + pad, axis=0)
    block_ref[z.rows : z.rows + z.code_rows, :] = codes.astype(F32).astype(BF16)


class Pieces:
    def __init__(self, z, refs):
        self.z, self.refs = z, refs
        self.count = len(refs) if len(refs) != 1 else refs[0].shape[0]
        self.per_group = 1 if len(refs) != 1 else z.per_group
        self.groups = self.count // self.per_group

    def block(self, s):
        return (self.refs[s], 0) if len(self.refs) != 1 else (self.refs[0], s)

    def codes(self, s):
        ref, i = self.block(s)
        return ref[i, self.z.rows : self.z.rows + self.z.code_rows, :].astype(F32)

    def rows(self, s):
        ref, i = self.block(s)
        return ref[i, 0 : self.z.rows, :]

    def place(self, s):
        n, tile = self.z.chunks, self.codes(s)
        return tile[0:n] * F32(self.z.slots) + F32(LANES) * tile[n : 2 * n] + tile[2 * n : 3 * n]

    def below(self, s, u):
        tile, at = self.codes(s), 3 * self.z.chunks + u
        return F32(LANES) * tile[at : at + 1] + tile[at + self.z.user_rows : at + self.z.user_rows + 1]


class Runs:
    def __init__(self, z, starts):
        self.z, self.starts = z, starts
        users = min(LANES, 8 * z.owners)
        self.columns = [jnp.broadcast_to(row, (8, LANES)).T[:users, 0:1] for row in starts]
        self.steps = []
        for u, row in enumerate(starts):
            before = pltpu.roll(row, 1, 1)
            first = starts[u - 1][:, LANES - 1 : LANES] if u else jnp.zeros((1, 1), F32)
            step = (row - jnp.where(iota((1, LANES), 1) == 0, first, before)).astype(I32)
            pair = [jnp.broadcast_to(part, (LANES, LANES)) for part in (step >> LOW, step & MASK)]
            self.steps.append(jnp.concatenate(pair, axis=0).astype(F32).astype(BF16))

    def root(self, position):
        total = jnp.zeros((position.shape[0], 2 * LANES), F32)
        for row, step in zip(self.starts, self.steps):
            total += lax.dot_general(ones_where(row <= position), step, NT, preferred_element_type=F32)
        start = F32(LANES) * total[:, :LANES] + total[:, LANES:]
        return lax.rsqrt(jnp.minimum(position - start, F32(self.z.window)) + F32(1))

    def until(self, row):
        after = jnp.full((1, LANES), FAR, F32)
        for column in self.columns:
            later = jnp.where(column > row, column, F32(FAR))
            after = jnp.minimum(after, jnp.min(later, axis=0, keepdims=True))
        return jnp.minimum(row + F32(self.z.window), after - F32(1))


def pack(z, pieces, base, marks_ref, codes_ref, rows_ref, from_ref):
    if not pieces.count:
        return
    spare = jnp.zeros((8 - z.chunks, LANES), F32)

    def mark(s, carry):
        local = pieces.place(s) - base
        near = local.astype(I32)
        codes_ref[s] = jnp.concatenate([near >> LOW, near & MASK], axis=0).astype(F32)
        own = (local >= 0) & (local < F32(z.slots))
        tail = (local >= F32(-z.window)) & (local < 0)
        marks_ref[0, s] = jnp.concatenate([jnp.where(own, F32(1), F32(0)), spare], axis=0)
        marks_ref[1, s] = jnp.concatenate([jnp.where(tail, F32(1), F32(0)), spare], axis=0)
        return carry

    loop(pieces.count, mark, 0)
    upper = ones_where(iota((LANES, LANES), 0) < iota((LANES, LANES), 1))
    full = jnp.ones((LANES, LANES), BF16)
    lines = pieces.count * 8
    at, by = iota((lines, lines), 0), iota((lines, lines), 1)
    earlier = ones_where(((at >> 3) == (by >> 3)) & (by < at))
    source = iota((lines, LANES), 0) >> 3
    offset = ((source & (pieces.per_group - 1)) * z.capacity).astype(F32)
    for kind in range(2):
        marked = marks_ref[kind].reshape(lines, LANES)
        mark = marked.astype(BF16)
        rank = dot(mark, upper) + dot(earlier, dot(mark, full).astype(BF16)) + offset
        marks_ref[kind] = jnp.where(marked > 0, rank, F32(-1)).reshape(pieces.count, 8, LANES)

    spots = iota((LANES, LANES), 0).astype(F32)
    code_line = iota((2 * z.chunks, LANES), 0) & (z.chunks - 1)
    for kind in range(2):
        for g in range(pieces.groups):

            def add(i, carry):
                values, places = carry
                s = g * pieces.per_group + i
                ranks = marks_ref[kind, s]
                codes = codes_ref[s]
                hot = jnp.concatenate([ones_where(spots == ranks[r : r + 1]) for r in range(z.chunks)], axis=1)
                wide = [jnp.where(code_line == r, codes, F32(0)).astype(BF16) for r in range(z.chunks)]
                values += dot(hot, pieces.rows(s))
                places += lax.dot_general(jnp.concatenate(wide, axis=1), hot, NT, preferred_element_type=F32)
                return values, places

            zero = (jnp.zeros((LANES, LANES), F32), jnp.zeros((2 * z.chunks, LANES), F32))
            values, places = loop(pieces.per_group, add, zero)
            line = kind * pieces.groups + g
            rows_ref[line * LANES : (line + 1) * LANES, :] = values.astype(BF16)
            high = jnp.sum(places[: z.chunks], axis=0, keepdims=True)
            low = jnp.sum(places[z.chunks :], axis=0, keepdims=True)
            from_ref[line : line + 1, :] = F32(LANES) * high + low


def held(position, bounds):
    one, nothing = BF16(1), BF16(0)
    masks = [jnp.where((position >= a) & (position <= b), one, nothing) for a, b in bounds]
    return jnp.concatenate(masks, axis=1)


def anchors(z, me):
    middle = F32(z.span * z.slots // 2)
    span_of = lambda owner: (owner.astype(I32) >> (z.span.bit_length() - 1)).astype(F32) * F32(z.span)
    own = (me - span_of(me)) * F32(z.slots) - middle
    tail = (me - span_of(me - F32(1))) * F32(z.slots) - middle
    return own, tail


def short(row):
    return row.astype(I32).astype(I16)


def early_kernel(z, count, *refs):
    own_ref, pieces = refs[0], Pieces(z, refs[1 : 1 + count])
    sums_ref, scale_ref, rows_ref, from_ref, marks_ref, codes_ref = refs[1 + count :]
    rate, me = own_ref[8:9, :], own_ref[9:10, :]
    runs = Runs(z, [own_ref[16 + u : 17 + u, :] for u in range(z.user_rows)])
    pack(z, pieces, me * F32(z.slots), marks_ref, codes_ref, rows_ref, from_ref)
    own_anchor, _ = anchors(z, me)
    inner = iota((BLOCK, LANES), 0)
    fall = jnp.exp(-rate * inner.astype(F32))
    bounds = []
    for g in range(pieces.groups if pieces.count else 0):
        begin = from_ref[g : g + 1, :]
        bounds.append((short(begin), short(runs.until(begin))))
    for b in range(z.slots // BLOCK):
        part = slice(b * BLOCK, (b + 1) * BLOCK)
        if bounds:
            mask = held((inner + b * BLOCK).astype(I16), bounds)
            sums_ref[part, :] = dot(mask, rows_ref[0 : len(bounds) * LANES, :])
        else:
            sums_ref[part, :] = jnp.zeros((BLOCK, LANES), F32)
        if b * BLOCK >= z.window:
            start = F32(b * BLOCK)
            scale_ref[part, :] = fall * jnp.exp(-rate * (start + own_anchor)) * runs.root(inner.astype(F32) + start)


def late_kernel(z, early, late, *refs):
    own_ref, sums_ref, scale_ref, tail_rows_ref, tail_from_ref = refs[:5]
    blocks = refs[5 : 5 + early + late]
    table_ref, feature_ref, place_ref, until_ref, rows_ref, from_ref, marks_ref, codes_ref = refs[5 + early + late :]
    pieces, last = Pieces(z, blocks), Pieces(z, blocks[early:])
    rate, me = own_ref[8:9, :], own_ref[9:10, :]
    base = me * F32(z.slots)
    starts = []
    for u in range(z.user_rows):
        add = lambda s, total: total + pieces.below(s, u)
        starts.append(loop(pieces.count, add, jnp.zeros((1, LANES), F32)))
    runs = Runs(z, starts)
    pack(z, last, base, marks_ref, codes_ref, rows_ref, from_ref)

    own_anchor, tail_anchor = anchors(z, me)
    inner = iota((BLOCK, LANES), 0)
    fall = jnp.exp(-rate * inner.astype(F32))
    bounds = []
    for ref, first, lines in ((from_ref, 0, 2 * last.groups), (tail_from_ref, early, early)):
        for g in range(first, first + lines):
            begin = ref[g : g + 1, :]
            bounds.append((short(begin), short(runs.until(begin + base) - base)))
    n = last.groups
    for b in range(z.slots // BLOCK):
        part = slice(b * BLOCK, (b + 1) * BLOCK)
        position = (inner + b * BLOCK).astype(I16)
        start = F32(b * BLOCK)
        value = sums_ref[part, :] + dot(held(position, bounds[:n]), rows_ref[0 : n * LANES, :])
        if b * BLOCK >= z.window:
            value = value * scale_ref[part, :]
        else:
            tail = dot(held(position, bounds[n : 2 * n]), rows_ref[n * LANES : 2 * n * LANES, :])
            if early:
                tail += dot(held(position, bounds[2 * n :]), tail_rows_ref[early * LANES : 2 * early * LANES, :])
            own_fall = jnp.exp(-rate * (start + own_anchor))
            if z.shifts == 1:
                value = (value + tail) * own_fall
            else:
                value = value * own_fall + tail * jnp.exp(-rate * (start + tail_anchor))
            value = value * fall * runs.root(inner.astype(F32) + (start + base))
        table_ref[part, :] = value.astype(BF16)

    narrow = z.owners * z.slots <= 32768

    def decode(s, carry):
        place = pieces.place(s)
        until = jnp.concatenate([runs.until(place[r : r + 1]) for r in range(z.chunks)], axis=0)
        if narrow:
            until = jnp.minimum(until, F32(32767))
        spare = jnp.zeros((8 - z.chunks, LANES), F32)
        place_ref[s] = jnp.concatenate([place, spare], axis=0)
        until_ref[s] = jnp.concatenate([until, spare], axis=0)
        return carry

    loop(pieces.count, decode, 0)
    columns = own_ref[0:8, :].T
    wide_column = lambda at: jnp.broadcast_to(columns[:, at : at + 1], (LANES, LANES))
    for t in range(z.rows // BLOCK):
        at = t * (BLOCK // LANES)
        position = jnp.concatenate([wide_column(at + k) for k in range(BLOCK // LANES)], axis=0)
        first = jnp.concatenate([wide_column(z.chunks + at + k) for k in range(BLOCK // LANES)], axis=0)
        point = short(position) if narrow else position
        total = jnp.zeros((BLOCK, LANES), F32)
        for shift in range(z.shifts):

            def add(s, value):
                begin, end = place_ref[s], until_ref[s]
                bounds = [(begin[r : r + 1], end[r : r + 1]) for r in range(z.chunks)]
                if narrow:
                    mask = held(point, [(short(a), short(b)) for a, b in bounds])
                else:
                    masks = []
                    for a, b in bounds:
                        inside = a >= first if shift == 0 else a < first
                        masks.append(ones_where((point >= a) & (point <= b) & inside))
                    mask = jnp.concatenate(masks, axis=1)
                return value + dot(mask, pieces.rows(s))

            value = loop(pieces.count, add, jnp.zeros((BLOCK, LANES), F32))
            center = first + F32(z.span * z.slots // 2 - shift * z.span * z.slots)
            total += value * jnp.exp(-rate * (position - center))
        feature_ref[t * BLOCK : (t + 1) * BLOCK, :] = (total * runs.root(position)).astype(BF16)


def swap(block, axis, distance):
    return lax.ppermute(block, axis, [(i, i ^ distance) for i in range(lax.axis_size(axis))])


def spread(blocks, axis, early=None):
    distance = lax.axis_size(axis) // 2
    while distance:
        for block in list(blocks):
            if early is not None and block is not blocks[0]:
                block, early = lax.optimization_barrier((block, early))
            blocks = blocks + [swap(block, axis, distance)]
        distance //= 2
    return blocks, early


def on_device(events, event_weight, route, bucket, segment, decay_rate):
    rows, width = events.shape
    shard_count = lax.axis_size("shard")
    owners = lax.axis_size("key") * shard_count
    slots = segment.shape[0]
    z = Sizes(owners, rows, slots)
    block_rows = rows + z.code_rows
    smem = pl.BlockSpec(memory_space=pltpu.SMEM)
    vmem = pl.BlockSpec(memory_space=pltpu.VMEM)
    shape = jax.ShapeDtypeStruct
    me = (lax.axis_index("key") * shard_count + lax.axis_index("shard")).astype(I32).reshape(1)
    block, own = pl.pallas_call(
        functools.partial(send_kernel, z),
        out_shape=(shape((block_rows, width), BF16), shape((16 + z.user_rows + 7, LANES), F32)),
        in_specs=[smem, smem] + [vmem] * 5,
        out_specs=(vmem, vmem),
        compiler_params=pltpu.CompilerParams(vmem_limit_bytes=56 * 1024 * 1024),
        name="weigh",
    )(
        me, decay_rate, events, event_weight.reshape(z.chunks, LANES), route.reshape(z.chunks, LANES),
        bucket.reshape(z.chunks, LANES), segment.reshape(slots // LANES, LANES),
    )
    if shard_count == 2:
        near = swap(block, "shard", 1)
        blocks, near = spread([block], "key", near)
        across = [swap(b, "shard", 1) for b in blocks[1:]]
        early, late = blocks + [near] + across[1:-1], across[:1] + across[-1:]
    else:
        blocks, _ = spread([block], "key")
        blocks, _ = spread(blocks, "shard")
        early, late = [], [jnp.concatenate(blocks, axis=0)]
    early = [b.reshape(-1, block_rows, width) for b in early]
    late = [b.reshape(-1, block_rows, width) for b in late]
    lines = max(8, 2 * len(early))
    late_lines = 2 * (len(late) if len(late) > 1 else z.groups)
    late_count = sum(b.shape[0] for b in late)
    grant = pltpu.CompilerParams(vmem_limit_bytes=(16 if owners <= 8 else 48) * 1024 * 1024)
    kept = pl.pallas_call(
        functools.partial(early_kernel, z, len(early)),
        out_shape=(
            shape((slots, width), F32),
            shape((slots, width), F32),
            shape((lines * LANES, LANES), BF16),
            shape((lines, LANES), F32),
        ),
        in_specs=[vmem] * (1 + len(early)),
        out_specs=(vmem,) * 4,
        scratch_shapes=[
            pltpu.VMEM((2, max(1, len(early)), 8, LANES), F32),
            pltpu.VMEM((max(1, len(early)), 2 * z.chunks, LANES), F32),
        ],
        compiler_params=grant,
        cost_estimate=pl.CostEstimate(flops=2 * slots * rows * 6 * LANES, bytes_accessed=6 * slots * LANES, transcendentals=0),
        name="early_sums",
    )(own, *early)
    return pl.pallas_call(
        functools.partial(late_kernel, z, len(early), len(late)),
        out_shape=(shape((slots, width), BF16), shape((rows, width), BF16)),
        in_specs=[vmem] * (5 + len(early) + len(late)),
        out_specs=(vmem, vmem),
        scratch_shapes=[
            pltpu.VMEM((owners, 8, LANES), F32),
            pltpu.VMEM((owners, 8, LANES), F32),
            pltpu.VMEM((late_lines * LANES, LANES), BF16),
            pltpu.VMEM((late_lines, LANES), F32),
            pltpu.VMEM((2, late_count, 8, LANES), F32),
            pltpu.VMEM((late_count, 2 * z.chunks, LANES), F32),
        ],
        compiler_params=grant,
        name="table_and_rows",
    )(own, *kept, *early, *late)


def solution(mesh):
    placed = (
        P(("groups", "key", "shard"), "lane"),
        P(("groups", "key", "shard")),
        P(("groups", "key", "shard"), None),
        P(("groups", "key", "shard")),
        P(("groups", "key", "shard")),
        P("lane"),
    )
    return jax.shard_map(
        on_device,
        mesh=mesh,
        in_specs=placed,
        out_specs=(P(("groups", "key", "shard"), "lane"), P(("groups", "key", "shard"), "lane")),
        check_vma=False,
    )
```

time: 37.8 us -> 31.2 us (0.83)
  waiting for transfers between devices: 14.3 us -> 8.98 us
  starting transfers between devices: 11.4 us -> 10.3 us
    ppermute x7, waiting for transfers between devices: 14.3 us -> 8.98 us  [swap(): lax.ppermute(block, axis, [(i, i ^ distance) for i in range(lax.axis_size...]
    ppermute x7, starting transfers between devices: 11.4 us -> 10.3 us  [swap(): lax.ppermute(block, axis, [(i, i ^ distance) for i in range(lax.axis_size...]
    pallas_call x1 -> x2, Pallas kernels: 7.58 us -> 7.35 us  [the longest x1 4.06 us: on_device(): pl.pallas_call(functools.partial(late_kernel, z, len(early), len(late)),...]
  transfers between devices with their start and end apart: 7 -> 7, of which waited for: 5 -> 3; matrix products, arithmetic and copies ran while one was open for 0% -> 0% of each run, Pallas kernels for 0% -> 11%
where the time goes in v5:
time: 31.2 us; the launch traced here: 31 us
  starting transfers between devices  10.3 us (33%)
  Pallas kernels  9.42 us (30%)
  waiting for transfers between devices  8.98 us (29%)
  local copies, waits for them, and re-layouts  1.61 us (5%)
  between operations  0.67 us (2%)
    ppermute x7, starting transfers between devices, swap(): lax.ppermute(block, axis, [(i, i ^ distance) for i in range(lax.axis_size...  10.3 us
    ppermute x7, waiting for transfers between devices, swap(): lax.ppermute(block, axis, [(i, i ^ distance) for i in range(lax.axis_size...  8.98 us
    pallas_call x1, Pallas kernels, on_device(): pl.pallas_call(functools.partial(late_kernel, z, len(early), len(late)),...  4.06 us
    pallas_call x1, Pallas kernels, on_device(): pl.pallas_call(functools.partial(early_kernel, z, len(early)), out_shape=...  3.29 us
    pallas_call x1, Pallas kernels, on_device(): pl.pallas_call(functools.partial(send_kernel, z), out_shape=(shape((block...  2.08 us
    unnamed x4, local copies, waits for them, and re-layouts  1.61 us
  transfers between devices with their start and end apart: 7, of which 3 were waited for; matrix products, arithmetic and copies ran while one was open for 0% of the time, Pallas kernels for 11%

profile of v5, /device:TPU:0, one launch (start us, length us, event | category | flops | bytes accessed | tf_op | source)
XLA Modules:
  0.0 31.0 jit_solution(5025570961526127991)
XLA Ops:
  0.6 2.1 %weigh.1 = (bf16[528,128]{1,0:T(8,128)(2,1)}, f32[24,128]{1,0:T(8,128)}) custom-call(s32[1]{0:T(128)} %bitcast.me_ref, f32[4]{0:T(128)} %rate_ref.1, bf16[512,128]{1,0:T(8,128)(2,1)} %events_ref.1, f32[4,128]{1,0:T(4,128)} %bitcast.28, s32[4,128]{1,0:T(4,128)} %bitcast.29, s32[4,128]{1,0:T(4,128)} %bitcast.30, s32[32,128]{1,0:T(8,128)} %bitcast.27), custom_call_target="tpu_custom_call" | custom-call | tf_op jit(solution)/shard_map/weigh/pallas_call | solution.py:354
  2.7 2.9 %collective-permute-start.2 = (bf16[528,128]{1,0:T(8,128)(2,1)}, bf16[528,128]{1,0:T(8,128)(2,1)S(1)}, u32[]{:S(2)}, u32[]{:S(2)}) collective-permute-start(bf16[528,128]{1,0:T(8,128)(2,1)} %get-tuple-element.11), channel_id=1, source_target_pairs={{0,2},{2,0},{1,3},{3,1},{4,6},{6,4},{5,7},{7,5},{8,10},{10,8},{9,1... | collective-permute-start | bytes 405512 | tf_op jit(solution)/shard_map/ppermute | solution.py:329
  5.7 2.6 %collective-permute-start = (bf16[528,128]{1,0:T(8,128)(2,1)}, bf16[528,128]{1,0:T(8,128)(2,1)S(1)}, u32[]{:S(2)}, u32[]{:S(2)}) collective-permute-start(bf16[528,128]{1,0:T(8,128)(2,1)} %get-tuple-element.11), channel_id=1, source_target_pairs={{0,8},{4,12},{8,0},{12,4},{1,9},{5,13},{9,1},{13,5},{2,10},{6,14},... | collective-permute-start | bytes 405512 | tf_op jit(solution)/shard_map/ppermute | solution.py:329
  8.2 1.6 %collective-permute-start.1 = (bf16[528,128]{1,0:T(8,128)(2,1)}, bf16[528,128]{1,0:T(8,128)(2,1)S(1)}, u32[]{:S(2)}, u32[]{:S(2)}) collective-permute-start(bf16[528,128]{1,0:T(8,128)(2,1)} %get-tuple-element.11), channel_id=1, source_target_pairs={{0,4},{4,0},{8,12},{12,8},{1,5},{5,1},{9,13},{13,9},{2,6},{6,2},{1... | collective-permute-start | bytes 405512 | tf_op jit(solution)/shard_map/ppermute | solution.py:329
  9.8 0.0 collective-permute-done.2
  9.8 5.0 %collective-permute-done = bf16[528,128]{1,0:T(8,128)(2,1)S(1)} collective-permute-done((bf16[528,128]{1,0:T(8,128)(2,1)}, bf16[528,128]{1,0:T(8,128)(2,1)S(1)}, u32[]{:S(2)}, u32[]{:S(2)}) %collective-permute-start) | collective-permute-done | bytes 135200 | tf_op jit(solution)/shard_map/ppermute | solution.py:329
  14.8 0.7 %collective-permute-start.3 = (bf16[528,128]{1,0:T(8,128)(2,1)S(1)}, bf16[528,128]{1,0:T(8,128)(2,1)S(1)}, u32[]{:S(2)}, u32[]{:S(2)}) collective-permute-start(bf16[528,128]{1,0:T(8,128)(2,1)S(1)} %collective-permute-done), channel_id=1, source_target_pairs={{0,4},{4,0},{8,12},{12,8},{1,5},{5,1},{9,13},{13,9},{2,6},{6,2},{1... | collective-permute-start | bytes 405512 | tf_op jit(solution)/shard_map/ppermute | solution.py:329
  15.5 0.0 collective-permute-done.1
  15.5 0.5 %collective-permute-start.4 = (bf16[528,128]{1,0:T(8,128)(2,1)S(1)}, bf16[528,128]{1,0:T(8,128)(2,1)S(1)}, u32[]{:S(2)}, u32[]{:S(2)}) collective-permute-start(bf16[528,128]{1,0:T(8,128)(2,1)S(1)} %collective-permute-done.1), channel_id=1, source_target_pairs={{0,2},{2,0},{1,3},{3,1},{4,6},{6,4},{5,7},{7,5},{8,10},{10,8},{9,1... | collective-permute-start | bytes 405512 | tf_op jit(solution)/shard_map/ppermute | solution.py:329
  16.0 1.5 %collective-permute-start.5 = (bf16[528,128]{1,0:T(8,128)(2,1)S(1)}, bf16[528,128]{1,0:T(8,128)(2,1)S(1)}, u32[]{:S(2)}, u32[]{:S(2)}) collective-permute-start(bf16[528,128]{1,0:T(8,128)(2,1)S(1)} %collective-permute-done), channel_id=1, source_target_pairs={{0,2},{2,0},{1,3},{3,1},{4,6},{6,4},{5,7},{7,5},{8,10},{10,8},{9,1... | collective-permute-start | bytes 405512 | tf_op jit(solution)/shard_map/ppermute | solution.py:329
  17.5 2.3 %collective-permute-done.3 = bf16[528,128]{1,0:T(8,128)(2,1)S(1)} collective-permute-done((bf16[528,128]{1,0:T(8,128)(2,1)S(1)}, bf16[528,128]{1,0:T(8,128)(2,1)S(1)}, u32[]{:S(2)}, u32[]{:S(2)}) %collective-permute-start.3) | collective-permute-done | bytes 135200 | tf_op jit(solution)/shard_map/ppermute | solution.py:329
  19.8 0.5 %collective-permute-start.6 = (bf16[528,128]{1,0:T(8,128)(2,1)S(1)}, bf16[528,128]{1,0:T(8,128)(2,1)S(1)}, u32[]{:S(2)}, u32[]{:S(2)}) collective-permute-start(bf16[528,128]{1,0:T(8,128)(2,1)S(1)} %collective-permute-done.3), channel_id=1, source_target_pairs={{0,2},{2,0},{1,3},{3,1},{4,6},{6,4},{5,7},{7,5},{8,10},{10,8},{9,1... | collective-permute-start | bytes 405512 | tf_op jit(solution)/shard_map/ppermute | solution.py:329
  20.3 1.6 %collective-permute-done.4 = bf16[528,128]{1,0:T(8,128)(2,1)S(1)} collective-permute-done((bf16[528,128]{1,0:T(8,128)(2,1)S(1)}, bf16[528,128]{1,0:T(8,128)(2,1)S(1)}, u32[]{:S(2)}, u32[]{:S(2)}) %collective-permute-start.4) | collective-permute-done | bytes 135200 | tf_op jit(solution)/shard_map/ppermute | solution.py:329
  22.0 0.0 copy-start
  22.0 0.9 %copy-done = bf16[528,128]{1,0:T(8,128)(2,1)S(1)} copy-done((bf16[528,128]{1,0:T(8,128)(2,1)S(1)}, bf16[528,128]{1,0:T(8,128)(2,1)}, u32[]{:S(2)}) %copy-start) | copy-done | bytes 135192
  22.9 0.0 copy-start.1
  22.9 0.7 %copy-done.1 = f32[24,128]{1,0:T(8,128)S(1)} copy-done((f32[24,128]{1,0:T(8,128)S(1)}, f32[24,128]{1,0:T(8,128)}, u32[]{:S(2)}) %copy-start.1) | copy-done | bytes 12312
  23.6 3.3 %early_sums.1 = (f32[4096,128]{1,0:T(8,128)S(1)}, f32[4096,128]{1,0:T(8,128)S(1)}, bf16[1536,128]{1,0:T(8,128)(2,1)S(1)}, f32[12,128]{1,0:T(8,128)S(1)}) custom-call(f32[24,128]{1,0:T(8,128)S(1)} %copy-done.1, bf16[1,528,128]{2,1,0:T(8,128)(2,1)S(1)} %bitcast.13, bf16[1,528,128]{2,1,0:T(8,128)(2,1)S(1)} %bitcast.17, bf16[1,528,128]{2,1,0:T(8,128)(2,1)S(1)} %bitcast.19, ...), custom_call_target="tpu_custom_call" | custom-call | flops 3221225472 | bytes 3145728 | tf_op jit(solution)/shard_map/early_sums/pallas_call | solution.py:380
  26.9 0.0 collective-permute-done.5
  26.9 0.0 collective-permute-done.6
  26.9 4.1 %table_and_rows.1 = (bf16[4096,128]{1,0:T(8,128)(2,1)}, bf16[512,128]{1,0:T(8,128)(2,1)}) custom-call(f32[24,128]{1,0:T(8,128)S(1)} %copy-done.1, f32[4096,128]{1,0:T(8,128)S(1)} %get-tuple-element.14.refs_1_, f32[4096,128]{1,0:T(8,128)S(1)} %get-tuple-element.15.refs_2_, bf16[1536,128]{1,0:T(8,128)(2,1)S(1)} %get-tuple-element.16.refs_3_, ...), custom_call_target="tpu_custom_call" | custom-call | tf_op jit(solution)/shard_map/table_and_rows/pallas_call | solution.py:398
Async XLA Ops:
  2.7 7.1 %collective-permute-start.2 = (bf16[528,128]{1,0:T(8,128)(2,1)}, bf16[528,128]{1,0:T(8,128)(2,1)S(1)}, u32[]{:S(2)}, u32[]{:S(2)}) collective-permute-start(bf16[528,128]{1,0:T(8,128)(2,1)} %get-tuple-element.11), channel_id=1, source_target_pairs={{0,2},{2,0},{1,3},{3,1},{4,6},{6,4},{5,7},{7,5},{8,10},{10,8},{9,1... | collective-permute-start | bytes 405512 | tf_op jit(solution)/shard_map/ppermute | solution.py:329
  5.7 9.2 %collective-permute-start = (bf16[528,128]{1,0:T(8,128)(2,1)}, bf16[528,128]{1,0:T(8,128)(2,1)S(1)}, u32[]{:S(2)}, u32[]{:S(2)}) collective-permute-start(bf16[528,128]{1,0:T(8,128)(2,1)} %get-tuple-element.11), channel_id=1, source_target_pairs={{0,8},{4,12},{8,0},{12,4},{1,9},{5,13},{9,1},{13,5},{2,10},{6,14},... | collective-permute-start | bytes 405512 | tf_op jit(solution)/shard_map/ppermute | solution.py:329
  8.2 7.2 %collective-permute-start.1 = (bf16[528,128]{1,0:T(8,128)(2,1)}, bf16[528,128]{1,0:T(8,128)(2,1)S(1)}, u32[]{:S(2)}, u32[]{:S(2)}) collective-permute-start(bf16[528,128]{1,0:T(8,128)(2,1)} %get-tuple-element.11), channel_id=1, source_target_pairs={{0,4},{4,0},{8,12},{12,8},{1,5},{5,1},{9,13},{13,9},{2,6},{6,2},{1... | collective-permute-start | bytes 405512 | tf_op jit(solution)/shard_map/ppermute | solution.py:329
  14.8 5.0 %collective-permute-start.3 = (bf16[528,128]{1,0:T(8,128)(2,1)S(1)}, bf16[528,128]{1,0:T(8,128)(2,1)S(1)}, u32[]{:S(2)}, u32[]{:S(2)}) collective-permute-start(bf16[528,128]{1,0:T(8,128)(2,1)S(1)} %collective-permute-done), channel_id=1, source_target_pairs={{0,4},{4,0},{8,12},{12,8},{1,5},{5,1},{9,13},{13,9},{2,6},{6,2},{1... | collective-permute-start | bytes 405512 | tf_op jit(solution)/shard_map/ppermute | solution.py:329
  15.5 6.5 %collective-permute-start.4 = (bf16[528,128]{1,0:T(8,128)(2,1)S(1)}, bf16[528,128]{1,0:T(8,128)(2,1)S(1)}, u32[]{:S(2)}, u32[]{:S(2)}) collective-permute-start(bf16[528,128]{1,0:T(8,128)(2,1)S(1)} %collective-permute-done.1), channel_id=1, source_target_pairs={{0,2},{2,0},{1,3},{3,1},{4,6},{6,4},{5,7},{7,5},{8,10},{10,8},{9,1... | collective-permute-start | bytes 405512 | tf_op jit(solution)/shard_map/ppermute | solution.py:329
  16.0 10.9 %collective-permute-start.5 = (bf16[528,128]{1,0:T(8,128)(2,1)S(1)}, bf16[528,128]{1,0:T(8,128)(2,1)S(1)}, u32[]{:S(2)}, u32[]{:S(2)}) collective-permute-start(bf16[528,128]{1,0:T(8,128)(2,1)S(1)} %collective-permute-done), channel_id=1, source_target_pairs={{0,2},{2,0},{1,3},{3,1},{4,6},{6,4},{5,7},{7,5},{8,10},{10,8},{9,1... | collective-permute-start | bytes 405512 | tf_op jit(solution)/shard_map/ppermute | solution.py:329
  19.8 7.0 %collective-permute-start.6 = (bf16[528,128]{1,0:T(8,128)(2,1)S(1)}, bf16[528,128]{1,0:T(8,128)(2,1)S(1)}, u32[]{:S(2)}, u32[]{:S(2)}) collective-permute-start(bf16[528,128]{1,0:T(8,128)(2,1)S(1)} %collective-permute-done.3), channel_id=1, source_target_pairs={{0,2},{2,0},{1,3},{3,1},{4,6},{6,4},{5,7},{7,5},{8,10},{10,8},{9,1... | collective-permute-start | bytes 405512 | tf_op jit(solution)/shard_map/ppermute | solution.py:329
  22.0 0.9 %copy-start = (bf16[528,128]{1,0:T(8,128)(2,1)S(1)}, bf16[528,128]{1,0:T(8,128)(2,1)}, u32[]{:S(2)}) copy-start(bf16[528,128]{1,0:T(8,128)(2,1)} %get-tuple-element.11) | copy-start | bytes 405508
  22.9 0.7 %copy-start.1 = (f32[24,128]{1,0:T(8,128)S(1)}, f32[24,128]{1,0:T(8,128)}, u32[]{:S(2)}) copy-start(f32[24,128]{1,0:T(8,128)} %get-tuple-element.10.refs_0_) | copy-start | bytes 36868

commit v6 on v5

--- a/solution.py
+++ b/solution.py
@@ -16,6 +16,7 @@
 FAR = 1e9
 NT = (((1,), (1,)), ((), ()))
 BLOCK = 256
+COST = 1 << 26
 
 
 class Sizes:
@@ -52,7 +53,7 @@
     return lax.fori_loop(0, count, body, carry)
 
 
-def send_kernel(z, me_ref, rate_ref, events_ref, weight_ref, route_ref, bucket_ref, segment_ref, block_ref, own_ref):
+def send_kernel(z, me_ref, rate_ref, events_ref, weight_ref, route_ref, bucket_ref, segment_ref, block_ref, first_ref, second_ref, own_ref):
     groups = rate_ref.shape[0]
     lane = iota((1, LANES), 1)
     rate = jnp.full((1, LANES), rate_ref[0], F32)
@@ -70,7 +71,11 @@
         part = slice(r * LANES, (r + 1) * LANES)
         weighted = (columns[:, r : r + 1] * events_ref[part, :].astype(F32)).astype(BF16)
         grown = weighted.astype(F32) * jnp.exp(columns[:, z.chunks + r : z.chunks + r + 1] * rate)
-        block_ref[part, :] = grown.astype(BF16)
+        grown = grown.astype(BF16)
+        block_ref[part, :] = grown
+        ref = first_ref if r < z.chunks // 2 else second_ref
+        at = r % (z.chunks // 2) * LANES
+        ref[at : at + LANES, :] = grown
     ones = jnp.ones((8, LANES), BF16)
     high, low = [], []
     for u in range(z.user_rows):
@@ -86,26 +91,31 @@
     spare = z.code_rows - 3 * z.chunks - 2 * z.user_rows
     pad = [jnp.zeros((spare, LANES), I32)] if spare else []
     codes = jnp.concatenate([route, bucket >> LOW, bucket & MASK] + high + low + pad, axis=0)
-    block_ref[z.rows : z.rows + z.code_rows, :] = codes.astype(F32).astype(BF16)
+    codes = codes.astype(F32).astype(BF16)
+    block_ref[z.rows : z.rows + z.code_rows, :] = codes
+    first_ref[z.rows // 2 : z.rows // 2 + z.code_rows, :] = codes
 
 
 class Pieces:
-    def __init__(self, z, refs):
-        self.z, self.refs = z, refs
-        self.count = len(refs) if len(refs) != 1 else refs[0].shape[0]
-        self.per_group = 1 if len(refs) != 1 else z.per_group
+    def __init__(self, z, form, refs):
+        self.z, refs = z, list(refs)
+        self.parts = [[refs.pop(0) for _ in range(n)] for n in form]
+        self.count = len(form) if len(form) != 1 else self.parts[0][0].shape[0]
+        self.per_group = 1 if len(form) != 1 else z.per_group
         self.groups = self.count // self.per_group
 
     def block(self, s):
-        return (self.refs[s], 0) if len(self.refs) != 1 else (self.refs[0], s)
+        return (self.parts[s], 0) if len(self.parts) != 1 else (self.parts[0], s)
 
     def codes(self, s):
-        ref, i = self.block(s)
-        return ref[i, self.z.rows : self.z.rows + self.z.code_rows, :].astype(F32)
+        parts, i = self.block(s)
+        first = parts[0].shape[1] - self.z.code_rows
+        return parts[0][i, first : first + self.z.code_rows, :].astype(F32)
 
     def rows(self, s):
-        ref, i = self.block(s)
-        return ref[i, 0 : self.z.rows, :]
+        parts, i = self.block(s)
+        first = parts[0][i, 0 : parts[0].shape[1] - self.z.code_rows, :]
+        return jnp.concatenate([first] + [part[i] for part in parts[1:]], axis=0)
 
     def place(self, s):
         n, tile = self.z.chunks, self.codes(s)
@@ -216,9 +226,14 @@
     return row.astype(I32).astype(I16)
 
 
-def early_kernel(z, count, *refs):
-    own_ref, pieces = refs[0], Pieces(z, refs[1 : 1 + count])
-    sums_ref, scale_ref, rows_ref, from_ref, marks_ref, codes_ref = refs[1 + count :]
+def early_kernel(z, form, before, *refs):
+    count = sum(form)
+    own_ref, pieces = refs[0], Pieces(z, form, refs[1 : 1 + count])
+    refs = refs[1 + count :]
+    if before:
+        before_ref, sums_ref, rows_ref, from_ref, marks_ref, codes_ref = refs
+    else:
+        sums_ref, scale_ref, rows_ref, from_ref, marks_ref, codes_ref = refs
     rate, me = own_ref[8:9, :], own_ref[9:10, :]
     runs = Runs(z, [own_ref[16 + u : 17 + u, :] for u in range(z.user_rows)])
     pack(z, pieces, me * F32(z.slots), marks_ref, codes_ref, rows_ref, from_ref)
@@ -233,19 +248,22 @@
         part = slice(b * BLOCK, (b + 1) * BLOCK)
         if bounds:
             mask = held((inner + b * BLOCK).astype(I16), bounds)
-            sums_ref[part, :] = dot(mask, rows_ref[0 : len(bounds) * LANES, :])
+            value = dot(mask, rows_ref[0 : len(bounds) * LANES, :])
         else:
-            sums_ref[part, :] = jnp.zeros((BLOCK, LANES), F32)
-        if b * BLOCK >= z.window:
+            value = jnp.zeros((BLOCK, LANES), F32)
+        sums_ref[part, :] = value + before_ref[part, :] if before else value
+        if b * BLOCK >= z.window and not before:
             start = F32(b * BLOCK)
             scale_ref[part, :] = fall * jnp.exp(-rate * (start + own_anchor)) * runs.root(inner.astype(F32) + start)
 
 
-def late_kernel(z, early, late, *refs):
-    own_ref, sums_ref, scale_ref, tail_rows_ref, tail_from_ref = refs[:5]
-    blocks = refs[5 : 5 + early + late]
-    table_ref, feature_ref, place_ref, until_ref, rows_ref, from_ref, marks_ref, codes_ref = refs[5 + early + late :]
-    pieces, last = Pieces(z, blocks), Pieces(z, blocks[early:])
+def late_kernel(z, earlier, form, late, *refs):
+    own_ref, sums_ref, scale_ref = refs[:3]
+    tails = [refs[3 + 2 * i : 5 + 2 * i] for i in range(len(earlier))]
+    refs = refs[3 + 2 * len(earlier) :]
+    count = sum(form)
+    table_ref, feature_ref, place_ref, until_ref, rows_ref, from_ref, marks_ref, codes_ref = refs[count:]
+    pieces, last = Pieces(z, form, refs[:count]), Pieces(z, form[-late:], refs[count - sum(form[-late:]) : count])
     rate, me = own_ref[8:9, :], own_ref[9:10, :]
     base = me * F32(z.slots)
     starts = []
@@ -259,7 +277,8 @@
     inner = iota((BLOCK, LANES), 0)
     fall = jnp.exp(-rate * inner.astype(F32))
     bounds = []
-    for ref, first, lines in ((from_ref, 0, 2 * last.groups), (tail_from_ref, early, early)):
+    listed = [(from_ref, 0, 2 * last.groups)] + [(ref, count, count) for (_, ref), count in zip(tails, earlier)]
+    for ref, first, lines in listed:
         for g in range(first, first + lines):
             begin = ref[g : g + 1, :]
             bounds.append((short(begin), short(runs.until(begin + base) - base)))
@@ -273,8 +292,10 @@
             value = value * scale_ref[part, :]
         else:
             tail = dot(held(position, bounds[n : 2 * n]), rows_ref[n * LANES : 2 * n * LANES, :])
-            if early:
-                tail += dot(held(position, bounds[2 * n :]), tail_rows_ref[early * LANES : 2 * early * LANES, :])
+            at = 2 * n
+            for (ref, _), count in zip(tails, earlier):
+                tail += dot(held(position, bounds[at : at + count]), ref[count * LANES : 2 * count * LANES, :])
+                at += count
             own_fall = jnp.exp(-rate * (start + own_anchor))
             if z.shifts == 1:
                 value = (value + tail) * own_fall
@@ -329,76 +350,94 @@
     return lax.ppermute(block, axis, [(i, i ^ distance) for i in range(lax.axis_size(axis))])
 
 
-def spread(blocks, axis, early=None):
+def spread(blocks, axis):
     distance = lax.axis_size(axis) // 2
     while distance:
-        for block in list(blocks):
-            if early is not None and block is not blocks[0]:
-                block, early = lax.optimization_barrier((block, early))
-            blocks = blocks + [swap(block, axis, distance)]
+        blocks = blocks + [swap(block, axis, distance) for block in blocks]
         distance //= 2
-    return blocks, early
+    return blocks
 
 
 def on_device(events, event_weight, route, bucket, segment, decay_rate):
     rows, width = events.shape
-    shard_count = lax.axis_size("shard")
-    owners = lax.axis_size("key") * shard_count
+    key_count, shard_count = lax.axis_size("key"), lax.axis_size("shard")
+    owners = key_count * shard_count
     slots = segment.shape[0]
     z = Sizes(owners, rows, slots)
     block_rows = rows + z.code_rows
     smem = pl.BlockSpec(memory_space=pltpu.SMEM)
     vmem = pl.BlockSpec(memory_space=pltpu.VMEM)
     shape = jax.ShapeDtypeStruct
+    grant = pltpu.CompilerParams(vmem_limit_bytes=(16 if owners <= 8 else 48) * 1024 * 1024)
     me = (lax.axis_index("key") * shard_count + lax.axis_index("shard")).astype(I32).reshape(1)
-    block, own = pl.pallas_call(
+    half = rows // 2
+    block, upper, lower, own = pl.pallas_call(
         functools.partial(send_kernel, z),
-        out_shape=(shape((block_rows, width), BF16), shape((16 + z.user_rows + 7, LANES), F32)),
+        out_shape=(
+            shape((block_rows, width), BF16),
+            shape((half + z.code_rows, width), BF16),
+            shape((half, width), BF16),
+            shape((16 + z.user_rows + 7, LANES), F32),
+        ),
         in_specs=[smem, smem] + [vmem] * 5,
-        out_specs=(vmem, vmem),
+        out_specs=(vmem,) * 4,
         compiler_params=pltpu.CompilerParams(vmem_limit_bytes=56 * 1024 * 1024),
         name="weigh",
     )(
         me, decay_rate, events, event_weight.reshape(z.chunks, LANES), route.reshape(z.chunks, LANES),
         bucket.reshape(z.chunks, LANES), segment.reshape(slots // LANES, LANES),
     )
-    if shard_count == 2:
-        near = swap(block, "shard", 1)
-        blocks, near = spread([block], "key", near)
-        across = [swap(b, "shard", 1) for b in blocks[1:]]
-        early, late = blocks + [near] + across[1:-1], across[:1] + across[-1:]
+
+    def flat(blocks):
+        return [part[None] if part.ndim == 2 else part for parts in blocks for part in parts]
+
+    def sums(blocks, before=()):
+        blocks, form, count = flat(blocks), tuple(map(len, blocks)), len(blocks)
+        lines = max(8, 2 * count)
+        whole = shape((slots, width), F32)
+        kept = (shape((lines * LANES, LANES), BF16), shape((lines, LANES), F32))
+        return pl.pallas_call(
+            functools.partial(early_kernel, z, form, len(before)),
+            out_shape=((whole,) if before else (whole, whole)) + kept,
+            in_specs=[vmem] * (1 + len(blocks) + len(before)),
+            out_specs=(vmem,) * (3 if before else 4),
+            scratch_shapes=[
+                pltpu.VMEM((2, max(1, count), 8, LANES), F32),
+                pltpu.VMEM((max(1, count), 2 * z.chunks, LANES), F32),
+            ],
+            compiler_params=grant,
+            cost_estimate=pl.CostEstimate(flops=COST * count, bytes_accessed=0, transcendentals=0),
+            name="more_sums" if before else "first_sums",
+        )(own, *blocks, *before)
+
+    if (key_count, shard_count) == (4, 2):
+        tie = lax.optimization_barrier
+        far = [swap(upper, "key", 2)]
+        side = swap(block, "shard", 1)
+        near = swap(block, "key", 1)
+        far.append(swap(lower, "key", 2))
+        side_near = swap(near, "shard", 1)
+        first = [(block,), (side,)]
+        total, scale, *tail = sums(first)
+        last = [swap(far[0], "key", 1)]
+        far[1], total = tie((far[1], total))
+        last.append(swap(far[1], "key", 1))
+        second = [far, (near,), (side_near,), last]
+        late = [[swap(part, "shard", 1) for part in parts] for parts in (far, last)]
+        total, *tail2 = sums(second, (total,))
+        early, earlier, tails = first + second, (2, 4), tail + tail2
     else:
-        blocks, _ = spread([block], "key")
-        blocks, _ = spread(blocks, "shard")
-        early, late = [], [jnp.concatenate(blocks, axis=0)]
-    early = [b.reshape(-1, block_rows, width) for b in early]
-    late = [b.reshape(-1, block_rows, width) for b in late]
-    lines = max(8, 2 * len(early))
+        blocks = spread(spread([block], "key"), "shard")
+        total, scale, *_ = sums([])
+        early, earlier, tails = [], (), []
+        late = [(jnp.concatenate(blocks, axis=0).reshape(owners, block_rows, width),)]
     late_lines = 2 * (len(late) if len(late) > 1 else z.groups)
-    late_count = sum(b.shape[0] for b in late)
-    grant = pltpu.CompilerParams(vmem_limit_bytes=(16 if owners <= 8 else 48) * 1024 * 1024)
-    kept = pl.pallas_call(
-        functools.partial(early_kernel, z, len(early)),
-        out_shape=(
-            shape((slots, width), F32),
-            shape((slots, width), F32),
-            shape((lines * LANES, LANES), BF16),
-            shape((lines, LANES), F32),
-        ),
-        in_specs=[vmem] * (1 + len(early)),
-        out_specs=(vmem,) * 4,
-        scratch_shapes=[
-            pltpu.VMEM((2, max(1, len(early)), 8, LANES), F32),
-            pltpu.VMEM((max(1, len(early)), 2 * z.chunks, LANES), F32),
-        ],
-        compiler_params=grant,
-        cost_estimate=pl.CostEstimate(flops=2 * slots * rows * 6 * LANES, bytes_accessed=6 * slots * LANES, transcendentals=0),
-        name="early_sums",
-    )(own, *early)
+    late_count = len(late) if len(late) > 1 else owners
+    form = tuple(map(len, early + late))
     return pl.pallas_call(
-        functools.partial(late_kernel, z, len(early), len(late)),
+        functools.partial(late_kernel, z, earlier, form, len(late)),
         out_shape=(shape((slots, width), BF16), shape((rows, width), BF16)),
-        in_specs=[vmem] * (5 + len(early) + len(late)),
+        in_specs=[vmem] * (3 + len(tails) + sum(form)),
         out_specs=(vmem, vmem),
         scratch_shapes=[
             pltpu.VMEM((owners, 8, LANES), F32),
@@ -410,7 +449,7 @@
         ],
         compiler_params=grant,
         name="table_and_rows",
-    )(own, *kept, *early, *late)
+    )(own, total, scale, *tails, *flat(early + late))
 
 
 def solution(mesh):

time: 31.2 us -> 32.5 us (1.042)
  waiting for transfers between devices: 8.98 us -> 3.83 us
  starting transfers between devices: 10.3 us -> 15.4 us
  local copies, waits for them, and re-layouts: 1.61 us -> 2.32 us
  Pallas kernels: 9.42 us -> 10.1 us
    ppermute x7 -> x11, waiting for transfers between devices: 8.98 us -> 3.83 us  [swap(): lax.ppermute(block, axis, [(i, i ^ distance) for i in range(lax.axis_size...]
    ppermute x7 -> x11, starting transfers between devices: 10.3 us -> 15.4 us  [swap(): lax.ppermute(block, axis, [(i, i ^ distance) for i in range(lax.axis_size...]
    unnamed x4 -> x8, local copies, waits for them, and re-layouts: 1.61 us -> 2.32 us
    pallas_call x2 -> x3, Pallas kernels: 7.35 us -> 7.95 us  [the longest x1 4.16 us: on_device(): pl.pallas_call(functools.partial(late_kernel, z, earlier, form, len(late)...]
  transfers between devices with their start and end apart: 7 -> 11, of which waited for: 3 -> 2; matrix products, arithmetic and copies ran while one was open for 0% -> 0% of each run, Pallas kernels for 11% -> 12%
where the time goes in v6:
time: 32.5 us; the launch traced here: 32.3 us
  starting transfers between devices  15.4 us (47%)
  Pallas kernels  10.1 us (31%)
  waiting for transfers between devices  3.83 us (12%)
  local copies, waits for them, and re-layouts  2.32 us (7%)
  between operations  0.7 us (2%)
    ppermute x11, starting transfers between devices, swap(): lax.ppermute(block, axis, [(i, i ^ distance) for i in range(lax.axis_size...  15.4 us
    pallas_call x1, Pallas kernels, on_device(): pl.pallas_call(functools.partial(late_kernel, z, earlier, form, len(late)...  4.16 us
    ppermute x11, waiting for transfers between devices, swap(): lax.ppermute(block, axis, [(i, i ^ distance) for i in range(lax.axis_size...  3.83 us
    pallas_call x2, Pallas kernels, sums(): pl.pallas_call(functools.partial(early_kernel, z, form, len(before)), out...  3.79 us
    unnamed x8, local copies, waits for them, and re-layouts  2.32 us
    pallas_call x1, Pallas kernels, on_device(): pl.pallas_call(functools.partial(send_kernel, z), out_shape=(shape((block...  2.11 us
  transfers between devices with their start and end apart: 11, of which 2 were waited for; matrix products, arithmetic and copies ran while one was open for 0% of the time, Pallas kernels for 12%

profile of v6, /device:TPU:0, one launch (start us, length us, event | category | flops | bytes accessed | tf_op | source)
XLA Modules:
  0.0 32.3 jit_solution(169308255828650510)
XLA Ops:
  0.6 2.1 %weigh.1 = (bf16[528,128]{1,0:T(8,128)(2,1)}, bf16[272,128]{1,0:T(8,128)(2,1)}, bf16[256,128]{1,0:T(8,128)(2,1)}, f32[24,128]{1,0:T(8,128)}) custom-call(s32[1]{0:T(128)} %bitcast.me_ref, f32[4]{0:T(128)} %rate_ref.1, bf16[512,128]{1,0:T(8,128)(2,1)} %events_ref.1, f32[4,128]{1,0:T(4,128)} %bitcast.38, s32[4,128]{1,0:T(4,128)} %bitcast.39, ...), custom_call_target="tpu_custom_call" | custom-call | tf_op jit(solution)/shard_map/weigh/pallas_call | solution.py:374
  2.8 3.0 %collective-permute-start.3 = (bf16[528,128]{1,0:T(8,128)(2,1)}, bf16[528,128]{1,0:T(8,128)(2,1)S(1)}, u32[]{:S(2)}, u32[]{:S(2)}) collective-permute-start(bf16[528,128]{1,0:T(8,128)(2,1)} %get-tuple-element.18), channel_id=1, source_target_pairs={{0,4},{4,0},{8,12},{12,8},{1,5},{5,1},{9,13},{13,9},{2,6},{6,2},{1... | collective-permute-start | bytes 405512 | tf_op jit(solution)/shard_map/ppermute | solution.py:350
  5.8 1.5 %collective-permute-start.2 = (bf16[528,128]{1,0:T(8,128)(2,1)}, bf16[528,128]{1,0:T(8,128)(2,1)S(1)}, u32[]{:S(2)}, u32[]{:S(2)}) collective-permute-start(bf16[528,128]{1,0:T(8,128)(2,1)} %get-tuple-element.18), channel_id=1, source_target_pairs={{0,2},{2,0},{1,3},{3,1},{4,6},{6,4},{5,7},{7,5},{8,10},{10,8},{9,1... | collective-permute-start | bytes 405512 | tf_op jit(solution)/shard_map/ppermute | solution.py:350
  7.3 2.6 %collective-permute-start = (bf16[272,128]{1,0:T(8,128)(2,1)}, bf16[272,128]{1,0:T(8,128)(2,1)S(1)}, u32[]{:S(2)}, u32[]{:S(2)}) collective-permute-start(bf16[272,128]{1,0:T(8,128)(2,1)} %get-tuple-element.16), channel_id=1, source_target_pairs={{0,8},{4,12},{8,0},{12,4},{1,9},{5,13},{9,1},{13,5},{2,10},{6,14},... | collective-permute-start | bytes 208904 | tf_op jit(solution)/shard_map/ppermute | solution.py:350
  9.9 0.3 %collective-permute-start.1 = (bf16[256,128]{1,0:T(8,128)(2,1)}, bf16[256,128]{1,0:T(8,128)(2,1)S(1)}, u32[]{:S(2)}, u32[]{:S(2)}) collective-permute-start(bf16[256,128]{1,0:T(8,128)(2,1)} %get-tuple-element.17), channel_id=1, source_target_pairs={{0,8},{4,12},{8,0},{12,4},{1,9},{5,13},{9,1},{13,5},{2,10},{6,14},... | collective-permute-start | bytes 196616 | tf_op jit(solution)/shard_map/ppermute | solution.py:350
  10.2 0.0 collective-permute-done.3
  10.2 1.8 %collective-permute-start.4 = (bf16[528,128]{1,0:T(8,128)(2,1)S(1)}, bf16[528,128]{1,0:T(8,128)(2,1)S(1)}, u32[]{:S(2)}, u32[]{:S(2)}) collective-permute-start(bf16[528,128]{1,0:T(8,128)(2,1)S(1)} %collective-permute-done.3), channel_id=1, source_target_pairs={{0,2},{2,0},{1,3},{3,1},{4,6},{6,4},{5,7},{7,5},{8,10},{10,8},{9,1... | collective-permute-start | bytes 405512 | tf_op jit(solution)/shard_map/ppermute | solution.py:350
  12.0 3.2 %collective-permute-done = bf16[272,128]{1,0:T(8,128)(2,1)S(1)} collective-permute-done((bf16[272,128]{1,0:T(8,128)(2,1)}, bf16[272,128]{1,0:T(8,128)(2,1)S(1)}, u32[]{:S(2)}, u32[]{:S(2)}) %collective-permute-start) | collective-permute-done | bytes 69664 | tf_op jit(solution)/shard_map/ppermute | solution.py:350
  15.2 0.9 %copy-done = bf16[528,128]{1,0:T(8,128)(2,1)S(1)} copy-done((bf16[528,128]{1,0:T(8,128)(2,1)S(1)}, bf16[528,128]{1,0:T(8,128)(2,1)}, u32[]{:S(2)}) %copy-start) | copy-done | bytes 135192
  16.1 0.7 %copy-done.2 = f32[24,128]{1,0:T(8,128)S(1)} copy-done((f32[24,128]{1,0:T(8,128)S(1)}, f32[24,128]{1,0:T(8,128)}, u32[]{:S(2)}) %copy-start.2) | copy-done | bytes 12312
  16.8 1.7 %first_sums.1 = (f32[4096,128]{1,0:T(8,128)S(1)}, f32[4096,128]{1,0:T(8,128)S(1)}, bf16[1024,128]{1,0:T(8,128)(2,1)S(1)}, f32[8,128]{1,0:T(8,128)S(1)}) custom-call(f32[24,128]{1,0:T(8,128)S(1)} %copy-done.2, bf16[1,528,128]{2,1,0:T(8,128)(2,1)S(1)} %bitcast.29, bf16[1,528,128]{2,1,0:T(8,128)(2,1)S(1)} %bitcast.31), custom_call_target="tpu_custom_call" | custom-call | flops 134217728 | tf_op jit(solution)/shard_map/first_sums/pallas_call | solution.py:399
  18.5 0.0 collective-permute-done.1
  18.6 2.1 %collective-permute-start.6 = (bf16[256,128]{1,0:T(8,128)(2,1)S(1)}, bf16[256,128]{1,0:T(8,128)(2,1)S(1)}, u32[]{:S(2)}, u32[]{:S(2)}) collective-permute-start(bf16[256,128]{1,0:T(8,128)(2,1)S(1)} %collective-permute-done.1), channel_id=1, source_target_pairs={{0,4},{4,0},{8,12},{12,8},{1,5},{5,1},{9,13},{13,9},{2,6},{6,2},{1... | collective-permute-start | bytes 196616 | tf_op jit(solution)/shard_map/ppermute | solution.py:350
  20.6 1.2 %collective-permute-start.7 = (bf16[272,128]{1,0:T(8,128)(2,1)S(1)}, bf16[272,128]{1,0:T(8,128)(2,1)S(1)}, u32[]{:S(2)}, u32[]{:S(2)}) collective-permute-start(bf16[272,128]{1,0:T(8,128)(2,1)S(1)} %collective-permute-done), channel_id=1, source_target_pairs={{0,2},{2,0},{1,3},{3,1},{4,6},{6,4},{5,7},{7,5},{8,10},{10,8},{9,1... | collective-permute-start | bytes 208904 | tf_op jit(solution)/shard_map/ppermute | solution.py:350
  21.8 0.0 collective-permute-done.5
  21.8 0.9 %collective-permute-start.9 = (bf16[272,128]{1,0:T(8,128)(2,1)S(1)}, bf16[272,128]{1,0:T(8,128)(2,1)S(1)}, u32[]{:S(2)}, u32[]{:S(2)}) collective-permute-start(bf16[272,128]{1,0:T(8,128)(2,1)S(1)} %collective-permute-done.5), channel_id=1, source_target_pairs={{0,2},{2,0},{1,3},{3,1},{4,6},{6,4},{5,7},{7,5},{8,10},{10,8},{9,1... | collective-permute-start | bytes 208904 | tf_op jit(solution)/shard_map/ppermute | solution.py:350
  22.7 1.2 %collective-permute-start.8 = (bf16[256,128]{1,0:T(8,128)(2,1)S(1)}, bf16[256,128]{1,0:T(8,128)(2,1)S(1)}, u32[]{:S(2)}, u32[]{:S(2)}) collective-permute-start(bf16[256,128]{1,0:T(8,128)(2,1)S(1)} %collective-permute-done.1), channel_id=1, source_target_pairs={{0,2},{2,0},{1,3},{3,1},{4,6},{6,4},{5,7},{7,5},{8,10},{10,8},{9,1... | collective-permute-start | bytes 196616 | tf_op jit(solution)/shard_map/ppermute | solution.py:350
  23.8 0.0 collective-permute-done.6
  23.9 0.9 %collective-permute-start.10 = (bf16[256,128]{1,0:T(8,128)(2,1)S(1)}, bf16[256,128]{1,0:T(8,128)(2,1)S(1)}, u32[]{:S(2)}, u32[]{:S(2)}) collective-permute-start(bf16[256,128]{1,0:T(8,128)(2,1)S(1)} %collective-permute-done.6), channel_id=1, source_target_pairs={{0,2},{2,0},{1,3},{3,1},{4,6},{6,4},{5,7},{7,5},{8,10},{10,8},{9,1... | collective-permute-start | bytes 196616 | tf_op jit(solution)/shard_map/ppermute | solution.py:350
  24.7 0.0 collective-permute-done.4
  24.7 0.7 %copy-done.3 = f32[24,128]{1,0:T(8,128)S(1)} copy-done((f32[24,128]{1,0:T(8,128)S(1)}, f32[24,128]{1,0:T(8,128)}, u32[]{:S(2)}) %copy-start.3) | copy-done | bytes 12312
  25.4 2.1 %more_sums.1 = (f32[4096,128]{1,0:T(8,128)S(1)}, bf16[1024,128]{1,0:T(8,128)(2,1)S(1)}, f32[8,128]{1,0:T(8,128)S(1)}) custom-call(f32[24,128]{1,0:T(8,128)S(1)} %copy-done.3, bf16[1,272,128]{2,1,0:T(8,128)(2,1)S(1)} %bitcast.21, bf16[1,256,128]{2,1,0:T(8,128)(2,1)S(1)} %bitcast.25, bf16[1,528,128]{2,1,0:T(8,128)(2,1)S(1)} %bitcast.17, ...), custom_call_target="tpu_custom_call" | custom-call | flops 268435456 | tf_op jit(solution)/shard_map/more_sums/pallas_call | solution.py:399
  27.5 0.6 %collective-permute-done.10 = bf16[256,128]{1,0:T(8,128)(2,1)S(1)} collective-permute-done((bf16[256,128]{1,0:T(8,128)(2,1)S(1)}, bf16[256,128]{1,0:T(8,128)(2,1)S(1)}, u32[]{:S(2)}, u32[]{:S(2)}) %collective-permute-start.10) | collective-permute-done | bytes 65568 | tf_op jit(solution)/shard_map/ppermute | solution.py:350
  28.1 4.2 %table_and_rows.1 = (bf16[4096,128]{1,0:T(8,128)(2,1)}, bf16[512,128]{1,0:T(8,128)(2,1)}) custom-call(f32[24,128]{1,0:T(8,128)S(1)} %copy-done.3, f32[4096,128]{1,0:T(8,128)S(1)} %get-tuple-element.22.refs_1_, f32[4096,128]{1,0:T(8,128)S(1)} %get-tuple-element.23.refs_2_, bf16[1024,128]{1,0:T(8,128)(2,1)S(1)} %get-tuple-element.24.refs_3_, ...), custom_call_target="tpu_custom_call" | custom-call | tf_op jit(solution)/shard_map/table_and_rows/pallas_call | solution.py:437
  (10 shorter events, 0.0 us)
Async XLA Ops:
  2.8 7.4 %collective-permute-start.3 = (bf16[528,128]{1,0:T(8,128)(2,1)}, bf16[528,128]{1,0:T(8,128)(2,1)S(1)}, u32[]{:S(2)}, u32[]{:S(2)}) collective-permute-start(bf16[528,128]{1,0:T(8,128)(2,1)} %get-tuple-element.18), channel_id=1, source_target_pairs={{0,4},{4,0},{8,12},{12,8},{1,5},{5,1},{9,13},{13,9},{2,6},{6,2},{1... | collective-permute-start | bytes 405512 | tf_op jit(solution)/shard_map/ppermute | solution.py:350
  5.8 9.4 %collective-permute-start.2 = (bf16[528,128]{1,0:T(8,128)(2,1)}, bf16[528,128]{1,0:T(8,128)(2,1)S(1)}, u32[]{:S(2)}, u32[]{:S(2)}) collective-permute-start(bf16[528,128]{1,0:T(8,128)(2,1)} %get-tuple-element.18), channel_id=1, source_target_pairs={{0,2},{2,0},{1,3},{3,1},{4,6},{6,4},{5,7},{7,5},{8,10},{10,8},{9,1... | collective-permute-start | bytes 405512 | tf_op jit(solution)/shard_map/ppermute | solution.py:350
  7.3 7.9 %collective-permute-start = (bf16[272,128]{1,0:T(8,128)(2,1)}, bf16[272,128]{1,0:T(8,128)(2,1)S(1)}, u32[]{:S(2)}, u32[]{:S(2)}) collective-permute-start(bf16[272,128]{1,0:T(8,128)(2,1)} %get-tuple-element.16), channel_id=1, source_target_pairs={{0,8},{4,12},{8,0},{12,4},{1,9},{5,13},{9,1},{13,5},{2,10},{6,14},... | collective-permute-start | bytes 208904 | tf_op jit(solution)/shard_map/ppermute | solution.py:350
  9.9 8.7 %collective-permute-start.1 = (bf16[256,128]{1,0:T(8,128)(2,1)}, bf16[256,128]{1,0:T(8,128)(2,1)S(1)}, u32[]{:S(2)}, u32[]{:S(2)}) collective-permute-start(bf16[256,128]{1,0:T(8,128)(2,1)} %get-tuple-element.17), channel_id=1, source_target_pairs={{0,8},{4,12},{8,0},{12,4},{1,9},{5,13},{9,1},{13,5},{2,10},{6,14},... | collective-permute-start | bytes 196616 | tf_op jit(solution)/shard_map/ppermute | solution.py:350
  10.2 14.5 %collective-permute-start.4 = (bf16[528,128]{1,0:T(8,128)(2,1)S(1)}, bf16[528,128]{1,0:T(8,128)(2,1)S(1)}, u32[]{:S(2)}, u32[]{:S(2)}) collective-permute-start(bf16[528,128]{1,0:T(8,128)(2,1)S(1)} %collective-permute-done.3), channel_id=1, source_target_pairs={{0,2},{2,0},{1,3},{3,1},{4,6},{6,4},{5,7},{7,5},{8,10},{10,8},{9,1... | collective-permute-start | bytes 405512 | tf_op jit(solution)/shard_map/ppermute | solution.py:350
  15.2 6.6 %collective-permute-start.5 = (bf16[272,128]{1,0:T(8,128)(2,1)S(1)}, bf16[272,128]{1,0:T(8,128)(2,1)S(1)}, u32[]{:S(2)}, u32[]{:S(2)}) collective-permute-start(bf16[272,128]{1,0:T(8,128)(2,1)S(1)} %collective-permute-done), channel_id=1, source_target_pairs={{0,4},{4,0},{8,12},{12,8},{1,5},{5,1},{9,13},{13,9},{2,6},{6,2},{1... | collective-permute-start | bytes 208904 | tf_op jit(solution)/shard_map/ppermute | solution.py:350
  15.2 0.9 %copy-start = (bf16[528,128]{1,0:T(8,128)(2,1)S(1)}, bf16[528,128]{1,0:T(8,128)(2,1)}, u32[]{:S(2)}) copy-start(bf16[528,128]{1,0:T(8,128)(2,1)} %get-tuple-element.18) | copy-start | bytes 405508
  16.1 0.7 %copy-start.2 = (f32[24,128]{1,0:T(8,128)S(1)}, f32[24,128]{1,0:T(8,128)}, u32[]{:S(2)}) copy-start(f32[24,128]{1,0:T(8,128)} %get-tuple-element.15.refs_0_) | copy-start | bytes 36868
  16.8 11.3 %copy-start.1 = (bf16[528,128]{1,0:T(8,128)(2,1)S(1)}, bf16[528,128]{1,0:T(8,128)(2,1)}, u32[]{:S(2)}) copy-start(bf16[528,128]{1,0:T(8,128)(2,1)} %get-tuple-element.18) | copy-start | bytes 405508
  18.6 5.3 %collective-permute-start.6 = (bf16[256,128]{1,0:T(8,128)(2,1)S(1)}, bf16[256,128]{1,0:T(8,128)(2,1)S(1)}, u32[]{:S(2)}, u32[]{:S(2)}) collective-permute-start(bf16[256,128]{1,0:T(8,128)(2,1)S(1)} %collective-permute-done.1), channel_id=1, source_target_pairs={{0,4},{4,0},{8,12},{12,8},{1,5},{5,1},{9,13},{13,9},{2,6},{6,2},{1... | collective-permute-start | bytes 196616 | tf_op jit(solution)/shard_map/ppermute | solution.py:350
  20.6 6.9 %collective-permute-start.7 = (bf16[272,128]{1,0:T(8,128)(2,1)S(1)}, bf16[272,128]{1,0:T(8,128)(2,1)S(1)}, u32[]{:S(2)}, u32[]{:S(2)}) collective-permute-start(bf16[272,128]{1,0:T(8,128)(2,1)S(1)} %collective-permute-done), channel_id=1, source_target_pairs={{0,2},{2,0},{1,3},{3,1},{4,6},{6,4},{5,7},{7,5},{8,10},{10,8},{9,1... | collective-permute-start | bytes 208904 | tf_op jit(solution)/shard_map/ppermute | solution.py:350
  21.8 5.7 %collective-permute-start.9 = (bf16[272,128]{1,0:T(8,128)(2,1)S(1)}, bf16[272,128]{1,0:T(8,128)(2,1)S(1)}, u32[]{:S(2)}, u32[]{:S(2)}) collective-permute-start(bf16[272,128]{1,0:T(8,128)(2,1)S(1)} %collective-permute-done.5), channel_id=1, source_target_pairs={{0,2},{2,0},{1,3},{3,1},{4,6},{6,4},{5,7},{7,5},{8,10},{10,8},{9,1... | collective-permute-start | bytes 208904 | tf_op jit(solution)/shard_map/ppermute | solution.py:350
  22.7 4.8 %collective-permute-start.8 = (bf16[256,128]{1,0:T(8,128)(2,1)S(1)}, bf16[256,128]{1,0:T(8,128)(2,1)S(1)}, u32[]{:S(2)}, u32[]{:S(2)}) collective-permute-start(bf16[256,128]{1,0:T(8,128)(2,1)S(1)} %collective-permute-done.1), channel_id=1, source_target_pairs={{0,2},{2,0},{1,3},{3,1},{4,6},{6,4},{5,7},{7,5},{8,10},{10,8},{9,1... | collective-permute-start | bytes 196616 | tf_op jit(solution)/shard_map/ppermute | solution.py:350
  23.9 4.3 %collective-permute-start.10 = (bf16[256,128]{1,0:T(8,128)(2,1)S(1)}, bf16[256,128]{1,0:T(8,128)(2,1)S(1)}, u32[]{:S(2)}, u32[]{:S(2)}) collective-permute-start(bf16[256,128]{1,0:T(8,128)(2,1)S(1)} %collective-permute-done.6), channel_id=1, source_target_pairs={{0,2},{2,0},{1,3},{3,1},{4,6},{6,4},{5,7},{7,5},{8,10},{10,8},{9,1... | collective-permute-start | bytes 196616 | tf_op jit(solution)/shard_map/ppermute | solution.py:350
  24.7 0.7 %copy-start.3 = (f32[24,128]{1,0:T(8,128)S(1)}, f32[24,128]{1,0:T(8,128)}, u32[]{:S(2)}) copy-start(f32[24,128]{1,0:T(8,128)} %get-tuple-element.15.refs_0_) | copy-start | bytes 36868

commit v7 on v6

--- a/solution.py
+++ b/solution.py
@@ -16,7 +16,7 @@
 FAR = 1e9
 NT = (((1,), (1,)), ((), ()))
 BLOCK = 256
-COST = 1 << 26
+COST = 1
 
 
 class Sizes:
@@ -53,7 +53,7 @@
     return lax.fori_loop(0, count, body, carry)
 
 
-def send_kernel(z, me_ref, rate_ref, events_ref, weight_ref, route_ref, bucket_ref, segment_ref, block_ref, first_ref, second_ref, own_ref):
+def send_kernel(z, me_ref, rate_ref, events_ref, weight_ref, route_ref, bucket_ref, segment_ref, block_ref, own_ref):
     groups = rate_ref.shape[0]
     lane = iota((1, LANES), 1)
     rate = jnp.full((1, LANES), rate_ref[0], F32)
@@ -71,11 +71,7 @@
         part = slice(r * LANES, (r + 1) * LANES)
         weighted = (columns[:, r : r + 1] * events_ref[part, :].astype(F32)).astype(BF16)
         grown = weighted.astype(F32) * jnp.exp(columns[:, z.chunks + r : z.chunks + r + 1] * rate)
-        grown = grown.astype(BF16)
-        block_ref[part, :] = grown
-        ref = first_ref if r < z.chunks // 2 else second_ref
-        at = r % (z.chunks // 2) * LANES
-        ref[at : at + LANES, :] = grown
+        block_ref[part, :] = grown.astype(BF16)
     ones = jnp.ones((8, LANES), BF16)
     high, low = [], []
     for u in range(z.user_rows):
@@ -91,9 +87,7 @@
     spare = z.code_rows - 3 * z.chunks - 2 * z.user_rows
     pad = [jnp.zeros((spare, LANES), I32)] if spare else []
     codes = jnp.concatenate([route, bucket >> LOW, bucket & MASK] + high + low + pad, axis=0)
-    codes = codes.astype(F32).astype(BF16)
-    block_ref[z.rows : z.rows + z.code_rows, :] = codes
-    first_ref[z.rows // 2 : z.rows // 2 + z.code_rows, :] = codes
+    block_ref[z.rows : z.rows + z.code_rows, :] = codes.astype(F32).astype(BF16)
 
 
 class Pieces:
@@ -370,17 +364,14 @@
     shape = jax.ShapeDtypeStruct
     grant = pltpu.CompilerParams(vmem_limit_bytes=(16 if owners <= 8 else 48) * 1024 * 1024)
     me = (lax.axis_index("key") * shard_count + lax.axis_index("shard")).astype(I32).reshape(1)
-    half = rows // 2
-    block, upper, lower, own = pl.pallas_call(
+    block, own = pl.pallas_call(
         functools.partial(send_kernel, z),
         out_shape=(
             shape((block_rows, width), BF16),
-            shape((half + z.code_rows, width), BF16),
-            shape((half, width), BF16),
             shape((16 + z.user_rows + 7, LANES), F32),
         ),
         in_specs=[smem, smem] + [vmem] * 5,
-        out_specs=(vmem,) * 4,
+        out_specs=(vmem, vmem),
         compiler_params=pltpu.CompilerParams(vmem_limit_bytes=56 * 1024 * 1024),
         name="weigh",
     )(
@@ -412,27 +403,28 @@
 
     if (key_count, shard_count) == (4, 2):
         tie = lax.optimization_barrier
-        far = [swap(upper, "key", 2)]
+        far = swap(block, "key", 2)
         side = swap(block, "shard", 1)
         near = swap(block, "key", 1)
-        far.append(swap(lower, "key", 2))
         side_near = swap(near, "shard", 1)
-        first = [(block,), (side,)]
+        first = [(block,), (near,)]
         total, scale, *tail = sums(first)
-        last = [swap(far[0], "key", 1)]
-        far[1], total = tie((far[1], total))
-        last.append(swap(far[1], "key", 1))
-        second = [far, (near,), (side_near,), last]
-        late = [[swap(part, "shard", 1) for part in parts] for parts in (far, last)]
+        far, total = tie((far, total))
+        last = swap(far, "key", 1)
+        sent, side_near, side = tie((far, side_near, side))
+        side_far = swap(sent, "shard", 1)
+        side_last = swap(last, "shard", 1)
+        second = [(far,), (side,), (side_near,), (last,), (side_far,)]
+        late = [(side_last,)]
         total, *tail2 = sums(second, (total,))
-        early, earlier, tails = first + second, (2, 4), tail + tail2
+        early, earlier, tails = first + second, (len(first), len(second)), tail + tail2
     else:
         blocks = spread(spread([block], "key"), "shard")
         total, scale, *_ = sums([])
         early, earlier, tails = [], (), []
         late = [(jnp.concatenate(blocks, axis=0).reshape(owners, block_rows, width),)]
-    late_lines = 2 * (len(late) if len(late) > 1 else z.groups)
-    late_count = len(late) if len(late) > 1 else owners
+    late_lines = 2 * (len(late) if earlier else z.groups)
+    late_count = len(late) if earlier else owners
     form = tuple(map(len, early + late))
     return pl.pallas_call(
         functools.partial(late_kernel, z, earlier, form, len(late)),

time: 32.5 us -> 30.8 us (0.948)
  starting transfers between devices: 15.4 us -> 10.8 us
  waiting for transfers between devices: 3.83 us -> 7.51 us
  local copies, waits for them, and re-layouts: 2.32 us -> 1.62 us
    ppermute x11 -> x7, starting transfers between devices: 15.4 us -> 10.8 us  [swap(): lax.ppermute(block, axis, [(i, i ^ distance) for i in range(lax.axis_size...]
    ppermute x11 -> x7, waiting for transfers between devices: 3.83 us -> 7.51 us  [swap(): lax.ppermute(block, axis, [(i, i ^ distance) for i in range(lax.axis_size...]
    unnamed x8 -> x6, local copies, waits for them, and re-layouts: 2.32 us -> 1.62 us
    pallas_call x1, Pallas kernels: 4.16 us -> 3.79 us  [on_device(): pl.pallas_call(functools.partial(late_kernel, z, earlier, form, len(late)...]
    pallas_call x2, Pallas kernels: 3.79 us -> 4.14 us  [sums(): pl.pallas_call(functools.partial(early_kernel, z, form, len(before)), out...]
  transfers between devices with their start and end apart: 11 -> 7, of which waited for: 2 -> 4; matrix products, arithmetic and copies ran while one was open for 0% -> 0% of each run, Pallas kernels for 12% -> 14%
where the time goes in v7:
time: 30.8 us; the launch traced here: 30.6 us
  starting transfers between devices  10.8 us (35%)
  Pallas kernels  10 us (32%)
  waiting for transfers between devices  7.51 us (24%)
  local copies, waits for them, and re-layouts  1.62 us (5%)
  between operations  0.69 us (2%)
    ppermute x7, starting transfers between devices, swap(): lax.ppermute(block, axis, [(i, i ^ distance) for i in range(lax.axis_size...  10.8 us
    ppermute x7, waiting for transfers between devices, swap(): lax.ppermute(block, axis, [(i, i ^ distance) for i in range(lax.axis_size...  7.51 us
    pallas_call x2, Pallas kernels, sums(): pl.pallas_call(functools.partial(early_kernel, z, form, len(before)), out...  4.14 us
    pallas_call x1, Pallas kernels, on_device(): pl.pallas_call(functools.partial(late_kernel, z, earlier, form, len(late)...  3.79 us
    pallas_call x1, Pallas kernels, on_device(): pl.pallas_call(functools.partial(send_kernel, z), out_shape=(shape((block...  2.08 us
    unnamed x6, local copies, waits for them, and re-layouts  1.62 us
  transfers between devices with their start and end apart: 7, of which 4 were waited for; matrix products, arithmetic and copies ran while one was open for 0% of the time, Pallas kernels for 14%

profile of v7, /device:TPU:0, one launch (start us, length us, event | category | flops | bytes accessed | tf_op | source)
XLA Modules:
  0.0 30.6 jit_solution(197255321623679092)
XLA Ops:
  0.6 2.1 %weigh.1 = (bf16[528,128]{1,0:T(8,128)(2,1)}, f32[24,128]{1,0:T(8,128)}) custom-call(s32[1]{0:T(128)} %bitcast.me_ref, f32[4]{0:T(128)} %rate_ref.1, bf16[512,128]{1,0:T(8,128)(2,1)} %events_ref.1, f32[4,128]{1,0:T(4,128)} %bitcast.29, s32[4,128]{1,0:T(4,128)} %bitcast.30, s32[4,128]{1,0:T(4,128)} %bitcast.31, s32[32,128]{1,0:T(8,128)} %bitcast.28), custom_call_target="tpu_custom_call" | custom-call | tf_op jit(solution)/shard_map/weigh/pallas_call | solution.py:367
  2.7 3.0 %collective-permute-start.1 = (bf16[528,128]{1,0:T(8,128)(2,1)}, bf16[528,128]{1,0:T(8,128)(2,1)S(1)}, u32[]{:S(2)}, u32[]{:S(2)}) collective-permute-start(bf16[528,128]{1,0:T(8,128)(2,1)} %get-tuple-element.17), channel_id=1, source_target_pairs={{0,4},{4,0},{8,12},{12,8},{1,5},{5,1},{9,13},{13,9},{2,6},{6,2},{1... | collective-permute-start | bytes 405512 | tf_op jit(solution)/shard_map/ppermute | solution.py:344
  5.7 2.6 %collective-permute-start = (bf16[528,128]{1,0:T(8,128)(2,1)}, bf16[528,128]{1,0:T(8,128)(2,1)S(1)}, u32[]{:S(2)}, u32[]{:S(2)}) collective-permute-start(bf16[528,128]{1,0:T(8,128)(2,1)} %get-tuple-element.17), channel_id=1, source_target_pairs={{0,8},{4,12},{8,0},{12,4},{1,9},{5,13},{9,1},{13,5},{2,10},{6,14},... | collective-permute-start | bytes 405512 | tf_op jit(solution)/shard_map/ppermute | solution.py:344
  8.3 1.5 %collective-permute-start.3 = (bf16[528,128]{1,0:T(8,128)(2,1)}, bf16[528,128]{1,0:T(8,128)(2,1)S(1)}, u32[]{:S(2)}, u32[]{:S(2)}) collective-permute-start(bf16[528,128]{1,0:T(8,128)(2,1)} %get-tuple-element.17), channel_id=1, source_target_pairs={{0,2},{2,0},{1,3},{3,1},{4,6},{6,4},{5,7},{7,5},{8,10},{10,8},{9,1... | collective-permute-start | bytes 405512 | tf_op jit(solution)/shard_map/ppermute | solution.py:344
  9.8 1.7 %collective-permute-done.1 = bf16[528,128]{1,0:T(8,128)(2,1)S(1)} collective-permute-done((bf16[528,128]{1,0:T(8,128)(2,1)}, bf16[528,128]{1,0:T(8,128)(2,1)S(1)}, u32[]{:S(2)}, u32[]{:S(2)}) %collective-permute-start.1) | collective-permute-done | bytes 135200 | tf_op jit(solution)/shard_map/ppermute | solution.py:344
  11.5 1.8 %collective-permute-start.2 = (bf16[528,128]{1,0:T(8,128)(2,1)S(1)}, bf16[528,128]{1,0:T(8,128)(2,1)S(1)}, u32[]{:S(2)}, u32[]{:S(2)}) collective-permute-start(bf16[528,128]{1,0:T(8,128)(2,1)S(1)} %collective-permute-done.1), channel_id=1, source_target_pairs={{0,2},{2,0},{1,3},{3,1},{4,6},{6,4},{5,7},{7,5},{8,10},{10,8},{9,1... | collective-permute-start | bytes 405512 | tf_op jit(solution)/shard_map/ppermute | solution.py:344
  13.3 0.0 copy-start
  13.3 0.9 %copy-done = bf16[528,128]{1,0:T(8,128)(2,1)S(1)} copy-done((bf16[528,128]{1,0:T(8,128)(2,1)S(1)}, bf16[528,128]{1,0:T(8,128)(2,1)}, u32[]{:S(2)}) %copy-start) | copy-done | bytes 135192
  14.2 0.0 copy-start.2
  14.2 0.7 %copy-done.2 = f32[24,128]{1,0:T(8,128)S(1)} copy-done((f32[24,128]{1,0:T(8,128)S(1)}, f32[24,128]{1,0:T(8,128)}, u32[]{:S(2)}) %copy-start.2) | copy-done | bytes 12312
  15.0 0.0 copy-start.1
  15.0 1.7 %first_sums.1 = (f32[4096,128]{1,0:T(8,128)S(1)}, f32[4096,128]{1,0:T(8,128)S(1)}, bf16[1024,128]{1,0:T(8,128)(2,1)S(1)}, f32[8,128]{1,0:T(8,128)S(1)}) custom-call(f32[24,128]{1,0:T(8,128)S(1)} %copy-done.2, bf16[1,528,128]{2,1,0:T(8,128)(2,1)S(1)} %bitcast.23, bf16[1,528,128]{2,1,0:T(8,128)(2,1)S(1)} %bitcast.25), custom_call_target="tpu_custom_call" | custom-call | flops 2 | tf_op jit(solution)/shard_map/first_sums/pallas_call | solution.py:390
  16.7 0.0 collective-permute-done
  16.7 0.1 collective-permute-start.4
  16.8 0.0 collective-permute-done.3
  16.8 0.0 collective-permute-done.2
  16.8 1.6 %collective-permute-start.5 = (bf16[528,128]{1,0:T(8,128)(2,1)S(1)}, bf16[528,128]{1,0:T(8,128)(2,1)S(1)}, u32[]{:S(2)}, u32[]{:S(2)}) collective-permute-start(bf16[528,128]{1,0:T(8,128)(2,1)S(1)} %collective-permute-done), channel_id=1, source_target_pairs={{0,2},{2,0},{1,3},{3,1},{4,6},{6,4},{5,7},{7,5},{8,10},{10,8},{9,1... | collective-permute-start | bytes 405512 | tf_op jit(solution)/shard_map/ppermute | solution.py:344
  18.4 3.4 %collective-permute-done.4 = bf16[528,128]{1,0:T(8,128)(2,1)S(1)} collective-permute-done((bf16[528,128]{1,0:T(8,128)(2,1)S(1)}, bf16[528,128]{1,0:T(8,128)(2,1)S(1)}, u32[]{:S(2)}, u32[]{:S(2)}) %collective-permute-start.4) | collective-permute-done | bytes 135200 | tf_op jit(solution)/shard_map/ppermute | solution.py:344
  21.8 0.2 collective-permute-start.6
  22.0 0.7 %collective-permute-done.5 = bf16[528,128]{1,0:T(8,128)(2,1)S(1)} collective-permute-done((bf16[528,128]{1,0:T(8,128)(2,1)S(1)}, bf16[528,128]{1,0:T(8,128)(2,1)S(1)}, u32[]{:S(2)}, u32[]{:S(2)}) %collective-permute-start.5) | collective-permute-done | bytes 135200 | tf_op jit(solution)/shard_map/ppermute | solution.py:344
  22.6 2.4 %more_sums.1 = (f32[4096,128]{1,0:T(8,128)S(1)}, bf16[1280,128]{1,0:T(8,128)(2,1)S(1)}, f32[10,128]{1,0:T(8,128)S(1)}) custom-call(f32[24,128]{1,0:T(8,128)S(1)} %copy-done.2, bf16[1,528,128]{2,1,0:T(8,128)(2,1)S(1)} %bitcast.13, bf16[1,528,128]{2,1,0:T(8,128)(2,1)S(1)} %bitcast.15, bf16[1,528,128]{2,1,0:T(8,128)(2,1)S(1)} %bitcast.17, ...), custom_call_target="tpu_custom_call" | custom-call | flops 5 | tf_op jit(solution)/shard_map/more_sums/pallas_call | solution.py:390
  25.1 1.7 %collective-permute-done.6 = bf16[528,128]{1,0:T(8,128)(2,1)S(1)} collective-permute-done((bf16[528,128]{1,0:T(8,128)(2,1)S(1)}, bf16[528,128]{1,0:T(8,128)(2,1)S(1)}, u32[]{:S(2)}, u32[]{:S(2)}) %collective-permute-start.6) | collective-permute-done | bytes 135200 | tf_op jit(solution)/shard_map/ppermute | solution.py:344
  26.8 0.0 copy-done.1
  26.8 3.8 %table_and_rows.1 = (bf16[4096,128]{1,0:T(8,128)(2,1)}, bf16[512,128]{1,0:T(8,128)(2,1)}) custom-call(f32[24,128]{1,0:T(8,128)S(1)} %copy-done.2, f32[4096,128]{1,0:T(8,128)S(1)} %get-tuple-element.24.refs_1_, f32[4096,128]{1,0:T(8,128)S(1)} %get-tuple-element.25.refs_2_, bf16[1024,128]{1,0:T(8,128)(2,1)S(1)} %get-tuple-element.26.refs_3_, ...), custom_call_target="tpu_custom_call" | custom-call | tf_op jit(solution)/shard_map/table_and_rows/pallas_call | solution.py:429
Async XLA Ops:
  2.7 8.8 %collective-permute-start.1 = (bf16[528,128]{1,0:T(8,128)(2,1)}, bf16[528,128]{1,0:T(8,128)(2,1)S(1)}, u32[]{:S(2)}, u32[]{:S(2)}) collective-permute-start(bf16[528,128]{1,0:T(8,128)(2,1)} %get-tuple-element.17), channel_id=1, source_target_pairs={{0,4},{4,0},{8,12},{12,8},{1,5},{5,1},{9,13},{13,9},{2,6},{6,2},{1... | collective-permute-start | bytes 405512 | tf_op jit(solution)/shard_map/ppermute | solution.py:344
  5.7 10.9 %collective-permute-start = (bf16[528,128]{1,0:T(8,128)(2,1)}, bf16[528,128]{1,0:T(8,128)(2,1)S(1)}, u32[]{:S(2)}, u32[]{:S(2)}) collective-permute-start(bf16[528,128]{1,0:T(8,128)(2,1)} %get-tuple-element.17), channel_id=1, source_target_pairs={{0,8},{4,12},{8,0},{12,4},{1,9},{5,13},{9,1},{13,5},{2,10},{6,14},... | collective-permute-start | bytes 405512 | tf_op jit(solution)/shard_map/ppermute | solution.py:344
  8.3 8.4 %collective-permute-start.3 = (bf16[528,128]{1,0:T(8,128)(2,1)}, bf16[528,128]{1,0:T(8,128)(2,1)S(1)}, u32[]{:S(2)}, u32[]{:S(2)}) collective-permute-start(bf16[528,128]{1,0:T(8,128)(2,1)} %get-tuple-element.17), channel_id=1, source_target_pairs={{0,2},{2,0},{1,3},{3,1},{4,6},{6,4},{5,7},{7,5},{8,10},{10,8},{9,1... | collective-permute-start | bytes 405512 | tf_op jit(solution)/shard_map/ppermute | solution.py:344
  11.5 5.3 %collective-permute-start.2 = (bf16[528,128]{1,0:T(8,128)(2,1)S(1)}, bf16[528,128]{1,0:T(8,128)(2,1)S(1)}, u32[]{:S(2)}, u32[]{:S(2)}) collective-permute-start(bf16[528,128]{1,0:T(8,128)(2,1)S(1)} %collective-permute-done.1), channel_id=1, source_target_pairs={{0,2},{2,0},{1,3},{3,1},{4,6},{6,4},{5,7},{7,5},{8,10},{10,8},{9,1... | collective-permute-start | bytes 405512 | tf_op jit(solution)/shard_map/ppermute | solution.py:344
  13.3 0.9 %copy-start = (bf16[528,128]{1,0:T(8,128)(2,1)S(1)}, bf16[528,128]{1,0:T(8,128)(2,1)}, u32[]{:S(2)}) copy-start(bf16[528,128]{1,0:T(8,128)(2,1)} %get-tuple-element.17) | copy-start | bytes 405508
  14.2 0.7 %copy-start.2 = (f32[24,128]{1,0:T(8,128)S(1)}, f32[24,128]{1,0:T(8,128)}, u32[]{:S(2)}) copy-start(f32[24,128]{1,0:T(8,128)} %get-tuple-element.16.refs_0_) | copy-start | bytes 36868
  15.0 11.8 %copy-start.1 = (bf16[528,128]{1,0:T(8,128)(2,1)S(1)}, bf16[528,128]{1,0:T(8,128)(2,1)}, u32[]{:S(2)}) copy-start(bf16[528,128]{1,0:T(8,128)(2,1)} %get-tuple-element.17) | copy-start | bytes 405508
  16.7 5.1 %collective-permute-start.4 = (bf16[528,128]{1,0:T(8,128)(2,1)S(1)}, bf16[528,128]{1,0:T(8,128)(2,1)S(1)}, u32[]{:S(2)}, u32[]{:S(2)}) collective-permute-start(bf16[528,128]{1,0:T(8,128)(2,1)S(1)} %collective-permute-done), channel_id=1, source_target_pairs={{0,4},{4,0},{8,12},{12,8},{1,5},{5,1},{9,13},{13,9},{2,6},{6,2},{1... | collective-permute-start | bytes 405512 | tf_op jit(solution)/shard_map/ppermute | solution.py:344
  16.8 5.9 %collective-permute-start.5 = (bf16[528,128]{1,0:T(8,128)(2,1)S(1)}, bf16[528,128]{1,0:T(8,128)(2,1)S(1)}, u32[]{:S(2)}, u32[]{:S(2)}) collective-permute-start(bf16[528,128]{1,0:T(8,128)(2,1)S(1)} %collective-permute-done), channel_id=1, source_target_pairs={{0,2},{2,0},{1,3},{3,1},{4,6},{6,4},{5,7},{7,5},{8,10},{10,8},{9,1... | collective-permute-start | bytes 405512 | tf_op jit(solution)/shard_map/ppermute | solution.py:344
  21.8 5.0 %collective-permute-start.6 = (bf16[528,128]{1,0:T(8,128)(2,1)S(1)}, bf16[528,128]{1,0:T(8,128)(2,1)S(1)}, u32[]{:S(2)}, u32[]{:S(2)}) collective-permute-start(bf16[528,128]{1,0:T(8,128)(2,1)S(1)} %collective-permute-done.4), channel_id=1, source_target_pairs={{0,2},{2,0},{1,3},{3,1},{4,6},{6,4},{5,7},{7,5},{8,10},{10,8},{9,1... | collective-permute-start | bytes 405512 | tf_op jit(solution)/shard_map/ppermute | solution.py:344

commit v8 on v7

--- a/solution.py
+++ b/solution.py
@@ -256,7 +256,9 @@
     tails = [refs[3 + 2 * i : 5 + 2 * i] for i in range(len(earlier))]
     refs = refs[3 + 2 * len(earlier) :]
     count = sum(form)
-    table_ref, feature_ref, place_ref, until_ref, rows_ref, from_ref, marks_ref, codes_ref = refs[count:]
+    (
+        out_ref, feature_ref, place_ref, until_ref, rows_ref, from_ref, marks_ref, codes_ref, table_ref, sems,
+    ) = refs[count:]
     pieces, last = Pieces(z, form, refs[:count]), Pieces(z, form[-late:], refs[count - sum(form[-late:]) : count])
     rate, me = own_ref[8:9, :], own_ref[9:10, :]
     base = me * F32(z.slots)
@@ -277,6 +279,7 @@
             begin = ref[g : g + 1, :]
             bounds.append((short(begin), short(runs.until(begin + base) - base)))
     n = last.groups
+    copies = []
     for b in range(z.slots // BLOCK):
         part = slice(b * BLOCK, (b + 1) * BLOCK)
         position = (inner + b * BLOCK).astype(I16)
@@ -297,6 +300,11 @@
                 value = value * own_fall + tail * jnp.exp(-rate * (start + tail_anchor))
             value = value * fall * runs.root(inner.astype(F32) + (start + base))
         table_ref[part, :] = value.astype(BF16)
+        if (b + 1) * BLOCK % z.window == 0:
+            done = slice((b + 1) * BLOCK - z.window, (b + 1) * BLOCK)
+            copy = pltpu.make_async_copy(table_ref.at[done, :], out_ref.at[done, :], sems.at[len(copies)])
+            copy.start()
+            copies.append(copy)
 
     narrow = z.owners * z.slots <= 32768
 
@@ -338,6 +346,8 @@
             center = first + F32(z.span * z.slots // 2 - shift * z.span * z.slots)
             total += value * jnp.exp(-rate * (position - center))
         feature_ref[t * BLOCK : (t + 1) * BLOCK, :] = (total * runs.root(position)).astype(BF16)
+    for copy in copies:
+        copy.wait()
 
 
 def swap(block, axis, distance):
@@ -406,16 +416,18 @@
         far = swap(block, "key", 2)
         side = swap(block, "shard", 1)
         near = swap(block, "key", 1)
-        side_near = swap(near, "shard", 1)
-        first = [(block,), (near,)]
+        side_near = swap(side, "key", 1)
+        held, waited = tie((block, far))
+        first = [(held,), (side,), (near,)]
         total, scale, *tail = sums(first)
-        far, total = tie((far, total))
+
         last = swap(far, "key", 1)
-        sent, side_near, side = tie((far, side_near, side))
+        last, total = tie((last, total))
+        sent = far
         side_far = swap(sent, "shard", 1)
         side_last = swap(last, "shard", 1)
-        second = [(far,), (side,), (side_near,), (last,), (side_far,)]
-        late = [(side_last,)]
+        second = [(far,), (last,), (side_far,)]
+        late = [(side_near,), (side_last,)]
         total, *tail2 = sums(second, (total,))
         early, earlier, tails = first + second, (len(first), len(second)), tail + tail2
     else:
@@ -430,7 +442,7 @@
         functools.partial(late_kernel, z, earlier, form, len(late)),
         out_shape=(shape((slots, width), BF16), shape((rows, width), BF16)),
         in_specs=[vmem] * (3 + len(tails) + sum(form)),
-        out_specs=(vmem, vmem),
+        out_specs=(pl.BlockSpec(memory_space=pl.ANY), vmem),
         scratch_shapes=[
             pltpu.VMEM((owners, 8, LANES), F32),
             pltpu.VMEM((owners, 8, LANES), F32),
@@ -438,6 +450,8 @@
             pltpu.VMEM((late_lines, LANES), F32),
             pltpu.VMEM((2, late_count, 8, LANES), F32),
             pltpu.VMEM((late_count, 2 * z.chunks, LANES), F32),
+            pltpu.VMEM((slots, width), BF16),
+            pltpu.SemaphoreType.DMA((slots // z.window,)),
         ],
         compiler_params=grant,
         name="table_and_rows",

time: 30.8 us -> 30.4 us (0.987)
  waiting for transfers between devices: 7.51 us -> 6.64 us
  starting transfers between devices: 10.8 us -> 11.2 us
    ppermute x7, waiting for transfers between devices: 7.51 us -> 6.64 us  [swap(): lax.ppermute(block, axis, [(i, i ^ distance) for i in range(lax.axis_size...]
    ppermute x7, starting transfers between devices: 10.8 us -> 11.2 us  [swap(): lax.ppermute(block, axis, [(i, i ^ distance) for i in range(lax.axis_size...]
    pallas_call x1, Pallas kernels: 3.79 us -> 4.18 us  [on_device(): pl.pallas_call(functools.partial(late_kernel, z, earlier, form, len(late)...]
    pallas_call x2, Pallas kernels: 4.14 us -> 3.76 us  [sums(): pl.pallas_call(functools.partial(early_kernel, z, form, len(before)), out...]
  transfers between devices with their start and end apart: 7 -> 7, of which waited for: 4 -> 3; matrix products, arithmetic and copies ran while one was open for 0% -> 0% of each run, Pallas kernels for 14% -> 12%
where the time goes in v8:
time: 30.4 us; the launch traced here: 30.2 us
  starting transfers between devices  11.2 us (37%)
  Pallas kernels  10 us (33%)
  waiting for transfers between devices  6.64 us (22%)
  local copies, waits for them, and re-layouts  1.61 us (5%)
  between operations  0.66 us (2%)
    ppermute x7, starting transfers between devices, swap(): lax.ppermute(block, axis, [(i, i ^ distance) for i in range(lax.axis_size...  11.2 us
    ppermute x7, waiting for transfers between devices, swap(): lax.ppermute(block, axis, [(i, i ^ distance) for i in range(lax.axis_size...  6.64 us
    pallas_call x1, Pallas kernels, on_device(): pl.pallas_call(functools.partial(late_kernel, z, earlier, form, len(late)...  4.18 us
    pallas_call x2, Pallas kernels, sums(): pl.pallas_call(functools.partial(early_kernel, z, form, len(before)), out...  3.76 us
    pallas_call x1, Pallas kernels, on_device(): pl.pallas_call(functools.partial(send_kernel, z), out_shape=(shape((block...  2.08 us
    unnamed x6, local copies, waits for them, and re-layouts  1.61 us
  transfers between devices with their start and end apart: 7, of which 3 were waited for; matrix products, arithmetic and copies ran while one was open for 0% of the time, Pallas kernels for 12%

profile of v8, /device:TPU:0, one launch (start us, length us, event | category | flops | bytes accessed | tf_op | source)
XLA Modules:
  0.0 30.2 jit_solution(10845660358995057181)
XLA Ops:
  0.6 2.1 %weigh.1 = (bf16[528,128]{1,0:T(8,128)(2,1)}, f32[24,128]{1,0:T(8,128)}) custom-call(s32[1]{0:T(128)} %bitcast.me_ref, f32[4]{0:T(128)} %rate_ref.1, bf16[512,128]{1,0:T(8,128)(2,1)} %events_ref.1, f32[4,128]{1,0:T(4,128)} %bitcast.28, s32[4,128]{1,0:T(4,128)} %bitcast.29, s32[4,128]{1,0:T(4,128)} %bitcast.30, s32[32,128]{1,0:T(8,128)} %bitcast.27), custom_call_target="tpu_custom_call" | custom-call | tf_op jit(solution)/shard_map/weigh/pallas_call | solution.py:377
  2.7 4.0 %collective-permute-start = (bf16[528,128]{1,0:T(8,128)(2,1)}, bf16[528,128]{1,0:T(8,128)(2,1)S(1)}, u32[]{:S(2)}, u32[]{:S(2)}) collective-permute-start(bf16[528,128]{1,0:T(8,128)(2,1)} %get-tuple-element.16), channel_id=1, source_target_pairs={{0,8},{4,12},{8,0},{12,4},{1,9},{5,13},{9,1},{13,5},{2,10},{6,14},... | collective-permute-start | bytes 405512 | tf_op jit(solution)/shard_map/ppermute | solution.py:354
  6.8 1.5 %collective-permute-start.2 = (bf16[528,128]{1,0:T(8,128)(2,1)}, bf16[528,128]{1,0:T(8,128)(2,1)S(1)}, u32[]{:S(2)}, u32[]{:S(2)}) collective-permute-start(bf16[528,128]{1,0:T(8,128)(2,1)} %get-tuple-element.16), channel_id=1, source_target_pairs={{0,2},{2,0},{1,3},{3,1},{4,6},{6,4},{5,7},{7,5},{8,10},{10,8},{9,1... | collective-permute-start | bytes 405512 | tf_op jit(solution)/shard_map/ppermute | solution.py:354
  8.2 1.6 %collective-permute-start.3 = (bf16[528,128]{1,0:T(8,128)(2,1)}, bf16[528,128]{1,0:T(8,128)(2,1)S(1)}, u32[]{:S(2)}, u32[]{:S(2)}) collective-permute-start(bf16[528,128]{1,0:T(8,128)(2,1)} %get-tuple-element.16), channel_id=1, source_target_pairs={{0,4},{4,0},{8,12},{12,8},{1,5},{5,1},{9,13},{13,9},{2,6},{6,2},{1... | collective-permute-start | bytes 405512 | tf_op jit(solution)/shard_map/ppermute | solution.py:354
  9.8 3.7 %collective-permute-done = bf16[528,128]{1,0:T(8,128)(2,1)S(1)} collective-permute-done((bf16[528,128]{1,0:T(8,128)(2,1)}, bf16[528,128]{1,0:T(8,128)(2,1)S(1)}, u32[]{:S(2)}, u32[]{:S(2)}) %collective-permute-start) | collective-permute-done | bytes 135200 | tf_op jit(solution)/shard_map/ppermute | solution.py:354
  13.5 0.8 %collective-permute-start.1 = (bf16[528,128]{1,0:T(8,128)(2,1)S(1)}, bf16[528,128]{1,0:T(8,128)(2,1)S(1)}, u32[]{:S(2)}, u32[]{:S(2)}) collective-permute-start(bf16[528,128]{1,0:T(8,128)(2,1)S(1)} %collective-permute-done), channel_id=1, source_target_pairs={{0,4},{4,0},{8,12},{12,8},{1,5},{5,1},{9,13},{13,9},{2,6},{6,2},{1... | collective-permute-start | bytes 405512 | tf_op jit(solution)/shard_map/ppermute | solution.py:354
  14.3 1.4 %collective-permute-start.4 = (bf16[528,128]{1,0:T(8,128)(2,1)S(1)}, bf16[528,128]{1,0:T(8,128)(2,1)S(1)}, u32[]{:S(2)}, u32[]{:S(2)}) collective-permute-start(bf16[528,128]{1,0:T(8,128)(2,1)S(1)} %collective-permute-done), channel_id=1, source_target_pairs={{0,2},{2,0},{1,3},{3,1},{4,6},{6,4},{5,7},{7,5},{8,10},{10,8},{9,1... | collective-permute-start | bytes 405512 | tf_op jit(solution)/shard_map/ppermute | solution.py:354
  15.8 0.0 collective-permute-done.2
  15.8 0.0 collective-permute-done.3
  15.8 0.0 copy-start
  15.8 0.9 %copy-done = bf16[528,128]{1,0:T(8,128)(2,1)S(1)} copy-done((bf16[528,128]{1,0:T(8,128)(2,1)S(1)}, bf16[528,128]{1,0:T(8,128)(2,1)}, u32[]{:S(2)}) %copy-start) | copy-done | bytes 135192
  16.7 0.0 copy-start.2
  16.7 0.7 %copy-done.2 = f32[24,128]{1,0:T(8,128)S(1)} copy-done((f32[24,128]{1,0:T(8,128)S(1)}, f32[24,128]{1,0:T(8,128)}, u32[]{:S(2)}) %copy-start.2) | copy-done | bytes 12312
  17.4 0.0 copy-start.1
  17.4 2.1 %first_sums.1 = (f32[4096,128]{1,0:T(8,128)S(1)}, f32[4096,128]{1,0:T(8,128)S(1)}, bf16[1024,128]{1,0:T(8,128)(2,1)S(1)}, f32[8,128]{1,0:T(8,128)S(1)}) custom-call(f32[24,128]{1,0:T(8,128)S(1)} %copy-done.2, bf16[1,528,128]{2,1,0:T(8,128)(2,1)S(1)} %bitcast.19, bf16[1,528,128]{2,1,0:T(8,128)(2,1)S(1)} %bitcast.21, bf16[1,528,128]{2,1,0:T(8,128)(2,1)S(1)} %bitcast.23), custom_call_target="tpu_custom_call" | custom-call | flops 3 | tf_op jit(solution)/shard_map/first_sums/pallas_call | solution.py:400
  19.5 1.4 %collective-permute-start.5 = (bf16[528,128]{1,0:T(8,128)(2,1)S(1)}, bf16[528,128]{1,0:T(8,128)(2,1)S(1)}, u32[]{:S(2)}, u32[]{:S(2)}) collective-permute-start(bf16[528,128]{1,0:T(8,128)(2,1)S(1)} %collective-permute-done.2), channel_id=1, source_target_pairs={{0,4},{4,0},{8,12},{12,8},{1,5},{5,1},{9,13},{13,9},{2,6},{6,2},{1... | collective-permute-start | bytes 405512 | tf_op jit(solution)/shard_map/ppermute | solution.py:354
  21.0 0.0 collective-permute-done.1
  21.0 0.5 %collective-permute-start.6 = (bf16[528,128]{1,0:T(8,128)(2,1)S(1)}, bf16[528,128]{1,0:T(8,128)(2,1)S(1)}, u32[]{:S(2)}, u32[]{:S(2)}) collective-permute-start(bf16[528,128]{1,0:T(8,128)(2,1)S(1)} %collective-permute-done.1), channel_id=1, source_target_pairs={{0,2},{2,0},{1,3},{3,1},{4,6},{6,4},{5,7},{7,5},{8,10},{10,8},{9,1... | collective-permute-start | bytes 405512 | tf_op jit(solution)/shard_map/ppermute | solution.py:354
  21.4 0.0 collective-permute-done.4
  21.4 1.6 %more_sums.1 = (f32[4096,128]{1,0:T(8,128)S(1)}, bf16[1024,128]{1,0:T(8,128)(2,1)S(1)}, f32[8,128]{1,0:T(8,128)S(1)}) custom-call(f32[24,128]{1,0:T(8,128)S(1)} %copy-done.2, bf16[1,528,128]{2,1,0:T(8,128)(2,1)S(1)} %bitcast.13, bf16[1,528,128]{2,1,0:T(8,128)(2,1)S(1)} %bitcast.15, bf16[1,528,128]{2,1,0:T(8,128)(2,1)S(1)} %bitcast.17, ...), custom_call_target="tpu_custom_call" | custom-call | flops 3 | tf_op jit(solution)/shard_map/more_sums/pallas_call | solution.py:400
  23.1 1.5 %collective-permute-done.5 = bf16[528,128]{1,0:T(8,128)(2,1)S(1)} collective-permute-done((bf16[528,128]{1,0:T(8,128)(2,1)S(1)}, bf16[528,128]{1,0:T(8,128)(2,1)S(1)}, u32[]{:S(2)}, u32[]{:S(2)}) %collective-permute-start.5) | collective-permute-done | bytes 135200 | tf_op jit(solution)/shard_map/ppermute | solution.py:354
  24.6 1.4 %collective-permute-done.6 = bf16[528,128]{1,0:T(8,128)(2,1)S(1)} collective-permute-done((bf16[528,128]{1,0:T(8,128)(2,1)S(1)}, bf16[528,128]{1,0:T(8,128)(2,1)S(1)}, u32[]{:S(2)}, u32[]{:S(2)}) %collective-permute-start.6) | collective-permute-done | bytes 135200 | tf_op jit(solution)/shard_map/ppermute | solution.py:354
  26.0 0.0 copy-done.1
  26.0 4.2 %table_and_rows.1 = (bf16[4096,128]{1,0:T(8,128)(2,1)}, bf16[512,128]{1,0:T(8,128)(2,1)}) custom-call(f32[24,128]{1,0:T(8,128)S(1)} %copy-done.2, f32[4096,128]{1,0:T(8,128)S(1)} %get-tuple-element.20.refs_1_, f32[4096,128]{1,0:T(8,128)S(1)} %get-tuple-element.21.refs_2_, bf16[1024,128]{1,0:T(8,128)(2,1)S(1)} %get-tuple-element.22.refs_3_, ...), custom_call_target="tpu_custom_call" | custom-call | tf_op jit(solution)/shard_map/table_and_rows/pallas_call | solution.py:441
Async XLA Ops:
  2.7 10.8 %collective-permute-start = (bf16[528,128]{1,0:T(8,128)(2,1)}, bf16[528,128]{1,0:T(8,128)(2,1)S(1)}, u32[]{:S(2)}, u32[]{:S(2)}) collective-permute-start(bf16[528,128]{1,0:T(8,128)(2,1)} %get-tuple-element.16), channel_id=1, source_target_pairs={{0,8},{4,12},{8,0},{12,4},{1,9},{5,13},{9,1},{13,5},{2,10},{6,14},... | collective-permute-start | bytes 405512 | tf_op jit(solution)/shard_map/ppermute | solution.py:354
  6.8 9.0 %collective-permute-start.2 = (bf16[528,128]{1,0:T(8,128)(2,1)}, bf16[528,128]{1,0:T(8,128)(2,1)S(1)}, u32[]{:S(2)}, u32[]{:S(2)}) collective-permute-start(bf16[528,128]{1,0:T(8,128)(2,1)} %get-tuple-element.16), channel_id=1, source_target_pairs={{0,2},{2,0},{1,3},{3,1},{4,6},{6,4},{5,7},{7,5},{8,10},{10,8},{9,1... | collective-permute-start | bytes 405512 | tf_op jit(solution)/shard_map/ppermute | solution.py:354
  8.2 7.5 %collective-permute-start.3 = (bf16[528,128]{1,0:T(8,128)(2,1)}, bf16[528,128]{1,0:T(8,128)(2,1)S(1)}, u32[]{:S(2)}, u32[]{:S(2)}) collective-permute-start(bf16[528,128]{1,0:T(8,128)(2,1)} %get-tuple-element.16), channel_id=1, source_target_pairs={{0,4},{4,0},{8,12},{12,8},{1,5},{5,1},{9,13},{13,9},{2,6},{6,2},{1... | collective-permute-start | bytes 405512 | tf_op jit(solution)/shard_map/ppermute | solution.py:354
  13.5 7.4 %collective-permute-start.1 = (bf16[528,128]{1,0:T(8,128)(2,1)S(1)}, bf16[528,128]{1,0:T(8,128)(2,1)S(1)}, u32[]{:S(2)}, u32[]{:S(2)}) collective-permute-start(bf16[528,128]{1,0:T(8,128)(2,1)S(1)} %collective-permute-done), channel_id=1, source_target_pairs={{0,4},{4,0},{8,12},{12,8},{1,5},{5,1},{9,13},{13,9},{2,6},{6,2},{1... | collective-permute-start | bytes 405512 | tf_op jit(solution)/shard_map/ppermute | solution.py:354
  14.3 7.1 %collective-permute-start.4 = (bf16[528,128]{1,0:T(8,128)(2,1)S(1)}, bf16[528,128]{1,0:T(8,128)(2,1)S(1)}, u32[]{:S(2)}, u32[]{:S(2)}) collective-permute-start(bf16[528,128]{1,0:T(8,128)(2,1)S(1)} %collective-permute-done), channel_id=1, source_target_pairs={{0,2},{2,0},{1,3},{3,1},{4,6},{6,4},{5,7},{7,5},{8,10},{10,8},{9,1... | collective-permute-start | bytes 405512 | tf_op jit(solution)/shard_map/ppermute | solution.py:354
  15.8 0.9 %copy-start = (bf16[528,128]{1,0:T(8,128)(2,1)S(1)}, bf16[528,128]{1,0:T(8,128)(2,1)}, u32[]{:S(2)}) copy-start(bf16[528,128]{1,0:T(8,128)(2,1)} %get-tuple-element.16) | copy-start | bytes 405508
  16.7 0.7 %copy-start.2 = (f32[24,128]{1,0:T(8,128)S(1)}, f32[24,128]{1,0:T(8,128)}, u32[]{:S(2)}) copy-start(f32[24,128]{1,0:T(8,128)} %get-tuple-element.14.refs_0_) | copy-start | bytes 36868
  17.4 8.6 %copy-start.1 = (bf16[528,128]{1,0:T(8,128)(2,1)S(1)}, bf16[528,128]{1,0:T(8,128)(2,1)}, u32[]{:S(2)}) copy-start(bf16[528,128]{1,0:T(8,128)(2,1)} %get-tuple-element.16) | copy-start | bytes 405508
  19.5 5.1 %collective-permute-start.5 = (bf16[528,128]{1,0:T(8,128)(2,1)S(1)}, bf16[528,128]{1,0:T(8,128)(2,1)S(1)}, u32[]{:S(2)}, u32[]{:S(2)}) collective-permute-start(bf16[528,128]{1,0:T(8,128)(2,1)S(1)} %collective-permute-done.2), channel_id=1, source_target_pairs={{0,4},{4,0},{8,12},{12,8},{1,5},{5,1},{9,13},{13,9},{2,6},{6,2},{1... | collective-permute-start | bytes 405512 | tf_op jit(solution)/shard_map/ppermute | solution.py:354
  21.0 5.0 %collective-permute-start.6 = (bf16[528,128]{1,0:T(8,128)(2,1)S(1)}, bf16[528,128]{1,0:T(8,128)(2,1)S(1)}, u32[]{:S(2)}, u32[]{:S(2)}) collective-permute-start(bf16[528,128]{1,0:T(8,128)(2,1)S(1)} %collective-permute-done.1), channel_id=1, source_target_pairs={{0,2},{2,0},{1,3},{3,1},{4,6},{6,4},{5,7},{7,5},{8,10},{10,8},{9,1... | collective-permute-start | bytes 405512 | tf_op jit(solution)/shard_map/ppermute | solution.py:354

commit v9 on v8

--- a/solution.py
+++ b/solution.py
@@ -15,7 +15,7 @@
 I16 = jnp.int16
 FAR = 1e9
 NT = (((1,), (1,)), ((), ()))
-BLOCK = 256
+BLOCK = 512
 COST = 1
 
 
@@ -417,19 +417,17 @@
         side = swap(block, "shard", 1)
         near = swap(block, "key", 1)
         side_near = swap(side, "key", 1)
-        held, waited = tie((block, far))
-        first = [(held,), (side,), (near,)]
-        total, scale, *tail = sums(first)
-
+        total, scale, *tail = sums([(block,)])
+        far, total = tie((far, total))
         last = swap(far, "key", 1)
+        side_far = swap(far, "shard", 1)
+        total, *tail2 = sums([(side,), (near,)], (total,))
         last, total = tie((last, total))
-        sent = far
-        side_far = swap(sent, "shard", 1)
         side_last = swap(last, "shard", 1)
         second = [(far,), (last,), (side_far,)]
         late = [(side_near,), (side_last,)]
-        total, *tail2 = sums(second, (total,))
-        early, earlier, tails = first + second, (len(first), len(second)), tail + tail2
+        total, *tail3 = sums(second, (total,))
+        early, earlier, tails = [(block,), (side,), (near,)] + second, (1, 2, 3), tail + tail2 + tail3
     else:
         blocks = spread(spread([block], "key"), "shard")
         total, scale, *_ = sums([])

time: 30.4 us -> 28.3 us (0.931)
  waiting for transfers between devices: 6.64 us -> 2.2 us
  starting transfers between devices: 11.2 us -> 12.7 us
  Pallas kernels: 10 us -> 10.8 us
    ppermute x7, waiting for transfers between devices: 6.64 us -> 2.2 us  [swap(): lax.ppermute(block, axis, [(i, i ^ distance) for i in range(lax.axis_size...]
    ppermute x7, starting transfers between devices: 11.2 us -> 12.7 us  [swap(): lax.ppermute(block, axis, [(i, i ^ distance) for i in range(lax.axis_size...]
    pallas_call x2 -> x3, Pallas kernels: 3.76 us -> 4.3 us  [sums(): pl.pallas_call(functools.partial(early_kernel, z, form, len(before)), out...]
  transfers between devices with their start and end apart: 7 -> 7, of which waited for: 3 -> 3; matrix products, arithmetic and copies ran while one was open for 0% -> 0% of each run, Pallas kernels for 12% -> 15%
where the time goes in v9:
time: 28.3 us; the launch traced here: 28 us
  starting transfers between devices  12.7 us (45%)
  Pallas kernels  10.8 us (38%)
  waiting for transfers between devices  2.2 us (8%)
  local copies, waits for them, and re-layouts  1.65 us (6%)
  between operations  0.68 us (2%)
    ppermute x7, starting transfers between devices, swap(): lax.ppermute(block, axis, [(i, i ^ distance) for i in range(lax.axis_size...  12.7 us
    pallas_call x1, Pallas kernels, on_device(): pl.pallas_call(functools.partial(late_kernel, z, earlier, form, len(late)...  4.45 us
    pallas_call x3, Pallas kernels, sums(): pl.pallas_call(functools.partial(early_kernel, z, form, len(before)), out...  4.3 us
    ppermute x7, waiting for transfers between devices, swap(): lax.ppermute(block, axis, [(i, i ^ distance) for i in range(lax.axis_size...  2.2 us
    pallas_call x1, Pallas kernels, on_device(): pl.pallas_call(functools.partial(send_kernel, z), out_shape=(shape((block...  2.08 us
    unnamed x6, local copies, waits for them, and re-layouts  1.65 us
  transfers between devices with their start and end apart: 7, of which 3 were waited for; matrix products, arithmetic and copies ran while one was open for 0% of the time, Pallas kernels for 15%

profile of v9, /device:TPU:0, one launch (start us, length us, event | category | flops | bytes accessed | tf_op | source)
XLA Modules:
  0.0 28.0 jit_solution(2493560061948759734)
XLA Ops:
  0.6 2.1 %weigh.1 = (bf16[528,128]{1,0:T(8,128)(2,1)}, f32[24,128]{1,0:T(8,128)}) custom-call(s32[1]{0:T(128)} %bitcast.me_ref, f32[4]{0:T(128)} %rate_ref.1, bf16[512,128]{1,0:T(8,128)(2,1)} %events_ref.1, f32[4,128]{1,0:T(4,128)} %bitcast.28, s32[4,128]{1,0:T(4,128)} %bitcast.29, s32[4,128]{1,0:T(4,128)} %bitcast.30, s32[32,128]{1,0:T(8,128)} %bitcast.27), custom_call_target="tpu_custom_call" | custom-call | tf_op jit(solution)/shard_map/weigh/pallas_call | solution.py:377
  2.7 4.0 %collective-permute-start = (bf16[528,128]{1,0:T(8,128)(2,1)}, bf16[528,128]{1,0:T(8,128)(2,1)S(1)}, u32[]{:S(2)}, u32[]{:S(2)}) collective-permute-start(bf16[528,128]{1,0:T(8,128)(2,1)} %get-tuple-element.19), channel_id=1, source_target_pairs={{0,8},{4,12},{8,0},{12,4},{1,9},{5,13},{9,1},{13,5},{2,10},{6,14},... | collective-permute-start | bytes 405512 | tf_op jit(solution)/shard_map/ppermute | solution.py:354
  6.8 1.5 %collective-permute-start.2 = (bf16[528,128]{1,0:T(8,128)(2,1)}, bf16[528,128]{1,0:T(8,128)(2,1)S(1)}, u32[]{:S(2)}, u32[]{:S(2)}) collective-permute-start(bf16[528,128]{1,0:T(8,128)(2,1)} %get-tuple-element.19), channel_id=1, source_target_pairs={{0,2},{2,0},{1,3},{3,1},{4,6},{6,4},{5,7},{7,5},{8,10},{10,8},{9,1... | collective-permute-start | bytes 405512 | tf_op jit(solution)/shard_map/ppermute | solution.py:354
  8.2 1.6 %collective-permute-start.3 = (bf16[528,128]{1,0:T(8,128)(2,1)}, bf16[528,128]{1,0:T(8,128)(2,1)S(1)}, u32[]{:S(2)}, u32[]{:S(2)}) collective-permute-start(bf16[528,128]{1,0:T(8,128)(2,1)} %get-tuple-element.19), channel_id=1, source_target_pairs={{0,4},{4,0},{8,12},{12,8},{1,5},{5,1},{9,13},{13,9},{2,6},{6,2},{1... | collective-permute-start | bytes 405512 | tf_op jit(solution)/shard_map/ppermute | solution.py:354
  9.8 0.0 copy-start
  9.8 0.9 %copy-done = bf16[528,128]{1,0:T(8,128)(2,1)S(1)} copy-done((bf16[528,128]{1,0:T(8,128)(2,1)S(1)}, bf16[528,128]{1,0:T(8,128)(2,1)}, u32[]{:S(2)}) %copy-start) | copy-done | bytes 135192
  10.8 0.0 copy-start.2
  10.8 0.7 %copy-done.2 = f32[24,128]{1,0:T(8,128)S(1)} copy-done((f32[24,128]{1,0:T(8,128)S(1)}, f32[24,128]{1,0:T(8,128)}, u32[]{:S(2)}) %copy-start.2) | copy-done | bytes 12312
  11.5 1.4 %first_sums.1 = (f32[4096,128]{1,0:T(8,128)S(1)}, f32[4096,128]{1,0:T(8,128)S(1)}, bf16[1024,128]{1,0:T(8,128)(2,1)S(1)}, f32[8,128]{1,0:T(8,128)S(1)}) custom-call(f32[24,128]{1,0:T(8,128)S(1)} %copy-done.2, bf16[1,528,128]{2,1,0:T(8,128)(2,1)S(1)} %bitcast.23), custom_call_target="tpu_custom_call" | custom-call | flops 1 | tf_op jit(solution)/shard_map/first_sums/pallas_call | solution.py:400
  12.9 0.6 %collective-permute-done = bf16[528,128]{1,0:T(8,128)(2,1)S(1)} collective-permute-done((bf16[528,128]{1,0:T(8,128)(2,1)}, bf16[528,128]{1,0:T(8,128)(2,1)S(1)}, u32[]{:S(2)}, u32[]{:S(2)}) %collective-permute-start) | collective-permute-done | bytes 135200 | tf_op jit(solution)/shard_map/ppermute | solution.py:354
  13.5 0.8 %collective-permute-start.1 = (bf16[528,128]{1,0:T(8,128)(2,1)S(1)}, bf16[528,128]{1,0:T(8,128)(2,1)S(1)}, u32[]{:S(2)}, u32[]{:S(2)}) collective-permute-start(bf16[528,128]{1,0:T(8,128)(2,1)S(1)} %collective-permute-done), channel_id=1, source_target_pairs={{0,4},{4,0},{8,12},{12,8},{1,5},{5,1},{9,13},{13,9},{2,6},{6,2},{1... | collective-permute-start | bytes 405512 | tf_op jit(solution)/shard_map/ppermute | solution.py:354
  14.3 1.4 %collective-permute-start.4 = (bf16[528,128]{1,0:T(8,128)(2,1)S(1)}, bf16[528,128]{1,0:T(8,128)(2,1)S(1)}, u32[]{:S(2)}, u32[]{:S(2)}) collective-permute-start(bf16[528,128]{1,0:T(8,128)(2,1)S(1)} %collective-permute-done), channel_id=1, source_target_pairs={{0,2},{2,0},{1,3},{3,1},{4,6},{6,4},{5,7},{7,5},{8,10},{10,8},{9,1... | collective-permute-start | bytes 405512 | tf_op jit(solution)/shard_map/ppermute | solution.py:354
  15.8 0.0 collective-permute-done.2
  15.8 0.0 collective-permute-done.3
  15.8 1.2 %more_sums.2 = (f32[4096,128]{1,0:T(8,128)S(1)}, bf16[1024,128]{1,0:T(8,128)(2,1)S(1)}, f32[8,128]{1,0:T(8,128)S(1)}) custom-call(f32[24,128]{1,0:T(8,128)S(1)} %copy-done.2, bf16[1,528,128]{2,1,0:T(8,128)(2,1)S(1)} %bitcast.15, bf16[1,528,128]{2,1,0:T(8,128)(2,1)S(1)} %bitcast.17, f32[4096,128]{1,0:T(8,128)S(1)} %get-tuple-element.22.refs_3_), custom_call_target="tpu_custom_call" | custom-call | flops 2 | tf_op jit(solution)/shard_map/more_sums/pallas_call | solution.py:400
  17.0 1.4 %collective-permute-start.5 = (bf16[528,128]{1,0:T(8,128)(2,1)S(1)}, bf16[528,128]{1,0:T(8,128)(2,1)S(1)}, u32[]{:S(2)}, u32[]{:S(2)}) collective-permute-start(bf16[528,128]{1,0:T(8,128)(2,1)S(1)} %collective-permute-done.2), channel_id=1, source_target_pairs={{0,4},{4,0},{8,12},{12,8},{1,5},{5,1},{9,13},{13,9},{2,6},{6,2},{1... | collective-permute-start | bytes 405512 | tf_op jit(solution)/shard_map/ppermute | solution.py:354
  18.4 0.1 collective-permute-done.1
  18.6 1.9 %collective-permute-start.6 = (bf16[528,128]{1,0:T(8,128)(2,1)S(1)}, bf16[528,128]{1,0:T(8,128)(2,1)S(1)}, u32[]{:S(2)}, u32[]{:S(2)}) collective-permute-start(bf16[528,128]{1,0:T(8,128)(2,1)S(1)} %collective-permute-done.1), channel_id=1, source_target_pairs={{0,2},{2,0},{1,3},{3,1},{4,6},{6,4},{5,7},{7,5},{8,10},{10,8},{9,1... | collective-permute-start | bytes 405512 | tf_op jit(solution)/shard_map/ppermute | solution.py:354
  20.5 0.0 collective-permute-done.4
  20.5 1.7 %more_sums.3 = (f32[4096,128]{1,0:T(8,128)S(1)}, bf16[1024,128]{1,0:T(8,128)(2,1)S(1)}, f32[8,128]{1,0:T(8,128)S(1)}) custom-call(f32[24,128]{1,0:T(8,128)S(1)} %copy-done.2, bf16[1,528,128]{2,1,0:T(8,128)(2,1)S(1)} %bitcast.13, bf16[1,528,128]{2,1,0:T(8,128)(2,1)S(1)} %bitcast.19, bf16[1,528,128]{2,1,0:T(8,128)(2,1)S(1)} %bitcast.21, ...), custom_call_target="tpu_custom_call" | custom-call | flops 3 | tf_op jit(solution)/shard_map/more_sums/pallas_call | solution.py:400
  22.2 0.0 collective-permute-done.5
  22.2 1.4 %collective-permute-done.6 = bf16[528,128]{1,0:T(8,128)(2,1)S(1)} collective-permute-done((bf16[528,128]{1,0:T(8,128)(2,1)S(1)}, bf16[528,128]{1,0:T(8,128)(2,1)S(1)}, u32[]{:S(2)}, u32[]{:S(2)}) %collective-permute-start.6) | collective-permute-done | bytes 135200 | tf_op jit(solution)/shard_map/ppermute | solution.py:354
  23.6 0.0 copy-done.1
  23.6 4.4 %table_and_rows.1 = (bf16[4096,128]{1,0:T(8,128)(2,1)}, bf16[512,128]{1,0:T(8,128)(2,1)}) custom-call(f32[24,128]{1,0:T(8,128)S(1)} %copy-done.2, f32[4096,128]{1,0:T(8,128)S(1)} %get-tuple-element.26.refs_1_, f32[4096,128]{1,0:T(8,128)S(1)} %get-tuple-element.27.refs_2_, bf16[1024,128]{1,0:T(8,128)(2,1)S(1)} %get-tuple-element.28.refs_3_, ...), custom_call_target="tpu_custom_call" | custom-call | tf_op jit(solution)/shard_map/table_and_rows/pallas_call | solution.py:439
  (1 shorter events, 0.0 us)
Async XLA Ops:
  2.7 10.8 %collective-permute-start = (bf16[528,128]{1,0:T(8,128)(2,1)}, bf16[528,128]{1,0:T(8,128)(2,1)S(1)}, u32[]{:S(2)}, u32[]{:S(2)}) collective-permute-start(bf16[528,128]{1,0:T(8,128)(2,1)} %get-tuple-element.19), channel_id=1, source_target_pairs={{0,8},{4,12},{8,0},{12,4},{1,9},{5,13},{9,1},{13,5},{2,10},{6,14},... | collective-permute-start | bytes 405512 | tf_op jit(solution)/shard_map/ppermute | solution.py:354
  6.8 9.0 %collective-permute-start.2 = (bf16[528,128]{1,0:T(8,128)(2,1)}, bf16[528,128]{1,0:T(8,128)(2,1)S(1)}, u32[]{:S(2)}, u32[]{:S(2)}) collective-permute-start(bf16[528,128]{1,0:T(8,128)(2,1)} %get-tuple-element.19), channel_id=1, source_target_pairs={{0,2},{2,0},{1,3},{3,1},{4,6},{6,4},{5,7},{7,5},{8,10},{10,8},{9,1... | collective-permute-start | bytes 405512 | tf_op jit(solution)/shard_map/ppermute | solution.py:354
  8.2 7.5 %collective-permute-start.3 = (bf16[528,128]{1,0:T(8,128)(2,1)}, bf16[528,128]{1,0:T(8,128)(2,1)S(1)}, u32[]{:S(2)}, u32[]{:S(2)}) collective-permute-start(bf16[528,128]{1,0:T(8,128)(2,1)} %get-tuple-element.19), channel_id=1, source_target_pairs={{0,4},{4,0},{8,12},{12,8},{1,5},{5,1},{9,13},{13,9},{2,6},{6,2},{1... | collective-permute-start | bytes 405512 | tf_op jit(solution)/shard_map/ppermute | solution.py:354
  9.8 0.9 %copy-start = (bf16[528,128]{1,0:T(8,128)(2,1)S(1)}, bf16[528,128]{1,0:T(8,128)(2,1)}, u32[]{:S(2)}) copy-start(bf16[528,128]{1,0:T(8,128)(2,1)} %get-tuple-element.19) | copy-start | bytes 405508
  10.8 0.7 %copy-start.2 = (f32[24,128]{1,0:T(8,128)S(1)}, f32[24,128]{1,0:T(8,128)}, u32[]{:S(2)}) copy-start(f32[24,128]{1,0:T(8,128)} %get-tuple-element.18.refs_0_) | copy-start | bytes 36868
  13.5 5.0 %collective-permute-start.1 = (bf16[528,128]{1,0:T(8,128)(2,1)S(1)}, bf16[528,128]{1,0:T(8,128)(2,1)S(1)}, u32[]{:S(2)}, u32[]{:S(2)}) collective-permute-start(bf16[528,128]{1,0:T(8,128)(2,1)S(1)} %collective-permute-done), channel_id=1, source_target_pairs={{0,4},{4,0},{8,12},{12,8},{1,5},{5,1},{9,13},{13,9},{2,6},{6,2},{1... | collective-permute-start | bytes 405512 | tf_op jit(solution)/shard_map/ppermute | solution.py:354
  14.3 6.2 %collective-permute-start.4 = (bf16[528,128]{1,0:T(8,128)(2,1)S(1)}, bf16[528,128]{1,0:T(8,128)(2,1)S(1)}, u32[]{:S(2)}, u32[]{:S(2)}) collective-permute-start(bf16[528,128]{1,0:T(8,128)(2,1)S(1)} %collective-permute-done), channel_id=1, source_target_pairs={{0,2},{2,0},{1,3},{3,1},{4,6},{6,4},{5,7},{7,5},{8,10},{10,8},{9,1... | collective-permute-start | bytes 405512 | tf_op jit(solution)/shard_map/ppermute | solution.py:354
  15.8 7.8 %copy-start.1 = (bf16[528,128]{1,0:T(8,128)(2,1)S(1)}, bf16[528,128]{1,0:T(8,128)(2,1)}, u32[]{:S(2)}) copy-start(bf16[528,128]{1,0:T(8,128)(2,1)} %get-tuple-element.19) | copy-start | bytes 405508
  17.0 5.2 %collective-permute-start.5 = (bf16[528,128]{1,0:T(8,128)(2,1)S(1)}, bf16[528,128]{1,0:T(8,128)(2,1)S(1)}, u32[]{:S(2)}, u32[]{:S(2)}) collective-permute-start(bf16[528,128]{1,0:T(8,128)(2,1)S(1)} %collective-permute-done.2), channel_id=1, source_target_pairs={{0,4},{4,0},{8,12},{12,8},{1,5},{5,1},{9,13},{13,9},{2,6},{6,2},{1... | collective-permute-start | bytes 405512 | tf_op jit(solution)/shard_map/ppermute | solution.py:354
  18.6 5.0 %collective-permute-start.6 = (bf16[528,128]{1,0:T(8,128)(2,1)S(1)}, bf16[528,128]{1,0:T(8,128)(2,1)S(1)}, u32[]{:S(2)}, u32[]{:S(2)}) collective-permute-start(bf16[528,128]{1,0:T(8,128)(2,1)S(1)} %collective-permute-done.1), channel_id=1, source_target_pairs={{0,2},{2,0},{1,3},{3,1},{4,6},{6,4},{5,7},{7,5},{8,10},{10,8},{9,1... | collective-permute-start | bytes 405512 | tf_op jit(solution)/shard_map/ppermute | solution.py:354

commit v10 on v9

--- a/solution.py
+++ b/solution.py
@@ -16,6 +16,7 @@
 FAR = 1e9
 NT = (((1,), (1,)), ((), ()))
 BLOCK = 512
+LATE_BLOCK = 256
 COST = 1
 
 
@@ -31,6 +32,7 @@
         self.capacity = 2 * rows // owners
         self.per_group = LANES // self.capacity
         self.groups = owners // self.per_group
+        self.narrow = owners * slots <= 32768
 
 
 def iota(shape, axis):
@@ -53,7 +55,7 @@
     return lax.fori_loop(0, count, body, carry)
 
 
-def send_kernel(z, me_ref, rate_ref, events_ref, weight_ref, route_ref, bucket_ref, segment_ref, block_ref, own_ref):
+def send_kernel(z, me_ref, rate_ref, events_ref, weight_ref, route_ref, bucket_ref, segment_ref, out_ref, own_ref, block_ref, sems):
     groups = rate_ref.shape[0]
     lane = iota((1, LANES), 1)
     rate = jnp.full((1, LANES), rate_ref[0], F32)
@@ -67,19 +69,31 @@
     own_ref[0:16, :] = jnp.concatenate([place, first, rate, me], axis=0)
     spot = place - first - F32(z.span * z.slots // 2)
     columns = jnp.concatenate([weight_ref[...], spot], axis=0).T
+    copies = []
+
+    def send(first, count):
+        part = pl.ds(first, count)
+        copies.append(pltpu.make_async_copy(block_ref.at[part, :], out_ref.at[part, :], sems.at[len(copies)]))
+        copies[-1].start()
+
     for r in range(z.chunks):
         part = slice(r * LANES, (r + 1) * LANES)
         weighted = (columns[:, r : r + 1] * events_ref[part, :].astype(F32)).astype(BF16)
         grown = weighted.astype(F32) * jnp.exp(columns[:, z.chunks + r : z.chunks + r + 1] * rate)
         block_ref[part, :] = grown.astype(BF16)
+        if (r + 1) % (z.chunks // 2) == 0:
+            send((r + 1) * LANES - z.rows // 2, z.rows // 2)
     ones = jnp.ones((8, LANES), BF16)
     high, low = [], []
+    users = min(LANES, 8 * z.owners)
     for u in range(z.user_rows):
-        user = iota((LANES, LANES), 0) + u * LANES
-        below = jnp.zeros((LANES, LANES), F32)
+        user = iota((users, LANES), 0) + u * LANES
+        below = jnp.zeros((users, LANES), F32)
         for r in range(z.slots // LANES):
             below += jnp.where(segment_ref[r : r + 1, :] < user, F32(1), F32(0))
         count = lax.dot_general(ones, below.astype(BF16), NT, preferred_element_type=F32)[0:1]
+        if users < LANES:
+            count = jnp.concatenate([count, jnp.full((1, LANES - users), z.slots, F32)], axis=1)
         own_ref[16 + u : 17 + u, :] = count
         count = count.astype(I32)
         high.append(count >> LOW)
@@ -88,6 +102,9 @@
     pad = [jnp.zeros((spare, LANES), I32)] if spare else []
     codes = jnp.concatenate([route, bucket >> LOW, bucket & MASK] + high + low + pad, axis=0)
     block_ref[z.rows : z.rows + z.code_rows, :] = codes.astype(F32).astype(BF16)
+    send(z.rows, z.code_rows)
+    for copy in copies:
+        copy.wait()
 
 
 class Pieces:
@@ -133,12 +150,17 @@
             pair = [jnp.broadcast_to(part, (LANES, LANES)) for part in (step >> LOW, step & MASK)]
             self.steps.append(jnp.concatenate(pair, axis=0).astype(F32).astype(BF16))
 
-    def root(self, position):
+    def start(self, position):
         total = jnp.zeros((position.shape[0], 2 * LANES), F32)
         for row, step in zip(self.starts, self.steps):
             total += lax.dot_general(ones_where(row <= position), step, NT, preferred_element_type=F32)
-        start = F32(LANES) * total[:, :LANES] + total[:, LANES:]
-        return lax.rsqrt(jnp.minimum(position - start, F32(self.z.window)) + F32(1))
+        return F32(LANES) * total[:, :LANES] + total[:, LANES:]
+
+    def start_row(self, row):
+        start = jnp.zeros((1, LANES), F32)
+        for column in self.columns:
+            start = jnp.maximum(start, jnp.max(jnp.where(column <= row, column, F32(0)), axis=0, keepdims=True))
+        return start
 
     def until(self, row):
         after = jnp.full((1, LANES), FAR, F32)
@@ -146,6 +168,10 @@
             later = jnp.where(column > row, column, F32(FAR))
             after = jnp.minimum(after, jnp.min(later, axis=0, keepdims=True))
         return jnp.minimum(row + F32(self.z.window), after - F32(1))
+
+
+def root(z, distance):
+    return lax.rsqrt(jnp.minimum(distance, F32(z.window)) + F32(1))
 
 
 def pack(z, pieces, base, marks_ref, codes_ref, rows_ref, from_ref):
@@ -208,6 +234,19 @@
     return jnp.concatenate(masks, axis=1)
 
 
+def within(low, high, rows):
+    if low.dtype == I16:
+        one, nothing = BF16(1), BF16(0)
+        return jnp.concatenate([jnp.where((low <= row) & (high >= row), one, nothing) for row in rows], axis=1)
+    return jnp.concatenate([ones_where((low <= row) & (high >= row)) for row in rows], axis=1)
+
+
+def wide_columns(rows):
+    count = rows.shape[0]
+    columns = jnp.concatenate([rows, jnp.zeros((8 - count, LANES), F32)], axis=0).T
+    return jnp.concatenate([jnp.broadcast_to(columns[:, r : r + 1], (LANES, LANES)) for r in range(count)], axis=0)
+
+
 def anchors(z, me):
     middle = F32(z.span * z.slots // 2)
     span_of = lambda owner: (owner.astype(I32) >> (z.span.bit_length() - 1)).astype(F32) * F32(z.span)
@@ -227,7 +266,7 @@
     if before:
         before_ref, sums_ref, rows_ref, from_ref, marks_ref, codes_ref = refs
     else:
-        sums_ref, scale_ref, rows_ref, from_ref, marks_ref, codes_ref = refs
+        sums_ref, scale_ref, rows_ref, from_ref, high_ref, factor_ref, marks_ref, codes_ref = refs
     rate, me = own_ref[8:9, :], own_ref[9:10, :]
     runs = Runs(z, [own_ref[16 + u : 17 + u, :] for u in range(z.user_rows)])
     pack(z, pieces, me * F32(z.slots), marks_ref, codes_ref, rows_ref, from_ref)
@@ -246,19 +285,30 @@
         else:
             value = jnp.zeros((BLOCK, LANES), F32)
         sums_ref[part, :] = value + before_ref[part, :] if before else value
-        if b * BLOCK >= z.window and not before:
-            start = F32(b * BLOCK)
-            scale_ref[part, :] = fall * jnp.exp(-rate * (start + own_anchor)) * runs.root(inner.astype(F32) + start)
+        if not before:
+            first = F32(b * BLOCK)
+            position = inner.astype(F32) + first
+            start = runs.start(position)
+            if b * BLOCK < z.window:
+                scale_ref[part, :] = start
+            else:
+                scale_ref[part, :] = fall * jnp.exp(-rate * (first + own_anchor)) * root(z, position - start)
+    if not before:
+        position, span_start = wide_columns(own_ref[0 : z.chunks, :]), wide_columns(own_ref[z.chunks : 2 * z.chunks, :])
+        for shift in range(z.shifts):
+            part = slice(shift * z.rows, (shift + 1) * z.rows)
+            center = span_start + F32(z.span * z.slots // 2 - shift * z.span * z.slots)
+            factor_ref[part, :] = jnp.exp(-rate * (position - center))
+            top = position if shift == 0 else span_start - F32(1)
+            high_ref[part, :] = short(top) if z.narrow else top
 
 
 def late_kernel(z, earlier, form, late, *refs):
-    own_ref, sums_ref, scale_ref = refs[:3]
-    tails = [refs[3 + 2 * i : 5 + 2 * i] for i in range(len(earlier))]
-    refs = refs[3 + 2 * len(earlier) :]
+    own_ref, sums_ref, scale_ref, high_ref, factor_ref = refs[:5]
+    tails = [refs[5 + 2 * i : 7 + 2 * i] for i in range(len(earlier))]
+    refs = refs[5 + 2 * len(earlier) :]
     count = sum(form)
-    (
-        out_ref, feature_ref, place_ref, until_ref, rows_ref, from_ref, marks_ref, codes_ref, table_ref, sems,
-    ) = refs[count:]
+    table_out, feature_out, rows_ref, from_ref, marks_ref, codes_ref, table_ref, feature_ref, sems = refs[count:]
     pieces, last = Pieces(z, form, refs[:count]), Pieces(z, form[-late:], refs[count - sum(form[-late:]) : count])
     rate, me = own_ref[8:9, :], own_ref[9:10, :]
     base = me * F32(z.slots)
@@ -267,11 +317,38 @@
         add = lambda s, total: total + pieces.below(s, u)
         starts.append(loop(pieces.count, add, jnp.zeros((1, LANES), F32)))
     runs = Runs(z, starts)
+    copies = []
+
+    def send(ref, out, part):
+        copies.append(pltpu.make_async_copy(ref.at[part, :], out.at[part, :], sems.at[len(copies)]))
+        copies[-1].start()
+
+    place = own_ref[0 : z.chunks, :]
+    start = jnp.concatenate([runs.start_row(place[r : r + 1]) for r in range(z.chunks)], axis=0)
+    scale = wide_columns(root(z, place - start))
+    low = wide_columns(jnp.maximum(place - F32(z.window), start))
+    span_start = wide_columns(own_ref[z.chunks : 2 * z.chunks, :]) if z.shifts > 1 else None
+    kind = short if z.narrow else lambda row: row
+    total = jnp.zeros((z.rows, LANES), F32)
+    for shift in range(z.shifts):
+        part = slice(shift * z.rows, (shift + 1) * z.rows)
+        bottom = kind(jnp.maximum(low, span_start) if shift == 0 and z.shifts > 1 else low)
+        top = high_ref[part, :]
+
+        def add(s, value):
+            rows = pieces.place(s)
+            mask = within(bottom, top, [kind(rows[r : r + 1]) for r in range(z.chunks)])
+            return value + dot(mask, pieces.rows(s))
+
+        total += loop(pieces.count, add, jnp.zeros((z.rows, LANES), F32)) * factor_ref[part, :]
+    feature_ref[...] = (total * scale).astype(BF16)
+    send(feature_ref, feature_out, slice(0, z.rows))
+
     pack(z, last, base, marks_ref, codes_ref, rows_ref, from_ref)
-
     own_anchor, tail_anchor = anchors(z, me)
-    inner = iota((BLOCK, LANES), 0)
+    inner = iota((LATE_BLOCK, LANES), 0)
     fall = jnp.exp(-rate * inner.astype(F32))
+    first_start = jnp.max(runs.start_row(base), axis=1, keepdims=True) - base
     bounds = []
     listed = [(from_ref, 0, 2 * last.groups)] + [(ref, count, count) for (_, ref), count in zip(tails, earlier)]
     for ref, first, lines in listed:
@@ -279,73 +356,31 @@
             begin = ref[g : g + 1, :]
             bounds.append((short(begin), short(runs.until(begin + base) - base)))
     n = last.groups
-    copies = []
-    for b in range(z.slots // BLOCK):
-        part = slice(b * BLOCK, (b + 1) * BLOCK)
-        position = (inner + b * BLOCK).astype(I16)
-        start = F32(b * BLOCK)
-        value = sums_ref[part, :] + dot(held(position, bounds[:n]), rows_ref[0 : n * LANES, :])
-        if b * BLOCK >= z.window:
-            value = value * scale_ref[part, :]
+    own_rows = rows_ref[0 : n * LANES, :]
+    tail_rows = [rows_ref[n * LANES : 2 * n * LANES, :]]
+    tail_rows += [ref[count * LANES : 2 * count * LANES, :] for (ref, _), count in zip(tails, earlier)]
+    tail_rows = jnp.concatenate(tail_rows, axis=0)
+    for b in range(z.slots // LATE_BLOCK):
+        part = slice(b * LATE_BLOCK, (b + 1) * LATE_BLOCK)
+        position = (inner + b * LATE_BLOCK).astype(I16)
+        first = F32(b * LATE_BLOCK)
+        value = sums_ref[part, :]
+        if b * LATE_BLOCK >= z.window:
+            value = (value + dot(held(position, bounds[:n]), own_rows)) * scale_ref[part, :]
         else:
-            tail = dot(held(position, bounds[n : 2 * n]), rows_ref[n * LANES : 2 * n * LANES, :])
-            at = 2 * n
-            for (ref, _), count in zip(tails, earlier):
-                tail += dot(held(position, bounds[at : at + count]), ref[count * LANES : 2 * count * LANES, :])
-                at += count
-            own_fall = jnp.exp(-rate * (start + own_anchor))
+            own_fall = jnp.exp(-rate * (first + own_anchor))
             if z.shifts == 1:
-                value = (value + tail) * own_fall
+                value += dot(held(position, bounds), jnp.concatenate([own_rows, tail_rows], axis=0))
+                value *= own_fall
             else:
-                value = value * own_fall + tail * jnp.exp(-rate * (start + tail_anchor))
-            value = value * fall * runs.root(inner.astype(F32) + (start + base))
+                value = (value + dot(held(position, bounds[:n]), own_rows)) * own_fall
+                value += dot(held(position, bounds[n:]), tail_rows) * jnp.exp(-rate * (first + tail_anchor))
+            start = scale_ref[part, :]
+            start = jnp.where(start > 0, start, first_start)
+            value = value * fall * root(z, inner.astype(F32) + first - start)
         table_ref[part, :] = value.astype(BF16)
-        if (b + 1) * BLOCK % z.window == 0:
-            done = slice((b + 1) * BLOCK - z.window, (b + 1) * BLOCK)
-            copy = pltpu.make_async_copy(table_ref.at[done, :], out_ref.at[done, :], sems.at[len(copies)])
-            copy.start()
-            copies.append(copy)
-
-    narrow = z.owners * z.slots <= 32768
-
-    def decode(s, carry):
-        place = pieces.place(s)
-        until = jnp.concatenate([runs.until(place[r : r + 1]) for r in range(z.chunks)], axis=0)
-        if narrow:
-            until = jnp.minimum(until, F32(32767))
-        spare = jnp.zeros((8 - z.chunks, LANES), F32)
-        place_ref[s] = jnp.concatenate([place, spare], axis=0)
-        until_ref[s] = jnp.concatenate([until, spare], axis=0)
-        return carry
-
-    loop(pieces.count, decode, 0)
-    columns = own_ref[0:8, :].T
-    wide_column = lambda at: jnp.broadcast_to(columns[:, at : at + 1], (LANES, LANES))
-    for t in range(z.rows // BLOCK):
-        at = t * (BLOCK // LANES)
-        position = jnp.concatenate([wide_column(at + k) for k in range(BLOCK // LANES)], axis=0)
-        first = jnp.concatenate([wide_column(z.chunks + at + k) for k in range(BLOCK // LANES)], axis=0)
-        point = short(position) if narrow else position
-        total = jnp.zeros((BLOCK, LANES), F32)
-        for shift in range(z.shifts):
-
-            def add(s, value):
-                begin, end = place_ref[s], until_ref[s]
-                bounds = [(begin[r : r + 1], end[r : r + 1]) for r in range(z.chunks)]
-                if narrow:
-                    mask = held(point, [(short(a), short(b)) for a, b in bounds])
-                else:
-                    masks = []
-                    for a, b in bounds:
-                        inside = a >= first if shift == 0 else a < first
-                        masks.append(ones_where((point >= a) & (point <= b) & inside))
-                    mask = jnp.concatenate(masks, axis=1)
-                return value + dot(mask, pieces.rows(s))
-
-            value = loop(pieces.count, add, jnp.zeros((BLOCK, LANES), F32))
-            center = first + F32(z.span * z.slots // 2 - shift * z.span * z.slots)
-            total += value * jnp.exp(-rate * (position - center))
-        feature_ref[t * BLOCK : (t + 1) * BLOCK, :] = (total * runs.root(position)).astype(BF16)
+        if (b + 1) * LATE_BLOCK % z.window == 0:
+            send(table_ref, table_out, slice((b + 1) * LATE_BLOCK - z.window, (b + 1) * LATE_BLOCK))
     for copy in copies:
         copy.wait()
 
@@ -381,7 +416,8 @@
             shape((16 + z.user_rows + 7, LANES), F32),
         ),
         in_specs=[smem, smem] + [vmem] * 5,
-        out_specs=(vmem, vmem),
+        out_specs=(pl.BlockSpec(memory_space=pl.ANY), vmem),
+        scratch_shapes=[pltpu.VMEM((block_rows, width), BF16), pltpu.SemaphoreType.DMA((3,))],
         compiler_params=pltpu.CompilerParams(vmem_limit_bytes=56 * 1024 * 1024),
         name="weigh",
     )(
@@ -397,11 +433,13 @@
         lines = max(8, 2 * count)
         whole = shape((slots, width), F32)
         kept = (shape((lines * LANES, LANES), BF16), shape((lines, LANES), F32))
+        factors = shape((z.shifts * rows, width), F32)
+        tops = shape((z.shifts * rows, width), I16 if z.narrow else F32)
         return pl.pallas_call(
             functools.partial(early_kernel, z, form, len(before)),
-            out_shape=((whole,) if before else (whole, whole)) + kept,
+            out_shape=(whole,) + kept if before else (whole, whole) + kept + (tops, factors),
             in_specs=[vmem] * (1 + len(blocks) + len(before)),
-            out_specs=(vmem,) * (3 if before else 4),
+            out_specs=(vmem,) * (3 if before else 6),
             scratch_shapes=[
                 pltpu.VMEM((2, max(1, count), 8, LANES), F32),
                 pltpu.VMEM((max(1, count), 2 * z.chunks, LANES), F32),
@@ -417,7 +455,7 @@
         side = swap(block, "shard", 1)
         near = swap(block, "key", 1)
         side_near = swap(side, "key", 1)
-        total, scale, *tail = sums([(block,)])
+        total, scale, *tail, tops, factors = sums([(block,)])
         far, total = tie((far, total))
         last = swap(far, "key", 1)
         side_far = swap(far, "shard", 1)
@@ -430,7 +468,7 @@
         early, earlier, tails = [(block,), (side,), (near,)] + second, (1, 2, 3), tail + tail2 + tail3
     else:
         blocks = spread(spread([block], "key"), "shard")
-        total, scale, *_ = sums([])
+        total, scale, _, _, tops, factors = sums([])
         early, earlier, tails = [], (), []
         late = [(jnp.concatenate(blocks, axis=0).reshape(owners, block_rows, width),)]
     late_lines = 2 * (len(late) if earlier else z.groups)
@@ -439,21 +477,20 @@
     return pl.pallas_call(
         functools.partial(late_kernel, z, earlier, form, len(late)),
         out_shape=(shape((slots, width), BF16), shape((rows, width), BF16)),
-        in_specs=[vmem] * (3 + len(tails) + sum(form)),
-        out_specs=(pl.BlockSpec(memory_space=pl.ANY), vmem),
+        in_specs=[vmem] * (5 + len(tails) + sum(form)),
+        out_specs=(pl.BlockSpec(memory_space=pl.ANY),) * 2,
         scratch_shapes=[
-            pltpu.VMEM((owners, 8, LANES), F32),
-            pltpu.VMEM((owners, 8, LANES), F32),
             pltpu.VMEM((late_lines * LANES, LANES), BF16),
             pltpu.VMEM((late_lines, LANES), F32),
             pltpu.VMEM((2, late_count, 8, LANES), F32),
             pltpu.VMEM((late_count, 2 * z.chunks, LANES), F32),
             pltpu.VMEM((slots, width), BF16),
-            pltpu.SemaphoreType.DMA((slots // z.window,)),
+            pltpu.VMEM((rows, width), BF16),
+            pltpu.SemaphoreType.DMA((1 + slots // z.window,)),
         ],
         compiler_params=grant,
         name="table_and_rows",
-    )(own, total, scale, *tails, *flat(early + late))
+    )(own, total, scale, tops, factors, *tails, *flat(early + late))
 
 
 def solution(mesh):

time: 28.3 us -> 28.4 us (level)
    pallas_call x1, Pallas kernels: 2.08 us -> 2.54 us  [on_device(): pl.pallas_call(functools.partial(send_kernel, z), out_shape=(shape((block...]
    pallas_call x1, Pallas kernels: 4.45 us -> 4.03 us  [on_device(): pl.pallas_call(functools.partial(late_kernel, z, earlier, form, len(late)...]
    unnamed x6 -> x8, local copies, waits for them, and re-layouts: 1.65 us -> 1.66 us
  transfers between devices with their start and end apart: 7 -> 7, of which waited for: 3 -> 3; matrix products, arithmetic and copies ran while one was open for 0% -> 0% of each run, Pallas kernels for 15% -> 16%
where the time goes in v10:
time: 28.4 us; the launch traced here: 28.1 us
  starting transfers between devices  12.7 us (45%)
  Pallas kernels  11 us (39%)
  waiting for transfers between devices  2.03 us (7%)
  local copies, waits for them, and re-layouts  1.66 us (6%)
  between operations  0.69 us (2%)
    ppermute x7, starting transfers between devices, swap(): lax.ppermute(block, axis, [(i, i ^ distance) for i in range(lax.axis_size...  12.7 us
    pallas_call x3, Pallas kernels, sums(): pl.pallas_call(functools.partial(early_kernel, z, form, len(before)), out...  4.47 us
    pallas_call x1, Pallas kernels, on_device(): pl.pallas_call(functools.partial(late_kernel, z, earlier, form, len(late)...  4.03 us
    pallas_call x1, Pallas kernels, on_device(): pl.pallas_call(functools.partial(send_kernel, z), out_shape=(shape((block...  2.54 us
    ppermute x7, waiting for transfers between devices, swap(): lax.ppermute(block, axis, [(i, i ^ distance) for i in range(lax.axis_size...  2.03 us
    unnamed x8, local copies, waits for them, and re-layouts  1.66 us
  transfers between devices with their start and end apart: 7, of which 3 were waited for; matrix products, arithmetic and copies ran while one was open for 0% of the time, Pallas kernels for 16%

profile of v10, /device:TPU:0, one launch (start us, length us, event | category | flops | bytes accessed | tf_op | source)
XLA Modules:
  0.0 28.1 jit_solution(1212300970658688637)
XLA Ops:
  0.6 2.5 %weigh.1 = (bf16[528,128]{1,0:T(8,128)(2,1)}, f32[24,128]{1,0:T(8,128)}) custom-call(s32[1]{0:T(128)} %bitcast.me_ref, f32[4]{0:T(128)} %rate_ref.1, bf16[512,128]{1,0:T(8,128)(2,1)} %events_ref.1, f32[4,128]{1,0:T(4,128)} %bitcast.28, s32[4,128]{1,0:T(4,128)} %bitcast.29, s32[4,128]{1,0:T(4,128)} %bitcast.30, s32[32,128]{1,0:T(8,128)} %bitcast.27), custom_call_target="tpu_custom_call" | custom-call | tf_op jit(solution)/shard_map/weigh/pallas_call | solution.py:412
  3.2 4.1 %collective-permute-start = (bf16[528,128]{1,0:T(8,128)(2,1)}, bf16[528,128]{1,0:T(8,128)(2,1)S(1)}, u32[]{:S(2)}, u32[]{:S(2)}) collective-permute-start(bf16[528,128]{1,0:T(8,128)(2,1)} %get-tuple-element.21), channel_id=1, source_target_pairs={{0,8},{4,12},{8,0},{12,4},{1,9},{5,13},{9,1},{13,5},{2,10},{6,14},... | collective-permute-start | bytes 405512 | tf_op jit(solution)/shard_map/ppermute | solution.py:389
  7.3 1.5 %collective-permute-start.2 = (bf16[528,128]{1,0:T(8,128)(2,1)}, bf16[528,128]{1,0:T(8,128)(2,1)S(1)}, u32[]{:S(2)}, u32[]{:S(2)}) collective-permute-start(bf16[528,128]{1,0:T(8,128)(2,1)} %get-tuple-element.21), channel_id=1, source_target_pairs={{0,2},{2,0},{1,3},{3,1},{4,6},{6,4},{5,7},{7,5},{8,10},{10,8},{9,1... | collective-permute-start | bytes 405512 | tf_op jit(solution)/shard_map/ppermute | solution.py:389
  8.8 1.6 %collective-permute-start.3 = (bf16[528,128]{1,0:T(8,128)(2,1)}, bf16[528,128]{1,0:T(8,128)(2,1)S(1)}, u32[]{:S(2)}, u32[]{:S(2)}) collective-permute-start(bf16[528,128]{1,0:T(8,128)(2,1)} %get-tuple-element.21), channel_id=1, source_target_pairs={{0,4},{4,0},{8,12},{12,8},{1,5},{5,1},{9,13},{13,9},{2,6},{6,2},{1... | collective-permute-start | bytes 405512 | tf_op jit(solution)/shard_map/ppermute | solution.py:389
  10.4 0.9 %copy-done = bf16[528,128]{1,0:T(8,128)(2,1)S(1)} copy-done((bf16[528,128]{1,0:T(8,128)(2,1)S(1)}, bf16[528,128]{1,0:T(8,128)(2,1)}, u32[]{:S(2)}) %copy-start) | copy-done | bytes 135192
  11.3 0.7 %copy-done.2 = f32[24,128]{1,0:T(8,128)S(1)} copy-done((f32[24,128]{1,0:T(8,128)S(1)}, f32[24,128]{1,0:T(8,128)}, u32[]{:S(2)}) %copy-start.2) | copy-done | bytes 12312
  12.0 1.6 %first_sums.1 = (f32[4096,128]{1,0:T(8,128)S(1)}, f32[4096,128]{1,0:T(8,128)S(1)}, bf16[1024,128]{1,0:T(8,128)(2,1)S(1)}, f32[8,128]{1,0:T(8,128)S(1)}, s16[512,...) custom-call(f32[24,128]{1,0:T(8,128)S(1)} %copy-done.2, bf16[1,528,128]{2,1,0:T(8,128)(2,1)S(1)} %bitcast.23), custom_call_target="tpu_custom_call" | custom-call | flops 1 | tf_op jit(solution)/shard_map/first_sums/pallas_call | solution.py:438
  13.6 0.5 %collective-permute-done = bf16[528,128]{1,0:T(8,128)(2,1)S(1)} collective-permute-done((bf16[528,128]{1,0:T(8,128)(2,1)}, bf16[528,128]{1,0:T(8,128)(2,1)S(1)}, u32[]{:S(2)}, u32[]{:S(2)}) %collective-permute-start) | collective-permute-done | bytes 135200 | tf_op jit(solution)/shard_map/ppermute | solution.py:389
  14.1 0.8 %collective-permute-start.1 = (bf16[528,128]{1,0:T(8,128)(2,1)S(1)}, bf16[528,128]{1,0:T(8,128)(2,1)S(1)}, u32[]{:S(2)}, u32[]{:S(2)}) collective-permute-start(bf16[528,128]{1,0:T(8,128)(2,1)S(1)} %collective-permute-done), channel_id=1, source_target_pairs={{0,4},{4,0},{8,12},{12,8},{1,5},{5,1},{9,13},{13,9},{2,6},{6,2},{1... | collective-permute-start | bytes 405512 | tf_op jit(solution)/shard_map/ppermute | solution.py:389
  14.9 1.4 %collective-permute-start.4 = (bf16[528,128]{1,0:T(8,128)(2,1)S(1)}, bf16[528,128]{1,0:T(8,128)(2,1)S(1)}, u32[]{:S(2)}, u32[]{:S(2)}) collective-permute-start(bf16[528,128]{1,0:T(8,128)(2,1)S(1)} %collective-permute-done), channel_id=1, source_target_pairs={{0,2},{2,0},{1,3},{3,1},{4,6},{6,4},{5,7},{7,5},{8,10},{10,8},{9,1... | collective-permute-start | bytes 405512 | tf_op jit(solution)/shard_map/ppermute | solution.py:389
  16.3 0.0 collective-permute-done.2
  16.3 0.0 collective-permute-done.3
  16.3 0.0 copy-start.3
  16.3 1.2 %more_sums.2 = (f32[4096,128]{1,0:T(8,128)S(1)}, bf16[1024,128]{1,0:T(8,128)(2,1)S(1)}, f32[8,128]{1,0:T(8,128)S(1)}) custom-call(f32[24,128]{1,0:T(8,128)S(1)} %copy-done.2, bf16[1,528,128]{2,1,0:T(8,128)(2,1)S(1)} %bitcast.15, bf16[1,528,128]{2,1,0:T(8,128)(2,1)S(1)} %bitcast.17, f32[4096,128]{1,0:T(8,128)S(1)} %get-tuple-element.24.refs_3_), custom_call_target="tpu_custom_call" | custom-call | flops 2 | tf_op jit(solution)/shard_map/more_sums/pallas_call | solution.py:438
  17.5 1.4 %collective-permute-start.5 = (bf16[528,128]{1,0:T(8,128)(2,1)S(1)}, bf16[528,128]{1,0:T(8,128)(2,1)S(1)}, u32[]{:S(2)}, u32[]{:S(2)}) collective-permute-start(bf16[528,128]{1,0:T(8,128)(2,1)S(1)} %collective-permute-done.2), channel_id=1, source_target_pairs={{0,4},{4,0},{8,12},{12,8},{1,5},{5,1},{9,13},{13,9},{2,6},{6,2},{1... | collective-permute-start | bytes 405512 | tf_op jit(solution)/shard_map/ppermute | solution.py:389
  19.0 0.1 collective-permute-done.1
  19.1 1.9 %collective-permute-start.6 = (bf16[528,128]{1,0:T(8,128)(2,1)S(1)}, bf16[528,128]{1,0:T(8,128)(2,1)S(1)}, u32[]{:S(2)}, u32[]{:S(2)}) collective-permute-start(bf16[528,128]{1,0:T(8,128)(2,1)S(1)} %collective-permute-done.1), channel_id=1, source_target_pairs={{0,2},{2,0},{1,3},{3,1},{4,6},{6,4},{5,7},{7,5},{8,10},{10,8},{9,1... | collective-permute-start | bytes 405512 | tf_op jit(solution)/shard_map/ppermute | solution.py:389
  21.0 0.0 collective-permute-done.4
  21.0 1.7 %more_sums.3 = (f32[4096,128]{1,0:T(8,128)S(1)}, bf16[1024,128]{1,0:T(8,128)(2,1)S(1)}, f32[8,128]{1,0:T(8,128)S(1)}) custom-call(f32[24,128]{1,0:T(8,128)S(1)} %copy-done.2, bf16[1,528,128]{2,1,0:T(8,128)(2,1)S(1)} %bitcast.13, bf16[1,528,128]{2,1,0:T(8,128)(2,1)S(1)} %bitcast.19, bf16[1,528,128]{2,1,0:T(8,128)(2,1)S(1)} %bitcast.21, ...), custom_call_target="tpu_custom_call" | custom-call | flops 3 | tf_op jit(solution)/shard_map/more_sums/pallas_call | solution.py:438
  22.7 0.0 collective-permute-done.5
  22.7 1.4 %collective-permute-done.6 = bf16[528,128]{1,0:T(8,128)(2,1)S(1)} collective-permute-done((bf16[528,128]{1,0:T(8,128)(2,1)S(1)}, bf16[528,128]{1,0:T(8,128)(2,1)S(1)}, u32[]{:S(2)}, u32[]{:S(2)}) %collective-permute-start.6) | collective-permute-done | bytes 135200 | tf_op jit(solution)/shard_map/ppermute | solution.py:389
  24.1 0.0 copy-done.1
  24.1 0.0 copy-done.3
  24.1 4.0 %table_and_rows.1 = (bf16[4096,128]{1,0:T(8,128)(2,1)}, bf16[512,128]{1,0:T(8,128)(2,1)}) custom-call(f32[24,128]{1,0:T(8,128)S(1)} %copy-done.3, f32[4096,128]{1,0:T(8,128)S(1)} %get-tuple-element.28.refs_1_, f32[4096,128]{1,0:T(8,128)S(1)} %get-tuple-element.29.refs_2_, s16[512,128]{1,0:T(8,128)(2,1)S(1)} %get-tuple-element.30.refs_3_, ...), custom_call_target="tpu_custom_call" | custom-call | tf_op jit(solution)/shard_map/table_and_rows/pallas_call | solution.py:477
  (3 shorter events, 0.0 us)
Async XLA Ops:
  3.2 10.9 %collective-permute-start = (bf16[528,128]{1,0:T(8,128)(2,1)}, bf16[528,128]{1,0:T(8,128)(2,1)S(1)}, u32[]{:S(2)}, u32[]{:S(2)}) collective-permute-start(bf16[528,128]{1,0:T(8,128)(2,1)} %get-tuple-element.21), channel_id=1, source_target_pairs={{0,8},{4,12},{8,0},{12,4},{1,9},{5,13},{9,1},{13,5},{2,10},{6,14},... | collective-permute-start | bytes 405512 | tf_op jit(solution)/shard_map/ppermute | solution.py:389
  7.3 9.0 %collective-permute-start.2 = (bf16[528,128]{1,0:T(8,128)(2,1)}, bf16[528,128]{1,0:T(8,128)(2,1)S(1)}, u32[]{:S(2)}, u32[]{:S(2)}) collective-permute-start(bf16[528,128]{1,0:T(8,128)(2,1)} %get-tuple-element.21), channel_id=1, source_target_pairs={{0,2},{2,0},{1,3},{3,1},{4,6},{6,4},{5,7},{7,5},{8,10},{10,8},{9,1... | collective-permute-start | bytes 405512 | tf_op jit(solution)/shard_map/ppermute | solution.py:389
  8.8 7.5 %collective-permute-start.3 = (bf16[528,128]{1,0:T(8,128)(2,1)}, bf16[528,128]{1,0:T(8,128)(2,1)S(1)}, u32[]{:S(2)}, u32[]{:S(2)}) collective-permute-start(bf16[528,128]{1,0:T(8,128)(2,1)} %get-tuple-element.21), channel_id=1, source_target_pairs={{0,4},{4,0},{8,12},{12,8},{1,5},{5,1},{9,13},{13,9},{2,6},{6,2},{1... | collective-permute-start | bytes 405512 | tf_op jit(solution)/shard_map/ppermute | solution.py:389
  10.4 0.9 %copy-start = (bf16[528,128]{1,0:T(8,128)(2,1)S(1)}, bf16[528,128]{1,0:T(8,128)(2,1)}, u32[]{:S(2)}) copy-start(bf16[528,128]{1,0:T(8,128)(2,1)} %get-tuple-element.21) | copy-start | bytes 405508
  11.3 0.7 %copy-start.2 = (f32[24,128]{1,0:T(8,128)S(1)}, f32[24,128]{1,0:T(8,128)}, u32[]{:S(2)}) copy-start(f32[24,128]{1,0:T(8,128)} %get-tuple-element.20.refs_0_) | copy-start | bytes 36868
  14.1 5.0 %collective-permute-start.1 = (bf16[528,128]{1,0:T(8,128)(2,1)S(1)}, bf16[528,128]{1,0:T(8,128)(2,1)S(1)}, u32[]{:S(2)}, u32[]{:S(2)}) collective-permute-start(bf16[528,128]{1,0:T(8,128)(2,1)S(1)} %collective-permute-done), channel_id=1, source_target_pairs={{0,4},{4,0},{8,12},{12,8},{1,5},{5,1},{9,13},{13,9},{2,6},{6,2},{1... | collective-permute-start | bytes 405512 | tf_op jit(solution)/shard_map/ppermute | solution.py:389
  14.9 6.2 %collective-permute-start.4 = (bf16[528,128]{1,0:T(8,128)(2,1)S(1)}, bf16[528,128]{1,0:T(8,128)(2,1)S(1)}, u32[]{:S(2)}, u32[]{:S(2)}) collective-permute-start(bf16[528,128]{1,0:T(8,128)(2,1)S(1)} %collective-permute-done), channel_id=1, source_target_pairs={{0,2},{2,0},{1,3},{3,1},{4,6},{6,4},{5,7},{7,5},{8,10},{10,8},{9,1... | collective-permute-start | bytes 405512 | tf_op jit(solution)/shard_map/ppermute | solution.py:389
  16.3 7.8 %copy-start.1 = (bf16[528,128]{1,0:T(8,128)(2,1)S(1)}, bf16[528,128]{1,0:T(8,128)(2,1)}, u32[]{:S(2)}) copy-start(bf16[528,128]{1,0:T(8,128)(2,1)} %get-tuple-element.21) | copy-start | bytes 405508
  16.3 7.8 %copy-start.3 = (f32[24,128]{1,0:T(8,128)S(1)}, f32[24,128]{1,0:T(8,128)}, u32[]{:S(2)}) copy-start(f32[24,128]{1,0:T(8,128)} %get-tuple-element.20.refs_0_) | copy-start | bytes 36868
  17.5 5.1 %collective-permute-start.5 = (bf16[528,128]{1,0:T(8,128)(2,1)S(1)}, bf16[528,128]{1,0:T(8,128)(2,1)S(1)}, u32[]{:S(2)}, u32[]{:S(2)}) collective-permute-start(bf16[528,128]{1,0:T(8,128)(2,1)S(1)} %collective-permute-done.2), channel_id=1, source_target_pairs={{0,4},{4,0},{8,12},{12,8},{1,5},{5,1},{9,13},{13,9},{2,6},{6,2},{1... | collective-permute-start | bytes 405512 | tf_op jit(solution)/shard_map/ppermute | solution.py:389
  19.1 5.0 %collective-permute-start.6 = (bf16[528,128]{1,0:T(8,128)(2,1)S(1)}, bf16[528,128]{1,0:T(8,128)(2,1)S(1)}, u32[]{:S(2)}, u32[]{:S(2)}) collective-permute-start(bf16[528,128]{1,0:T(8,128)(2,1)S(1)} %collective-permute-done.1), channel_id=1, source_target_pairs={{0,2},{2,0},{1,3},{3,1},{4,6},{6,4},{5,7},{7,5},{8,10},{10,8},{9,1... | collective-permute-start | bytes 405512 | tf_op jit(solution)/shard_map/ppermute | solution.py:389

commit v11 on v10

--- a/solution.py
+++ b/solution.py
@@ -55,7 +55,7 @@
     return lax.fori_loop(0, count, body, carry)
 
 
-def send_kernel(z, me_ref, rate_ref, events_ref, weight_ref, route_ref, bucket_ref, segment_ref, out_ref, own_ref, block_ref, sems):
+def send_kernel(z, me_ref, rate_ref, events_ref, weight_ref, route_ref, bucket_ref, segment_ref, block_ref, own_ref):
     groups = rate_ref.shape[0]
     lane = iota((1, LANES), 1)
     rate = jnp.full((1, LANES), rate_ref[0], F32)
@@ -69,20 +69,11 @@
     own_ref[0:16, :] = jnp.concatenate([place, first, rate, me], axis=0)
     spot = place - first - F32(z.span * z.slots // 2)
     columns = jnp.concatenate([weight_ref[...], spot], axis=0).T
-    copies = []
-
-    def send(first, count):
-        part = pl.ds(first, count)
-        copies.append(pltpu.make_async_copy(block_ref.at[part, :], out_ref.at[part, :], sems.at[len(copies)]))
-        copies[-1].start()
-
     for r in range(z.chunks):
         part = slice(r * LANES, (r + 1) * LANES)
         weighted = (columns[:, r : r + 1] * events_ref[part, :].astype(F32)).astype(BF16)
         grown = weighted.astype(F32) * jnp.exp(columns[:, z.chunks + r : z.chunks + r + 1] * rate)
         block_ref[part, :] = grown.astype(BF16)
-        if (r + 1) % (z.chunks // 2) == 0:
-            send((r + 1) * LANES - z.rows // 2, z.rows // 2)
     ones = jnp.ones((8, LANES), BF16)
     high, low = [], []
     users = min(LANES, 8 * z.owners)
@@ -102,9 +93,6 @@
     pad = [jnp.zeros((spare, LANES), I32)] if spare else []
     codes = jnp.concatenate([route, bucket >> LOW, bucket & MASK] + high + low + pad, axis=0)
     block_ref[z.rows : z.rows + z.code_rows, :] = codes.astype(F32).astype(BF16)
-    send(z.rows, z.code_rows)
-    for copy in copies:
-        copy.wait()
 
 
 class Pieces:
@@ -308,7 +296,7 @@
     tails = [refs[5 + 2 * i : 7 + 2 * i] for i in range(len(earlier))]
     refs = refs[5 + 2 * len(earlier) :]
     count = sum(form)
-    table_out, feature_out, rows_ref, from_ref, marks_ref, codes_ref, table_ref, feature_ref, sems = refs[count:]
+    table_ref, feature_ref, rows_ref, from_ref, marks_ref, codes_ref = refs[count:]
     pieces, last = Pieces(z, form, refs[:count]), Pieces(z, form[-late:], refs[count - sum(form[-late:]) : count])
     rate, me = own_ref[8:9, :], own_ref[9:10, :]
     base = me * F32(z.slots)
@@ -317,11 +305,6 @@
         add = lambda s, total: total + pieces.below(s, u)
         starts.append(loop(pieces.count, add, jnp.zeros((1, LANES), F32)))
     runs = Runs(z, starts)
-    copies = []
-
-    def send(ref, out, part):
-        copies.append(pltpu.make_async_copy(ref.at[part, :], out.at[part, :], sems.at[len(copies)]))
-        copies[-1].start()
 
     place = own_ref[0 : z.chunks, :]
     start = jnp.concatenate([runs.start_row(place[r : r + 1]) for r in range(z.chunks)], axis=0)
@@ -342,7 +325,6 @@
 
         total += loop(pieces.count, add, jnp.zeros((z.rows, LANES), F32)) * factor_ref[part, :]
     feature_ref[...] = (total * scale).astype(BF16)
-    send(feature_ref, feature_out, slice(0, z.rows))
 
     pack(z, last, base, marks_ref, codes_ref, rows_ref, from_ref)
     own_anchor, tail_anchor = anchors(z, me)
@@ -379,10 +361,6 @@
             start = jnp.where(start > 0, start, first_start)
             value = value * fall * root(z, inner.astype(F32) + first - start)
         table_ref[part, :] = value.astype(BF16)
-        if (b + 1) * LATE_BLOCK % z.window == 0:
-            send(table_ref, table_out, slice((b + 1) * LATE_BLOCK - z.window, (b + 1) * LATE_BLOCK))
-    for copy in copies:
-        copy.wait()
 
 
 def swap(block, axis, distance):
@@ -416,8 +394,7 @@
             shape((16 + z.user_rows + 7, LANES), F32),
         ),
         in_specs=[smem, smem] + [vmem] * 5,
-        out_specs=(pl.BlockSpec(memory_space=pl.ANY), vmem),
-        scratch_shapes=[pltpu.VMEM((block_rows, width), BF16), pltpu.SemaphoreType.DMA((3,))],
+        out_specs=(vmem, vmem),
         compiler_params=pltpu.CompilerParams(vmem_limit_bytes=56 * 1024 * 1024),
         name="weigh",
     )(
@@ -478,15 +455,12 @@
         functools.partial(late_kernel, z, earlier, form, len(late)),
         out_shape=(shape((slots, width), BF16), shape((rows, width), BF16)),
         in_specs=[vmem] * (5 + len(tails) + sum(form)),
-        out_specs=(pl.BlockSpec(memory_space=pl.ANY),) * 2,
+        out_specs=(vmem, vmem),
         scratch_shapes=[
             pltpu.VMEM((late_lines * LANES, LANES), BF16),
             pltpu.VMEM((late_lines, LANES), F32),
             pltpu.VMEM((2, late_count, 8, LANES), F32),
             pltpu.VMEM((late_count, 2 * z.chunks, LANES), F32),
-            pltpu.VMEM((slots, width), BF16),
-            pltpu.VMEM((rows, width), BF16),
-            pltpu.SemaphoreType.DMA((1 + slots // z.window,)),
         ],
         compiler_params=grant,
         name="table_and_rows",

time: 28.4 us -> 27.9 us (0.982)
  Pallas kernels: 11 us -> 10.6 us
    pallas_call x1, Pallas kernels: 2.54 us -> 1.96 us  [on_device(): pl.pallas_call(functools.partial(send_kernel, z), out_shape=(shape((block...]
where the time goes in v11:
time: 27.9 us; the launch traced here: 27.7 us
  starting transfers between devices  12.7 us (46%)
  Pallas kernels  10.6 us (38%)
  waiting for transfers between devices  2.03 us (7%)
  local copies, waits for them, and re-layouts  1.66 us (6%)
  between operations  0.69 us (2%)
    ppermute x7, starting transfers between devices, swap(): lax.ppermute(block, axis, [(i, i ^ distance) for i in range(lax.axis_size...  12.7 us
    pallas_call x3, Pallas kernels, sums(): pl.pallas_call(functools.partial(early_kernel, z, form, len(before)), out...  4.47 us
    pallas_call x1, Pallas kernels, on_device(): pl.pallas_call(functools.partial(late_kernel, z, earlier, form, len(late)...  4.21 us
    ppermute x7, waiting for transfers between devices, swap(): lax.ppermute(block, axis, [(i, i ^ distance) for i in range(lax.axis_size...  2.03 us
    pallas_call x1, Pallas kernels, on_device(): pl.pallas_call(functools.partial(send_kernel, z), out_shape=(shape((block...  1.96 us
    unnamed x8, local copies, waits for them, and re-layouts  1.66 us
  transfers between devices with their start and end apart: 7, of which 3 were waited for; matrix products, arithmetic and copies ran while one was open for 0% of the time, Pallas kernels for 16%

profile of v11, /device:TPU:0, one launch (start us, length us, event | category | flops | bytes accessed | tf_op | source)
XLA Modules:
  0.0 27.7 jit_solution(4773593740988216347)
XLA Ops:
  0.6 2.0 %weigh.1 = (bf16[528,128]{1,0:T(8,128)(2,1)}, f32[24,128]{1,0:T(8,128)}) custom-call(s32[1]{0:T(128)} %bitcast.me_ref, f32[4]{0:T(128)} %rate_ref.1, bf16[512,128]{1,0:T(8,128)(2,1)} %events_ref.1, f32[4,128]{1,0:T(4,128)} %bitcast.28, s32[4,128]{1,0:T(4,128)} %bitcast.29, s32[4,128]{1,0:T(4,128)} %bitcast.30, s32[32,128]{1,0:T(8,128)} %bitcast.27), custom_call_target="tpu_custom_call" | custom-call | tf_op jit(solution)/shard_map/weigh/pallas_call | solution.py:390
  2.6 4.0 %collective-permute-start = (bf16[528,128]{1,0:T(8,128)(2,1)}, bf16[528,128]{1,0:T(8,128)(2,1)S(1)}, u32[]{:S(2)}, u32[]{:S(2)}) collective-permute-start(bf16[528,128]{1,0:T(8,128)(2,1)} %get-tuple-element.21), channel_id=1, source_target_pairs={{0,8},{4,12},{8,0},{12,4},{1,9},{5,13},{9,1},{13,5},{2,10},{6,14},... | collective-permute-start | bytes 405512 | tf_op jit(solution)/shard_map/ppermute | solution.py:367
  6.6 1.5 %collective-permute-start.2 = (bf16[528,128]{1,0:T(8,128)(2,1)}, bf16[528,128]{1,0:T(8,128)(2,1)S(1)}, u32[]{:S(2)}, u32[]{:S(2)}) collective-permute-start(bf16[528,128]{1,0:T(8,128)(2,1)} %get-tuple-element.21), channel_id=1, source_target_pairs={{0,2},{2,0},{1,3},{3,1},{4,6},{6,4},{5,7},{7,5},{8,10},{10,8},{9,1... | collective-permute-start | bytes 405512 | tf_op jit(solution)/shard_map/ppermute | solution.py:367
  8.1 1.6 %collective-permute-start.3 = (bf16[528,128]{1,0:T(8,128)(2,1)}, bf16[528,128]{1,0:T(8,128)(2,1)S(1)}, u32[]{:S(2)}, u32[]{:S(2)}) collective-permute-start(bf16[528,128]{1,0:T(8,128)(2,1)} %get-tuple-element.21), channel_id=1, source_target_pairs={{0,4},{4,0},{8,12},{12,8},{1,5},{5,1},{9,13},{13,9},{2,6},{6,2},{1... | collective-permute-start | bytes 405512 | tf_op jit(solution)/shard_map/ppermute | solution.py:367
  9.7 0.9 %copy-done = bf16[528,128]{1,0:T(8,128)(2,1)S(1)} copy-done((bf16[528,128]{1,0:T(8,128)(2,1)S(1)}, bf16[528,128]{1,0:T(8,128)(2,1)}, u32[]{:S(2)}) %copy-start) | copy-done | bytes 135192
  10.6 0.7 %copy-done.2 = f32[24,128]{1,0:T(8,128)S(1)} copy-done((f32[24,128]{1,0:T(8,128)S(1)}, f32[24,128]{1,0:T(8,128)}, u32[]{:S(2)}) %copy-start.2) | copy-done | bytes 12312
  11.4 1.6 %first_sums.1 = (f32[4096,128]{1,0:T(8,128)S(1)}, f32[4096,128]{1,0:T(8,128)S(1)}, bf16[1024,128]{1,0:T(8,128)(2,1)S(1)}, f32[8,128]{1,0:T(8,128)S(1)}, s16[512,...) custom-call(f32[24,128]{1,0:T(8,128)S(1)} %copy-done.2, bf16[1,528,128]{2,1,0:T(8,128)(2,1)S(1)} %bitcast.23), custom_call_target="tpu_custom_call" | custom-call | flops 1 | tf_op jit(solution)/shard_map/first_sums/pallas_call | solution.py:415
  13.0 0.5 %collective-permute-done = bf16[528,128]{1,0:T(8,128)(2,1)S(1)} collective-permute-done((bf16[528,128]{1,0:T(8,128)(2,1)}, bf16[528,128]{1,0:T(8,128)(2,1)S(1)}, u32[]{:S(2)}, u32[]{:S(2)}) %collective-permute-start) | collective-permute-done | bytes 135200 | tf_op jit(solution)/shard_map/ppermute | solution.py:367
  13.4 0.8 %collective-permute-start.1 = (bf16[528,128]{1,0:T(8,128)(2,1)S(1)}, bf16[528,128]{1,0:T(8,128)(2,1)S(1)}, u32[]{:S(2)}, u32[]{:S(2)}) collective-permute-start(bf16[528,128]{1,0:T(8,128)(2,1)S(1)} %collective-permute-done), channel_id=1, source_target_pairs={{0,4},{4,0},{8,12},{12,8},{1,5},{5,1},{9,13},{13,9},{2,6},{6,2},{1... | collective-permute-start | bytes 405512 | tf_op jit(solution)/shard_map/ppermute | solution.py:367
  14.2 1.4 %collective-permute-start.4 = (bf16[528,128]{1,0:T(8,128)(2,1)S(1)}, bf16[528,128]{1,0:T(8,128)(2,1)S(1)}, u32[]{:S(2)}, u32[]{:S(2)}) collective-permute-start(bf16[528,128]{1,0:T(8,128)(2,1)S(1)} %collective-permute-done), channel_id=1, source_target_pairs={{0,2},{2,0},{1,3},{3,1},{4,6},{6,4},{5,7},{7,5},{8,10},{10,8},{9,1... | collective-permute-start | bytes 405512 | tf_op jit(solution)/shard_map/ppermute | solution.py:367
  15.6 0.0 collective-permute-done.2
  15.7 0.0 collective-permute-done.3
  15.7 0.0 copy-start.3
  15.7 1.2 %more_sums.2 = (f32[4096,128]{1,0:T(8,128)S(1)}, bf16[1024,128]{1,0:T(8,128)(2,1)S(1)}, f32[8,128]{1,0:T(8,128)S(1)}) custom-call(f32[24,128]{1,0:T(8,128)S(1)} %copy-done.2, bf16[1,528,128]{2,1,0:T(8,128)(2,1)S(1)} %bitcast.15, bf16[1,528,128]{2,1,0:T(8,128)(2,1)S(1)} %bitcast.17, f32[4096,128]{1,0:T(8,128)S(1)} %get-tuple-element.24.refs_3_), custom_call_target="tpu_custom_call" | custom-call | flops 2 | tf_op jit(solution)/shard_map/more_sums/pallas_call | solution.py:415
  16.9 1.4 %collective-permute-start.5 = (bf16[528,128]{1,0:T(8,128)(2,1)S(1)}, bf16[528,128]{1,0:T(8,128)(2,1)S(1)}, u32[]{:S(2)}, u32[]{:S(2)}) collective-permute-start(bf16[528,128]{1,0:T(8,128)(2,1)S(1)} %collective-permute-done.2), channel_id=1, source_target_pairs={{0,4},{4,0},{8,12},{12,8},{1,5},{5,1},{9,13},{13,9},{2,6},{6,2},{1... | collective-permute-start | bytes 405512 | tf_op jit(solution)/shard_map/ppermute | solution.py:367
  18.3 0.1 collective-permute-done.1
  18.4 1.9 %collective-permute-start.6 = (bf16[528,128]{1,0:T(8,128)(2,1)S(1)}, bf16[528,128]{1,0:T(8,128)(2,1)S(1)}, u32[]{:S(2)}, u32[]{:S(2)}) collective-permute-start(bf16[528,128]{1,0:T(8,128)(2,1)S(1)} %collective-permute-done.1), channel_id=1, source_target_pairs={{0,2},{2,0},{1,3},{3,1},{4,6},{6,4},{5,7},{7,5},{8,10},{10,8},{9,1... | collective-permute-start | bytes 405512 | tf_op jit(solution)/shard_map/ppermute | solution.py:367
  20.4 0.0 collective-permute-done.4
  20.4 1.7 %more_sums.3 = (f32[4096,128]{1,0:T(8,128)S(1)}, bf16[1024,128]{1,0:T(8,128)(2,1)S(1)}, f32[8,128]{1,0:T(8,128)S(1)}) custom-call(f32[24,128]{1,0:T(8,128)S(1)} %copy-done.2, bf16[1,528,128]{2,1,0:T(8,128)(2,1)S(1)} %bitcast.13, bf16[1,528,128]{2,1,0:T(8,128)(2,1)S(1)} %bitcast.19, bf16[1,528,128]{2,1,0:T(8,128)(2,1)S(1)} %bitcast.21, ...), custom_call_target="tpu_custom_call" | custom-call | flops 3 | tf_op jit(solution)/shard_map/more_sums/pallas_call | solution.py:415
  22.0 0.0 collective-permute-done.5
  22.0 1.4 %collective-permute-done.6 = bf16[528,128]{1,0:T(8,128)(2,1)S(1)} collective-permute-done((bf16[528,128]{1,0:T(8,128)(2,1)S(1)}, bf16[528,128]{1,0:T(8,128)(2,1)S(1)}, u32[]{:S(2)}, u32[]{:S(2)}) %collective-permute-start.6) | collective-permute-done | bytes 135200 | tf_op jit(solution)/shard_map/ppermute | solution.py:367
  23.5 0.0 copy-done.1
  23.5 0.0 copy-done.3
  23.5 4.2 %table_and_rows.1 = (bf16[4096,128]{1,0:T(8,128)(2,1)}, bf16[512,128]{1,0:T(8,128)(2,1)}) custom-call(f32[24,128]{1,0:T(8,128)S(1)} %copy-done.3, f32[4096,128]{1,0:T(8,128)S(1)} %get-tuple-element.28.refs_1_, f32[4096,128]{1,0:T(8,128)S(1)} %get-tuple-element.29.refs_2_, s16[512,128]{1,0:T(8,128)(2,1)S(1)} %get-tuple-element.30.refs_3_, ...), custom_call_target="tpu_custom_call" | custom-call | tf_op jit(solution)/shard_map/table_and_rows/pallas_call | solution.py:454
  (3 shorter events, 0.0 us)
Async XLA Ops:
  2.6 10.8 %collective-permute-start = (bf16[528,128]{1,0:T(8,128)(2,1)}, bf16[528,128]{1,0:T(8,128)(2,1)S(1)}, u32[]{:S(2)}, u32[]{:S(2)}) collective-permute-start(bf16[528,128]{1,0:T(8,128)(2,1)} %get-tuple-element.21), channel_id=1, source_target_pairs={{0,8},{4,12},{8,0},{12,4},{1,9},{5,13},{9,1},{13,5},{2,10},{6,14},... | collective-permute-start | bytes 405512 | tf_op jit(solution)/shard_map/ppermute | solution.py:367
  6.6 9.0 %collective-permute-start.2 = (bf16[528,128]{1,0:T(8,128)(2,1)}, bf16[528,128]{1,0:T(8,128)(2,1)S(1)}, u32[]{:S(2)}, u32[]{:S(2)}) collective-permute-start(bf16[528,128]{1,0:T(8,128)(2,1)} %get-tuple-element.21), channel_id=1, source_target_pairs={{0,2},{2,0},{1,3},{3,1},{4,6},{6,4},{5,7},{7,5},{8,10},{10,8},{9,1... | collective-permute-start | bytes 405512 | tf_op jit(solution)/shard_map/ppermute | solution.py:367
  8.1 7.5 %collective-permute-start.3 = (bf16[528,128]{1,0:T(8,128)(2,1)}, bf16[528,128]{1,0:T(8,128)(2,1)S(1)}, u32[]{:S(2)}, u32[]{:S(2)}) collective-permute-start(bf16[528,128]{1,0:T(8,128)(2,1)} %get-tuple-element.21), channel_id=1, source_target_pairs={{0,4},{4,0},{8,12},{12,8},{1,5},{5,1},{9,13},{13,9},{2,6},{6,2},{1... | collective-permute-start | bytes 405512 | tf_op jit(solution)/shard_map/ppermute | solution.py:367
  9.7 0.9 %copy-start = (bf16[528,128]{1,0:T(8,128)(2,1)S(1)}, bf16[528,128]{1,0:T(8,128)(2,1)}, u32[]{:S(2)}) copy-start(bf16[528,128]{1,0:T(8,128)(2,1)} %get-tuple-element.21) | copy-start | bytes 405508
  10.6 0.7 %copy-start.2 = (f32[24,128]{1,0:T(8,128)S(1)}, f32[24,128]{1,0:T(8,128)}, u32[]{:S(2)}) copy-start(f32[24,128]{1,0:T(8,128)} %get-tuple-element.20.refs_0_) | copy-start | bytes 36868
  13.4 5.0 %collective-permute-start.1 = (bf16[528,128]{1,0:T(8,128)(2,1)S(1)}, bf16[528,128]{1,0:T(8,128)(2,1)S(1)}, u32[]{:S(2)}, u32[]{:S(2)}) collective-permute-start(bf16[528,128]{1,0:T(8,128)(2,1)S(1)} %collective-permute-done), channel_id=1, source_target_pairs={{0,4},{4,0},{8,12},{12,8},{1,5},{5,1},{9,13},{13,9},{2,6},{6,2},{1... | collective-permute-start | bytes 405512 | tf_op jit(solution)/shard_map/ppermute | solution.py:367
  14.2 6.2 %collective-permute-start.4 = (bf16[528,128]{1,0:T(8,128)(2,1)S(1)}, bf16[528,128]{1,0:T(8,128)(2,1)S(1)}, u32[]{:S(2)}, u32[]{:S(2)}) collective-permute-start(bf16[528,128]{1,0:T(8,128)(2,1)S(1)} %collective-permute-done), channel_id=1, source_target_pairs={{0,2},{2,0},{1,3},{3,1},{4,6},{6,4},{5,7},{7,5},{8,10},{10,8},{9,1... | collective-permute-start | bytes 405512 | tf_op jit(solution)/shard_map/ppermute | solution.py:367
  15.7 7.8 %copy-start.1 = (bf16[528,128]{1,0:T(8,128)(2,1)S(1)}, bf16[528,128]{1,0:T(8,128)(2,1)}, u32[]{:S(2)}) copy-start(bf16[528,128]{1,0:T(8,128)(2,1)} %get-tuple-element.21) | copy-start | bytes 405508
  15.7 7.8 %copy-start.3 = (f32[24,128]{1,0:T(8,128)S(1)}, f32[24,128]{1,0:T(8,128)}, u32[]{:S(2)}) copy-start(f32[24,128]{1,0:T(8,128)} %get-tuple-element.20.refs_0_) | copy-start | bytes 36868
  16.9 5.1 %collective-permute-start.5 = (bf16[528,128]{1,0:T(8,128)(2,1)S(1)}, bf16[528,128]{1,0:T(8,128)(2,1)S(1)}, u32[]{:S(2)}, u32[]{:S(2)}) collective-permute-start(bf16[528,128]{1,0:T(8,128)(2,1)S(1)} %collective-permute-done.2), channel_id=1, source_target_pairs={{0,4},{4,0},{8,12},{12,8},{1,5},{5,1},{9,13},{13,9},{2,6},{6,2},{1... | collective-permute-start | bytes 405512 | tf_op jit(solution)/shard_map/ppermute | solution.py:367
  18.4 5.0 %collective-permute-start.6 = (bf16[528,128]{1,0:T(8,128)(2,1)S(1)}, bf16[528,128]{1,0:T(8,128)(2,1)S(1)}, u32[]{:S(2)}, u32[]{:S(2)}) collective-permute-start(bf16[528,128]{1,0:T(8,128)(2,1)S(1)} %collective-permute-done.1), channel_id=1, source_target_pairs={{0,2},{2,0},{1,3},{3,1},{4,6},{6,4},{5,7},{7,5},{8,10},{10,8},{9,1... | collective-permute-start | bytes 405512 | tf_op jit(solution)/shard_map/ppermute | solution.py:367

commit v12 on v10

--- a/solution.py
+++ b/solution.py
@@ -55,7 +55,7 @@
     return lax.fori_loop(0, count, body, carry)
 
 
-def send_kernel(z, me_ref, rate_ref, events_ref, weight_ref, route_ref, bucket_ref, segment_ref, out_ref, own_ref, block_ref, sems):
+def send_kernel(z, me_ref, rate_ref, events_ref, weight_ref, route_ref, bucket_ref, segment_ref, block_ref, own_ref):
     groups = rate_ref.shape[0]
     lane = iota((1, LANES), 1)
     rate = jnp.full((1, LANES), rate_ref[0], F32)
@@ -69,20 +69,11 @@
     own_ref[0:16, :] = jnp.concatenate([place, first, rate, me], axis=0)
     spot = place - first - F32(z.span * z.slots // 2)
     columns = jnp.concatenate([weight_ref[...], spot], axis=0).T
-    copies = []
-
-    def send(first, count):
-        part = pl.ds(first, count)
-        copies.append(pltpu.make_async_copy(block_ref.at[part, :], out_ref.at[part, :], sems.at[len(copies)]))
-        copies[-1].start()
-
     for r in range(z.chunks):
         part = slice(r * LANES, (r + 1) * LANES)
         weighted = (columns[:, r : r + 1] * events_ref[part, :].astype(F32)).astype(BF16)
         grown = weighted.astype(F32) * jnp.exp(columns[:, z.chunks + r : z.chunks + r + 1] * rate)
         block_ref[part, :] = grown.astype(BF16)
-        if (r + 1) % (z.chunks // 2) == 0:
-            send((r + 1) * LANES - z.rows // 2, z.rows // 2)
     ones = jnp.ones((8, LANES), BF16)
     high, low = [], []
     users = min(LANES, 8 * z.owners)
@@ -102,9 +93,6 @@
     pad = [jnp.zeros((spare, LANES), I32)] if spare else []
     codes = jnp.concatenate([route, bucket >> LOW, bucket & MASK] + high + low + pad, axis=0)
     block_ref[z.rows : z.rows + z.code_rows, :] = codes.astype(F32).astype(BF16)
-    send(z.rows, z.code_rows)
-    for copy in copies:
-        copy.wait()
 
 
 class Pieces:
@@ -323,6 +311,8 @@
         copies.append(pltpu.make_async_copy(ref.at[part, :], out.at[part, :], sems.at[len(copies)]))
         copies[-1].start()
 
+    pack(z, last, base, marks_ref, codes_ref, rows_ref, from_ref)
+
     place = own_ref[0 : z.chunks, :]
     start = jnp.concatenate([runs.start_row(place[r : r + 1]) for r in range(z.chunks)], axis=0)
     scale = wide_columns(root(z, place - start))
@@ -344,7 +334,6 @@
     feature_ref[...] = (total * scale).astype(BF16)
     send(feature_ref, feature_out, slice(0, z.rows))
 
-    pack(z, last, base, marks_ref, codes_ref, rows_ref, from_ref)
     own_anchor, tail_anchor = anchors(z, me)
     inner = iota((LATE_BLOCK, LANES), 0)
     fall = jnp.exp(-rate * inner.astype(F32))
@@ -416,8 +405,7 @@
             shape((16 + z.user_rows + 7, LANES), F32),
         ),
         in_specs=[smem, smem] + [vmem] * 5,
-        out_specs=(pl.BlockSpec(memory_space=pl.ANY), vmem),
-        scratch_shapes=[pltpu.VMEM((block_rows, width), BF16), pltpu.SemaphoreType.DMA((3,))],
+        out_specs=(vmem, vmem),
         compiler_params=pltpu.CompilerParams(vmem_limit_bytes=56 * 1024 * 1024),
         name="weigh",
     )(
@@ -463,9 +451,10 @@
         last, total = tie((last, total))
         side_last = swap(last, "shard", 1)
         second = [(far,), (last,), (side_far,)]
-        late = [(side_near,), (side_last,)]
         total, *tail3 = sums(second, (total,))
-        early, earlier, tails = [(block,), (side,), (near,)] + second, (1, 2, 3), tail + tail2 + tail3
+        total, *tail4 = sums([(side_near,)], (total,))
+        early = [(block,), (side,), (near,)] + second + [(side_near,)]
+        earlier, tails, late = (1, 2, 3, 1), tail + tail2 + tail3 + tail4, [(side_last,)]
     else:
         blocks = spread(spread([block], "key"), "shard")
         total, scale, _, _, tops, factors = sums([])

time: 28.4 us -> 28.3 us (level)
  starting transfers between devices: 12.7 us -> 11.7 us
  local copies, waits for them, and re-layouts: 1.66 us -> 2.35 us
  Pallas kernels: 11 us -> 11.3 us
    ppermute x7, starting transfers between devices: 12.7 us -> 11.7 us  [swap(): lax.ppermute(block, axis, [(i, i ^ distance) for i in range(lax.axis_size...]
    pallas_call x3 -> x4, Pallas kernels: 4.47 us -> 5.42 us  [sums(): pl.pallas_call(functools.partial(early_kernel, z, form, len(before)), out...]
    unnamed x8, local copies, waits for them, and re-layouts: 1.66 us -> 2.35 us
    pallas_call x1, Pallas kernels: 2.54 us -> 1.96 us  [on_device(): pl.pallas_call(functools.partial(send_kernel, z), out_shape=(shape((block...]
  transfers between devices with their start and end apart: 7 -> 7, of which waited for: 3 -> 3; matrix products, arithmetic and copies ran while one was open for 0% -> 0% of each run, Pallas kernels for 16% -> 19%
where the time goes in v12:
time: 28.3 us; the launch traced here: 28 us
  starting transfers between devices  11.7 us (41%)
  Pallas kernels  11.3 us (40%)
  local copies, waits for them, and re-layouts  2.35 us (8%)
  waiting for transfers between devices  1.89 us (7%)
  between operations  0.68 us (2%)
    ppermute x7, starting transfers between devices, swap(): lax.ppermute(block, axis, [(i, i ^ distance) for i in range(lax.axis_size...  11.7 us
    pallas_call x4, Pallas kernels, sums(): pl.pallas_call(functools.partial(early_kernel, z, form, len(before)), out...  5.42 us
    pallas_call x1, Pallas kernels, on_device(): pl.pallas_call(functools.partial(late_kernel, z, earlier, form, len(late)...  3.95 us
    unnamed x8, local copies, waits for them, and re-layouts  2.35 us
    pallas_call x1, Pallas kernels, on_device(): pl.pallas_call(functools.partial(send_kernel, z), out_shape=(shape((block...  1.96 us
    ppermute x7, waiting for transfers between devices, swap(): lax.ppermute(block, axis, [(i, i ^ distance) for i in range(lax.axis_size...  1.89 us
  transfers between devices with their start and end apart: 7, of which 3 were waited for; matrix products, arithmetic and copies ran while one was open for 0% of the time, Pallas kernels for 19%

profile of v12, /device:TPU:0, one launch (start us, length us, event | category | flops | bytes accessed | tf_op | source)
XLA Modules:
  0.0 28.0 jit_solution(13893604864026553308)
XLA Ops:
  0.6 2.0 %weigh.1 = (bf16[528,128]{1,0:T(8,128)(2,1)}, f32[24,128]{1,0:T(8,128)}) custom-call(s32[1]{0:T(128)} %bitcast.me_ref, f32[4]{0:T(128)} %rate_ref.1, bf16[512,128]{1,0:T(8,128)(2,1)} %events_ref.1, f32[4,128]{1,0:T(4,128)} %bitcast.29, s32[4,128]{1,0:T(4,128)} %bitcast.30, s32[4,128]{1,0:T(4,128)} %bitcast.31, s32[32,128]{1,0:T(8,128)} %bitcast.28), custom_call_target="tpu_custom_call" | custom-call | tf_op jit(solution)/shard_map/weigh/pallas_call | solution.py:401
  2.6 4.0 %collective-permute-start.2 = (bf16[528,128]{1,0:T(8,128)(2,1)}, bf16[528,128]{1,0:T(8,128)(2,1)S(1)}, u32[]{:S(2)}, u32[]{:S(2)}) collective-permute-start(bf16[528,128]{1,0:T(8,128)(2,1)} %get-tuple-element.24), channel_id=1, source_target_pairs={{0,8},{4,12},{8,0},{12,4},{1,9},{5,13},{9,1},{13,5},{2,10},{6,14},... | collective-permute-start | bytes 405512 | tf_op jit(solution)/shard_map/ppermute | solution.py:378
  6.6 1.5 %collective-permute-start = (bf16[528,128]{1,0:T(8,128)(2,1)}, bf16[528,128]{1,0:T(8,128)(2,1)S(1)}, u32[]{:S(2)}, u32[]{:S(2)}) collective-permute-start(bf16[528,128]{1,0:T(8,128)(2,1)} %get-tuple-element.24), channel_id=1, source_target_pairs={{0,2},{2,0},{1,3},{3,1},{4,6},{6,4},{5,7},{7,5},{8,10},{10,8},{9,1... | collective-permute-start | bytes 405512 | tf_op jit(solution)/shard_map/ppermute | solution.py:378
  8.1 1.6 %collective-permute-start.4 = (bf16[528,128]{1,0:T(8,128)(2,1)}, bf16[528,128]{1,0:T(8,128)(2,1)S(1)}, u32[]{:S(2)}, u32[]{:S(2)}) collective-permute-start(bf16[528,128]{1,0:T(8,128)(2,1)} %get-tuple-element.24), channel_id=1, source_target_pairs={{0,4},{4,0},{8,12},{12,8},{1,5},{5,1},{9,13},{13,9},{2,6},{6,2},{1... | collective-permute-start | bytes 405512 | tf_op jit(solution)/shard_map/ppermute | solution.py:378
  9.7 0.9 %copy-done = bf16[528,128]{1,0:T(8,128)(2,1)S(1)} copy-done((bf16[528,128]{1,0:T(8,128)(2,1)S(1)}, bf16[528,128]{1,0:T(8,128)(2,1)}, u32[]{:S(2)}) %copy-start) | copy-done | bytes 135192
  10.6 0.7 %copy-done.2 = f32[24,128]{1,0:T(8,128)S(1)} copy-done((f32[24,128]{1,0:T(8,128)S(1)}, f32[24,128]{1,0:T(8,128)}, u32[]{:S(2)}) %copy-start.2) | copy-done | bytes 12312
  11.4 1.6 %first_sums.1 = (f32[4096,128]{1,0:T(8,128)S(1)}, f32[4096,128]{1,0:T(8,128)S(1)}, bf16[1024,128]{1,0:T(8,128)(2,1)S(1)}, f32[8,128]{1,0:T(8,128)S(1)}, s16[512,...) custom-call(f32[24,128]{1,0:T(8,128)S(1)} %copy-done.2, bf16[1,528,128]{2,1,0:T(8,128)(2,1)S(1)} %bitcast.25), custom_call_target="tpu_custom_call" | custom-call | flops 1 | tf_op jit(solution)/shard_map/first_sums/pallas_call | solution.py:426
  13.0 0.5 %collective-permute-done.2 = bf16[528,128]{1,0:T(8,128)(2,1)S(1)} collective-permute-done((bf16[528,128]{1,0:T(8,128)(2,1)}, bf16[528,128]{1,0:T(8,128)(2,1)S(1)}, u32[]{:S(2)}, u32[]{:S(2)}) %collective-permute-start.2) | collective-permute-done | bytes 135200 | tf_op jit(solution)/shard_map/ppermute | solution.py:378
  13.4 0.8 %collective-permute-start.3 = (bf16[528,128]{1,0:T(8,128)(2,1)S(1)}, bf16[528,128]{1,0:T(8,128)(2,1)S(1)}, u32[]{:S(2)}, u32[]{:S(2)}) collective-permute-start(bf16[528,128]{1,0:T(8,128)(2,1)S(1)} %collective-permute-done.2), channel_id=1, source_target_pairs={{0,4},{4,0},{8,12},{12,8},{1,5},{5,1},{9,13},{13,9},{2,6},{6,2},{1... | collective-permute-start | bytes 405512 | tf_op jit(solution)/shard_map/ppermute | solution.py:378
  14.2 1.4 %collective-permute-start.5 = (bf16[528,128]{1,0:T(8,128)(2,1)S(1)}, bf16[528,128]{1,0:T(8,128)(2,1)S(1)}, u32[]{:S(2)}, u32[]{:S(2)}) collective-permute-start(bf16[528,128]{1,0:T(8,128)(2,1)S(1)} %collective-permute-done.2), channel_id=1, source_target_pairs={{0,2},{2,0},{1,3},{3,1},{4,6},{6,4},{5,7},{7,5},{8,10},{10,8},{9,1... | collective-permute-start | bytes 405512 | tf_op jit(solution)/shard_map/ppermute | solution.py:378
  15.6 0.0 collective-permute-done
  15.7 0.0 collective-permute-done.4
  15.7 0.7 %copy-done.3 = f32[24,128]{1,0:T(8,128)S(1)} copy-done((f32[24,128]{1,0:T(8,128)S(1)}, f32[24,128]{1,0:T(8,128)}, u32[]{:S(2)}) %copy-start.3) | copy-done | bytes 12312
  16.4 1.2 %more_sums.3 = (f32[4096,128]{1,0:T(8,128)S(1)}, bf16[1024,128]{1,0:T(8,128)(2,1)S(1)}, f32[8,128]{1,0:T(8,128)S(1)}) custom-call(f32[24,128]{1,0:T(8,128)S(1)} %copy-done.3, bf16[1,528,128]{2,1,0:T(8,128)(2,1)S(1)} %bitcast.15, bf16[1,528,128]{2,1,0:T(8,128)(2,1)S(1)} %bitcast.17, f32[4096,128]{1,0:T(8,128)S(1)} %get-tuple-element.27.refs_3_), custom_call_target="tpu_custom_call" | custom-call | flops 2 | tf_op jit(solution)/shard_map/more_sums/pallas_call | solution.py:426
  17.6 1.4 %collective-permute-start.1 = (bf16[528,128]{1,0:T(8,128)(2,1)S(1)}, bf16[528,128]{1,0:T(8,128)(2,1)S(1)}, u32[]{:S(2)}, u32[]{:S(2)}) collective-permute-start(bf16[528,128]{1,0:T(8,128)(2,1)S(1)} %collective-permute-done), channel_id=1, source_target_pairs={{0,4},{4,0},{8,12},{12,8},{1,5},{5,1},{9,13},{13,9},{2,6},{6,2},{1... | collective-permute-start | bytes 405512 | tf_op jit(solution)/shard_map/ppermute | solution.py:378
  19.0 0.0 collective-permute-done.3
  19.0 1.0 %collective-permute-start.6 = (bf16[528,128]{1,0:T(8,128)(2,1)S(1)}, bf16[528,128]{1,0:T(8,128)(2,1)S(1)}, u32[]{:S(2)}, u32[]{:S(2)}) collective-permute-start(bf16[528,128]{1,0:T(8,128)(2,1)S(1)} %collective-permute-done.3), channel_id=1, source_target_pairs={{0,2},{2,0},{1,3},{3,1},{4,6},{6,4},{5,7},{7,5},{8,10},{10,8},{9,1... | collective-permute-start | bytes 405512 | tf_op jit(solution)/shard_map/ppermute | solution.py:378
  20.0 0.0 collective-permute-done.5
  20.0 1.7 %more_sums.4 = (f32[4096,128]{1,0:T(8,128)S(1)}, bf16[1024,128]{1,0:T(8,128)(2,1)S(1)}, f32[8,128]{1,0:T(8,128)S(1)}) custom-call(f32[24,128]{1,0:T(8,128)S(1)} %copy-done.3, bf16[1,528,128]{2,1,0:T(8,128)(2,1)S(1)} %bitcast.13, bf16[1,528,128]{2,1,0:T(8,128)(2,1)S(1)} %bitcast.19, bf16[1,528,128]{2,1,0:T(8,128)(2,1)S(1)} %bitcast.21, ...), custom_call_target="tpu_custom_call" | custom-call | flops 3 | tf_op jit(solution)/shard_map/more_sums/pallas_call | solution.py:426
  21.6 1.0 %collective-permute-done.1 = bf16[528,128]{1,0:T(8,128)(2,1)S(1)} collective-permute-done((bf16[528,128]{1,0:T(8,128)(2,1)S(1)}, bf16[528,128]{1,0:T(8,128)(2,1)S(1)}, u32[]{:S(2)}, u32[]{:S(2)}) %collective-permute-start.1) | collective-permute-done | bytes 135200 | tf_op jit(solution)/shard_map/ppermute | solution.py:378
  22.7 1.0 %more_sums.5 = (f32[4096,128]{1,0:T(8,128)S(1)}, bf16[1024,128]{1,0:T(8,128)(2,1)S(1)}, f32[8,128]{1,0:T(8,128)S(1)}) custom-call(f32[24,128]{1,0:T(8,128)S(1)} %copy-done.3, bf16[1,528,128]{2,1,0:T(8,128)(2,1)S(1)} %bitcast.23, f32[4096,128]{1,0:T(8,128)S(1)} %get-tuple-element.31.refs_2_), custom_call_target="tpu_custom_call" | custom-call | flops 1 | tf_op jit(solution)/shard_map/more_sums/pallas_call | solution.py:426
  23.6 0.4 %collective-permute-done.6 = bf16[528,128]{1,0:T(8,128)(2,1)S(1)} collective-permute-done((bf16[528,128]{1,0:T(8,128)(2,1)S(1)}, bf16[528,128]{1,0:T(8,128)(2,1)S(1)}, u32[]{:S(2)}, u32[]{:S(2)}) %collective-permute-start.6) | collective-permute-done | bytes 135200 | tf_op jit(solution)/shard_map/ppermute | solution.py:378
  24.0 0.0 copy-done.1
  24.0 4.0 %table_and_rows.1 = (bf16[4096,128]{1,0:T(8,128)(2,1)}, bf16[512,128]{1,0:T(8,128)(2,1)}) custom-call(f32[24,128]{1,0:T(8,128)S(1)} %copy-done.3, f32[4096,128]{1,0:T(8,128)S(1)} %get-tuple-element.32.refs_1_, f32[4096,128]{1,0:T(8,128)S(1)} %get-tuple-element.33.refs_2_, s16[512,128]{1,0:T(8,128)(2,1)S(1)} %get-tuple-element.34.refs_3_, ...), custom_call_target="tpu_custom_call" | custom-call | tf_op jit(solution)/shard_map/table_and_rows/pallas_call | solution.py:466
  (4 shorter events, 0.0 us)
Async XLA Ops:
  2.6 10.8 %collective-permute-start.2 = (bf16[528,128]{1,0:T(8,128)(2,1)}, bf16[528,128]{1,0:T(8,128)(2,1)S(1)}, u32[]{:S(2)}, u32[]{:S(2)}) collective-permute-start(bf16[528,128]{1,0:T(8,128)(2,1)} %get-tuple-element.24), channel_id=1, source_target_pairs={{0,8},{4,12},{8,0},{12,4},{1,9},{5,13},{9,1},{13,5},{2,10},{6,14},... | collective-permute-start | bytes 405512 | tf_op jit(solution)/shard_map/ppermute | solution.py:378
  6.6 9.0 %collective-permute-start = (bf16[528,128]{1,0:T(8,128)(2,1)}, bf16[528,128]{1,0:T(8,128)(2,1)S(1)}, u32[]{:S(2)}, u32[]{:S(2)}) collective-permute-start(bf16[528,128]{1,0:T(8,128)(2,1)} %get-tuple-element.24), channel_id=1, source_target_pairs={{0,2},{2,0},{1,3},{3,1},{4,6},{6,4},{5,7},{7,5},{8,10},{10,8},{9,1... | collective-permute-start | bytes 405512 | tf_op jit(solution)/shard_map/ppermute | solution.py:378
  8.1 7.5 %collective-permute-start.4 = (bf16[528,128]{1,0:T(8,128)(2,1)}, bf16[528,128]{1,0:T(8,128)(2,1)S(1)}, u32[]{:S(2)}, u32[]{:S(2)}) collective-permute-start(bf16[528,128]{1,0:T(8,128)(2,1)} %get-tuple-element.24), channel_id=1, source_target_pairs={{0,4},{4,0},{8,12},{12,8},{1,5},{5,1},{9,13},{13,9},{2,6},{6,2},{1... | collective-permute-start | bytes 405512 | tf_op jit(solution)/shard_map/ppermute | solution.py:378
  9.7 0.9 %copy-start = (bf16[528,128]{1,0:T(8,128)(2,1)S(1)}, bf16[528,128]{1,0:T(8,128)(2,1)}, u32[]{:S(2)}) copy-start(bf16[528,128]{1,0:T(8,128)(2,1)} %get-tuple-element.24) | copy-start | bytes 405508
  10.6 0.7 %copy-start.2 = (f32[24,128]{1,0:T(8,128)S(1)}, f32[24,128]{1,0:T(8,128)}, u32[]{:S(2)}) copy-start(f32[24,128]{1,0:T(8,128)} %get-tuple-element.23.refs_0_) | copy-start | bytes 36868
  13.4 5.6 %collective-permute-start.3 = (bf16[528,128]{1,0:T(8,128)(2,1)S(1)}, bf16[528,128]{1,0:T(8,128)(2,1)S(1)}, u32[]{:S(2)}, u32[]{:S(2)}) collective-permute-start(bf16[528,128]{1,0:T(8,128)(2,1)S(1)} %collective-permute-done.2), channel_id=1, source_target_pairs={{0,4},{4,0},{8,12},{12,8},{1,5},{5,1},{9,13},{13,9},{2,6},{6,2},{1... | collective-permute-start | bytes 405512 | tf_op jit(solution)/shard_map/ppermute | solution.py:378
  14.2 5.8 %collective-permute-start.5 = (bf16[528,128]{1,0:T(8,128)(2,1)S(1)}, bf16[528,128]{1,0:T(8,128)(2,1)S(1)}, u32[]{:S(2)}, u32[]{:S(2)}) collective-permute-start(bf16[528,128]{1,0:T(8,128)(2,1)S(1)} %collective-permute-done.2), channel_id=1, source_target_pairs={{0,2},{2,0},{1,3},{3,1},{4,6},{6,4},{5,7},{7,5},{8,10},{10,8},{9,1... | collective-permute-start | bytes 405512 | tf_op jit(solution)/shard_map/ppermute | solution.py:378
  15.7 0.7 %copy-start.3 = (f32[24,128]{1,0:T(8,128)S(1)}, f32[24,128]{1,0:T(8,128)}, u32[]{:S(2)}) copy-start(f32[24,128]{1,0:T(8,128)} %get-tuple-element.23.refs_0_) | copy-start | bytes 36868
  17.6 5.1 %collective-permute-start.1 = (bf16[528,128]{1,0:T(8,128)(2,1)S(1)}, bf16[528,128]{1,0:T(8,128)(2,1)S(1)}, u32[]{:S(2)}, u32[]{:S(2)}) collective-permute-start(bf16[528,128]{1,0:T(8,128)(2,1)S(1)} %collective-permute-done), channel_id=1, source_target_pairs={{0,4},{4,0},{8,12},{12,8},{1,5},{5,1},{9,13},{13,9},{2,6},{6,2},{1... | collective-permute-start | bytes 405512 | tf_op jit(solution)/shard_map/ppermute | solution.py:378
  19.0 5.0 %collective-permute-start.6 = (bf16[528,128]{1,0:T(8,128)(2,1)S(1)}, bf16[528,128]{1,0:T(8,128)(2,1)S(1)}, u32[]{:S(2)}, u32[]{:S(2)}) collective-permute-start(bf16[528,128]{1,0:T(8,128)(2,1)S(1)} %collective-permute-done.3), channel_id=1, source_target_pairs={{0,2},{2,0},{1,3},{3,1},{4,6},{6,4},{5,7},{7,5},{8,10},{10,8},{9,1... | collective-permute-start | bytes 405512 | tf_op jit(solution)/shard_map/ppermute | solution.py:378
  20.0 4.0 %copy-start.1 = (bf16[528,128]{1,0:T(8,128)(2,1)S(1)}, bf16[528,128]{1,0:T(8,128)(2,1)}, u32[]{:S(2)}) copy-start(bf16[528,128]{1,0:T(8,128)(2,1)} %get-tuple-element.24) | copy-start | bytes 405508

commit v13 on v12

--- a/solution.py
+++ b/solution.py
@@ -311,8 +311,6 @@
         copies.append(pltpu.make_async_copy(ref.at[part, :], out.at[part, :], sems.at[len(copies)]))
         copies[-1].start()
 
-    pack(z, last, base, marks_ref, codes_ref, rows_ref, from_ref)
-
     place = own_ref[0 : z.chunks, :]
     start = jnp.concatenate([runs.start_row(place[r : r + 1]) for r in range(z.chunks)], axis=0)
     scale = wide_columns(root(z, place - start))
@@ -334,6 +332,7 @@
     feature_ref[...] = (total * scale).astype(BF16)
     send(feature_ref, feature_out, slice(0, z.rows))
 
+    pack(z, last, base, marks_ref, codes_ref, rows_ref, from_ref)
     own_anchor, tail_anchor = anchors(z, me)
     inner = iota((LATE_BLOCK, LANES), 0)
     fall = jnp.exp(-rate * inner.astype(F32))
@@ -349,27 +348,36 @@
     tail_rows = [rows_ref[n * LANES : 2 * n * LANES, :]]
     tail_rows += [ref[count * LANES : 2 * count * LANES, :] for (ref, _), count in zip(tails, earlier)]
     tail_rows = jnp.concatenate(tail_rows, axis=0)
-    for b in range(z.slots // LATE_BLOCK):
+    steps = z.window // LATE_BLOCK
+    for b in range(steps):
         part = slice(b * LATE_BLOCK, (b + 1) * LATE_BLOCK)
         position = (inner + b * LATE_BLOCK).astype(I16)
         first = F32(b * LATE_BLOCK)
         value = sums_ref[part, :]
-        if b * LATE_BLOCK >= z.window:
-            value = (value + dot(held(position, bounds[:n]), own_rows)) * scale_ref[part, :]
+        own_fall = jnp.exp(-rate * (first + own_anchor))
+        if z.shifts == 1:
+            value += dot(held(position, bounds), jnp.concatenate([own_rows, tail_rows], axis=0))
+            value *= own_fall
         else:
-            own_fall = jnp.exp(-rate * (first + own_anchor))
-            if z.shifts == 1:
-                value += dot(held(position, bounds), jnp.concatenate([own_rows, tail_rows], axis=0))
-                value *= own_fall
-            else:
-                value = (value + dot(held(position, bounds[:n]), own_rows)) * own_fall
-                value += dot(held(position, bounds[n:]), tail_rows) * jnp.exp(-rate * (first + tail_anchor))
-            start = scale_ref[part, :]
-            start = jnp.where(start > 0, start, first_start)
-            value = value * fall * root(z, inner.astype(F32) + first - start)
+            value = (value + dot(held(position, bounds[:n]), own_rows)) * own_fall
+            value += dot(held(position, bounds[n:]), tail_rows) * jnp.exp(-rate * (first + tail_anchor))
+        start = scale_ref[part, :]
+        start = jnp.where(start > 0, start, first_start)
+        value = value * fall * root(z, inner.astype(F32) + first - start)
         table_ref[part, :] = value.astype(BF16)
-        if (b + 1) * LATE_BLOCK % z.window == 0:
-            send(table_ref, table_out, slice((b + 1) * LATE_BLOCK - z.window, (b + 1) * LATE_BLOCK))
+    send(table_ref, table_out, slice(0, z.window))
+
+    def window(w, carry):
+        for k in range(steps):
+            first = w * z.window + k * LATE_BLOCK
+            part = pl.ds(pl.multiple_of(first, LATE_BLOCK), LATE_BLOCK)
+            position = (inner + first).astype(I16)
+            value = sums_ref[part, :] + dot(held(position, bounds[:n]), own_rows)
+            table_ref[part, :] = (value * scale_ref[part, :]).astype(BF16)
+        return carry
+
+    lax.fori_loop(1, z.slots // z.window, window, 0)
+    send(table_ref, table_out, slice(z.window, z.slots))
     for copy in copies:
         copy.wait()
 
@@ -451,10 +459,9 @@
         last, total = tie((last, total))
         side_last = swap(last, "shard", 1)
         second = [(far,), (last,), (side_far,)]
+        late = [(side_near,), (side_last,)]
         total, *tail3 = sums(second, (total,))
-        total, *tail4 = sums([(side_near,)], (total,))
-        early = [(block,), (side,), (near,)] + second + [(side_near,)]
-        earlier, tails, late = (1, 2, 3, 1), tail + tail2 + tail3 + tail4, [(side_last,)]
+        early, earlier, tails = [(block,), (side,), (near,)] + second, (1, 2, 3), tail + tail2 + tail3
     else:
         blocks = spread(spread([block], "key"), "shard")
         total, scale, _, _, tops, factors = sums([])
@@ -475,7 +482,7 @@
             pltpu.VMEM((late_count, 2 * z.chunks, LANES), F32),
             pltpu.VMEM((slots, width), BF16),
             pltpu.VMEM((rows, width), BF16),
-            pltpu.SemaphoreType.DMA((1 + slots // z.window,)),
+            pltpu.SemaphoreType.DMA((3,)),
         ],
         compiler_params=grant,
         name="table_and_rows",

time: 28.3 us -> 28.5 us (level)
  starting transfers between devices: 11.7 us -> 12.7 us
  local copies, waits for them, and re-layouts: 2.35 us -> 1.66 us
    pallas_call x4 -> x3, Pallas kernels: 5.42 us -> 4.47 us  [sums(): pl.pallas_call(functools.partial(early_kernel, z, form, len(before)), out...]
    ppermute x7, starting transfers between devices: 11.7 us -> 12.7 us  [swap(): lax.ppermute(block, axis, [(i, i ^ distance) for i in range(lax.axis_size...]
    pallas_call x1, Pallas kernels: 3.95 us -> 4.76 us  [on_device(): pl.pallas_call(functools.partial(late_kernel, z, earlier, form, len(late)...]
    unnamed x8, local copies, waits for them, and re-layouts: 2.35 us -> 1.66 us
  transfers between devices with their start and end apart: 7 -> 7, of which waited for: 3 -> 3; matrix products, arithmetic and copies ran while one was open for 0% -> 0% of each run, Pallas kernels for 19% -> 16%
where the time goes in v13:
time: 28.5 us; the launch traced here: 28.2 us
  starting transfers between devices  12.7 us (45%)
  Pallas kernels  11.2 us (39%)
  waiting for transfers between devices  2.03 us (7%)
  local copies, waits for them, and re-layouts  1.66 us (6%)
  between operations  0.69 us (2%)
    ppermute x7, starting transfers between devices, swap(): lax.ppermute(block, axis, [(i, i ^ distance) for i in range(lax.axis_size...  12.7 us
    pallas_call x1, Pallas kernels, on_device(): pl.pallas_call(functools.partial(late_kernel, z, earlier, form, len(late)...  4.76 us
    pallas_call x3, Pallas kernels, sums(): pl.pallas_call(functools.partial(early_kernel, z, form, len(before)), out...  4.47 us
    ppermute x7, waiting for transfers between devices, swap(): lax.ppermute(block, axis, [(i, i ^ distance) for i in range(lax.axis_size...  2.03 us
    pallas_call x1, Pallas kernels, on_device(): pl.pallas_call(functools.partial(send_kernel, z), out_shape=(shape((block...  1.96 us
    unnamed x8, local copies, waits for them, and re-layouts  1.66 us
  transfers between devices with their start and end apart: 7, of which 3 were waited for; matrix products, arithmetic and copies ran while one was open for 0% of the time, Pallas kernels for 16%

profile of v13, /device:TPU:0, one launch (start us, length us, event | category | flops | bytes accessed | tf_op | source)
XLA Modules:
  0.0 28.2 jit_solution(14089555049417665169)
XLA Ops:
  0.6 2.0 %weigh.1 = (bf16[528,128]{1,0:T(8,128)(2,1)}, f32[24,128]{1,0:T(8,128)}) custom-call(s32[1]{0:T(128)} %bitcast.me_ref, f32[4]{0:T(128)} %rate_ref.1, bf16[512,128]{1,0:T(8,128)(2,1)} %events_ref.1, f32[4,128]{1,0:T(4,128)} %bitcast.28, s32[4,128]{1,0:T(4,128)} %bitcast.29, s32[4,128]{1,0:T(4,128)} %bitcast.30, s32[32,128]{1,0:T(8,128)} %bitcast.27), custom_call_target="tpu_custom_call" | custom-call | tf_op jit(solution)/shard_map/weigh/pallas_call | solution.py:409
  2.6 4.0 %collective-permute-start = (bf16[528,128]{1,0:T(8,128)(2,1)}, bf16[528,128]{1,0:T(8,128)(2,1)S(1)}, u32[]{:S(2)}, u32[]{:S(2)}) collective-permute-start(bf16[528,128]{1,0:T(8,128)(2,1)} %get-tuple-element.21), channel_id=1, source_target_pairs={{0,8},{4,12},{8,0},{12,4},{1,9},{5,13},{9,1},{13,5},{2,10},{6,14},... | collective-permute-start | bytes 405512 | tf_op jit(solution)/shard_map/ppermute | solution.py:386
  6.6 1.5 %collective-permute-start.2 = (bf16[528,128]{1,0:T(8,128)(2,1)}, bf16[528,128]{1,0:T(8,128)(2,1)S(1)}, u32[]{:S(2)}, u32[]{:S(2)}) collective-permute-start(bf16[528,128]{1,0:T(8,128)(2,1)} %get-tuple-element.21), channel_id=1, source_target_pairs={{0,2},{2,0},{1,3},{3,1},{4,6},{6,4},{5,7},{7,5},{8,10},{10,8},{9,1... | collective-permute-start | bytes 405512 | tf_op jit(solution)/shard_map/ppermute | solution.py:386
  8.1 1.6 %collective-permute-start.3 = (bf16[528,128]{1,0:T(8,128)(2,1)}, bf16[528,128]{1,0:T(8,128)(2,1)S(1)}, u32[]{:S(2)}, u32[]{:S(2)}) collective-permute-start(bf16[528,128]{1,0:T(8,128)(2,1)} %get-tuple-element.21), channel_id=1, source_target_pairs={{0,4},{4,0},{8,12},{12,8},{1,5},{5,1},{9,13},{13,9},{2,6},{6,2},{1... | collective-permute-start | bytes 405512 | tf_op jit(solution)/shard_map/ppermute | solution.py:386
  9.7 0.9 %copy-done = bf16[528,128]{1,0:T(8,128)(2,1)S(1)} copy-done((bf16[528,128]{1,0:T(8,128)(2,1)S(1)}, bf16[528,128]{1,0:T(8,128)(2,1)}, u32[]{:S(2)}) %copy-start) | copy-done | bytes 135192
  10.6 0.7 %copy-done.2 = f32[24,128]{1,0:T(8,128)S(1)} copy-done((f32[24,128]{1,0:T(8,128)S(1)}, f32[24,128]{1,0:T(8,128)}, u32[]{:S(2)}) %copy-start.2) | copy-done | bytes 12312
  11.4 1.6 %first_sums.1 = (f32[4096,128]{1,0:T(8,128)S(1)}, f32[4096,128]{1,0:T(8,128)S(1)}, bf16[1024,128]{1,0:T(8,128)(2,1)S(1)}, f32[8,128]{1,0:T(8,128)S(1)}, s16[512,...) custom-call(f32[24,128]{1,0:T(8,128)S(1)} %copy-done.2, bf16[1,528,128]{2,1,0:T(8,128)(2,1)S(1)} %bitcast.23), custom_call_target="tpu_custom_call" | custom-call | flops 1 | tf_op jit(solution)/shard_map/first_sums/pallas_call | solution.py:434
  13.0 0.5 %collective-permute-done = bf16[528,128]{1,0:T(8,128)(2,1)S(1)} collective-permute-done((bf16[528,128]{1,0:T(8,128)(2,1)}, bf16[528,128]{1,0:T(8,128)(2,1)S(1)}, u32[]{:S(2)}, u32[]{:S(2)}) %collective-permute-start) | collective-permute-done | bytes 135200 | tf_op jit(solution)/shard_map/ppermute | solution.py:386
  13.4 0.8 %collective-permute-start.1 = (bf16[528,128]{1,0:T(8,128)(2,1)S(1)}, bf16[528,128]{1,0:T(8,128)(2,1)S(1)}, u32[]{:S(2)}, u32[]{:S(2)}) collective-permute-start(bf16[528,128]{1,0:T(8,128)(2,1)S(1)} %collective-permute-done), channel_id=1, source_target_pairs={{0,4},{4,0},{8,12},{12,8},{1,5},{5,1},{9,13},{13,9},{2,6},{6,2},{1... | collective-permute-start | bytes 405512 | tf_op jit(solution)/shard_map/ppermute | solution.py:386
  14.2 1.4 %collective-permute-start.4 = (bf16[528,128]{1,0:T(8,128)(2,1)S(1)}, bf16[528,128]{1,0:T(8,128)(2,1)S(1)}, u32[]{:S(2)}, u32[]{:S(2)}) collective-permute-start(bf16[528,128]{1,0:T(8,128)(2,1)S(1)} %collective-permute-done), channel_id=1, source_target_pairs={{0,2},{2,0},{1,3},{3,1},{4,6},{6,4},{5,7},{7,5},{8,10},{10,8},{9,1... | collective-permute-start | bytes 405512 | tf_op jit(solution)/shard_map/ppermute | solution.py:386
  15.6 0.0 collective-permute-done.2
  15.7 0.0 collective-permute-done.3
  15.7 0.0 copy-start.3
  15.7 1.2 %more_sums.2 = (f32[4096,128]{1,0:T(8,128)S(1)}, bf16[1024,128]{1,0:T(8,128)(2,1)S(1)}, f32[8,128]{1,0:T(8,128)S(1)}) custom-call(f32[24,128]{1,0:T(8,128)S(1)} %copy-done.2, bf16[1,528,128]{2,1,0:T(8,128)(2,1)S(1)} %bitcast.15, bf16[1,528,128]{2,1,0:T(8,128)(2,1)S(1)} %bitcast.17, f32[4096,128]{1,0:T(8,128)S(1)} %get-tuple-element.24.refs_3_), custom_call_target="tpu_custom_call" | custom-call | flops 2 | tf_op jit(solution)/shard_map/more_sums/pallas_call | solution.py:434
  16.9 1.4 %collective-permute-start.5 = (bf16[528,128]{1,0:T(8,128)(2,1)S(1)}, bf16[528,128]{1,0:T(8,128)(2,1)S(1)}, u32[]{:S(2)}, u32[]{:S(2)}) collective-permute-start(bf16[528,128]{1,0:T(8,128)(2,1)S(1)} %collective-permute-done.2), channel_id=1, source_target_pairs={{0,4},{4,0},{8,12},{12,8},{1,5},{5,1},{9,13},{13,9},{2,6},{6,2},{1... | collective-permute-start | bytes 405512 | tf_op jit(solution)/shard_map/ppermute | solution.py:386
  18.3 0.1 collective-permute-done.1
  18.4 1.9 %collective-permute-start.6 = (bf16[528,128]{1,0:T(8,128)(2,1)S(1)}, bf16[528,128]{1,0:T(8,128)(2,1)S(1)}, u32[]{:S(2)}, u32[]{:S(2)}) collective-permute-start(bf16[528,128]{1,0:T(8,128)(2,1)S(1)} %collective-permute-done.1), channel_id=1, source_target_pairs={{0,2},{2,0},{1,3},{3,1},{4,6},{6,4},{5,7},{7,5},{8,10},{10,8},{9,1... | collective-permute-start | bytes 405512 | tf_op jit(solution)/shard_map/ppermute | solution.py:386
  20.4 0.0 collective-permute-done.4
  20.4 1.7 %more_sums.3 = (f32[4096,128]{1,0:T(8,128)S(1)}, bf16[1024,128]{1,0:T(8,128)(2,1)S(1)}, f32[8,128]{1,0:T(8,128)S(1)}) custom-call(f32[24,128]{1,0:T(8,128)S(1)} %copy-done.2, bf16[1,528,128]{2,1,0:T(8,128)(2,1)S(1)} %bitcast.13, bf16[1,528,128]{2,1,0:T(8,128)(2,1)S(1)} %bitcast.19, bf16[1,528,128]{2,1,0:T(8,128)(2,1)S(1)} %bitcast.21, ...), custom_call_target="tpu_custom_call" | custom-call | flops 3 | tf_op jit(solution)/shard_map/more_sums/pallas_call | solution.py:434
  22.0 0.0 collective-permute-done.5
  22.0 1.4 %collective-permute-done.6 = bf16[528,128]{1,0:T(8,128)(2,1)S(1)} collective-permute-done((bf16[528,128]{1,0:T(8,128)(2,1)S(1)}, bf16[528,128]{1,0:T(8,128)(2,1)S(1)}, u32[]{:S(2)}, u32[]{:S(2)}) %collective-permute-start.6) | collective-permute-done | bytes 135200 | tf_op jit(solution)/shard_map/ppermute | solution.py:386
  23.5 0.0 copy-done.1
  23.5 0.0 copy-done.3
  23.5 4.8 %table_and_rows.1 = (bf16[4096,128]{1,0:T(8,128)(2,1)}, bf16[512,128]{1,0:T(8,128)(2,1)}) custom-call(f32[24,128]{1,0:T(8,128)S(1)} %copy-done.3, f32[4096,128]{1,0:T(8,128)S(1)} %get-tuple-element.28.refs_1_, f32[4096,128]{1,0:T(8,128)S(1)} %get-tuple-element.29.refs_2_, s16[512,128]{1,0:T(8,128)(2,1)S(1)} %get-tuple-element.30.refs_3_, ...), custom_call_target="tpu_custom_call" | custom-call | tf_op jit(solution)/shard_map/table_and_rows/pallas_call | solution.py:473
  (3 shorter events, 0.0 us)
Async XLA Ops:
  2.6 10.8 %collective-permute-start = (bf16[528,128]{1,0:T(8,128)(2,1)}, bf16[528,128]{1,0:T(8,128)(2,1)S(1)}, u32[]{:S(2)}, u32[]{:S(2)}) collective-permute-start(bf16[528,128]{1,0:T(8,128)(2,1)} %get-tuple-element.21), channel_id=1, source_target_pairs={{0,8},{4,12},{8,0},{12,4},{1,9},{5,13},{9,1},{13,5},{2,10},{6,14},... | collective-permute-start | bytes 405512 | tf_op jit(solution)/shard_map/ppermute | solution.py:386
  6.6 9.0 %collective-permute-start.2 = (bf16[528,128]{1,0:T(8,128)(2,1)}, bf16[528,128]{1,0:T(8,128)(2,1)S(1)}, u32[]{:S(2)}, u32[]{:S(2)}) collective-permute-start(bf16[528,128]{1,0:T(8,128)(2,1)} %get-tuple-element.21), channel_id=1, source_target_pairs={{0,2},{2,0},{1,3},{3,1},{4,6},{6,4},{5,7},{7,5},{8,10},{10,8},{9,1... | collective-permute-start | bytes 405512 | tf_op jit(solution)/shard_map/ppermute | solution.py:386
  8.1 7.5 %collective-permute-start.3 = (bf16[528,128]{1,0:T(8,128)(2,1)}, bf16[528,128]{1,0:T(8,128)(2,1)S(1)}, u32[]{:S(2)}, u32[]{:S(2)}) collective-permute-start(bf16[528,128]{1,0:T(8,128)(2,1)} %get-tuple-element.21), channel_id=1, source_target_pairs={{0,4},{4,0},{8,12},{12,8},{1,5},{5,1},{9,13},{13,9},{2,6},{6,2},{1... | collective-permute-start | bytes 405512 | tf_op jit(solution)/shard_map/ppermute | solution.py:386
  9.7 0.9 %copy-start = (bf16[528,128]{1,0:T(8,128)(2,1)S(1)}, bf16[528,128]{1,0:T(8,128)(2,1)}, u32[]{:S(2)}) copy-start(bf16[528,128]{1,0:T(8,128)(2,1)} %get-tuple-element.21) | copy-start | bytes 405508
  10.6 0.7 %copy-start.2 = (f32[24,128]{1,0:T(8,128)S(1)}, f32[24,128]{1,0:T(8,128)}, u32[]{:S(2)}) copy-start(f32[24,128]{1,0:T(8,128)} %get-tuple-element.20.refs_0_) | copy-start | bytes 36868
  13.4 5.0 %collective-permute-start.1 = (bf16[528,128]{1,0:T(8,128)(2,1)S(1)}, bf16[528,128]{1,0:T(8,128)(2,1)S(1)}, u32[]{:S(2)}, u32[]{:S(2)}) collective-permute-start(bf16[528,128]{1,0:T(8,128)(2,1)S(1)} %collective-permute-done), channel_id=1, source_target_pairs={{0,4},{4,0},{8,12},{12,8},{1,5},{5,1},{9,13},{13,9},{2,6},{6,2},{1... | collective-permute-start | bytes 405512 | tf_op jit(solution)/shard_map/ppermute | solution.py:386
  14.2 6.2 %collective-permute-start.4 = (bf16[528,128]{1,0:T(8,128)(2,1)S(1)}, bf16[528,128]{1,0:T(8,128)(2,1)S(1)}, u32[]{:S(2)}, u32[]{:S(2)}) collective-permute-start(bf16[528,128]{1,0:T(8,128)(2,1)S(1)} %collective-permute-done), channel_id=1, source_target_pairs={{0,2},{2,0},{1,3},{3,1},{4,6},{6,4},{5,7},{7,5},{8,10},{10,8},{9,1... | collective-permute-start | bytes 405512 | tf_op jit(solution)/shard_map/ppermute | solution.py:386
  15.7 7.8 %copy-start.1 = (bf16[528,128]{1,0:T(8,128)(2,1)S(1)}, bf16[528,128]{1,0:T(8,128)(2,1)}, u32[]{:S(2)}) copy-start(bf16[528,128]{1,0:T(8,128)(2,1)} %get-tuple-element.21) | copy-start | bytes 405508
  15.7 7.8 %copy-start.3 = (f32[24,128]{1,0:T(8,128)S(1)}, f32[24,128]{1,0:T(8,128)}, u32[]{:S(2)}) copy-start(f32[24,128]{1,0:T(8,128)} %get-tuple-element.20.refs_0_) | copy-start | bytes 36868
  16.9 5.1 %collective-permute-start.5 = (bf16[528,128]{1,0:T(8,128)(2,1)S(1)}, bf16[528,128]{1,0:T(8,128)(2,1)S(1)}, u32[]{:S(2)}, u32[]{:S(2)}) collective-permute-start(bf16[528,128]{1,0:T(8,128)(2,1)S(1)} %collective-permute-done.2), channel_id=1, source_target_pairs={{0,4},{4,0},{8,12},{12,8},{1,5},{5,1},{9,13},{13,9},{2,6},{6,2},{1... | collective-permute-start | bytes 405512 | tf_op jit(solution)/shard_map/ppermute | solution.py:386
  18.4 5.0 %collective-permute-start.6 = (bf16[528,128]{1,0:T(8,128)(2,1)S(1)}, bf16[528,128]{1,0:T(8,128)(2,1)S(1)}, u32[]{:S(2)}, u32[]{:S(2)}) collective-permute-start(bf16[528,128]{1,0:T(8,128)(2,1)S(1)} %collective-permute-done.1), channel_id=1, source_target_pairs={{0,2},{2,0},{1,3},{3,1},{4,6},{6,4},{5,7},{7,5},{8,10},{10,8},{9,1... | collective-permute-start | bytes 405512 | tf_op jit(solution)/shard_map/ppermute | solution.py:386

commit v14 on v12

--- a/solution.py
+++ b/solution.py
@@ -14,6 +14,7 @@
 I32 = jnp.int32
 I16 = jnp.int16
 FAR = 1e9
+TOP = 32768
 NT = (((1,), (1,)), ((), ()))
 BLOCK = 512
 LATE_BLOCK = 256
@@ -218,21 +219,22 @@
 
 def held(position, bounds):
     one, nothing = BF16(1), BF16(0)
-    masks = [jnp.where((position >= a) & (position <= b), one, nothing) for a, b in bounds]
+    masks = [jnp.where(position - first <= length, one, nothing) for first, length in bounds]
     return jnp.concatenate(masks, axis=1)
 
 
-def within(low, high, rows):
-    if low.dtype == I16:
+def within(top, span, rows):
+    if top.dtype == I16:
         one, nothing = BF16(1), BF16(0)
-        return jnp.concatenate([jnp.where((low <= row) & (high >= row), one, nothing) for row in rows], axis=1)
-    return jnp.concatenate([ones_where((low <= row) & (high >= row)) for row in rows], axis=1)
-
-
-def wide_columns(rows):
-    count = rows.shape[0]
-    columns = jnp.concatenate([rows, jnp.zeros((8 - count, LANES), F32)], axis=0).T
-    return jnp.concatenate([jnp.broadcast_to(columns[:, r : r + 1], (LANES, LANES)) for r in range(count)], axis=0)
+        return jnp.concatenate([jnp.where(top - row <= span, one, nothing) for row in rows], axis=1)
+    return jnp.concatenate([ones_where((top - row >= 0) & (top - row <= span)) for row in rows], axis=1)
+
+
+def wide_columns(*sets):
+    count = sets[0].shape[0]
+    columns = jnp.concatenate(sets, axis=0).T
+    wide = lambda at: jnp.broadcast_to(columns[:, at : at + 1], (LANES, LANES))
+    return [jnp.concatenate([wide(i * count + r) for r in range(count)], axis=0) for i in range(len(sets))]
 
 
 def anchors(z, me):
@@ -264,11 +266,11 @@
     bounds = []
     for g in range(pieces.groups if pieces.count else 0):
         begin = from_ref[g : g + 1, :]
-        bounds.append((short(begin), short(runs.until(begin))))
+        bounds.append((short(begin), short(runs.until(begin) - begin - F32(TOP))))
     for b in range(z.slots // BLOCK):
         part = slice(b * BLOCK, (b + 1) * BLOCK)
         if bounds:
-            mask = held((inner + b * BLOCK).astype(I16), bounds)
+            mask = held((inner + (b * BLOCK - TOP)).astype(I16), bounds)
             value = dot(mask, rows_ref[0 : len(bounds) * LANES, :])
         else:
             value = jnp.zeros((BLOCK, LANES), F32)
@@ -282,13 +284,13 @@
             else:
                 scale_ref[part, :] = fall * jnp.exp(-rate * (first + own_anchor)) * root(z, position - start)
     if not before:
-        position, span_start = wide_columns(own_ref[0 : z.chunks, :]), wide_columns(own_ref[z.chunks : 2 * z.chunks, :])
+        position, span_start = wide_columns(own_ref[0 : z.chunks, :], own_ref[z.chunks : 2 * z.chunks, :])
         for shift in range(z.shifts):
             part = slice(shift * z.rows, (shift + 1) * z.rows)
             center = span_start + F32(z.span * z.slots // 2 - shift * z.span * z.slots)
             factor_ref[part, :] = jnp.exp(-rate * (position - center))
             top = position if shift == 0 else span_start - F32(1)
-            high_ref[part, :] = short(top) if z.narrow else top
+            high_ref[part, :] = short(top - F32(TOP)) if z.narrow else top
 
 
 def late_kernel(z, earlier, form, late, *refs):
@@ -311,29 +313,33 @@
         copies.append(pltpu.make_async_copy(ref.at[part, :], out.at[part, :], sems.at[len(copies)]))
         copies[-1].start()
 
-    pack(z, last, base, marks_ref, codes_ref, rows_ref, from_ref)
-
     place = own_ref[0 : z.chunks, :]
     start = jnp.concatenate([runs.start_row(place[r : r + 1]) for r in range(z.chunks)], axis=0)
-    scale = wide_columns(root(z, place - start))
-    low = wide_columns(jnp.maximum(place - F32(z.window), start))
-    span_start = wide_columns(own_ref[z.chunks : 2 * z.chunks, :]) if z.shifts > 1 else None
+    distance = place - start
+    reach = jnp.minimum(distance, F32(z.window))
+    scale, reach = wide_columns(root(z, distance), reach - F32(TOP) if z.narrow else reach)
+    position, span_start = (None, None) if z.narrow else wide_columns(place, own_ref[z.chunks : 2 * z.chunks, :])
     kind = short if z.narrow else lambda row: row
     total = jnp.zeros((z.rows, LANES), F32)
     for shift in range(z.shifts):
         part = slice(shift * z.rows, (shift + 1) * z.rows)
-        bottom = kind(jnp.maximum(low, span_start) if shift == 0 and z.shifts > 1 else low)
         top = high_ref[part, :]
+        if z.narrow:
+            span = short(reach)
+        else:
+            low = position - reach
+            span = top - (jnp.maximum(low, span_start) if shift == 0 else low)
 
         def add(s, value):
             rows = pieces.place(s)
-            mask = within(bottom, top, [kind(rows[r : r + 1]) for r in range(z.chunks)])
+            mask = within(top, span, [kind(rows[r : r + 1]) for r in range(z.chunks)])
             return value + dot(mask, pieces.rows(s))
 
         total += loop(pieces.count, add, jnp.zeros((z.rows, LANES), F32)) * factor_ref[part, :]
     feature_ref[...] = (total * scale).astype(BF16)
     send(feature_ref, feature_out, slice(0, z.rows))
 
+    pack(z, last, base, marks_ref, codes_ref, rows_ref, from_ref)
     own_anchor, tail_anchor = anchors(z, me)
     inner = iota((LATE_BLOCK, LANES), 0)
     fall = jnp.exp(-rate * inner.astype(F32))
@@ -343,7 +349,7 @@
     for ref, first, lines in listed:
         for g in range(first, first + lines):
             begin = ref[g : g + 1, :]
-            bounds.append((short(begin), short(runs.until(begin + base) - base)))
+            bounds.append((short(begin), short(runs.until(begin + base) - (begin + base) - F32(TOP))))
     n = last.groups
     own_rows = rows_ref[0 : n * LANES, :]
     tail_rows = [rows_ref[n * LANES : 2 * n * LANES, :]]
@@ -351,7 +357,7 @@
     tail_rows = jnp.concatenate(tail_rows, axis=0)
     for b in range(z.slots // LATE_BLOCK):
         part = slice(b * LATE_BLOCK, (b + 1) * LATE_BLOCK)
-        position = (inner + b * LATE_BLOCK).astype(I16)
+        position = (inner + (b * LATE_BLOCK - TOP)).astype(I16)
         first = F32(b * LATE_BLOCK)
         value = sums_ref[part, :]
         if b * LATE_BLOCK >= z.window:
@@ -451,10 +457,9 @@
         last, total = tie((last, total))
         side_last = swap(last, "shard", 1)
         second = [(far,), (last,), (side_far,)]
+        late = [(side_near,), (side_last,)]
         total, *tail3 = sums(second, (total,))
-        total, *tail4 = sums([(side_near,)], (total,))
-        early = [(block,), (side,), (near,)] + second + [(side_near,)]
-        earlier, tails, late = (1, 2, 3, 1), tail + tail2 + tail3 + tail4, [(side_last,)]
+        early, earlier, tails = [(block,), (side,), (near,)] + second, (1, 2, 3), tail + tail2 + tail3
     else:
         blocks = spread(spread([block], "key"), "shard")
         total, scale, _, _, tops, factors = sums([])

time: 28.3 us -> 27.7 us (0.979)
  Pallas kernels: 11.3 us -> 10.3 us
  starting transfers between devices: 11.7 us -> 12.7 us
  local copies, waits for them, and re-layouts: 2.35 us -> 1.66 us
    pallas_call x4 -> x3, Pallas kernels: 5.42 us -> 4.45 us  [sums(): pl.pallas_call(functools.partial(early_kernel, z, form, len(before)), out...]
    ppermute x7, starting transfers between devices: 11.7 us -> 12.7 us  [swap(): lax.ppermute(block, axis, [(i, i ^ distance) for i in range(lax.axis_size...]
    unnamed x8, local copies, waits for them, and re-layouts: 2.35 us -> 1.66 us
  transfers between devices with their start and end apart: 7 -> 7, of which waited for: 3 -> 3; matrix products, arithmetic and copies ran while one was open for 0% -> 0% of each run, Pallas kernels for 19% -> 16%
where the time goes in v14:
time: 27.7 us; the launch traced here: 27.4 us
  starting transfers between devices  12.7 us (46%)
  Pallas kernels  10.3 us (37%)
  waiting for transfers between devices  2.05 us (7%)
  local copies, waits for them, and re-layouts  1.66 us (6%)
  between operations  0.69 us (2%)
    ppermute x7, starting transfers between devices, swap(): lax.ppermute(block, axis, [(i, i ^ distance) for i in range(lax.axis_size...  12.7 us
    pallas_call x3, Pallas kernels, sums(): pl.pallas_call(functools.partial(early_kernel, z, form, len(before)), out...  4.45 us
    pallas_call x1, Pallas kernels, on_device(): pl.pallas_call(functools.partial(late_kernel, z, earlier, form, len(late)...  3.93 us
    ppermute x7, waiting for transfers between devices, swap(): lax.ppermute(block, axis, [(i, i ^ distance) for i in range(lax.axis_size...  2.05 us
    pallas_call x1, Pallas kernels, on_device(): pl.pallas_call(functools.partial(send_kernel, z), out_shape=(shape((block...  1.96 us
    unnamed x8, local copies, waits for them, and re-layouts  1.66 us
  transfers between devices with their start and end apart: 7, of which 3 were waited for; matrix products, arithmetic and copies ran while one was open for 0% of the time, Pallas kernels for 16%

profile of v14, /device:TPU:0, one launch (start us, length us, event | category | flops | bytes accessed | tf_op | source)
XLA Modules:
  0.0 27.4 jit_solution(715407271953194578)
XLA Ops:
  0.6 2.0 %weigh.1 = (bf16[528,128]{1,0:T(8,128)(2,1)}, f32[24,128]{1,0:T(8,128)}) custom-call(s32[1]{0:T(128)} %bitcast.me_ref, f32[4]{0:T(128)} %rate_ref.1, bf16[512,128]{1,0:T(8,128)(2,1)} %events_ref.1, f32[4,128]{1,0:T(4,128)} %bitcast.28, s32[4,128]{1,0:T(4,128)} %bitcast.29, s32[4,128]{1,0:T(4,128)} %bitcast.30, s32[32,128]{1,0:T(8,128)} %bitcast.27), custom_call_target="tpu_custom_call" | custom-call | tf_op jit(solution)/shard_map/weigh/pallas_call | solution.py:407
  2.6 4.0 %collective-permute-start = (bf16[528,128]{1,0:T(8,128)(2,1)}, bf16[528,128]{1,0:T(8,128)(2,1)S(1)}, u32[]{:S(2)}, u32[]{:S(2)}) collective-permute-start(bf16[528,128]{1,0:T(8,128)(2,1)} %get-tuple-element.21), channel_id=1, source_target_pairs={{0,8},{4,12},{8,0},{12,4},{1,9},{5,13},{9,1},{13,5},{2,10},{6,14},... | collective-permute-start | bytes 405512 | tf_op jit(solution)/shard_map/ppermute | solution.py:384
  6.6 1.5 %collective-permute-start.2 = (bf16[528,128]{1,0:T(8,128)(2,1)}, bf16[528,128]{1,0:T(8,128)(2,1)S(1)}, u32[]{:S(2)}, u32[]{:S(2)}) collective-permute-start(bf16[528,128]{1,0:T(8,128)(2,1)} %get-tuple-element.21), channel_id=1, source_target_pairs={{0,2},{2,0},{1,3},{3,1},{4,6},{6,4},{5,7},{7,5},{8,10},{10,8},{9,1... | collective-permute-start | bytes 405512 | tf_op jit(solution)/shard_map/ppermute | solution.py:384
  8.1 1.6 %collective-permute-start.3 = (bf16[528,128]{1,0:T(8,128)(2,1)}, bf16[528,128]{1,0:T(8,128)(2,1)S(1)}, u32[]{:S(2)}, u32[]{:S(2)}) collective-permute-start(bf16[528,128]{1,0:T(8,128)(2,1)} %get-tuple-element.21), channel_id=1, source_target_pairs={{0,4},{4,0},{8,12},{12,8},{1,5},{5,1},{9,13},{13,9},{2,6},{6,2},{1... | collective-permute-start | bytes 405512 | tf_op jit(solution)/shard_map/ppermute | solution.py:384
  9.7 0.9 %copy-done = bf16[528,128]{1,0:T(8,128)(2,1)S(1)} copy-done((bf16[528,128]{1,0:T(8,128)(2,1)S(1)}, bf16[528,128]{1,0:T(8,128)(2,1)}, u32[]{:S(2)}) %copy-start) | copy-done | bytes 135192
  10.6 0.7 %copy-done.2 = f32[24,128]{1,0:T(8,128)S(1)} copy-done((f32[24,128]{1,0:T(8,128)S(1)}, f32[24,128]{1,0:T(8,128)}, u32[]{:S(2)}) %copy-start.2) | copy-done | bytes 12312
  11.4 1.6 %first_sums.1 = (f32[4096,128]{1,0:T(8,128)S(1)}, f32[4096,128]{1,0:T(8,128)S(1)}, bf16[1024,128]{1,0:T(8,128)(2,1)S(1)}, f32[8,128]{1,0:T(8,128)S(1)}, s16[512,...) custom-call(f32[24,128]{1,0:T(8,128)S(1)} %copy-done.2, bf16[1,528,128]{2,1,0:T(8,128)(2,1)S(1)} %bitcast.23), custom_call_target="tpu_custom_call" | custom-call | flops 1 | tf_op jit(solution)/shard_map/first_sums/pallas_call | solution.py:432
  12.9 0.5 %collective-permute-done = bf16[528,128]{1,0:T(8,128)(2,1)S(1)} collective-permute-done((bf16[528,128]{1,0:T(8,128)(2,1)}, bf16[528,128]{1,0:T(8,128)(2,1)S(1)}, u32[]{:S(2)}, u32[]{:S(2)}) %collective-permute-start) | collective-permute-done | bytes 135200 | tf_op jit(solution)/shard_map/ppermute | solution.py:384
  13.4 0.8 %collective-permute-start.1 = (bf16[528,128]{1,0:T(8,128)(2,1)S(1)}, bf16[528,128]{1,0:T(8,128)(2,1)S(1)}, u32[]{:S(2)}, u32[]{:S(2)}) collective-permute-start(bf16[528,128]{1,0:T(8,128)(2,1)S(1)} %collective-permute-done), channel_id=1, source_target_pairs={{0,4},{4,0},{8,12},{12,8},{1,5},{5,1},{9,13},{13,9},{2,6},{6,2},{1... | collective-permute-start | bytes 405512 | tf_op jit(solution)/shard_map/ppermute | solution.py:384
  14.2 1.4 %collective-permute-start.4 = (bf16[528,128]{1,0:T(8,128)(2,1)S(1)}, bf16[528,128]{1,0:T(8,128)(2,1)S(1)}, u32[]{:S(2)}, u32[]{:S(2)}) collective-permute-start(bf16[528,128]{1,0:T(8,128)(2,1)S(1)} %collective-permute-done), channel_id=1, source_target_pairs={{0,2},{2,0},{1,3},{3,1},{4,6},{6,4},{5,7},{7,5},{8,10},{10,8},{9,1... | collective-permute-start | bytes 405512 | tf_op jit(solution)/shard_map/ppermute | solution.py:384
  15.6 0.0 collective-permute-done.2
  15.7 0.0 collective-permute-done.3
  15.7 0.0 copy-start.3
  15.7 1.2 %more_sums.2 = (f32[4096,128]{1,0:T(8,128)S(1)}, bf16[1024,128]{1,0:T(8,128)(2,1)S(1)}, f32[8,128]{1,0:T(8,128)S(1)}) custom-call(f32[24,128]{1,0:T(8,128)S(1)} %copy-done.2, bf16[1,528,128]{2,1,0:T(8,128)(2,1)S(1)} %bitcast.15, bf16[1,528,128]{2,1,0:T(8,128)(2,1)S(1)} %bitcast.17, f32[4096,128]{1,0:T(8,128)S(1)} %get-tuple-element.24.refs_3_), custom_call_target="tpu_custom_call" | custom-call | flops 2 | tf_op jit(solution)/shard_map/more_sums/pallas_call | solution.py:432
  16.9 1.4 %collective-permute-start.5 = (bf16[528,128]{1,0:T(8,128)(2,1)S(1)}, bf16[528,128]{1,0:T(8,128)(2,1)S(1)}, u32[]{:S(2)}, u32[]{:S(2)}) collective-permute-start(bf16[528,128]{1,0:T(8,128)(2,1)S(1)} %collective-permute-done.2), channel_id=1, source_target_pairs={{0,4},{4,0},{8,12},{12,8},{1,5},{5,1},{9,13},{13,9},{2,6},{6,2},{1... | collective-permute-start | bytes 405512 | tf_op jit(solution)/shard_map/ppermute | solution.py:384
  18.3 0.1 collective-permute-done.1
  18.4 1.9 %collective-permute-start.6 = (bf16[528,128]{1,0:T(8,128)(2,1)S(1)}, bf16[528,128]{1,0:T(8,128)(2,1)S(1)}, u32[]{:S(2)}, u32[]{:S(2)}) collective-permute-start(bf16[528,128]{1,0:T(8,128)(2,1)S(1)} %collective-permute-done.1), channel_id=1, source_target_pairs={{0,2},{2,0},{1,3},{3,1},{4,6},{6,4},{5,7},{7,5},{8,10},{10,8},{9,1... | collective-permute-start | bytes 405512 | tf_op jit(solution)/shard_map/ppermute | solution.py:384
  20.4 0.0 collective-permute-done.4
  20.4 1.7 %more_sums.3 = (f32[4096,128]{1,0:T(8,128)S(1)}, bf16[1024,128]{1,0:T(8,128)(2,1)S(1)}, f32[8,128]{1,0:T(8,128)S(1)}) custom-call(f32[24,128]{1,0:T(8,128)S(1)} %copy-done.2, bf16[1,528,128]{2,1,0:T(8,128)(2,1)S(1)} %bitcast.13, bf16[1,528,128]{2,1,0:T(8,128)(2,1)S(1)} %bitcast.19, bf16[1,528,128]{2,1,0:T(8,128)(2,1)S(1)} %bitcast.21, ...), custom_call_target="tpu_custom_call" | custom-call | flops 3 | tf_op jit(solution)/shard_map/more_sums/pallas_call | solution.py:432
  22.0 0.0 collective-permute-done.5
  22.1 1.4 %collective-permute-done.6 = bf16[528,128]{1,0:T(8,128)(2,1)S(1)} collective-permute-done((bf16[528,128]{1,0:T(8,128)(2,1)S(1)}, bf16[528,128]{1,0:T(8,128)(2,1)S(1)}, u32[]{:S(2)}, u32[]{:S(2)}) %collective-permute-start.6) | collective-permute-done | bytes 135200 | tf_op jit(solution)/shard_map/ppermute | solution.py:384
  23.5 0.0 copy-done.1
  23.5 0.0 copy-done.3
  23.5 3.9 %table_and_rows.1 = (bf16[4096,128]{1,0:T(8,128)(2,1)}, bf16[512,128]{1,0:T(8,128)(2,1)}) custom-call(f32[24,128]{1,0:T(8,128)S(1)} %copy-done.3, f32[4096,128]{1,0:T(8,128)S(1)} %get-tuple-element.28.refs_1_, f32[4096,128]{1,0:T(8,128)S(1)} %get-tuple-element.29.refs_2_, s16[512,128]{1,0:T(8,128)(2,1)S(1)} %get-tuple-element.30.refs_3_, ...), custom_call_target="tpu_custom_call" | custom-call | tf_op jit(solution)/shard_map/table_and_rows/pallas_call | solution.py:471
  (3 shorter events, 0.0 us)
Async XLA Ops:
  2.6 10.8 %collective-permute-start = (bf16[528,128]{1,0:T(8,128)(2,1)}, bf16[528,128]{1,0:T(8,128)(2,1)S(1)}, u32[]{:S(2)}, u32[]{:S(2)}) collective-permute-start(bf16[528,128]{1,0:T(8,128)(2,1)} %get-tuple-element.21), channel_id=1, source_target_pairs={{0,8},{4,12},{8,0},{12,4},{1,9},{5,13},{9,1},{13,5},{2,10},{6,14},... | collective-permute-start | bytes 405512 | tf_op jit(solution)/shard_map/ppermute | solution.py:384
  6.6 9.0 %collective-permute-start.2 = (bf16[528,128]{1,0:T(8,128)(2,1)}, bf16[528,128]{1,0:T(8,128)(2,1)S(1)}, u32[]{:S(2)}, u32[]{:S(2)}) collective-permute-start(bf16[528,128]{1,0:T(8,128)(2,1)} %get-tuple-element.21), channel_id=1, source_target_pairs={{0,2},{2,0},{1,3},{3,1},{4,6},{6,4},{5,7},{7,5},{8,10},{10,8},{9,1... | collective-permute-start | bytes 405512 | tf_op jit(solution)/shard_map/ppermute | solution.py:384
  8.1 7.5 %collective-permute-start.3 = (bf16[528,128]{1,0:T(8,128)(2,1)}, bf16[528,128]{1,0:T(8,128)(2,1)S(1)}, u32[]{:S(2)}, u32[]{:S(2)}) collective-permute-start(bf16[528,128]{1,0:T(8,128)(2,1)} %get-tuple-element.21), channel_id=1, source_target_pairs={{0,4},{4,0},{8,12},{12,8},{1,5},{5,1},{9,13},{13,9},{2,6},{6,2},{1... | collective-permute-start | bytes 405512 | tf_op jit(solution)/shard_map/ppermute | solution.py:384
  9.7 0.9 %copy-start = (bf16[528,128]{1,0:T(8,128)(2,1)S(1)}, bf16[528,128]{1,0:T(8,128)(2,1)}, u32[]{:S(2)}) copy-start(bf16[528,128]{1,0:T(8,128)(2,1)} %get-tuple-element.21) | copy-start | bytes 405508
  10.6 0.7 %copy-start.2 = (f32[24,128]{1,0:T(8,128)S(1)}, f32[24,128]{1,0:T(8,128)}, u32[]{:S(2)}) copy-start(f32[24,128]{1,0:T(8,128)} %get-tuple-element.20.refs_0_) | copy-start | bytes 36868
  13.4 5.0 %collective-permute-start.1 = (bf16[528,128]{1,0:T(8,128)(2,1)S(1)}, bf16[528,128]{1,0:T(8,128)(2,1)S(1)}, u32[]{:S(2)}, u32[]{:S(2)}) collective-permute-start(bf16[528,128]{1,0:T(8,128)(2,1)S(1)} %collective-permute-done), channel_id=1, source_target_pairs={{0,4},{4,0},{8,12},{12,8},{1,5},{5,1},{9,13},{13,9},{2,6},{6,2},{1... | collective-permute-start | bytes 405512 | tf_op jit(solution)/shard_map/ppermute | solution.py:384
  14.2 6.2 %collective-permute-start.4 = (bf16[528,128]{1,0:T(8,128)(2,1)S(1)}, bf16[528,128]{1,0:T(8,128)(2,1)S(1)}, u32[]{:S(2)}, u32[]{:S(2)}) collective-permute-start(bf16[528,128]{1,0:T(8,128)(2,1)S(1)} %collective-permute-done), channel_id=1, source_target_pairs={{0,2},{2,0},{1,3},{3,1},{4,6},{6,4},{5,7},{7,5},{8,10},{10,8},{9,1... | collective-permute-start | bytes 405512 | tf_op jit(solution)/shard_map/ppermute | solution.py:384
  15.7 7.8 %copy-start.1 = (bf16[528,128]{1,0:T(8,128)(2,1)S(1)}, bf16[528,128]{1,0:T(8,128)(2,1)}, u32[]{:S(2)}) copy-start(bf16[528,128]{1,0:T(8,128)(2,1)} %get-tuple-element.21) | copy-start | bytes 405508
  15.7 7.8 %copy-start.3 = (f32[24,128]{1,0:T(8,128)S(1)}, f32[24,128]{1,0:T(8,128)}, u32[]{:S(2)}) copy-start(f32[24,128]{1,0:T(8,128)} %get-tuple-element.20.refs_0_) | copy-start | bytes 36868
  16.9 5.2 %collective-permute-start.5 = (bf16[528,128]{1,0:T(8,128)(2,1)S(1)}, bf16[528,128]{1,0:T(8,128)(2,1)S(1)}, u32[]{:S(2)}, u32[]{:S(2)}) collective-permute-start(bf16[528,128]{1,0:T(8,128)(2,1)S(1)} %collective-permute-done.2), channel_id=1, source_target_pairs={{0,4},{4,0},{8,12},{12,8},{1,5},{5,1},{9,13},{13,9},{2,6},{6,2},{1... | collective-permute-start | bytes 405512 | tf_op jit(solution)/shard_map/ppermute | solution.py:384
  18.4 5.0 %collective-permute-start.6 = (bf16[528,128]{1,0:T(8,128)(2,1)S(1)}, bf16[528,128]{1,0:T(8,128)(2,1)S(1)}, u32[]{:S(2)}, u32[]{:S(2)}) collective-permute-start(bf16[528,128]{1,0:T(8,128)(2,1)S(1)} %collective-permute-done.1), channel_id=1, source_target_pairs={{0,2},{2,0},{1,3},{3,1},{4,6},{6,4},{5,7},{7,5},{8,10},{10,8},{9,1... | collective-permute-start | bytes 405512 | tf_op jit(solution)/shard_map/ppermute | solution.py:384

commit v15 on v14

--- a/solution.py
+++ b/solution.py
@@ -457,9 +457,10 @@
         last, total = tie((last, total))
         side_last = swap(last, "shard", 1)
         second = [(far,), (last,), (side_far,)]
-        late = [(side_near,), (side_last,)]
         total, *tail3 = sums(second, (total,))
-        early, earlier, tails = [(block,), (side,), (near,)] + second, (1, 2, 3), tail + tail2 + tail3
+        total, *tail4 = sums([(side_near,)], (total,))
+        early = [(block,), (side,), (near,)] + second + [(side_near,)]
+        earlier, tails, late = (1, 2, 3, 1), tail + tail2 + tail3 + tail4, [(side_last,)]
     else:
         blocks = spread(spread([block], "key"), "shard")
         total, scale, _, _, tops, factors = sums([])

time: 27.7 us -> 28.3 us (1.022)
  starting transfers between devices: 12.7 us -> 11.7 us
  Pallas kernels: 10.3 us -> 11.2 us
  local copies, waits for them, and re-layouts: 1.66 us -> 2.35 us
    ppermute x7, starting transfers between devices: 12.7 us -> 11.7 us  [swap(): lax.ppermute(block, axis, [(i, i ^ distance) for i in range(lax.axis_size...]
    pallas_call x3 -> x4, Pallas kernels: 4.45 us -> 5.37 us  [sums(): pl.pallas_call(functools.partial(early_kernel, z, form, len(before)), out...]
    unnamed x8, local copies, waits for them, and re-layouts: 1.66 us -> 2.35 us
  transfers between devices with their start and end apart: 7 -> 7, of which waited for: 3 -> 3; matrix products, arithmetic and copies ran while one was open for 0% -> 0% of each run, Pallas kernels for 16% -> 19%
where the time goes in v15:
time: 28.3 us; the launch traced here: 27.9 us
  starting transfers between devices  11.7 us (41%)
  Pallas kernels  11.2 us (40%)
  local copies, waits for them, and re-layouts  2.35 us (8%)
  waiting for transfers between devices  1.94 us (7%)
  between operations  0.68 us (2%)
    ppermute x7, starting transfers between devices, swap(): lax.ppermute(block, axis, [(i, i ^ distance) for i in range(lax.axis_size...  11.7 us
    pallas_call x4, Pallas kernels, sums(): pl.pallas_call(functools.partial(early_kernel, z, form, len(before)), out...  5.37 us
    pallas_call x1, Pallas kernels, on_device(): pl.pallas_call(functools.partial(late_kernel, z, earlier, form, len(late)...  3.9 us
    unnamed x8, local copies, waits for them, and re-layouts  2.35 us
    pallas_call x1, Pallas kernels, on_device(): pl.pallas_call(functools.partial(send_kernel, z), out_shape=(shape((block...  1.96 us
    ppermute x7, waiting for transfers between devices, swap(): lax.ppermute(block, axis, [(i, i ^ distance) for i in range(lax.axis_size...  1.94 us
  transfers between devices with their start and end apart: 7, of which 3 were waited for; matrix products, arithmetic and copies ran while one was open for 0% of the time, Pallas kernels for 19%

profile of v15, /device:TPU:0, one launch (start us, length us, event | category | flops | bytes accessed | tf_op | source)
XLA Modules:
  0.0 27.9 jit_solution(13314849931702352296)
XLA Ops:
  0.6 2.0 %weigh.1 = (bf16[528,128]{1,0:T(8,128)(2,1)}, f32[24,128]{1,0:T(8,128)}) custom-call(s32[1]{0:T(128)} %bitcast.me_ref, f32[4]{0:T(128)} %rate_ref.1, bf16[512,128]{1,0:T(8,128)(2,1)} %events_ref.1, f32[4,128]{1,0:T(4,128)} %bitcast.29, s32[4,128]{1,0:T(4,128)} %bitcast.30, s32[4,128]{1,0:T(4,128)} %bitcast.31, s32[32,128]{1,0:T(8,128)} %bitcast.28), custom_call_target="tpu_custom_call" | custom-call | tf_op jit(solution)/shard_map/weigh/pallas_call | solution.py:407
  2.6 4.0 %collective-permute-start.2 = (bf16[528,128]{1,0:T(8,128)(2,1)}, bf16[528,128]{1,0:T(8,128)(2,1)S(1)}, u32[]{:S(2)}, u32[]{:S(2)}) collective-permute-start(bf16[528,128]{1,0:T(8,128)(2,1)} %get-tuple-element.24), channel_id=1, source_target_pairs={{0,8},{4,12},{8,0},{12,4},{1,9},{5,13},{9,1},{13,5},{2,10},{6,14},... | collective-permute-start | bytes 405512 | tf_op jit(solution)/shard_map/ppermute | solution.py:384
  6.6 1.5 %collective-permute-start = (bf16[528,128]{1,0:T(8,128)(2,1)}, bf16[528,128]{1,0:T(8,128)(2,1)S(1)}, u32[]{:S(2)}, u32[]{:S(2)}) collective-permute-start(bf16[528,128]{1,0:T(8,128)(2,1)} %get-tuple-element.24), channel_id=1, source_target_pairs={{0,2},{2,0},{1,3},{3,1},{4,6},{6,4},{5,7},{7,5},{8,10},{10,8},{9,1... | collective-permute-start | bytes 405512 | tf_op jit(solution)/shard_map/ppermute | solution.py:384
  8.1 1.6 %collective-permute-start.4 = (bf16[528,128]{1,0:T(8,128)(2,1)}, bf16[528,128]{1,0:T(8,128)(2,1)S(1)}, u32[]{:S(2)}, u32[]{:S(2)}) collective-permute-start(bf16[528,128]{1,0:T(8,128)(2,1)} %get-tuple-element.24), channel_id=1, source_target_pairs={{0,4},{4,0},{8,12},{12,8},{1,5},{5,1},{9,13},{13,9},{2,6},{6,2},{1... | collective-permute-start | bytes 405512 | tf_op jit(solution)/shard_map/ppermute | solution.py:384
  9.7 0.9 %copy-done = bf16[528,128]{1,0:T(8,128)(2,1)S(1)} copy-done((bf16[528,128]{1,0:T(8,128)(2,1)S(1)}, bf16[528,128]{1,0:T(8,128)(2,1)}, u32[]{:S(2)}) %copy-start) | copy-done | bytes 135192
  10.6 0.7 %copy-done.2 = f32[24,128]{1,0:T(8,128)S(1)} copy-done((f32[24,128]{1,0:T(8,128)S(1)}, f32[24,128]{1,0:T(8,128)}, u32[]{:S(2)}) %copy-start.2) | copy-done | bytes 12312
  11.4 1.6 %first_sums.1 = (f32[4096,128]{1,0:T(8,128)S(1)}, f32[4096,128]{1,0:T(8,128)S(1)}, bf16[1024,128]{1,0:T(8,128)(2,1)S(1)}, f32[8,128]{1,0:T(8,128)S(1)}, s16[512,...) custom-call(f32[24,128]{1,0:T(8,128)S(1)} %copy-done.2, bf16[1,528,128]{2,1,0:T(8,128)(2,1)S(1)} %bitcast.25), custom_call_target="tpu_custom_call" | custom-call | flops 1 | tf_op jit(solution)/shard_map/first_sums/pallas_call | solution.py:432
  12.9 0.5 %collective-permute-done.2 = bf16[528,128]{1,0:T(8,128)(2,1)S(1)} collective-permute-done((bf16[528,128]{1,0:T(8,128)(2,1)}, bf16[528,128]{1,0:T(8,128)(2,1)S(1)}, u32[]{:S(2)}, u32[]{:S(2)}) %collective-permute-start.2) | collective-permute-done | bytes 135200 | tf_op jit(solution)/shard_map/ppermute | solution.py:384
  13.4 0.8 %collective-permute-start.3 = (bf16[528,128]{1,0:T(8,128)(2,1)S(1)}, bf16[528,128]{1,0:T(8,128)(2,1)S(1)}, u32[]{:S(2)}, u32[]{:S(2)}) collective-permute-start(bf16[528,128]{1,0:T(8,128)(2,1)S(1)} %collective-permute-done.2), channel_id=1, source_target_pairs={{0,4},{4,0},{8,12},{12,8},{1,5},{5,1},{9,13},{13,9},{2,6},{6,2},{1... | collective-permute-start | bytes 405512 | tf_op jit(solution)/shard_map/ppermute | solution.py:384
  14.2 1.4 %collective-permute-start.5 = (bf16[528,128]{1,0:T(8,128)(2,1)S(1)}, bf16[528,128]{1,0:T(8,128)(2,1)S(1)}, u32[]{:S(2)}, u32[]{:S(2)}) collective-permute-start(bf16[528,128]{1,0:T(8,128)(2,1)S(1)} %collective-permute-done.2), channel_id=1, source_target_pairs={{0,2},{2,0},{1,3},{3,1},{4,6},{6,4},{5,7},{7,5},{8,10},{10,8},{9,1... | collective-permute-start | bytes 405512 | tf_op jit(solution)/shard_map/ppermute | solution.py:384
  15.6 0.0 collective-permute-done
  15.7 0.0 collective-permute-done.4
  15.7 0.7 %copy-done.3 = f32[24,128]{1,0:T(8,128)S(1)} copy-done((f32[24,128]{1,0:T(8,128)S(1)}, f32[24,128]{1,0:T(8,128)}, u32[]{:S(2)}) %copy-start.3) | copy-done | bytes 12312
  16.4 1.2 %more_sums.3 = (f32[4096,128]{1,0:T(8,128)S(1)}, bf16[1024,128]{1,0:T(8,128)(2,1)S(1)}, f32[8,128]{1,0:T(8,128)S(1)}) custom-call(f32[24,128]{1,0:T(8,128)S(1)} %copy-done.3, bf16[1,528,128]{2,1,0:T(8,128)(2,1)S(1)} %bitcast.15, bf16[1,528,128]{2,1,0:T(8,128)(2,1)S(1)} %bitcast.17, f32[4096,128]{1,0:T(8,128)S(1)} %get-tuple-element.27.refs_3_), custom_call_target="tpu_custom_call" | custom-call | flops 2 | tf_op jit(solution)/shard_map/more_sums/pallas_call | solution.py:432
  17.6 1.4 %collective-permute-start.1 = (bf16[528,128]{1,0:T(8,128)(2,1)S(1)}, bf16[528,128]{1,0:T(8,128)(2,1)S(1)}, u32[]{:S(2)}, u32[]{:S(2)}) collective-permute-start(bf16[528,128]{1,0:T(8,128)(2,1)S(1)} %collective-permute-done), channel_id=1, source_target_pairs={{0,4},{4,0},{8,12},{12,8},{1,5},{5,1},{9,13},{13,9},{2,6},{6,2},{1... | collective-permute-start | bytes 405512 | tf_op jit(solution)/shard_map/ppermute | solution.py:384
  19.0 0.0 collective-permute-done.3
  19.0 1.0 %collective-permute-start.6 = (bf16[528,128]{1,0:T(8,128)(2,1)S(1)}, bf16[528,128]{1,0:T(8,128)(2,1)S(1)}, u32[]{:S(2)}, u32[]{:S(2)}) collective-permute-start(bf16[528,128]{1,0:T(8,128)(2,1)S(1)} %collective-permute-done.3), channel_id=1, source_target_pairs={{0,2},{2,0},{1,3},{3,1},{4,6},{6,4},{5,7},{7,5},{8,10},{10,8},{9,1... | collective-permute-start | bytes 405512 | tf_op jit(solution)/shard_map/ppermute | solution.py:384
  20.0 0.0 collective-permute-done.5
  20.0 1.7 %more_sums.4 = (f32[4096,128]{1,0:T(8,128)S(1)}, bf16[1024,128]{1,0:T(8,128)(2,1)S(1)}, f32[8,128]{1,0:T(8,128)S(1)}) custom-call(f32[24,128]{1,0:T(8,128)S(1)} %copy-done.3, bf16[1,528,128]{2,1,0:T(8,128)(2,1)S(1)} %bitcast.13, bf16[1,528,128]{2,1,0:T(8,128)(2,1)S(1)} %bitcast.19, bf16[1,528,128]{2,1,0:T(8,128)(2,1)S(1)} %bitcast.21, ...), custom_call_target="tpu_custom_call" | custom-call | flops 3 | tf_op jit(solution)/shard_map/more_sums/pallas_call | solution.py:432
  21.7 1.0 %collective-permute-done.1 = bf16[528,128]{1,0:T(8,128)(2,1)S(1)} collective-permute-done((bf16[528,128]{1,0:T(8,128)(2,1)S(1)}, bf16[528,128]{1,0:T(8,128)(2,1)S(1)}, u32[]{:S(2)}, u32[]{:S(2)}) %collective-permute-start.1) | collective-permute-done | bytes 135200 | tf_op jit(solution)/shard_map/ppermute | solution.py:384
  22.7 0.9 %more_sums.5 = (f32[4096,128]{1,0:T(8,128)S(1)}, bf16[1024,128]{1,0:T(8,128)(2,1)S(1)}, f32[8,128]{1,0:T(8,128)S(1)}) custom-call(f32[24,128]{1,0:T(8,128)S(1)} %copy-done.3, bf16[1,528,128]{2,1,0:T(8,128)(2,1)S(1)} %bitcast.23, f32[4096,128]{1,0:T(8,128)S(1)} %get-tuple-element.31.refs_2_), custom_call_target="tpu_custom_call" | custom-call | flops 1 | tf_op jit(solution)/shard_map/more_sums/pallas_call | solution.py:432
  23.6 0.4 %collective-permute-done.6 = bf16[528,128]{1,0:T(8,128)(2,1)S(1)} collective-permute-done((bf16[528,128]{1,0:T(8,128)(2,1)S(1)}, bf16[528,128]{1,0:T(8,128)(2,1)S(1)}, u32[]{:S(2)}, u32[]{:S(2)}) %collective-permute-start.6) | collective-permute-done | bytes 135200 | tf_op jit(solution)/shard_map/ppermute | solution.py:384
  24.0 0.0 copy-done.1
  24.0 3.9 %table_and_rows.1 = (bf16[4096,128]{1,0:T(8,128)(2,1)}, bf16[512,128]{1,0:T(8,128)(2,1)}) custom-call(f32[24,128]{1,0:T(8,128)S(1)} %copy-done.3, f32[4096,128]{1,0:T(8,128)S(1)} %get-tuple-element.32.refs_1_, f32[4096,128]{1,0:T(8,128)S(1)} %get-tuple-element.33.refs_2_, s16[512,128]{1,0:T(8,128)(2,1)S(1)} %get-tuple-element.34.refs_3_, ...), custom_call_target="tpu_custom_call" | custom-call | tf_op jit(solution)/shard_map/table_and_rows/pallas_call | solution.py:472
  (4 shorter events, 0.0 us)
Async XLA Ops:
  2.6 10.8 %collective-permute-start.2 = (bf16[528,128]{1,0:T(8,128)(2,1)}, bf16[528,128]{1,0:T(8,128)(2,1)S(1)}, u32[]{:S(2)}, u32[]{:S(2)}) collective-permute-start(bf16[528,128]{1,0:T(8,128)(2,1)} %get-tuple-element.24), channel_id=1, source_target_pairs={{0,8},{4,12},{8,0},{12,4},{1,9},{5,13},{9,1},{13,5},{2,10},{6,14},... | collective-permute-start | bytes 405512 | tf_op jit(solution)/shard_map/ppermute | solution.py:384
  6.6 9.0 %collective-permute-start = (bf16[528,128]{1,0:T(8,128)(2,1)}, bf16[528,128]{1,0:T(8,128)(2,1)S(1)}, u32[]{:S(2)}, u32[]{:S(2)}) collective-permute-start(bf16[528,128]{1,0:T(8,128)(2,1)} %get-tuple-element.24), channel_id=1, source_target_pairs={{0,2},{2,0},{1,3},{3,1},{4,6},{6,4},{5,7},{7,5},{8,10},{10,8},{9,1... | collective-permute-start | bytes 405512 | tf_op jit(solution)/shard_map/ppermute | solution.py:384
  8.1 7.5 %collective-permute-start.4 = (bf16[528,128]{1,0:T(8,128)(2,1)}, bf16[528,128]{1,0:T(8,128)(2,1)S(1)}, u32[]{:S(2)}, u32[]{:S(2)}) collective-permute-start(bf16[528,128]{1,0:T(8,128)(2,1)} %get-tuple-element.24), channel_id=1, source_target_pairs={{0,4},{4,0},{8,12},{12,8},{1,5},{5,1},{9,13},{13,9},{2,6},{6,2},{1... | collective-permute-start | bytes 405512 | tf_op jit(solution)/shard_map/ppermute | solution.py:384
  9.7 0.9 %copy-start = (bf16[528,128]{1,0:T(8,128)(2,1)S(1)}, bf16[528,128]{1,0:T(8,128)(2,1)}, u32[]{:S(2)}) copy-start(bf16[528,128]{1,0:T(8,128)(2,1)} %get-tuple-element.24) | copy-start | bytes 405508
  10.6 0.7 %copy-start.2 = (f32[24,128]{1,0:T(8,128)S(1)}, f32[24,128]{1,0:T(8,128)}, u32[]{:S(2)}) copy-start(f32[24,128]{1,0:T(8,128)} %get-tuple-element.23.refs_0_) | copy-start | bytes 36868
  13.4 5.6 %collective-permute-start.3 = (bf16[528,128]{1,0:T(8,128)(2,1)S(1)}, bf16[528,128]{1,0:T(8,128)(2,1)S(1)}, u32[]{:S(2)}, u32[]{:S(2)}) collective-permute-start(bf16[528,128]{1,0:T(8,128)(2,1)S(1)} %collective-permute-done.2), channel_id=1, source_target_pairs={{0,4},{4,0},{8,12},{12,8},{1,5},{5,1},{9,13},{13,9},{2,6},{6,2},{1... | collective-permute-start | bytes 405512 | tf_op jit(solution)/shard_map/ppermute | solution.py:384
  14.2 5.8 %collective-permute-start.5 = (bf16[528,128]{1,0:T(8,128)(2,1)S(1)}, bf16[528,128]{1,0:T(8,128)(2,1)S(1)}, u32[]{:S(2)}, u32[]{:S(2)}) collective-permute-start(bf16[528,128]{1,0:T(8,128)(2,1)S(1)} %collective-permute-done.2), channel_id=1, source_target_pairs={{0,2},{2,0},{1,3},{3,1},{4,6},{6,4},{5,7},{7,5},{8,10},{10,8},{9,1... | collective-permute-start | bytes 405512 | tf_op jit(solution)/shard_map/ppermute | solution.py:384
  15.7 0.7 %copy-start.3 = (f32[24,128]{1,0:T(8,128)S(1)}, f32[24,128]{1,0:T(8,128)}, u32[]{:S(2)}) copy-start(f32[24,128]{1,0:T(8,128)} %get-tuple-element.23.refs_0_) | copy-start | bytes 36868
  17.6 5.1 %collective-permute-start.1 = (bf16[528,128]{1,0:T(8,128)(2,1)S(1)}, bf16[528,128]{1,0:T(8,128)(2,1)S(1)}, u32[]{:S(2)}, u32[]{:S(2)}) collective-permute-start(bf16[528,128]{1,0:T(8,128)(2,1)S(1)} %collective-permute-done), channel_id=1, source_target_pairs={{0,4},{4,0},{8,12},{12,8},{1,5},{5,1},{9,13},{13,9},{2,6},{6,2},{1... | collective-permute-start | bytes 405512 | tf_op jit(solution)/shard_map/ppermute | solution.py:384
  19.0 5.0 %collective-permute-start.6 = (bf16[528,128]{1,0:T(8,128)(2,1)S(1)}, bf16[528,128]{1,0:T(8,128)(2,1)S(1)}, u32[]{:S(2)}, u32[]{:S(2)}) collective-permute-start(bf16[528,128]{1,0:T(8,128)(2,1)S(1)} %collective-permute-done.3), channel_id=1, source_target_pairs={{0,2},{2,0},{1,3},{3,1},{4,6},{6,4},{5,7},{7,5},{8,10},{10,8},{9,1... | collective-permute-start | bytes 405512 | tf_op jit(solution)/shard_map/ppermute | solution.py:384
  20.0 4.0 %copy-start.1 = (bf16[528,128]{1,0:T(8,128)(2,1)S(1)}, bf16[528,128]{1,0:T(8,128)(2,1)}, u32[]{:S(2)}) copy-start(bf16[528,128]{1,0:T(8,128)(2,1)} %get-tuple-element.24) | copy-start | bytes 405508

commit v16 on v14

--- a/solution.py
+++ b/solution.py
@@ -320,23 +320,25 @@
     scale, reach = wide_columns(root(z, distance), reach - F32(TOP) if z.narrow else reach)
     position, span_start = (None, None) if z.narrow else wide_columns(place, own_ref[z.chunks : 2 * z.chunks, :])
     kind = short if z.narrow else lambda row: row
-    total = jnp.zeros((z.rows, LANES), F32)
-    for shift in range(z.shifts):
-        part = slice(shift * z.rows, (shift + 1) * z.rows)
-        top = high_ref[part, :]
-        if z.narrow:
-            span = short(reach)
-        else:
-            low = position - reach
-            span = top - (jnp.maximum(low, span_start) if shift == 0 else low)
-
-        def add(s, value):
-            rows = pieces.place(s)
-            mask = within(top, span, [kind(rows[r : r + 1]) for r in range(z.chunks)])
-            return value + dot(mask, pieces.rows(s))
-
-        total += loop(pieces.count, add, jnp.zeros((z.rows, LANES), F32)) * factor_ref[part, :]
-    feature_ref[...] = (total * scale).astype(BF16)
+    for t in range(0, z.rows, LATE_BLOCK):
+        block = slice(t, t + LATE_BLOCK)
+        total = jnp.zeros((LATE_BLOCK, LANES), F32)
+        for shift in range(z.shifts):
+            part = slice(shift * z.rows + t, shift * z.rows + t + LATE_BLOCK)
+            top = high_ref[part, :]
+            if z.narrow:
+                span = short(reach[block])
+            else:
+                low = position[block] - reach[block]
+                span = top - (jnp.maximum(low, span_start[block]) if shift == 0 else low)
+
+            def add(s, value):
+                rows = pieces.place(s)
+                mask = within(top, span, [kind(rows[r : r + 1]) for r in range(z.chunks)])
+                return value + dot(mask, pieces.rows(s))
+
+            total += loop(pieces.count, add, jnp.zeros((LATE_BLOCK, LANES), F32)) * factor_ref[part, :]
+        feature_ref[block, :] = (total * scale[block]).astype(BF16)
     send(feature_ref, feature_out, slice(0, z.rows))
 
     pack(z, last, base, marks_ref, codes_ref, rows_ref, from_ref)

time: 27.7 us -> 28.2 us (1.018)
  Pallas kernels: 10.3 us -> 10.9 us
    pallas_call x1, Pallas kernels: 3.93 us -> 4.49 us  [on_device(): pl.pallas_call(functools.partial(late_kernel, z, earlier, form, len(late)...]
where the time goes in v16:
time: 28.2 us; the launch traced here: 28 us
  starting transfers between devices  12.7 us (45%)
  Pallas kernels  10.9 us (39%)
  waiting for transfers between devices  2.05 us (7%)
  local copies, waits for them, and re-layouts  1.66 us (6%)
  between operations  0.69 us (2%)
    ppermute x7, starting transfers between devices, swap(): lax.ppermute(block, axis, [(i, i ^ distance) for i in range(lax.axis_size...  12.7 us
    pallas_call x1, Pallas kernels, on_device(): pl.pallas_call(functools.partial(late_kernel, z, earlier, form, len(late)...  4.49 us
    pallas_call x3, Pallas kernels, sums(): pl.pallas_call(functools.partial(early_kernel, z, form, len(before)), out...  4.45 us
    ppermute x7, waiting for transfers between devices, swap(): lax.ppermute(block, axis, [(i, i ^ distance) for i in range(lax.axis_size...  2.05 us
    pallas_call x1, Pallas kernels, on_device(): pl.pallas_call(functools.partial(send_kernel, z), out_shape=(shape((block...  1.96 us
    unnamed x8, local copies, waits for them, and re-layouts  1.66 us
  transfers between devices with their start and end apart: 7, of which 3 were waited for; matrix products, arithmetic and copies ran while one was open for 0% of the time, Pallas kernels for 16%

profile of v16, /device:TPU:0, one launch (start us, length us, event | category | flops | bytes accessed | tf_op | source)
XLA Modules:
  0.0 28.0 jit_solution(8442471929277819564)
XLA Ops:
  0.6 2.0 %weigh.1 = (bf16[528,128]{1,0:T(8,128)(2,1)}, f32[24,128]{1,0:T(8,128)}) custom-call(s32[1]{0:T(128)} %bitcast.me_ref, f32[4]{0:T(128)} %rate_ref.1, bf16[512,128]{1,0:T(8,128)(2,1)} %events_ref.1, f32[4,128]{1,0:T(4,128)} %bitcast.28, s32[4,128]{1,0:T(4,128)} %bitcast.29, s32[4,128]{1,0:T(4,128)} %bitcast.30, s32[32,128]{1,0:T(8,128)} %bitcast.27), custom_call_target="tpu_custom_call" | custom-call | tf_op jit(solution)/shard_map/weigh/pallas_call | solution.py:409
  2.6 4.0 %collective-permute-start = (bf16[528,128]{1,0:T(8,128)(2,1)}, bf16[528,128]{1,0:T(8,128)(2,1)S(1)}, u32[]{:S(2)}, u32[]{:S(2)}) collective-permute-start(bf16[528,128]{1,0:T(8,128)(2,1)} %get-tuple-element.21), channel_id=1, source_target_pairs={{0,8},{4,12},{8,0},{12,4},{1,9},{5,13},{9,1},{13,5},{2,10},{6,14},... | collective-permute-start | bytes 405512 | tf_op jit(solution)/shard_map/ppermute | solution.py:386
  6.6 1.5 %collective-permute-start.2 = (bf16[528,128]{1,0:T(8,128)(2,1)}, bf16[528,128]{1,0:T(8,128)(2,1)S(1)}, u32[]{:S(2)}, u32[]{:S(2)}) collective-permute-start(bf16[528,128]{1,0:T(8,128)(2,1)} %get-tuple-element.21), channel_id=1, source_target_pairs={{0,2},{2,0},{1,3},{3,1},{4,6},{6,4},{5,7},{7,5},{8,10},{10,8},{9,1... | collective-permute-start | bytes 405512 | tf_op jit(solution)/shard_map/ppermute | solution.py:386
  8.1 1.6 %collective-permute-start.3 = (bf16[528,128]{1,0:T(8,128)(2,1)}, bf16[528,128]{1,0:T(8,128)(2,1)S(1)}, u32[]{:S(2)}, u32[]{:S(2)}) collective-permute-start(bf16[528,128]{1,0:T(8,128)(2,1)} %get-tuple-element.21), channel_id=1, source_target_pairs={{0,4},{4,0},{8,12},{12,8},{1,5},{5,1},{9,13},{13,9},{2,6},{6,2},{1... | collective-permute-start | bytes 405512 | tf_op jit(solution)/shard_map/ppermute | solution.py:386
  9.7 0.9 %copy-done = bf16[528,128]{1,0:T(8,128)(2,1)S(1)} copy-done((bf16[528,128]{1,0:T(8,128)(2,1)S(1)}, bf16[528,128]{1,0:T(8,128)(2,1)}, u32[]{:S(2)}) %copy-start) | copy-done | bytes 135192
  10.6 0.7 %copy-done.2 = f32[24,128]{1,0:T(8,128)S(1)} copy-done((f32[24,128]{1,0:T(8,128)S(1)}, f32[24,128]{1,0:T(8,128)}, u32[]{:S(2)}) %copy-start.2) | copy-done | bytes 12312
  11.4 1.6 %first_sums.1 = (f32[4096,128]{1,0:T(8,128)S(1)}, f32[4096,128]{1,0:T(8,128)S(1)}, bf16[1024,128]{1,0:T(8,128)(2,1)S(1)}, f32[8,128]{1,0:T(8,128)S(1)}, s16[512,...) custom-call(f32[24,128]{1,0:T(8,128)S(1)} %copy-done.2, bf16[1,528,128]{2,1,0:T(8,128)(2,1)S(1)} %bitcast.23), custom_call_target="tpu_custom_call" | custom-call | flops 1 | tf_op jit(solution)/shard_map/first_sums/pallas_call | solution.py:434
  12.9 0.5 %collective-permute-done = bf16[528,128]{1,0:T(8,128)(2,1)S(1)} collective-permute-done((bf16[528,128]{1,0:T(8,128)(2,1)}, bf16[528,128]{1,0:T(8,128)(2,1)S(1)}, u32[]{:S(2)}, u32[]{:S(2)}) %collective-permute-start) | collective-permute-done | bytes 135200 | tf_op jit(solution)/shard_map/ppermute | solution.py:386
  13.4 0.8 %collective-permute-start.1 = (bf16[528,128]{1,0:T(8,128)(2,1)S(1)}, bf16[528,128]{1,0:T(8,128)(2,1)S(1)}, u32[]{:S(2)}, u32[]{:S(2)}) collective-permute-start(bf16[528,128]{1,0:T(8,128)(2,1)S(1)} %collective-permute-done), channel_id=1, source_target_pairs={{0,4},{4,0},{8,12},{12,8},{1,5},{5,1},{9,13},{13,9},{2,6},{6,2},{1... | collective-permute-start | bytes 405512 | tf_op jit(solution)/shard_map/ppermute | solution.py:386
  14.2 1.4 %collective-permute-start.4 = (bf16[528,128]{1,0:T(8,128)(2,1)S(1)}, bf16[528,128]{1,0:T(8,128)(2,1)S(1)}, u32[]{:S(2)}, u32[]{:S(2)}) collective-permute-start(bf16[528,128]{1,0:T(8,128)(2,1)S(1)} %collective-permute-done), channel_id=1, source_target_pairs={{0,2},{2,0},{1,3},{3,1},{4,6},{6,4},{5,7},{7,5},{8,10},{10,8},{9,1... | collective-permute-start | bytes 405512 | tf_op jit(solution)/shard_map/ppermute | solution.py:386
  15.6 0.0 collective-permute-done.2
  15.7 0.0 collective-permute-done.3
  15.7 0.0 copy-start.3
  15.7 1.2 %more_sums.2 = (f32[4096,128]{1,0:T(8,128)S(1)}, bf16[1024,128]{1,0:T(8,128)(2,1)S(1)}, f32[8,128]{1,0:T(8,128)S(1)}) custom-call(f32[24,128]{1,0:T(8,128)S(1)} %copy-done.2, bf16[1,528,128]{2,1,0:T(8,128)(2,1)S(1)} %bitcast.15, bf16[1,528,128]{2,1,0:T(8,128)(2,1)S(1)} %bitcast.17, f32[4096,128]{1,0:T(8,128)S(1)} %get-tuple-element.24.refs_3_), custom_call_target="tpu_custom_call" | custom-call | flops 2 | tf_op jit(solution)/shard_map/more_sums/pallas_call | solution.py:434
  16.9 1.4 %collective-permute-start.5 = (bf16[528,128]{1,0:T(8,128)(2,1)S(1)}, bf16[528,128]{1,0:T(8,128)(2,1)S(1)}, u32[]{:S(2)}, u32[]{:S(2)}) collective-permute-start(bf16[528,128]{1,0:T(8,128)(2,1)S(1)} %collective-permute-done.2), channel_id=1, source_target_pairs={{0,4},{4,0},{8,12},{12,8},{1,5},{5,1},{9,13},{13,9},{2,6},{6,2},{1... | collective-permute-start | bytes 405512 | tf_op jit(solution)/shard_map/ppermute | solution.py:386
  18.3 0.1 collective-permute-done.1
  18.4 1.9 %collective-permute-start.6 = (bf16[528,128]{1,0:T(8,128)(2,1)S(1)}, bf16[528,128]{1,0:T(8,128)(2,1)S(1)}, u32[]{:S(2)}, u32[]{:S(2)}) collective-permute-start(bf16[528,128]{1,0:T(8,128)(2,1)S(1)} %collective-permute-done.1), channel_id=1, source_target_pairs={{0,2},{2,0},{1,3},{3,1},{4,6},{6,4},{5,7},{7,5},{8,10},{10,8},{9,1... | collective-permute-start | bytes 405512 | tf_op jit(solution)/shard_map/ppermute | solution.py:386
  20.4 0.0 collective-permute-done.4
  20.4 1.7 %more_sums.3 = (f32[4096,128]{1,0:T(8,128)S(1)}, bf16[1024,128]{1,0:T(8,128)(2,1)S(1)}, f32[8,128]{1,0:T(8,128)S(1)}) custom-call(f32[24,128]{1,0:T(8,128)S(1)} %copy-done.2, bf16[1,528,128]{2,1,0:T(8,128)(2,1)S(1)} %bitcast.13, bf16[1,528,128]{2,1,0:T(8,128)(2,1)S(1)} %bitcast.19, bf16[1,528,128]{2,1,0:T(8,128)(2,1)S(1)} %bitcast.21, ...), custom_call_target="tpu_custom_call" | custom-call | flops 3 | tf_op jit(solution)/shard_map/more_sums/pallas_call | solution.py:434
  22.0 0.0 collective-permute-done.5
  22.1 1.4 %collective-permute-done.6 = bf16[528,128]{1,0:T(8,128)(2,1)S(1)} collective-permute-done((bf16[528,128]{1,0:T(8,128)(2,1)S(1)}, bf16[528,128]{1,0:T(8,128)(2,1)S(1)}, u32[]{:S(2)}, u32[]{:S(2)}) %collective-permute-start.6) | collective-permute-done | bytes 135200 | tf_op jit(solution)/shard_map/ppermute | solution.py:386
  23.5 0.0 copy-done.1
  23.5 0.0 copy-done.3
  23.5 4.5 %table_and_rows.1 = (bf16[4096,128]{1,0:T(8,128)(2,1)}, bf16[512,128]{1,0:T(8,128)(2,1)}) custom-call(f32[24,128]{1,0:T(8,128)S(1)} %copy-done.3, f32[4096,128]{1,0:T(8,128)S(1)} %get-tuple-element.28.refs_1_, f32[4096,128]{1,0:T(8,128)S(1)} %get-tuple-element.29.refs_2_, s16[512,128]{1,0:T(8,128)(2,1)S(1)} %get-tuple-element.30.refs_3_, ...), custom_call_target="tpu_custom_call" | custom-call | tf_op jit(solution)/shard_map/table_and_rows/pallas_call | solution.py:473
  (3 shorter events, 0.0 us)
Async XLA Ops:
  2.6 10.8 %collective-permute-start = (bf16[528,128]{1,0:T(8,128)(2,1)}, bf16[528,128]{1,0:T(8,128)(2,1)S(1)}, u32[]{:S(2)}, u32[]{:S(2)}) collective-permute-start(bf16[528,128]{1,0:T(8,128)(2,1)} %get-tuple-element.21), channel_id=1, source_target_pairs={{0,8},{4,12},{8,0},{12,4},{1,9},{5,13},{9,1},{13,5},{2,10},{6,14},... | collective-permute-start | bytes 405512 | tf_op jit(solution)/shard_map/ppermute | solution.py:386
  6.6 9.0 %collective-permute-start.2 = (bf16[528,128]{1,0:T(8,128)(2,1)}, bf16[528,128]{1,0:T(8,128)(2,1)S(1)}, u32[]{:S(2)}, u32[]{:S(2)}) collective-permute-start(bf16[528,128]{1,0:T(8,128)(2,1)} %get-tuple-element.21), channel_id=1, source_target_pairs={{0,2},{2,0},{1,3},{3,1},{4,6},{6,4},{5,7},{7,5},{8,10},{10,8},{9,1... | collective-permute-start | bytes 405512 | tf_op jit(solution)/shard_map/ppermute | solution.py:386
  8.1 7.5 %collective-permute-start.3 = (bf16[528,128]{1,0:T(8,128)(2,1)}, bf16[528,128]{1,0:T(8,128)(2,1)S(1)}, u32[]{:S(2)}, u32[]{:S(2)}) collective-permute-start(bf16[528,128]{1,0:T(8,128)(2,1)} %get-tuple-element.21), channel_id=1, source_target_pairs={{0,4},{4,0},{8,12},{12,8},{1,5},{5,1},{9,13},{13,9},{2,6},{6,2},{1... | collective-permute-start | bytes 405512 | tf_op jit(solution)/shard_map/ppermute | solution.py:386
  9.7 0.9 %copy-start = (bf16[528,128]{1,0:T(8,128)(2,1)S(1)}, bf16[528,128]{1,0:T(8,128)(2,1)}, u32[]{:S(2)}) copy-start(bf16[528,128]{1,0:T(8,128)(2,1)} %get-tuple-element.21) | copy-start | bytes 405508
  10.6 0.7 %copy-start.2 = (f32[24,128]{1,0:T(8,128)S(1)}, f32[24,128]{1,0:T(8,128)}, u32[]{:S(2)}) copy-start(f32[24,128]{1,0:T(8,128)} %get-tuple-element.20.refs_0_) | copy-start | bytes 36868
  13.4 5.0 %collective-permute-start.1 = (bf16[528,128]{1,0:T(8,128)(2,1)S(1)}, bf16[528,128]{1,0:T(8,128)(2,1)S(1)}, u32[]{:S(2)}, u32[]{:S(2)}) collective-permute-start(bf16[528,128]{1,0:T(8,128)(2,1)S(1)} %collective-permute-done), channel_id=1, source_target_pairs={{0,4},{4,0},{8,12},{12,8},{1,5},{5,1},{9,13},{13,9},{2,6},{6,2},{1... | collective-permute-start | bytes 405512 | tf_op jit(solution)/shard_map/ppermute | solution.py:386
  14.2 6.2 %collective-permute-start.4 = (bf16[528,128]{1,0:T(8,128)(2,1)S(1)}, bf16[528,128]{1,0:T(8,128)(2,1)S(1)}, u32[]{:S(2)}, u32[]{:S(2)}) collective-permute-start(bf16[528,128]{1,0:T(8,128)(2,1)S(1)} %collective-permute-done), channel_id=1, source_target_pairs={{0,2},{2,0},{1,3},{3,1},{4,6},{6,4},{5,7},{7,5},{8,10},{10,8},{9,1... | collective-permute-start | bytes 405512 | tf_op jit(solution)/shard_map/ppermute | solution.py:386
  15.7 7.8 %copy-start.1 = (bf16[528,128]{1,0:T(8,128)(2,1)S(1)}, bf16[528,128]{1,0:T(8,128)(2,1)}, u32[]{:S(2)}) copy-start(bf16[528,128]{1,0:T(8,128)(2,1)} %get-tuple-element.21) | copy-start | bytes 405508
  15.7 7.8 %copy-start.3 = (f32[24,128]{1,0:T(8,128)S(1)}, f32[24,128]{1,0:T(8,128)}, u32[]{:S(2)}) copy-start(f32[24,128]{1,0:T(8,128)} %get-tuple-element.20.refs_0_) | copy-start | bytes 36868
  16.9 5.2 %collective-permute-start.5 = (bf16[528,128]{1,0:T(8,128)(2,1)S(1)}, bf16[528,128]{1,0:T(8,128)(2,1)S(1)}, u32[]{:S(2)}, u32[]{:S(2)}) collective-permute-start(bf16[528,128]{1,0:T(8,128)(2,1)S(1)} %collective-permute-done.2), channel_id=1, source_target_pairs={{0,4},{4,0},{8,12},{12,8},{1,5},{5,1},{9,13},{13,9},{2,6},{6,2},{1... | collective-permute-start | bytes 405512 | tf_op jit(solution)/shard_map/ppermute | solution.py:386
  18.4 5.0 %collective-permute-start.6 = (bf16[528,128]{1,0:T(8,128)(2,1)S(1)}, bf16[528,128]{1,0:T(8,128)(2,1)S(1)}, u32[]{:S(2)}, u32[]{:S(2)}) collective-permute-start(bf16[528,128]{1,0:T(8,128)(2,1)S(1)} %collective-permute-done.1), channel_id=1, source_target_pairs={{0,2},{2,0},{1,3},{3,1},{4,6},{6,4},{5,7},{7,5},{8,10},{10,8},{9,1... | collective-permute-start | bytes 405512 | tf_op jit(solution)/shard_map/ppermute | solution.py:386

commit v17 on v14

--- a/solution.py
+++ b/solution.py
@@ -217,16 +217,27 @@
             from_ref[line : line + 1, :] = F32(LANES) * high + low
 
 
+def tiles(values):
+    return values.reshape(values.shape[0] // 16, 16, LANES)
+
+
+def tile_of(row):
+    return jnp.broadcast_to(row.astype(I32), (16, LANES)).astype(I16)
+
+
 def held(position, bounds):
-    one, nothing = BF16(1), BF16(0)
-    masks = [jnp.where(position - first <= length, one, nothing) for first, length in bounds]
-    return jnp.concatenate(masks, axis=1)
+    one, nothing, count = BF16(1), BF16(0), position.shape[0]
+    position = tiles(position)
+    masks = [jnp.where(position - first[None] <= length[None], one, nothing) for first, length in bounds]
+    return jnp.concatenate([mask.reshape(count, LANES) for mask in masks], axis=1)
 
 
 def within(top, span, rows):
     if top.dtype == I16:
-        one, nothing = BF16(1), BF16(0)
-        return jnp.concatenate([jnp.where(top - row <= span, one, nothing) for row in rows], axis=1)
+        one, nothing, count = BF16(1), BF16(0), top.shape[0]
+        top, span = tiles(top), tiles(span)
+        masks = [jnp.where(top - tile_of(row)[None] <= span, one, nothing) for row in rows]
+        return jnp.concatenate([mask.reshape(count, LANES) for mask in masks], axis=1)
     return jnp.concatenate([ones_where((top - row >= 0) & (top - row <= span)) for row in rows], axis=1)
 
 
@@ -266,7 +277,7 @@
     bounds = []
     for g in range(pieces.groups if pieces.count else 0):
         begin = from_ref[g : g + 1, :]
-        bounds.append((short(begin), short(runs.until(begin) - begin - F32(TOP))))
+        bounds.append((tile_of(begin), tile_of(runs.until(begin) - begin - F32(TOP))))
     for b in range(z.slots // BLOCK):
         part = slice(b * BLOCK, (b + 1) * BLOCK)
         if bounds:
@@ -319,7 +330,6 @@
     reach = jnp.minimum(distance, F32(z.window))
     scale, reach = wide_columns(root(z, distance), reach - F32(TOP) if z.narrow else reach)
     position, span_start = (None, None) if z.narrow else wide_columns(place, own_ref[z.chunks : 2 * z.chunks, :])
-    kind = short if z.narrow else lambda row: row
     total = jnp.zeros((z.rows, LANES), F32)
     for shift in range(z.shifts):
         part = slice(shift * z.rows, (shift + 1) * z.rows)
@@ -332,7 +342,7 @@
 
         def add(s, value):
             rows = pieces.place(s)
-            mask = within(top, span, [kind(rows[r : r + 1]) for r in range(z.chunks)])
+            mask = within(top, span, [rows[r : r + 1] for r in range(z.chunks)])
             return value + dot(mask, pieces.rows(s))
 
         total += loop(pieces.count, add, jnp.zeros((z.rows, LANES), F32)) * factor_ref[part, :]
@@ -349,7 +359,7 @@
     for ref, first, lines in listed:
         for g in range(first, first + lines):
             begin = ref[g : g + 1, :]
-            bounds.append((short(begin), short(runs.until(begin + base) - (begin + base) - F32(TOP))))
+            bounds.append((tile_of(begin), tile_of(runs.until(begin + base) - (begin + base) - F32(TOP))))
     n = last.groups
     own_rows = rows_ref[0 : n * LANES, :]
     tail_rows = [rows_ref[n * LANES : 2 * n * LANES, :]]

time: 27.7 us -> 27.7 us (level)
  no operation moved by 1% of the time
where the time goes in v17:
time: 27.7 us; the launch traced here: 27.4 us
  starting transfers between devices  12.7 us (46%)
  Pallas kernels  10.3 us (37%)
  waiting for transfers between devices  2.06 us (7%)
  local copies, waits for them, and re-layouts  1.66 us (6%)
  between operations  0.69 us (2%)
    ppermute x7, starting transfers between devices, swap(): lax.ppermute(block, axis, [(i, i ^ distance) for i in range(lax.axis_size...  12.7 us
    pallas_call x3, Pallas kernels, sums(): pl.pallas_call(functools.partial(early_kernel, z, form, len(before)), out...  4.44 us
    pallas_call x1, Pallas kernels, on_device(): pl.pallas_call(functools.partial(late_kernel, z, earlier, form, len(late)...  3.94 us
    ppermute x7, waiting for transfers between devices, swap(): lax.ppermute(block, axis, [(i, i ^ distance) for i in range(lax.axis_size...  2.06 us
    pallas_call x1, Pallas kernels, on_device(): pl.pallas_call(functools.partial(send_kernel, z), out_shape=(shape((block...  1.96 us
    unnamed x8, local copies, waits for them, and re-layouts  1.66 us
  transfers between devices with their start and end apart: 7, of which 3 were waited for; matrix products, arithmetic and copies ran while one was open for 0% of the time, Pallas kernels for 16%

profile of v17, /device:TPU:0, one launch (start us, length us, event | category | flops | bytes accessed | tf_op | source)
XLA Modules:
  0.0 27.4 jit_solution(9914277711361948884)
XLA Ops:
  0.6 2.0 %weigh.1 = (bf16[528,128]{1,0:T(8,128)(2,1)}, f32[24,128]{1,0:T(8,128)}) custom-call(s32[1]{0:T(128)} %bitcast.me_ref, f32[4]{0:T(128)} %rate_ref.1, bf16[512,128]{1,0:T(8,128)(2,1)} %events_ref.1, f32[4,128]{1,0:T(4,128)} %bitcast.28, s32[4,128]{1,0:T(4,128)} %bitcast.29, s32[4,128]{1,0:T(4,128)} %bitcast.30, s32[32,128]{1,0:T(8,128)} %bitcast.27), custom_call_target="tpu_custom_call" | custom-call | tf_op jit(solution)/shard_map/weigh/pallas_call | solution.py:417
  2.6 4.0 %collective-permute-start = (bf16[528,128]{1,0:T(8,128)(2,1)}, bf16[528,128]{1,0:T(8,128)(2,1)S(1)}, u32[]{:S(2)}, u32[]{:S(2)}) collective-permute-start(bf16[528,128]{1,0:T(8,128)(2,1)} %get-tuple-element.21), channel_id=1, source_target_pairs={{0,8},{4,12},{8,0},{12,4},{1,9},{5,13},{9,1},{13,5},{2,10},{6,14},... | collective-permute-start | bytes 405512 | tf_op jit(solution)/shard_map/ppermute | solution.py:394
  6.6 1.5 %collective-permute-start.2 = (bf16[528,128]{1,0:T(8,128)(2,1)}, bf16[528,128]{1,0:T(8,128)(2,1)S(1)}, u32[]{:S(2)}, u32[]{:S(2)}) collective-permute-start(bf16[528,128]{1,0:T(8,128)(2,1)} %get-tuple-element.21), channel_id=1, source_target_pairs={{0,2},{2,0},{1,3},{3,1},{4,6},{6,4},{5,7},{7,5},{8,10},{10,8},{9,1... | collective-permute-start | bytes 405512 | tf_op jit(solution)/shard_map/ppermute | solution.py:394
  8.1 1.6 %collective-permute-start.3 = (bf16[528,128]{1,0:T(8,128)(2,1)}, bf16[528,128]{1,0:T(8,128)(2,1)S(1)}, u32[]{:S(2)}, u32[]{:S(2)}) collective-permute-start(bf16[528,128]{1,0:T(8,128)(2,1)} %get-tuple-element.21), channel_id=1, source_target_pairs={{0,4},{4,0},{8,12},{12,8},{1,5},{5,1},{9,13},{13,9},{2,6},{6,2},{1... | collective-permute-start | bytes 405512 | tf_op jit(solution)/shard_map/ppermute | solution.py:394
  9.7 0.9 %copy-done = bf16[528,128]{1,0:T(8,128)(2,1)S(1)} copy-done((bf16[528,128]{1,0:T(8,128)(2,1)S(1)}, bf16[528,128]{1,0:T(8,128)(2,1)}, u32[]{:S(2)}) %copy-start) | copy-done | bytes 135192
  10.6 0.7 %copy-done.2 = f32[24,128]{1,0:T(8,128)S(1)} copy-done((f32[24,128]{1,0:T(8,128)S(1)}, f32[24,128]{1,0:T(8,128)}, u32[]{:S(2)}) %copy-start.2) | copy-done | bytes 12312
  11.4 1.6 %first_sums.1 = (f32[4096,128]{1,0:T(8,128)S(1)}, f32[4096,128]{1,0:T(8,128)S(1)}, bf16[1024,128]{1,0:T(8,128)(2,1)S(1)}, f32[8,128]{1,0:T(8,128)S(1)}, s16[512,...) custom-call(f32[24,128]{1,0:T(8,128)S(1)} %copy-done.2, bf16[1,528,128]{2,1,0:T(8,128)(2,1)S(1)} %bitcast.23), custom_call_target="tpu_custom_call" | custom-call | flops 1 | tf_op jit(solution)/shard_map/first_sums/pallas_call | solution.py:442
  12.9 0.5 %collective-permute-done = bf16[528,128]{1,0:T(8,128)(2,1)S(1)} collective-permute-done((bf16[528,128]{1,0:T(8,128)(2,1)}, bf16[528,128]{1,0:T(8,128)(2,1)S(1)}, u32[]{:S(2)}, u32[]{:S(2)}) %collective-permute-start) | collective-permute-done | bytes 135200 | tf_op jit(solution)/shard_map/ppermute | solution.py:394
  13.4 0.8 %collective-permute-start.1 = (bf16[528,128]{1,0:T(8,128)(2,1)S(1)}, bf16[528,128]{1,0:T(8,128)(2,1)S(1)}, u32[]{:S(2)}, u32[]{:S(2)}) collective-permute-start(bf16[528,128]{1,0:T(8,128)(2,1)S(1)} %collective-permute-done), channel_id=1, source_target_pairs={{0,4},{4,0},{8,12},{12,8},{1,5},{5,1},{9,13},{13,9},{2,6},{6,2},{1... | collective-permute-start | bytes 405512 | tf_op jit(solution)/shard_map/ppermute | solution.py:394
  14.2 1.4 %collective-permute-start.4 = (bf16[528,128]{1,0:T(8,128)(2,1)S(1)}, bf16[528,128]{1,0:T(8,128)(2,1)S(1)}, u32[]{:S(2)}, u32[]{:S(2)}) collective-permute-start(bf16[528,128]{1,0:T(8,128)(2,1)S(1)} %collective-permute-done), channel_id=1, source_target_pairs={{0,2},{2,0},{1,3},{3,1},{4,6},{6,4},{5,7},{7,5},{8,10},{10,8},{9,1... | collective-permute-start | bytes 405512 | tf_op jit(solution)/shard_map/ppermute | solution.py:394
  15.6 0.0 collective-permute-done.2
  15.7 0.0 collective-permute-done.3
  15.7 0.0 copy-start.3
  15.7 1.2 %more_sums.2 = (f32[4096,128]{1,0:T(8,128)S(1)}, bf16[1024,128]{1,0:T(8,128)(2,1)S(1)}, f32[8,128]{1,0:T(8,128)S(1)}) custom-call(f32[24,128]{1,0:T(8,128)S(1)} %copy-done.2, bf16[1,528,128]{2,1,0:T(8,128)(2,1)S(1)} %bitcast.15, bf16[1,528,128]{2,1,0:T(8,128)(2,1)S(1)} %bitcast.17, f32[4096,128]{1,0:T(8,128)S(1)} %get-tuple-element.24.refs_3_), custom_call_target="tpu_custom_call" | custom-call | flops 2 | tf_op jit(solution)/shard_map/more_sums/pallas_call | solution.py:442
  16.9 1.4 %collective-permute-start.5 = (bf16[528,128]{1,0:T(8,128)(2,1)S(1)}, bf16[528,128]{1,0:T(8,128)(2,1)S(1)}, u32[]{:S(2)}, u32[]{:S(2)}) collective-permute-start(bf16[528,128]{1,0:T(8,128)(2,1)S(1)} %collective-permute-done.2), channel_id=1, source_target_pairs={{0,4},{4,0},{8,12},{12,8},{1,5},{5,1},{9,13},{13,9},{2,6},{6,2},{1... | collective-permute-start | bytes 405512 | tf_op jit(solution)/shard_map/ppermute | solution.py:394
  18.3 0.1 collective-permute-done.1
  18.4 1.9 %collective-permute-start.6 = (bf16[528,128]{1,0:T(8,128)(2,1)S(1)}, bf16[528,128]{1,0:T(8,128)(2,1)S(1)}, u32[]{:S(2)}, u32[]{:S(2)}) collective-permute-start(bf16[528,128]{1,0:T(8,128)(2,1)S(1)} %collective-permute-done.1), channel_id=1, source_target_pairs={{0,2},{2,0},{1,3},{3,1},{4,6},{6,4},{5,7},{7,5},{8,10},{10,8},{9,1... | collective-permute-start | bytes 405512 | tf_op jit(solution)/shard_map/ppermute | solution.py:394
  20.4 0.0 collective-permute-done.4
  20.4 1.7 %more_sums.3 = (f32[4096,128]{1,0:T(8,128)S(1)}, bf16[1024,128]{1,0:T(8,128)(2,1)S(1)}, f32[8,128]{1,0:T(8,128)S(1)}) custom-call(f32[24,128]{1,0:T(8,128)S(1)} %copy-done.2, bf16[1,528,128]{2,1,0:T(8,128)(2,1)S(1)} %bitcast.13, bf16[1,528,128]{2,1,0:T(8,128)(2,1)S(1)} %bitcast.19, bf16[1,528,128]{2,1,0:T(8,128)(2,1)S(1)} %bitcast.21, ...), custom_call_target="tpu_custom_call" | custom-call | flops 3 | tf_op jit(solution)/shard_map/more_sums/pallas_call | solution.py:442
  22.0 0.0 collective-permute-done.5
  22.1 1.4 %collective-permute-done.6 = bf16[528,128]{1,0:T(8,128)(2,1)S(1)} collective-permute-done((bf16[528,128]{1,0:T(8,128)(2,1)S(1)}, bf16[528,128]{1,0:T(8,128)(2,1)S(1)}, u32[]{:S(2)}, u32[]{:S(2)}) %collective-permute-start.6) | collective-permute-done | bytes 135200 | tf_op jit(solution)/shard_map/ppermute | solution.py:394
  23.5 0.0 copy-done.1
  23.5 0.0 copy-done.3
  23.5 3.9 %table_and_rows.1 = (bf16[4096,128]{1,0:T(8,128)(2,1)}, bf16[512,128]{1,0:T(8,128)(2,1)}) custom-call(f32[24,128]{1,0:T(8,128)S(1)} %copy-done.3, f32[4096,128]{1,0:T(8,128)S(1)} %get-tuple-element.28.refs_1_, f32[4096,128]{1,0:T(8,128)S(1)} %get-tuple-element.29.refs_2_, s16[512,128]{1,0:T(8,128)(2,1)S(1)} %get-tuple-element.30.refs_3_, ...), custom_call_target="tpu_custom_call" | custom-call | tf_op jit(solution)/shard_map/table_and_rows/pallas_call | solution.py:481
  (3 shorter events, 0.0 us)
Async XLA Ops:
  2.6 10.8 %collective-permute-start = (bf16[528,128]{1,0:T(8,128)(2,1)}, bf16[528,128]{1,0:T(8,128)(2,1)S(1)}, u32[]{:S(2)}, u32[]{:S(2)}) collective-permute-start(bf16[528,128]{1,0:T(8,128)(2,1)} %get-tuple-element.21), channel_id=1, source_target_pairs={{0,8},{4,12},{8,0},{12,4},{1,9},{5,13},{9,1},{13,5},{2,10},{6,14},... | collective-permute-start | bytes 405512 | tf_op jit(solution)/shard_map/ppermute | solution.py:394
  6.6 9.0 %collective-permute-start.2 = (bf16[528,128]{1,0:T(8,128)(2,1)}, bf16[528,128]{1,0:T(8,128)(2,1)S(1)}, u32[]{:S(2)}, u32[]{:S(2)}) collective-permute-start(bf16[528,128]{1,0:T(8,128)(2,1)} %get-tuple-element.21), channel_id=1, source_target_pairs={{0,2},{2,0},{1,3},{3,1},{4,6},{6,4},{5,7},{7,5},{8,10},{10,8},{9,1... | collective-permute-start | bytes 405512 | tf_op jit(solution)/shard_map/ppermute | solution.py:394
  8.1 7.5 %collective-permute-start.3 = (bf16[528,128]{1,0:T(8,128)(2,1)}, bf16[528,128]{1,0:T(8,128)(2,1)S(1)}, u32[]{:S(2)}, u32[]{:S(2)}) collective-permute-start(bf16[528,128]{1,0:T(8,128)(2,1)} %get-tuple-element.21), channel_id=1, source_target_pairs={{0,4},{4,0},{8,12},{12,8},{1,5},{5,1},{9,13},{13,9},{2,6},{6,2},{1... | collective-permute-start | bytes 405512 | tf_op jit(solution)/shard_map/ppermute | solution.py:394
  9.7 0.9 %copy-start = (bf16[528,128]{1,0:T(8,128)(2,1)S(1)}, bf16[528,128]{1,0:T(8,128)(2,1)}, u32[]{:S(2)}) copy-start(bf16[528,128]{1,0:T(8,128)(2,1)} %get-tuple-element.21) | copy-start | bytes 405508
  10.6 0.7 %copy-start.2 = (f32[24,128]{1,0:T(8,128)S(1)}, f32[24,128]{1,0:T(8,128)}, u32[]{:S(2)}) copy-start(f32[24,128]{1,0:T(8,128)} %get-tuple-element.20.refs_0_) | copy-start | bytes 36868
  13.4 5.0 %collective-permute-start.1 = (bf16[528,128]{1,0:T(8,128)(2,1)S(1)}, bf16[528,128]{1,0:T(8,128)(2,1)S(1)}, u32[]{:S(2)}, u32[]{:S(2)}) collective-permute-start(bf16[528,128]{1,0:T(8,128)(2,1)S(1)} %collective-permute-done), channel_id=1, source_target_pairs={{0,4},{4,0},{8,12},{12,8},{1,5},{5,1},{9,13},{13,9},{2,6},{6,2},{1... | collective-permute-start | bytes 405512 | tf_op jit(solution)/shard_map/ppermute | solution.py:394
  14.2 6.2 %collective-permute-start.4 = (bf16[528,128]{1,0:T(8,128)(2,1)S(1)}, bf16[528,128]{1,0:T(8,128)(2,1)S(1)}, u32[]{:S(2)}, u32[]{:S(2)}) collective-permute-start(bf16[528,128]{1,0:T(8,128)(2,1)S(1)} %collective-permute-done), channel_id=1, source_target_pairs={{0,2},{2,0},{1,3},{3,1},{4,6},{6,4},{5,7},{7,5},{8,10},{10,8},{9,1... | collective-permute-start | bytes 405512 | tf_op jit(solution)/shard_map/ppermute | solution.py:394
  15.7 7.8 %copy-start.1 = (bf16[528,128]{1,0:T(8,128)(2,1)S(1)}, bf16[528,128]{1,0:T(8,128)(2,1)}, u32[]{:S(2)}) copy-start(bf16[528,128]{1,0:T(8,128)(2,1)} %get-tuple-element.21) | copy-start | bytes 405508
  15.7 7.8 %copy-start.3 = (f32[24,128]{1,0:T(8,128)S(1)}, f32[24,128]{1,0:T(8,128)}, u32[]{:S(2)}) copy-start(f32[24,128]{1,0:T(8,128)} %get-tuple-element.20.refs_0_) | copy-start | bytes 36868
  16.9 5.2 %collective-permute-start.5 = (bf16[528,128]{1,0:T(8,128)(2,1)S(1)}, bf16[528,128]{1,0:T(8,128)(2,1)S(1)}, u32[]{:S(2)}, u32[]{:S(2)}) collective-permute-start(bf16[528,128]{1,0:T(8,128)(2,1)S(1)} %collective-permute-done.2), channel_id=1, source_target_pairs={{0,4},{4,0},{8,12},{12,8},{1,5},{5,1},{9,13},{13,9},{2,6},{6,2},{1... | collective-permute-start | bytes 405512 | tf_op jit(solution)/shard_map/ppermute | solution.py:394
  18.4 5.0 %collective-permute-start.6 = (bf16[528,128]{1,0:T(8,128)(2,1)S(1)}, bf16[528,128]{1,0:T(8,128)(2,1)S(1)}, u32[]{:S(2)}, u32[]{:S(2)}) collective-permute-start(bf16[528,128]{1,0:T(8,128)(2,1)S(1)} %collective-permute-done.1), channel_id=1, source_target_pairs={{0,2},{2,0},{1,3},{3,1},{4,6},{6,4},{5,7},{7,5},{8,10},{10,8},{9,1... | collective-permute-start | bytes 405512 | tf_op jit(solution)/shard_map/ppermute | solution.py:394

commit v18 on v17

--- a/solution.py
+++ b/solution.py
@@ -18,6 +18,8 @@
 NT = (((1,), (1,)), ((), ()))
 BLOCK = 512
 LATE_BLOCK = 256
+TALL_FIRST = 512
+TALL = 1024
 COST = 1
 
 
@@ -365,27 +367,34 @@
     tail_rows = [rows_ref[n * LANES : 2 * n * LANES, :]]
     tail_rows += [ref[count * LANES : 2 * count * LANES, :] for (ref, _), count in zip(tails, earlier)]
     tail_rows = jnp.concatenate(tail_rows, axis=0)
-    for b in range(z.slots // LATE_BLOCK):
-        part = slice(b * LATE_BLOCK, (b + 1) * LATE_BLOCK)
-        position = (inner + (b * LATE_BLOCK - TOP)).astype(I16)
-        first = F32(b * LATE_BLOCK)
-        value = sums_ref[part, :]
-        if b * LATE_BLOCK >= z.window:
-            value = (value + dot(held(position, bounds[:n]), own_rows)) * scale_ref[part, :]
+    masks = lambda first, tall, bounds: held((iota((tall, LANES), 0) + (first - TOP)).astype(I16), bounds)
+    first = 0
+    while first < z.slots:
+        inside = first < z.window
+        tall = min(TALL_FIRST if inside else TALL, z.window)
+        if inside and z.shifts == 1:
+            sums = dot(masks(first, tall, bounds), jnp.concatenate([own_rows, tail_rows], axis=0))
         else:
-            own_fall = jnp.exp(-rate * (first + own_anchor))
-            if z.shifts == 1:
-                value += dot(held(position, bounds), jnp.concatenate([own_rows, tail_rows], axis=0))
-                value *= own_fall
+            sums = dot(masks(first, tall, bounds[:n]), own_rows)
+        if inside and z.shifts > 1:
+            tail_sums = dot(masks(first, tall, bounds[n:]), tail_rows)
+        for k in range(0, tall, LATE_BLOCK):
+            at = first + k
+            part = slice(at, at + LATE_BLOCK)
+            value = sums_ref[part, :] + sums[k : k + LATE_BLOCK]
+            if inside:
+                value *= jnp.exp(-rate * (F32(at) + own_anchor))
+                if z.shifts > 1:
+                    value += tail_sums[k : k + LATE_BLOCK] * jnp.exp(-rate * (F32(at) + tail_anchor))
+                start = scale_ref[part, :]
+                start = jnp.where(start > 0, start, first_start)
+                value = value * fall * root(z, inner.astype(F32) + F32(at) - start)
             else:
-                value = (value + dot(held(position, bounds[:n]), own_rows)) * own_fall
-                value += dot(held(position, bounds[n:]), tail_rows) * jnp.exp(-rate * (first + tail_anchor))
-            start = scale_ref[part, :]
-            start = jnp.where(start > 0, start, first_start)
-            value = value * fall * root(z, inner.astype(F32) + first - start)
-        table_ref[part, :] = value.astype(BF16)
-        if (b + 1) * LATE_BLOCK % z.window == 0:
-            send(table_ref, table_out, slice((b + 1) * LATE_BLOCK - z.window, (b + 1) * LATE_BLOCK))
+                value = value * scale_ref[part, :]
+            table_ref[part, :] = value.astype(BF16)
+        first += tall
+        if first % z.window == 0:
+            send(table_ref, table_out, slice(first - z.window, first))
     for copy in copies:
         copy.wait()
 

time: 27.7 us -> 27.7 us (level)
  no operation moved by 1% of the time
where the time goes in v18:
time: 27.7 us; the launch traced here: 27.5 us
  starting transfers between devices  12.7 us (46%)
  Pallas kernels  10.4 us (38%)
  waiting for transfers between devices  2.06 us (7%)
  local copies, waits for them, and re-layouts  1.66 us (6%)
  between operations  0.69 us (2%)
    ppermute x7, starting transfers between devices, swap(): lax.ppermute(block, axis, [(i, i ^ distance) for i in range(lax.axis_size...  12.7 us
    pallas_call x3, Pallas kernels, sums(): pl.pallas_call(functools.partial(early_kernel, z, form, len(before)), out...  4.44 us
    pallas_call x1, Pallas kernels, on_device(): pl.pallas_call(functools.partial(late_kernel, z, earlier, form, len(late)...  4 us
    ppermute x7, waiting for transfers between devices, swap(): lax.ppermute(block, axis, [(i, i ^ distance) for i in range(lax.axis_size...  2.06 us
    pallas_call x1, Pallas kernels, on_device(): pl.pallas_call(functools.partial(send_kernel, z), out_shape=(shape((block...  1.96 us
    unnamed x8, local copies, waits for them, and re-layouts  1.66 us
  transfers between devices with their start and end apart: 7, of which 3 were waited for; matrix products, arithmetic and copies ran while one was open for 0% of the time, Pallas kernels for 16%

profile of v18, /device:TPU:0, one launch (start us, length us, event | category | flops | bytes accessed | tf_op | source)
XLA Modules:
  0.0 27.5 jit_solution(4723924931752097277)
XLA Ops:
  0.6 2.0 %weigh.1 = (bf16[528,128]{1,0:T(8,128)(2,1)}, f32[24,128]{1,0:T(8,128)}) custom-call(s32[1]{0:T(128)} %bitcast.me_ref, f32[4]{0:T(128)} %rate_ref.1, bf16[512,128]{1,0:T(8,128)(2,1)} %events_ref.1, f32[4,128]{1,0:T(4,128)} %bitcast.28, s32[4,128]{1,0:T(4,128)} %bitcast.29, s32[4,128]{1,0:T(4,128)} %bitcast.30, s32[32,128]{1,0:T(8,128)} %bitcast.27), custom_call_target="tpu_custom_call" | custom-call | tf_op jit(solution)/shard_map/weigh/pallas_call | solution.py:426
  2.6 4.0 %collective-permute-start = (bf16[528,128]{1,0:T(8,128)(2,1)}, bf16[528,128]{1,0:T(8,128)(2,1)S(1)}, u32[]{:S(2)}, u32[]{:S(2)}) collective-permute-start(bf16[528,128]{1,0:T(8,128)(2,1)} %get-tuple-element.21), channel_id=1, source_target_pairs={{0,8},{4,12},{8,0},{12,4},{1,9},{5,13},{9,1},{13,5},{2,10},{6,14},... | collective-permute-start | bytes 405512 | tf_op jit(solution)/shard_map/ppermute | solution.py:403
  6.6 1.5 %collective-permute-start.2 = (bf16[528,128]{1,0:T(8,128)(2,1)}, bf16[528,128]{1,0:T(8,128)(2,1)S(1)}, u32[]{:S(2)}, u32[]{:S(2)}) collective-permute-start(bf16[528,128]{1,0:T(8,128)(2,1)} %get-tuple-element.21), channel_id=1, source_target_pairs={{0,2},{2,0},{1,3},{3,1},{4,6},{6,4},{5,7},{7,5},{8,10},{10,8},{9,1... | collective-permute-start | bytes 405512 | tf_op jit(solution)/shard_map/ppermute | solution.py:403
  8.1 1.6 %collective-permute-start.3 = (bf16[528,128]{1,0:T(8,128)(2,1)}, bf16[528,128]{1,0:T(8,128)(2,1)S(1)}, u32[]{:S(2)}, u32[]{:S(2)}) collective-permute-start(bf16[528,128]{1,0:T(8,128)(2,1)} %get-tuple-element.21), channel_id=1, source_target_pairs={{0,4},{4,0},{8,12},{12,8},{1,5},{5,1},{9,13},{13,9},{2,6},{6,2},{1... | collective-permute-start | bytes 405512 | tf_op jit(solution)/shard_map/ppermute | solution.py:403
  9.7 0.9 %copy-done = bf16[528,128]{1,0:T(8,128)(2,1)S(1)} copy-done((bf16[528,128]{1,0:T(8,128)(2,1)S(1)}, bf16[528,128]{1,0:T(8,128)(2,1)}, u32[]{:S(2)}) %copy-start) | copy-done | bytes 135192
  10.6 0.7 %copy-done.2 = f32[24,128]{1,0:T(8,128)S(1)} copy-done((f32[24,128]{1,0:T(8,128)S(1)}, f32[24,128]{1,0:T(8,128)}, u32[]{:S(2)}) %copy-start.2) | copy-done | bytes 12312
  11.4 1.6 %first_sums.1 = (f32[4096,128]{1,0:T(8,128)S(1)}, f32[4096,128]{1,0:T(8,128)S(1)}, bf16[1024,128]{1,0:T(8,128)(2,1)S(1)}, f32[8,128]{1,0:T(8,128)S(1)}, s16[512,...) custom-call(f32[24,128]{1,0:T(8,128)S(1)} %copy-done.2, bf16[1,528,128]{2,1,0:T(8,128)(2,1)S(1)} %bitcast.23), custom_call_target="tpu_custom_call" | custom-call | flops 1 | tf_op jit(solution)/shard_map/first_sums/pallas_call | solution.py:451
  12.9 0.5 %collective-permute-done = bf16[528,128]{1,0:T(8,128)(2,1)S(1)} collective-permute-done((bf16[528,128]{1,0:T(8,128)(2,1)}, bf16[528,128]{1,0:T(8,128)(2,1)S(1)}, u32[]{:S(2)}, u32[]{:S(2)}) %collective-permute-start) | collective-permute-done | bytes 135200 | tf_op jit(solution)/shard_map/ppermute | solution.py:403
  13.4 0.8 %collective-permute-start.1 = (bf16[528,128]{1,0:T(8,128)(2,1)S(1)}, bf16[528,128]{1,0:T(8,128)(2,1)S(1)}, u32[]{:S(2)}, u32[]{:S(2)}) collective-permute-start(bf16[528,128]{1,0:T(8,128)(2,1)S(1)} %collective-permute-done), channel_id=1, source_target_pairs={{0,4},{4,0},{8,12},{12,8},{1,5},{5,1},{9,13},{13,9},{2,6},{6,2},{1... | collective-permute-start | bytes 405512 | tf_op jit(solution)/shard_map/ppermute | solution.py:403
  14.2 1.4 %collective-permute-start.4 = (bf16[528,128]{1,0:T(8,128)(2,1)S(1)}, bf16[528,128]{1,0:T(8,128)(2,1)S(1)}, u32[]{:S(2)}, u32[]{:S(2)}) collective-permute-start(bf16[528,128]{1,0:T(8,128)(2,1)S(1)} %collective-permute-done), channel_id=1, source_target_pairs={{0,2},{2,0},{1,3},{3,1},{4,6},{6,4},{5,7},{7,5},{8,10},{10,8},{9,1... | collective-permute-start | bytes 405512 | tf_op jit(solution)/shard_map/ppermute | solution.py:403
  15.6 0.0 collective-permute-done.2
  15.7 0.0 collective-permute-done.3
  15.7 0.0 copy-start.3
  15.7 1.2 %more_sums.2 = (f32[4096,128]{1,0:T(8,128)S(1)}, bf16[1024,128]{1,0:T(8,128)(2,1)S(1)}, f32[8,128]{1,0:T(8,128)S(1)}) custom-call(f32[24,128]{1,0:T(8,128)S(1)} %copy-done.2, bf16[1,528,128]{2,1,0:T(8,128)(2,1)S(1)} %bitcast.15, bf16[1,528,128]{2,1,0:T(8,128)(2,1)S(1)} %bitcast.17, f32[4096,128]{1,0:T(8,128)S(1)} %get-tuple-element.24.refs_3_), custom_call_target="tpu_custom_call" | custom-call | flops 2 | tf_op jit(solution)/shard_map/more_sums/pallas_call | solution.py:451
  16.9 1.4 %collective-permute-start.5 = (bf16[528,128]{1,0:T(8,128)(2,1)S(1)}, bf16[528,128]{1,0:T(8,128)(2,1)S(1)}, u32[]{:S(2)}, u32[]{:S(2)}) collective-permute-start(bf16[528,128]{1,0:T(8,128)(2,1)S(1)} %collective-permute-done.2), channel_id=1, source_target_pairs={{0,4},{4,0},{8,12},{12,8},{1,5},{5,1},{9,13},{13,9},{2,6},{6,2},{1... | collective-permute-start | bytes 405512 | tf_op jit(solution)/shard_map/ppermute | solution.py:403
  18.3 0.1 collective-permute-done.1
  18.4 1.9 %collective-permute-start.6 = (bf16[528,128]{1,0:T(8,128)(2,1)S(1)}, bf16[528,128]{1,0:T(8,128)(2,1)S(1)}, u32[]{:S(2)}, u32[]{:S(2)}) collective-permute-start(bf16[528,128]{1,0:T(8,128)(2,1)S(1)} %collective-permute-done.1), channel_id=1, source_target_pairs={{0,2},{2,0},{1,3},{3,1},{4,6},{6,4},{5,7},{7,5},{8,10},{10,8},{9,1... | collective-permute-start | bytes 405512 | tf_op jit(solution)/shard_map/ppermute | solution.py:403
  20.4 0.0 collective-permute-done.4
  20.4 1.7 %more_sums.3 = (f32[4096,128]{1,0:T(8,128)S(1)}, bf16[1024,128]{1,0:T(8,128)(2,1)S(1)}, f32[8,128]{1,0:T(8,128)S(1)}) custom-call(f32[24,128]{1,0:T(8,128)S(1)} %copy-done.2, bf16[1,528,128]{2,1,0:T(8,128)(2,1)S(1)} %bitcast.13, bf16[1,528,128]{2,1,0:T(8,128)(2,1)S(1)} %bitcast.19, bf16[1,528,128]{2,1,0:T(8,128)(2,1)S(1)} %bitcast.21, ...), custom_call_target="tpu_custom_call" | custom-call | flops 3 | tf_op jit(solution)/shard_map/more_sums/pallas_call | solution.py:451
  22.0 0.0 collective-permute-done.5
  22.1 1.4 %collective-permute-done.6 = bf16[528,128]{1,0:T(8,128)(2,1)S(1)} collective-permute-done((bf16[528,128]{1,0:T(8,128)(2,1)S(1)}, bf16[528,128]{1,0:T(8,128)(2,1)S(1)}, u32[]{:S(2)}, u32[]{:S(2)}) %collective-permute-start.6) | collective-permute-done | bytes 135200 | tf_op jit(solution)/shard_map/ppermute | solution.py:403
  23.5 0.0 copy-done.1
  23.5 0.0 copy-done.3
  23.5 4.0 %table_and_rows.1 = (bf16[4096,128]{1,0:T(8,128)(2,1)}, bf16[512,128]{1,0:T(8,128)(2,1)}) custom-call(f32[24,128]{1,0:T(8,128)S(1)} %copy-done.3, f32[4096,128]{1,0:T(8,128)S(1)} %get-tuple-element.28.refs_1_, f32[4096,128]{1,0:T(8,128)S(1)} %get-tuple-element.29.refs_2_, s16[512,128]{1,0:T(8,128)(2,1)S(1)} %get-tuple-element.30.refs_3_, ...), custom_call_target="tpu_custom_call" | custom-call | tf_op jit(solution)/shard_map/table_and_rows/pallas_call | solution.py:490
  (3 shorter events, 0.0 us)
Async XLA Ops:
  2.6 10.8 %collective-permute-start = (bf16[528,128]{1,0:T(8,128)(2,1)}, bf16[528,128]{1,0:T(8,128)(2,1)S(1)}, u32[]{:S(2)}, u32[]{:S(2)}) collective-permute-start(bf16[528,128]{1,0:T(8,128)(2,1)} %get-tuple-element.21), channel_id=1, source_target_pairs={{0,8},{4,12},{8,0},{12,4},{1,9},{5,13},{9,1},{13,5},{2,10},{6,14},... | collective-permute-start | bytes 405512 | tf_op jit(solution)/shard_map/ppermute | solution.py:403
  6.6 9.0 %collective-permute-start.2 = (bf16[528,128]{1,0:T(8,128)(2,1)}, bf16[528,128]{1,0:T(8,128)(2,1)S(1)}, u32[]{:S(2)}, u32[]{:S(2)}) collective-permute-start(bf16[528,128]{1,0:T(8,128)(2,1)} %get-tuple-element.21), channel_id=1, source_target_pairs={{0,2},{2,0},{1,3},{3,1},{4,6},{6,4},{5,7},{7,5},{8,10},{10,8},{9,1... | collective-permute-start | bytes 405512 | tf_op jit(solution)/shard_map/ppermute | solution.py:403
  8.1 7.5 %collective-permute-start.3 = (bf16[528,128]{1,0:T(8,128)(2,1)}, bf16[528,128]{1,0:T(8,128)(2,1)S(1)}, u32[]{:S(2)}, u32[]{:S(2)}) collective-permute-start(bf16[528,128]{1,0:T(8,128)(2,1)} %get-tuple-element.21), channel_id=1, source_target_pairs={{0,4},{4,0},{8,12},{12,8},{1,5},{5,1},{9,13},{13,9},{2,6},{6,2},{1... | collective-permute-start | bytes 405512 | tf_op jit(solution)/shard_map/ppermute | solution.py:403
  9.7 0.9 %copy-start = (bf16[528,128]{1,0:T(8,128)(2,1)S(1)}, bf16[528,128]{1,0:T(8,128)(2,1)}, u32[]{:S(2)}) copy-start(bf16[528,128]{1,0:T(8,128)(2,1)} %get-tuple-element.21) | copy-start | bytes 405508
  10.6 0.7 %copy-start.2 = (f32[24,128]{1,0:T(8,128)S(1)}, f32[24,128]{1,0:T(8,128)}, u32[]{:S(2)}) copy-start(f32[24,128]{1,0:T(8,128)} %get-tuple-element.20.refs_0_) | copy-start | bytes 36868
  13.4 5.0 %collective-permute-start.1 = (bf16[528,128]{1,0:T(8,128)(2,1)S(1)}, bf16[528,128]{1,0:T(8,128)(2,1)S(1)}, u32[]{:S(2)}, u32[]{:S(2)}) collective-permute-start(bf16[528,128]{1,0:T(8,128)(2,1)S(1)} %collective-permute-done), channel_id=1, source_target_pairs={{0,4},{4,0},{8,12},{12,8},{1,5},{5,1},{9,13},{13,9},{2,6},{6,2},{1... | collective-permute-start | bytes 405512 | tf_op jit(solution)/shard_map/ppermute | solution.py:403
  14.2 6.2 %collective-permute-start.4 = (bf16[528,128]{1,0:T(8,128)(2,1)S(1)}, bf16[528,128]{1,0:T(8,128)(2,1)S(1)}, u32[]{:S(2)}, u32[]{:S(2)}) collective-permute-start(bf16[528,128]{1,0:T(8,128)(2,1)S(1)} %collective-permute-done), channel_id=1, source_target_pairs={{0,2},{2,0},{1,3},{3,1},{4,6},{6,4},{5,7},{7,5},{8,10},{10,8},{9,1... | collective-permute-start | bytes 405512 | tf_op jit(solution)/shard_map/ppermute | solution.py:403
  15.7 7.8 %copy-start.1 = (bf16[528,128]{1,0:T(8,128)(2,1)S(1)}, bf16[528,128]{1,0:T(8,128)(2,1)}, u32[]{:S(2)}) copy-start(bf16[528,128]{1,0:T(8,128)(2,1)} %get-tuple-element.21) | copy-start | bytes 405508
  15.7 7.8 %copy-start.3 = (f32[24,128]{1,0:T(8,128)S(1)}, f32[24,128]{1,0:T(8,128)}, u32[]{:S(2)}) copy-start(f32[24,128]{1,0:T(8,128)} %get-tuple-element.20.refs_0_) | copy-start | bytes 36868
  16.9 5.2 %collective-permute-start.5 = (bf16[528,128]{1,0:T(8,128)(2,1)S(1)}, bf16[528,128]{1,0:T(8,128)(2,1)S(1)}, u32[]{:S(2)}, u32[]{:S(2)}) collective-permute-start(bf16[528,128]{1,0:T(8,128)(2,1)S(1)} %collective-permute-done.2), channel_id=1, source_target_pairs={{0,4},{4,0},{8,12},{12,8},{1,5},{5,1},{9,13},{13,9},{2,6},{6,2},{1... | collective-permute-start | bytes 405512 | tf_op jit(solution)/shard_map/ppermute | solution.py:403
  18.4 5.0 %collective-permute-start.6 = (bf16[528,128]{1,0:T(8,128)(2,1)S(1)}, bf16[528,128]{1,0:T(8,128)(2,1)S(1)}, u32[]{:S(2)}, u32[]{:S(2)}) collective-permute-start(bf16[528,128]{1,0:T(8,128)(2,1)S(1)} %collective-permute-done.1), channel_id=1, source_target_pairs={{0,2},{2,0},{1,3},{3,1},{4,6},{6,4},{5,7},{7,5},{8,10},{10,8},{9,1... | collective-permute-start | bytes 405512 | tf_op jit(solution)/shard_map/ppermute | solution.py:403

commit v19 on v17

--- a/solution.py
+++ b/solution.py
@@ -345,7 +345,13 @@
             mask = within(top, span, [rows[r : r + 1] for r in range(z.chunks)])
             return value + dot(mask, pieces.rows(s))
 
-        total += loop(pieces.count, add, jnp.zeros((z.rows, LANES), F32)) * factor_ref[part, :]
+        if z.narrow:
+            sources = range(pieces.count)
+            lines = [row for s in sources for row in jnp.split(pieces.place(s), z.chunks, axis=0)]
+            value = dot(within(top, span, lines), jnp.concatenate([pieces.rows(s) for s in sources], axis=0))
+        else:
+            value = loop(pieces.count, add, jnp.zeros((z.rows, LANES), F32))
+        total += value * factor_ref[part, :]
     feature_ref[...] = (total * scale).astype(BF16)
     send(feature_ref, feature_out, slice(0, z.rows))
 

time: 27.7 us -> 27.7 us (level)
  no operation moved by 1% of the time
where the time goes in v19:
time: 27.7 us; the launch traced here: 27.4 us
  starting transfers between devices  12.7 us (46%)
  Pallas kernels  10.4 us (38%)
  waiting for transfers between devices  2.06 us (7%)
  local copies, waits for them, and re-layouts  1.66 us (6%)
  between operations  0.69 us (2%)
    ppermute x7, starting transfers between devices, swap(): lax.ppermute(block, axis, [(i, i ^ distance) for i in range(lax.axis_size...  12.7 us
    pallas_call x3, Pallas kernels, sums(): pl.pallas_call(functools.partial(early_kernel, z, form, len(before)), out...  4.44 us
    pallas_call x1, Pallas kernels, on_device(): pl.pallas_call(functools.partial(late_kernel, z, earlier, form, len(late)...  3.95 us
    ppermute x7, waiting for transfers between devices, swap(): lax.ppermute(block, axis, [(i, i ^ distance) for i in range(lax.axis_size...  2.06 us
    pallas_call x1, Pallas kernels, on_device(): pl.pallas_call(functools.partial(send_kernel, z), out_shape=(shape((block...  1.96 us
    unnamed x8, local copies, waits for them, and re-layouts  1.66 us
  transfers between devices with their start and end apart: 7, of which 3 were waited for; matrix products, arithmetic and copies ran while one was open for 0% of the time, Pallas kernels for 16%

profile of v19, /device:TPU:0, one launch (start us, length us, event | category | flops | bytes accessed | tf_op | source)
XLA Modules:
  0.0 27.4 jit_solution(11359136237935881794)
XLA Ops:
  0.6 2.0 %weigh.1 = (bf16[528,128]{1,0:T(8,128)(2,1)}, f32[24,128]{1,0:T(8,128)}) custom-call(s32[1]{0:T(128)} %bitcast.me_ref, f32[4]{0:T(128)} %rate_ref.1, bf16[512,128]{1,0:T(8,128)(2,1)} %events_ref.1, f32[4,128]{1,0:T(4,128)} %bitcast.28, s32[4,128]{1,0:T(4,128)} %bitcast.29, s32[4,128]{1,0:T(4,128)} %bitcast.30, s32[32,128]{1,0:T(8,128)} %bitcast.27), custom_call_target="tpu_custom_call" | custom-call | tf_op jit(solution)/shard_map/weigh/pallas_call | solution.py:423
  2.6 4.0 %collective-permute-start = (bf16[528,128]{1,0:T(8,128)(2,1)}, bf16[528,128]{1,0:T(8,128)(2,1)S(1)}, u32[]{:S(2)}, u32[]{:S(2)}) collective-permute-start(bf16[528,128]{1,0:T(8,128)(2,1)} %get-tuple-element.21), channel_id=1, source_target_pairs={{0,8},{4,12},{8,0},{12,4},{1,9},{5,13},{9,1},{13,5},{2,10},{6,14},... | collective-permute-start | bytes 405512 | tf_op jit(solution)/shard_map/ppermute | solution.py:400
  6.6 1.5 %collective-permute-start.2 = (bf16[528,128]{1,0:T(8,128)(2,1)}, bf16[528,128]{1,0:T(8,128)(2,1)S(1)}, u32[]{:S(2)}, u32[]{:S(2)}) collective-permute-start(bf16[528,128]{1,0:T(8,128)(2,1)} %get-tuple-element.21), channel_id=1, source_target_pairs={{0,2},{2,0},{1,3},{3,1},{4,6},{6,4},{5,7},{7,5},{8,10},{10,8},{9,1... | collective-permute-start | bytes 405512 | tf_op jit(solution)/shard_map/ppermute | solution.py:400
  8.1 1.6 %collective-permute-start.3 = (bf16[528,128]{1,0:T(8,128)(2,1)}, bf16[528,128]{1,0:T(8,128)(2,1)S(1)}, u32[]{:S(2)}, u32[]{:S(2)}) collective-permute-start(bf16[528,128]{1,0:T(8,128)(2,1)} %get-tuple-element.21), channel_id=1, source_target_pairs={{0,4},{4,0},{8,12},{12,8},{1,5},{5,1},{9,13},{13,9},{2,6},{6,2},{1... | collective-permute-start | bytes 405512 | tf_op jit(solution)/shard_map/ppermute | solution.py:400
  9.7 0.9 %copy-done = bf16[528,128]{1,0:T(8,128)(2,1)S(1)} copy-done((bf16[528,128]{1,0:T(8,128)(2,1)S(1)}, bf16[528,128]{1,0:T(8,128)(2,1)}, u32[]{:S(2)}) %copy-start) | copy-done | bytes 135192
  10.6 0.7 %copy-done.2 = f32[24,128]{1,0:T(8,128)S(1)} copy-done((f32[24,128]{1,0:T(8,128)S(1)}, f32[24,128]{1,0:T(8,128)}, u32[]{:S(2)}) %copy-start.2) | copy-done | bytes 12312
  11.4 1.6 %first_sums.1 = (f32[4096,128]{1,0:T(8,128)S(1)}, f32[4096,128]{1,0:T(8,128)S(1)}, bf16[1024,128]{1,0:T(8,128)(2,1)S(1)}, f32[8,128]{1,0:T(8,128)S(1)}, s16[512,...) custom-call(f32[24,128]{1,0:T(8,128)S(1)} %copy-done.2, bf16[1,528,128]{2,1,0:T(8,128)(2,1)S(1)} %bitcast.23), custom_call_target="tpu_custom_call" | custom-call | flops 1 | tf_op jit(solution)/shard_map/first_sums/pallas_call | solution.py:448
  12.9 0.5 %collective-permute-done = bf16[528,128]{1,0:T(8,128)(2,1)S(1)} collective-permute-done((bf16[528,128]{1,0:T(8,128)(2,1)}, bf16[528,128]{1,0:T(8,128)(2,1)S(1)}, u32[]{:S(2)}, u32[]{:S(2)}) %collective-permute-start) | collective-permute-done | bytes 135200 | tf_op jit(solution)/shard_map/ppermute | solution.py:400
  13.4 0.8 %collective-permute-start.1 = (bf16[528,128]{1,0:T(8,128)(2,1)S(1)}, bf16[528,128]{1,0:T(8,128)(2,1)S(1)}, u32[]{:S(2)}, u32[]{:S(2)}) collective-permute-start(bf16[528,128]{1,0:T(8,128)(2,1)S(1)} %collective-permute-done), channel_id=1, source_target_pairs={{0,4},{4,0},{8,12},{12,8},{1,5},{5,1},{9,13},{13,9},{2,6},{6,2},{1... | collective-permute-start | bytes 405512 | tf_op jit(solution)/shard_map/ppermute | solution.py:400
  14.2 1.4 %collective-permute-start.4 = (bf16[528,128]{1,0:T(8,128)(2,1)S(1)}, bf16[528,128]{1,0:T(8,128)(2,1)S(1)}, u32[]{:S(2)}, u32[]{:S(2)}) collective-permute-start(bf16[528,128]{1,0:T(8,128)(2,1)S(1)} %collective-permute-done), channel_id=1, source_target_pairs={{0,2},{2,0},{1,3},{3,1},{4,6},{6,4},{5,7},{7,5},{8,10},{10,8},{9,1... | collective-permute-start | bytes 405512 | tf_op jit(solution)/shard_map/ppermute | solution.py:400
  15.6 0.0 collective-permute-done.2
  15.7 0.0 collective-permute-done.3
  15.7 0.0 copy-start.3
  15.7 1.2 %more_sums.2 = (f32[4096,128]{1,0:T(8,128)S(1)}, bf16[1024,128]{1,0:T(8,128)(2,1)S(1)}, f32[8,128]{1,0:T(8,128)S(1)}) custom-call(f32[24,128]{1,0:T(8,128)S(1)} %copy-done.2, bf16[1,528,128]{2,1,0:T(8,128)(2,1)S(1)} %bitcast.15, bf16[1,528,128]{2,1,0:T(8,128)(2,1)S(1)} %bitcast.17, f32[4096,128]{1,0:T(8,128)S(1)} %get-tuple-element.24.refs_3_), custom_call_target="tpu_custom_call" | custom-call | flops 2 | tf_op jit(solution)/shard_map/more_sums/pallas_call | solution.py:448
  16.9 1.4 %collective-permute-start.5 = (bf16[528,128]{1,0:T(8,128)(2,1)S(1)}, bf16[528,128]{1,0:T(8,128)(2,1)S(1)}, u32[]{:S(2)}, u32[]{:S(2)}) collective-permute-start(bf16[528,128]{1,0:T(8,128)(2,1)S(1)} %collective-permute-done.2), channel_id=1, source_target_pairs={{0,4},{4,0},{8,12},{12,8},{1,5},{5,1},{9,13},{13,9},{2,6},{6,2},{1... | collective-permute-start | bytes 405512 | tf_op jit(solution)/shard_map/ppermute | solution.py:400
  18.3 0.1 collective-permute-done.1
  18.4 1.9 %collective-permute-start.6 = (bf16[528,128]{1,0:T(8,128)(2,1)S(1)}, bf16[528,128]{1,0:T(8,128)(2,1)S(1)}, u32[]{:S(2)}, u32[]{:S(2)}) collective-permute-start(bf16[528,128]{1,0:T(8,128)(2,1)S(1)} %collective-permute-done.1), channel_id=1, source_target_pairs={{0,2},{2,0},{1,3},{3,1},{4,6},{6,4},{5,7},{7,5},{8,10},{10,8},{9,1... | collective-permute-start | bytes 405512 | tf_op jit(solution)/shard_map/ppermute | solution.py:400
  20.4 0.0 collective-permute-done.4
  20.4 1.7 %more_sums.3 = (f32[4096,128]{1,0:T(8,128)S(1)}, bf16[1024,128]{1,0:T(8,128)(2,1)S(1)}, f32[8,128]{1,0:T(8,128)S(1)}) custom-call(f32[24,128]{1,0:T(8,128)S(1)} %copy-done.2, bf16[1,528,128]{2,1,0:T(8,128)(2,1)S(1)} %bitcast.13, bf16[1,528,128]{2,1,0:T(8,128)(2,1)S(1)} %bitcast.19, bf16[1,528,128]{2,1,0:T(8,128)(2,1)S(1)} %bitcast.21, ...), custom_call_target="tpu_custom_call" | custom-call | flops 3 | tf_op jit(solution)/shard_map/more_sums/pallas_call | solution.py:448
  22.0 0.0 collective-permute-done.5
  22.1 1.4 %collective-permute-done.6 = bf16[528,128]{1,0:T(8,128)(2,1)S(1)} collective-permute-done((bf16[528,128]{1,0:T(8,128)(2,1)S(1)}, bf16[528,128]{1,0:T(8,128)(2,1)S(1)}, u32[]{:S(2)}, u32[]{:S(2)}) %collective-permute-start.6) | collective-permute-done | bytes 135200 | tf_op jit(solution)/shard_map/ppermute | solution.py:400
  23.5 0.0 copy-done.1
  23.5 0.0 copy-done.3
  23.5 3.9 %table_and_rows.1 = (bf16[4096,128]{1,0:T(8,128)(2,1)}, bf16[512,128]{1,0:T(8,128)(2,1)}) custom-call(f32[24,128]{1,0:T(8,128)S(1)} %copy-done.3, f32[4096,128]{1,0:T(8,128)S(1)} %get-tuple-element.28.refs_1_, f32[4096,128]{1,0:T(8,128)S(1)} %get-tuple-element.29.refs_2_, s16[512,128]{1,0:T(8,128)(2,1)S(1)} %get-tuple-element.30.refs_3_, ...), custom_call_target="tpu_custom_call" | custom-call | tf_op jit(solution)/shard_map/table_and_rows/pallas_call | solution.py:487
  (3 shorter events, 0.0 us)
Async XLA Ops:
  2.6 10.8 %collective-permute-start = (bf16[528,128]{1,0:T(8,128)(2,1)}, bf16[528,128]{1,0:T(8,128)(2,1)S(1)}, u32[]{:S(2)}, u32[]{:S(2)}) collective-permute-start(bf16[528,128]{1,0:T(8,128)(2,1)} %get-tuple-element.21), channel_id=1, source_target_pairs={{0,8},{4,12},{8,0},{12,4},{1,9},{5,13},{9,1},{13,5},{2,10},{6,14},... | collective-permute-start | bytes 405512 | tf_op jit(solution)/shard_map/ppermute | solution.py:400
  6.6 9.0 %collective-permute-start.2 = (bf16[528,128]{1,0:T(8,128)(2,1)}, bf16[528,128]{1,0:T(8,128)(2,1)S(1)}, u32[]{:S(2)}, u32[]{:S(2)}) collective-permute-start(bf16[528,128]{1,0:T(8,128)(2,1)} %get-tuple-element.21), channel_id=1, source_target_pairs={{0,2},{2,0},{1,3},{3,1},{4,6},{6,4},{5,7},{7,5},{8,10},{10,8},{9,1... | collective-permute-start | bytes 405512 | tf_op jit(solution)/shard_map/ppermute | solution.py:400
  8.1 7.5 %collective-permute-start.3 = (bf16[528,128]{1,0:T(8,128)(2,1)}, bf16[528,128]{1,0:T(8,128)(2,1)S(1)}, u32[]{:S(2)}, u32[]{:S(2)}) collective-permute-start(bf16[528,128]{1,0:T(8,128)(2,1)} %get-tuple-element.21), channel_id=1, source_target_pairs={{0,4},{4,0},{8,12},{12,8},{1,5},{5,1},{9,13},{13,9},{2,6},{6,2},{1... | collective-permute-start | bytes 405512 | tf_op jit(solution)/shard_map/ppermute | solution.py:400
  9.7 0.9 %copy-start = (bf16[528,128]{1,0:T(8,128)(2,1)S(1)}, bf16[528,128]{1,0:T(8,128)(2,1)}, u32[]{:S(2)}) copy-start(bf16[528,128]{1,0:T(8,128)(2,1)} %get-tuple-element.21) | copy-start | bytes 405508
  10.6 0.7 %copy-start.2 = (f32[24,128]{1,0:T(8,128)S(1)}, f32[24,128]{1,0:T(8,128)}, u32[]{:S(2)}) copy-start(f32[24,128]{1,0:T(8,128)} %get-tuple-element.20.refs_0_) | copy-start | bytes 36868
  13.4 5.0 %collective-permute-start.1 = (bf16[528,128]{1,0:T(8,128)(2,1)S(1)}, bf16[528,128]{1,0:T(8,128)(2,1)S(1)}, u32[]{:S(2)}, u32[]{:S(2)}) collective-permute-start(bf16[528,128]{1,0:T(8,128)(2,1)S(1)} %collective-permute-done), channel_id=1, source_target_pairs={{0,4},{4,0},{8,12},{12,8},{1,5},{5,1},{9,13},{13,9},{2,6},{6,2},{1... | collective-permute-start | bytes 405512 | tf_op jit(solution)/shard_map/ppermute | solution.py:400
  14.2 6.2 %collective-permute-start.4 = (bf16[528,128]{1,0:T(8,128)(2,1)S(1)}, bf16[528,128]{1,0:T(8,128)(2,1)S(1)}, u32[]{:S(2)}, u32[]{:S(2)}) collective-permute-start(bf16[528,128]{1,0:T(8,128)(2,1)S(1)} %collective-permute-done), channel_id=1, source_target_pairs={{0,2},{2,0},{1,3},{3,1},{4,6},{6,4},{5,7},{7,5},{8,10},{10,8},{9,1... | collective-permute-start | bytes 405512 | tf_op jit(solution)/shard_map/ppermute | solution.py:400
  15.7 7.8 %copy-start.1 = (bf16[528,128]{1,0:T(8,128)(2,1)S(1)}, bf16[528,128]{1,0:T(8,128)(2,1)}, u32[]{:S(2)}) copy-start(bf16[528,128]{1,0:T(8,128)(2,1)} %get-tuple-element.21) | copy-start | bytes 405508
  15.7 7.8 %copy-start.3 = (f32[24,128]{1,0:T(8,128)S(1)}, f32[24,128]{1,0:T(8,128)}, u32[]{:S(2)}) copy-start(f32[24,128]{1,0:T(8,128)} %get-tuple-element.20.refs_0_) | copy-start | bytes 36868
  16.9 5.2 %collective-permute-start.5 = (bf16[528,128]{1,0:T(8,128)(2,1)S(1)}, bf16[528,128]{1,0:T(8,128)(2,1)S(1)}, u32[]{:S(2)}, u32[]{:S(2)}) collective-permute-start(bf16[528,128]{1,0:T(8,128)(2,1)S(1)} %collective-permute-done.2), channel_id=1, source_target_pairs={{0,4},{4,0},{8,12},{12,8},{1,5},{5,1},{9,13},{13,9},{2,6},{6,2},{1... | collective-permute-start | bytes 405512 | tf_op jit(solution)/shard_map/ppermute | solution.py:400
  18.4 5.0 %collective-permute-start.6 = (bf16[528,128]{1,0:T(8,128)(2,1)S(1)}, bf16[528,128]{1,0:T(8,128)(2,1)S(1)}, u32[]{:S(2)}, u32[]{:S(2)}) collective-permute-start(bf16[528,128]{1,0:T(8,128)(2,1)S(1)} %collective-permute-done.1), channel_id=1, source_target_pairs={{0,2},{2,0},{1,3},{3,1},{4,6},{6,4},{5,7},{7,5},{8,10},{10,8},{9,1... | collective-permute-start | bytes 405512 | tf_op jit(solution)/shard_map/ppermute | solution.py:400

commit v20 on v17

--- a/solution.py
+++ b/solution.py
@@ -324,31 +324,6 @@
         copies.append(pltpu.make_async_copy(ref.at[part, :], out.at[part, :], sems.at[len(copies)]))
         copies[-1].start()
 
-    place = own_ref[0 : z.chunks, :]
-    start = jnp.concatenate([runs.start_row(place[r : r + 1]) for r in range(z.chunks)], axis=0)
-    distance = place - start
-    reach = jnp.minimum(distance, F32(z.window))
-    scale, reach = wide_columns(root(z, distance), reach - F32(TOP) if z.narrow else reach)
-    position, span_start = (None, None) if z.narrow else wide_columns(place, own_ref[z.chunks : 2 * z.chunks, :])
-    total = jnp.zeros((z.rows, LANES), F32)
-    for shift in range(z.shifts):
-        part = slice(shift * z.rows, (shift + 1) * z.rows)
-        top = high_ref[part, :]
-        if z.narrow:
-            span = short(reach)
-        else:
-            low = position - reach
-            span = top - (jnp.maximum(low, span_start) if shift == 0 else low)
-
-        def add(s, value):
-            rows = pieces.place(s)
-            mask = within(top, span, [rows[r : r + 1] for r in range(z.chunks)])
-            return value + dot(mask, pieces.rows(s))
-
-        total += loop(pieces.count, add, jnp.zeros((z.rows, LANES), F32)) * factor_ref[part, :]
-    feature_ref[...] = (total * scale).astype(BF16)
-    send(feature_ref, feature_out, slice(0, z.rows))
-
     pack(z, last, base, marks_ref, codes_ref, rows_ref, from_ref)
     own_anchor, tail_anchor = anchors(z, me)
     inner = iota((LATE_BLOCK, LANES), 0)
@@ -365,6 +340,31 @@
     tail_rows = [rows_ref[n * LANES : 2 * n * LANES, :]]
     tail_rows += [ref[count * LANES : 2 * count * LANES, :] for (ref, _), count in zip(tails, earlier)]
     tail_rows = jnp.concatenate(tail_rows, axis=0)
+
+    place = own_ref[0 : z.chunks, :]
+    start = jnp.concatenate([runs.start_row(place[r : r + 1]) for r in range(z.chunks)], axis=0)
+    distance = place - start
+    reach = jnp.minimum(distance, F32(z.window))
+    scale, reach = wide_columns(root(z, distance), reach - F32(TOP) if z.narrow else reach)
+    position, span_start = (None, None) if z.narrow else wide_columns(place, own_ref[z.chunks : 2 * z.chunks, :])
+    total = jnp.zeros((z.rows, LANES), F32)
+    for shift in range(z.shifts):
+        part = slice(shift * z.rows, (shift + 1) * z.rows)
+        top = high_ref[part, :]
+        if z.narrow:
+            span = short(reach)
+        else:
+            low = position - reach
+            span = top - (jnp.maximum(low, span_start) if shift == 0 else low)
+
+        def add(s, value):
+            rows = pieces.place(s)
+            mask = within(top, span, [rows[r : r + 1] for r in range(z.chunks)])
+            return value + dot(mask, pieces.rows(s))
+
+        total += loop(pieces.count, add, jnp.zeros((z.rows, LANES), F32)) * factor_ref[part, :]
+    feature_ref[...] = (total * scale).astype(BF16)
+
     for b in range(z.slots // LATE_BLOCK):
         part = slice(b * LATE_BLOCK, (b + 1) * LATE_BLOCK)
         position = (inner + (b * LATE_BLOCK - TOP)).astype(I16)
@@ -386,6 +386,8 @@
         table_ref[part, :] = value.astype(BF16)
         if (b + 1) * LATE_BLOCK % z.window == 0:
             send(table_ref, table_out, slice((b + 1) * LATE_BLOCK - z.window, (b + 1) * LATE_BLOCK))
+            if len(copies) == 1:
+                send(feature_ref, feature_out, slice(0, z.rows))
     for copy in copies:
         copy.wait()
 

time: 27.7 us -> 27.8 us (level)
  no operation moved by 1% of the time
where the time goes in v20:
time: 27.8 us; the launch traced here: 27.5 us
  starting transfers between devices  12.7 us (46%)
  Pallas kernels  10.5 us (38%)
  waiting for transfers between devices  2.06 us (7%)
  local copies, waits for them, and re-layouts  1.66 us (6%)
  between operations  0.69 us (2%)
    ppermute x7, starting transfers between devices, swap(): lax.ppermute(block, axis, [(i, i ^ distance) for i in range(lax.axis_size...  12.7 us
    pallas_call x3, Pallas kernels, sums(): pl.pallas_call(functools.partial(early_kernel, z, form, len(before)), out...  4.44 us
    pallas_call x1, Pallas kernels, on_device(): pl.pallas_call(functools.partial(late_kernel, z, earlier, form, len(late)...  4.08 us
    ppermute x7, waiting for transfers between devices, swap(): lax.ppermute(block, axis, [(i, i ^ distance) for i in range(lax.axis_size...  2.06 us
    pallas_call x1, Pallas kernels, on_device(): pl.pallas_call(functools.partial(send_kernel, z), out_shape=(shape((block...  1.96 us
    unnamed x8, local copies, waits for them, and re-layouts  1.66 us
  transfers between devices with their start and end apart: 7, of which 3 were waited for; matrix products, arithmetic and copies ran while one was open for 0% of the time, Pallas kernels for 16%

profile of v20, /device:TPU:0, one launch (start us, length us, event | category | flops | bytes accessed | tf_op | source)
XLA Modules:
  0.0 27.5 jit_solution(10541129150250918387)
XLA Ops:
  0.6 2.0 %weigh.1 = (bf16[528,128]{1,0:T(8,128)(2,1)}, f32[24,128]{1,0:T(8,128)}) custom-call(s32[1]{0:T(128)} %bitcast.me_ref, f32[4]{0:T(128)} %rate_ref.1, bf16[512,128]{1,0:T(8,128)(2,1)} %events_ref.1, f32[4,128]{1,0:T(4,128)} %bitcast.28, s32[4,128]{1,0:T(4,128)} %bitcast.29, s32[4,128]{1,0:T(4,128)} %bitcast.30, s32[32,128]{1,0:T(8,128)} %bitcast.27), custom_call_target="tpu_custom_call" | custom-call | tf_op jit(solution)/shard_map/weigh/pallas_call | solution.py:419
  2.6 4.0 %collective-permute-start = (bf16[528,128]{1,0:T(8,128)(2,1)}, bf16[528,128]{1,0:T(8,128)(2,1)S(1)}, u32[]{:S(2)}, u32[]{:S(2)}) collective-permute-start(bf16[528,128]{1,0:T(8,128)(2,1)} %get-tuple-element.21), channel_id=1, source_target_pairs={{0,8},{4,12},{8,0},{12,4},{1,9},{5,13},{9,1},{13,5},{2,10},{6,14},... | collective-permute-start | bytes 405512 | tf_op jit(solution)/shard_map/ppermute | solution.py:396
  6.6 1.5 %collective-permute-start.2 = (bf16[528,128]{1,0:T(8,128)(2,1)}, bf16[528,128]{1,0:T(8,128)(2,1)S(1)}, u32[]{:S(2)}, u32[]{:S(2)}) collective-permute-start(bf16[528,128]{1,0:T(8,128)(2,1)} %get-tuple-element.21), channel_id=1, source_target_pairs={{0,2},{2,0},{1,3},{3,1},{4,6},{6,4},{5,7},{7,5},{8,10},{10,8},{9,1... | collective-permute-start | bytes 405512 | tf_op jit(solution)/shard_map/ppermute | solution.py:396
  8.1 1.6 %collective-permute-start.3 = (bf16[528,128]{1,0:T(8,128)(2,1)}, bf16[528,128]{1,0:T(8,128)(2,1)S(1)}, u32[]{:S(2)}, u32[]{:S(2)}) collective-permute-start(bf16[528,128]{1,0:T(8,128)(2,1)} %get-tuple-element.21), channel_id=1, source_target_pairs={{0,4},{4,0},{8,12},{12,8},{1,5},{5,1},{9,13},{13,9},{2,6},{6,2},{1... | collective-permute-start | bytes 405512 | tf_op jit(solution)/shard_map/ppermute | solution.py:396
  9.7 0.9 %copy-done = bf16[528,128]{1,0:T(8,128)(2,1)S(1)} copy-done((bf16[528,128]{1,0:T(8,128)(2,1)S(1)}, bf16[528,128]{1,0:T(8,128)(2,1)}, u32[]{:S(2)}) %copy-start) | copy-done | bytes 135192
  10.6 0.7 %copy-done.2 = f32[24,128]{1,0:T(8,128)S(1)} copy-done((f32[24,128]{1,0:T(8,128)S(1)}, f32[24,128]{1,0:T(8,128)}, u32[]{:S(2)}) %copy-start.2) | copy-done | bytes 12312
  11.4 1.6 %first_sums.1 = (f32[4096,128]{1,0:T(8,128)S(1)}, f32[4096,128]{1,0:T(8,128)S(1)}, bf16[1024,128]{1,0:T(8,128)(2,1)S(1)}, f32[8,128]{1,0:T(8,128)S(1)}, s16[512,...) custom-call(f32[24,128]{1,0:T(8,128)S(1)} %copy-done.2, bf16[1,528,128]{2,1,0:T(8,128)(2,1)S(1)} %bitcast.23), custom_call_target="tpu_custom_call" | custom-call | flops 1 | tf_op jit(solution)/shard_map/first_sums/pallas_call | solution.py:444
  12.9 0.5 %collective-permute-done = bf16[528,128]{1,0:T(8,128)(2,1)S(1)} collective-permute-done((bf16[528,128]{1,0:T(8,128)(2,1)}, bf16[528,128]{1,0:T(8,128)(2,1)S(1)}, u32[]{:S(2)}, u32[]{:S(2)}) %collective-permute-start) | collective-permute-done | bytes 135200 | tf_op jit(solution)/shard_map/ppermute | solution.py:396
  13.4 0.8 %collective-permute-start.1 = (bf16[528,128]{1,0:T(8,128)(2,1)S(1)}, bf16[528,128]{1,0:T(8,128)(2,1)S(1)}, u32[]{:S(2)}, u32[]{:S(2)}) collective-permute-start(bf16[528,128]{1,0:T(8,128)(2,1)S(1)} %collective-permute-done), channel_id=1, source_target_pairs={{0,4},{4,0},{8,12},{12,8},{1,5},{5,1},{9,13},{13,9},{2,6},{6,2},{1... | collective-permute-start | bytes 405512 | tf_op jit(solution)/shard_map/ppermute | solution.py:396
  14.2 1.4 %collective-permute-start.4 = (bf16[528,128]{1,0:T(8,128)(2,1)S(1)}, bf16[528,128]{1,0:T(8,128)(2,1)S(1)}, u32[]{:S(2)}, u32[]{:S(2)}) collective-permute-start(bf16[528,128]{1,0:T(8,128)(2,1)S(1)} %collective-permute-done), channel_id=1, source_target_pairs={{0,2},{2,0},{1,3},{3,1},{4,6},{6,4},{5,7},{7,5},{8,10},{10,8},{9,1... | collective-permute-start | bytes 405512 | tf_op jit(solution)/shard_map/ppermute | solution.py:396
  15.6 0.0 collective-permute-done.2
  15.7 0.0 collective-permute-done.3
  15.7 0.0 copy-start.3
  15.7 1.2 %more_sums.2 = (f32[4096,128]{1,0:T(8,128)S(1)}, bf16[1024,128]{1,0:T(8,128)(2,1)S(1)}, f32[8,128]{1,0:T(8,128)S(1)}) custom-call(f32[24,128]{1,0:T(8,128)S(1)} %copy-done.2, bf16[1,528,128]{2,1,0:T(8,128)(2,1)S(1)} %bitcast.15, bf16[1,528,128]{2,1,0:T(8,128)(2,1)S(1)} %bitcast.17, f32[4096,128]{1,0:T(8,128)S(1)} %get-tuple-element.24.refs_3_), custom_call_target="tpu_custom_call" | custom-call | flops 2 | tf_op jit(solution)/shard_map/more_sums/pallas_call | solution.py:444
  16.9 1.4 %collective-permute-start.5 = (bf16[528,128]{1,0:T(8,128)(2,1)S(1)}, bf16[528,128]{1,0:T(8,128)(2,1)S(1)}, u32[]{:S(2)}, u32[]{:S(2)}) collective-permute-start(bf16[528,128]{1,0:T(8,128)(2,1)S(1)} %collective-permute-done.2), channel_id=1, source_target_pairs={{0,4},{4,0},{8,12},{12,8},{1,5},{5,1},{9,13},{13,9},{2,6},{6,2},{1... | collective-permute-start | bytes 405512 | tf_op jit(solution)/shard_map/ppermute | solution.py:396
  18.3 0.1 collective-permute-done.1
  18.4 1.9 %collective-permute-start.6 = (bf16[528,128]{1,0:T(8,128)(2,1)S(1)}, bf16[528,128]{1,0:T(8,128)(2,1)S(1)}, u32[]{:S(2)}, u32[]{:S(2)}) collective-permute-start(bf16[528,128]{1,0:T(8,128)(2,1)S(1)} %collective-permute-done.1), channel_id=1, source_target_pairs={{0,2},{2,0},{1,3},{3,1},{4,6},{6,4},{5,7},{7,5},{8,10},{10,8},{9,1... | collective-permute-start | bytes 405512 | tf_op jit(solution)/shard_map/ppermute | solution.py:396
  20.4 0.0 collective-permute-done.4
  20.4 1.7 %more_sums.3 = (f32[4096,128]{1,0:T(8,128)S(1)}, bf16[1024,128]{1,0:T(8,128)(2,1)S(1)}, f32[8,128]{1,0:T(8,128)S(1)}) custom-call(f32[24,128]{1,0:T(8,128)S(1)} %copy-done.2, bf16[1,528,128]{2,1,0:T(8,128)(2,1)S(1)} %bitcast.13, bf16[1,528,128]{2,1,0:T(8,128)(2,1)S(1)} %bitcast.19, bf16[1,528,128]{2,1,0:T(8,128)(2,1)S(1)} %bitcast.21, ...), custom_call_target="tpu_custom_call" | custom-call | flops 3 | tf_op jit(solution)/shard_map/more_sums/pallas_call | solution.py:444
  22.0 0.0 collective-permute-done.5
  22.1 1.4 %collective-permute-done.6 = bf16[528,128]{1,0:T(8,128)(2,1)S(1)} collective-permute-done((bf16[528,128]{1,0:T(8,128)(2,1)S(1)}, bf16[528,128]{1,0:T(8,128)(2,1)S(1)}, u32[]{:S(2)}, u32[]{:S(2)}) %collective-permute-start.6) | collective-permute-done | bytes 135200 | tf_op jit(solution)/shard_map/ppermute | solution.py:396
  23.5 0.0 copy-done.1
  23.5 0.0 copy-done.3
  23.5 4.1 %table_and_rows.1 = (bf16[4096,128]{1,0:T(8,128)(2,1)}, bf16[512,128]{1,0:T(8,128)(2,1)}) custom-call(f32[24,128]{1,0:T(8,128)S(1)} %copy-done.3, f32[4096,128]{1,0:T(8,128)S(1)} %get-tuple-element.28.refs_1_, f32[4096,128]{1,0:T(8,128)S(1)} %get-tuple-element.29.refs_2_, s16[512,128]{1,0:T(8,128)(2,1)S(1)} %get-tuple-element.30.refs_3_, ...), custom_call_target="tpu_custom_call" | custom-call | tf_op jit(solution)/shard_map/table_and_rows/pallas_call | solution.py:483
  (3 shorter events, 0.0 us)
Async XLA Ops:
  2.6 10.8 %collective-permute-start = (bf16[528,128]{1,0:T(8,128)(2,1)}, bf16[528,128]{1,0:T(8,128)(2,1)S(1)}, u32[]{:S(2)}, u32[]{:S(2)}) collective-permute-start(bf16[528,128]{1,0:T(8,128)(2,1)} %get-tuple-element.21), channel_id=1, source_target_pairs={{0,8},{4,12},{8,0},{12,4},{1,9},{5,13},{9,1},{13,5},{2,10},{6,14},... | collective-permute-start | bytes 405512 | tf_op jit(solution)/shard_map/ppermute | solution.py:396
  6.6 9.0 %collective-permute-start.2 = (bf16[528,128]{1,0:T(8,128)(2,1)}, bf16[528,128]{1,0:T(8,128)(2,1)S(1)}, u32[]{:S(2)}, u32[]{:S(2)}) collective-permute-start(bf16[528,128]{1,0:T(8,128)(2,1)} %get-tuple-element.21), channel_id=1, source_target_pairs={{0,2},{2,0},{1,3},{3,1},{4,6},{6,4},{5,7},{7,5},{8,10},{10,8},{9,1... | collective-permute-start | bytes 405512 | tf_op jit(solution)/shard_map/ppermute | solution.py:396
  8.1 7.5 %collective-permute-start.3 = (bf16[528,128]{1,0:T(8,128)(2,1)}, bf16[528,128]{1,0:T(8,128)(2,1)S(1)}, u32[]{:S(2)}, u32[]{:S(2)}) collective-permute-start(bf16[528,128]{1,0:T(8,128)(2,1)} %get-tuple-element.21), channel_id=1, source_target_pairs={{0,4},{4,0},{8,12},{12,8},{1,5},{5,1},{9,13},{13,9},{2,6},{6,2},{1... | collective-permute-start | bytes 405512 | tf_op jit(solution)/shard_map/ppermute | solution.py:396
  9.7 0.9 %copy-start = (bf16[528,128]{1,0:T(8,128)(2,1)S(1)}, bf16[528,128]{1,0:T(8,128)(2,1)}, u32[]{:S(2)}) copy-start(bf16[528,128]{1,0:T(8,128)(2,1)} %get-tuple-element.21) | copy-start | bytes 405508
  10.6 0.7 %copy-start.2 = (f32[24,128]{1,0:T(8,128)S(1)}, f32[24,128]{1,0:T(8,128)}, u32[]{:S(2)}) copy-start(f32[24,128]{1,0:T(8,128)} %get-tuple-element.20.refs_0_) | copy-start | bytes 36868
  13.4 5.0 %collective-permute-start.1 = (bf16[528,128]{1,0:T(8,128)(2,1)S(1)}, bf16[528,128]{1,0:T(8,128)(2,1)S(1)}, u32[]{:S(2)}, u32[]{:S(2)}) collective-permute-start(bf16[528,128]{1,0:T(8,128)(2,1)S(1)} %collective-permute-done), channel_id=1, source_target_pairs={{0,4},{4,0},{8,12},{12,8},{1,5},{5,1},{9,13},{13,9},{2,6},{6,2},{1... | collective-permute-start | bytes 405512 | tf_op jit(solution)/shard_map/ppermute | solution.py:396
  14.2 6.2 %collective-permute-start.4 = (bf16[528,128]{1,0:T(8,128)(2,1)S(1)}, bf16[528,128]{1,0:T(8,128)(2,1)S(1)}, u32[]{:S(2)}, u32[]{:S(2)}) collective-permute-start(bf16[528,128]{1,0:T(8,128)(2,1)S(1)} %collective-permute-done), channel_id=1, source_target_pairs={{0,2},{2,0},{1,3},{3,1},{4,6},{6,4},{5,7},{7,5},{8,10},{10,8},{9,1... | collective-permute-start | bytes 405512 | tf_op jit(solution)/shard_map/ppermute | solution.py:396
  15.7 7.8 %copy-start.1 = (bf16[528,128]{1,0:T(8,128)(2,1)S(1)}, bf16[528,128]{1,0:T(8,128)(2,1)}, u32[]{:S(2)}) copy-start(bf16[528,128]{1,0:T(8,128)(2,1)} %get-tuple-element.21) | copy-start | bytes 405508
  15.7 7.8 %copy-start.3 = (f32[24,128]{1,0:T(8,128)S(1)}, f32[24,128]{1,0:T(8,128)}, u32[]{:S(2)}) copy-start(f32[24,128]{1,0:T(8,128)} %get-tuple-element.20.refs_0_) | copy-start | bytes 36868
  16.9 5.2 %collective-permute-start.5 = (bf16[528,128]{1,0:T(8,128)(2,1)S(1)}, bf16[528,128]{1,0:T(8,128)(2,1)S(1)}, u32[]{:S(2)}, u32[]{:S(2)}) collective-permute-start(bf16[528,128]{1,0:T(8,128)(2,1)S(1)} %collective-permute-done.2), channel_id=1, source_target_pairs={{0,4},{4,0},{8,12},{12,8},{1,5},{5,1},{9,13},{13,9},{2,6},{6,2},{1... | collective-permute-start | bytes 405512 | tf_op jit(solution)/shard_map/ppermute | solution.py:396
  18.4 5.0 %collective-permute-start.6 = (bf16[528,128]{1,0:T(8,128)(2,1)S(1)}, bf16[528,128]{1,0:T(8,128)(2,1)S(1)}, u32[]{:S(2)}, u32[]{:S(2)}) collective-permute-start(bf16[528,128]{1,0:T(8,128)(2,1)S(1)} %collective-permute-done.1), channel_id=1, source_target_pairs={{0,2},{2,0},{1,3},{3,1},{4,6},{6,4},{5,7},{7,5},{8,10},{10,8},{9,1... | collective-permute-start | bytes 405512 | tf_op jit(solution)/shard_map/ppermute | solution.py:396

commit v21 on v17

--- a/solution.py
+++ b/solution.py
@@ -324,31 +324,6 @@
         copies.append(pltpu.make_async_copy(ref.at[part, :], out.at[part, :], sems.at[len(copies)]))
         copies[-1].start()
 
-    place = own_ref[0 : z.chunks, :]
-    start = jnp.concatenate([runs.start_row(place[r : r + 1]) for r in range(z.chunks)], axis=0)
-    distance = place - start
-    reach = jnp.minimum(distance, F32(z.window))
-    scale, reach = wide_columns(root(z, distance), reach - F32(TOP) if z.narrow else reach)
-    position, span_start = (None, None) if z.narrow else wide_columns(place, own_ref[z.chunks : 2 * z.chunks, :])
-    total = jnp.zeros((z.rows, LANES), F32)
-    for shift in range(z.shifts):
-        part = slice(shift * z.rows, (shift + 1) * z.rows)
-        top = high_ref[part, :]
-        if z.narrow:
-            span = short(reach)
-        else:
-            low = position - reach
-            span = top - (jnp.maximum(low, span_start) if shift == 0 else low)
-
-        def add(s, value):
-            rows = pieces.place(s)
-            mask = within(top, span, [rows[r : r + 1] for r in range(z.chunks)])
-            return value + dot(mask, pieces.rows(s))
-
-        total += loop(pieces.count, add, jnp.zeros((z.rows, LANES), F32)) * factor_ref[part, :]
-    feature_ref[...] = (total * scale).astype(BF16)
-    send(feature_ref, feature_out, slice(0, z.rows))
-
     pack(z, last, base, marks_ref, codes_ref, rows_ref, from_ref)
     own_anchor, tail_anchor = anchors(z, me)
     inner = iota((LATE_BLOCK, LANES), 0)
@@ -386,6 +361,31 @@
         table_ref[part, :] = value.astype(BF16)
         if (b + 1) * LATE_BLOCK % z.window == 0:
             send(table_ref, table_out, slice((b + 1) * LATE_BLOCK - z.window, (b + 1) * LATE_BLOCK))
+
+    place = own_ref[0 : z.chunks, :]
+    start = jnp.concatenate([runs.start_row(place[r : r + 1]) for r in range(z.chunks)], axis=0)
+    distance = place - start
+    reach = jnp.minimum(distance, F32(z.window))
+    scale, reach = wide_columns(root(z, distance), reach - F32(TOP) if z.narrow else reach)
+    position, span_start = (None, None) if z.narrow else wide_columns(place, own_ref[z.chunks : 2 * z.chunks, :])
+    total = jnp.zeros((z.rows, LANES), F32)
+    for shift in range(z.shifts):
+        part = slice(shift * z.rows, (shift + 1) * z.rows)
+        top = high_ref[part, :]
+        if z.narrow:
+            span = short(reach)
+        else:
+            low = position - reach
+            span = top - (jnp.maximum(low, span_start) if shift == 0 else low)
+
+        def add(s, value):
+            rows = pieces.place(s)
+            mask = within(top, span, [rows[r : r + 1] for r in range(z.chunks)])
+            return value + dot(mask, pieces.rows(s))
+
+        total += loop(pieces.count, add, jnp.zeros((z.rows, LANES), F32)) * factor_ref[part, :]
+    feature_ref[...] = (total * scale).astype(BF16)
+    send(feature_ref, feature_out, slice(0, z.rows))
     for copy in copies:
         copy.wait()
 

time: 27.7 us -> 27.7 us (level)
  no operation moved by 1% of the time
where the time goes in v21:
time: 27.7 us; the launch traced here: 27.4 us
  starting transfers between devices  12.7 us (46%)
  Pallas kernels  10.4 us (38%)
  waiting for transfers between devices  2.06 us (7%)
  local copies, waits for them, and re-layouts  1.66 us (6%)
  between operations  0.69 us (2%)
    ppermute x7, starting transfers between devices, swap(): lax.ppermute(block, axis, [(i, i ^ distance) for i in range(lax.axis_size...  12.7 us
    pallas_call x3, Pallas kernels, sums(): pl.pallas_call(functools.partial(early_kernel, z, form, len(before)), out...  4.44 us
    pallas_call x1, Pallas kernels, on_device(): pl.pallas_call(functools.partial(late_kernel, z, earlier, form, len(late)...  3.95 us
    ppermute x7, waiting for transfers between devices, swap(): lax.ppermute(block, axis, [(i, i ^ distance) for i in range(lax.axis_size...  2.06 us
    pallas_call x1, Pallas kernels, on_device(): pl.pallas_call(functools.partial(send_kernel, z), out_shape=(shape((block...  1.96 us
    unnamed x8, local copies, waits for them, and re-layouts  1.66 us
  transfers between devices with their start and end apart: 7, of which 3 were waited for; matrix products, arithmetic and copies ran while one was open for 0% of the time, Pallas kernels for 16%

profile of v21, /device:TPU:0, one launch (start us, length us, event | category | flops | bytes accessed | tf_op | source)
XLA Modules:
  0.0 27.4 jit_solution(12832803682441036785)
XLA Ops:
  0.6 2.0 %weigh.1 = (bf16[528,128]{1,0:T(8,128)(2,1)}, f32[24,128]{1,0:T(8,128)}) custom-call(s32[1]{0:T(128)} %bitcast.me_ref, f32[4]{0:T(128)} %rate_ref.1, bf16[512,128]{1,0:T(8,128)(2,1)} %events_ref.1, f32[4,128]{1,0:T(4,128)} %bitcast.28, s32[4,128]{1,0:T(4,128)} %bitcast.29, s32[4,128]{1,0:T(4,128)} %bitcast.30, s32[32,128]{1,0:T(8,128)} %bitcast.27), custom_call_target="tpu_custom_call" | custom-call | tf_op jit(solution)/shard_map/weigh/pallas_call | solution.py:417
  2.6 4.0 %collective-permute-start = (bf16[528,128]{1,0:T(8,128)(2,1)}, bf16[528,128]{1,0:T(8,128)(2,1)S(1)}, u32[]{:S(2)}, u32[]{:S(2)}) collective-permute-start(bf16[528,128]{1,0:T(8,128)(2,1)} %get-tuple-element.21), channel_id=1, source_target_pairs={{0,8},{4,12},{8,0},{12,4},{1,9},{5,13},{9,1},{13,5},{2,10},{6,14},... | collective-permute-start | bytes 405512 | tf_op jit(solution)/shard_map/ppermute | solution.py:394
  6.6 1.5 %collective-permute-start.2 = (bf16[528,128]{1,0:T(8,128)(2,1)}, bf16[528,128]{1,0:T(8,128)(2,1)S(1)}, u32[]{:S(2)}, u32[]{:S(2)}) collective-permute-start(bf16[528,128]{1,0:T(8,128)(2,1)} %get-tuple-element.21), channel_id=1, source_target_pairs={{0,2},{2,0},{1,3},{3,1},{4,6},{6,4},{5,7},{7,5},{8,10},{10,8},{9,1... | collective-permute-start | bytes 405512 | tf_op jit(solution)/shard_map/ppermute | solution.py:394
  8.1 1.6 %collective-permute-start.3 = (bf16[528,128]{1,0:T(8,128)(2,1)}, bf16[528,128]{1,0:T(8,128)(2,1)S(1)}, u32[]{:S(2)}, u32[]{:S(2)}) collective-permute-start(bf16[528,128]{1,0:T(8,128)(2,1)} %get-tuple-element.21), channel_id=1, source_target_pairs={{0,4},{4,0},{8,12},{12,8},{1,5},{5,1},{9,13},{13,9},{2,6},{6,2},{1... | collective-permute-start | bytes 405512 | tf_op jit(solution)/shard_map/ppermute | solution.py:394
  9.7 0.9 %copy-done = bf16[528,128]{1,0:T(8,128)(2,1)S(1)} copy-done((bf16[528,128]{1,0:T(8,128)(2,1)S(1)}, bf16[528,128]{1,0:T(8,128)(2,1)}, u32[]{:S(2)}) %copy-start) | copy-done | bytes 135192
  10.6 0.7 %copy-done.2 = f32[24,128]{1,0:T(8,128)S(1)} copy-done((f32[24,128]{1,0:T(8,128)S(1)}, f32[24,128]{1,0:T(8,128)}, u32[]{:S(2)}) %copy-start.2) | copy-done | bytes 12312
  11.4 1.6 %first_sums.1 = (f32[4096,128]{1,0:T(8,128)S(1)}, f32[4096,128]{1,0:T(8,128)S(1)}, bf16[1024,128]{1,0:T(8,128)(2,1)S(1)}, f32[8,128]{1,0:T(8,128)S(1)}, s16[512,...) custom-call(f32[24,128]{1,0:T(8,128)S(1)} %copy-done.2, bf16[1,528,128]{2,1,0:T(8,128)(2,1)S(1)} %bitcast.23), custom_call_target="tpu_custom_call" | custom-call | flops 1 | tf_op jit(solution)/shard_map/first_sums/pallas_call | solution.py:442
  12.9 0.5 %collective-permute-done = bf16[528,128]{1,0:T(8,128)(2,1)S(1)} collective-permute-done((bf16[528,128]{1,0:T(8,128)(2,1)}, bf16[528,128]{1,0:T(8,128)(2,1)S(1)}, u32[]{:S(2)}, u32[]{:S(2)}) %collective-permute-start) | collective-permute-done | bytes 135200 | tf_op jit(solution)/shard_map/ppermute | solution.py:394
  13.4 0.8 %collective-permute-start.1 = (bf16[528,128]{1,0:T(8,128)(2,1)S(1)}, bf16[528,128]{1,0:T(8,128)(2,1)S(1)}, u32[]{:S(2)}, u32[]{:S(2)}) collective-permute-start(bf16[528,128]{1,0:T(8,128)(2,1)S(1)} %collective-permute-done), channel_id=1, source_target_pairs={{0,4},{4,0},{8,12},{12,8},{1,5},{5,1},{9,13},{13,9},{2,6},{6,2},{1... | collective-permute-start | bytes 405512 | tf_op jit(solution)/shard_map/ppermute | solution.py:394
  14.2 1.4 %collective-permute-start.4 = (bf16[528,128]{1,0:T(8,128)(2,1)S(1)}, bf16[528,128]{1,0:T(8,128)(2,1)S(1)}, u32[]{:S(2)}, u32[]{:S(2)}) collective-permute-start(bf16[528,128]{1,0:T(8,128)(2,1)S(1)} %collective-permute-done), channel_id=1, source_target_pairs={{0,2},{2,0},{1,3},{3,1},{4,6},{6,4},{5,7},{7,5},{8,10},{10,8},{9,1... | collective-permute-start | bytes 405512 | tf_op jit(solution)/shard_map/ppermute | solution.py:394
  15.6 0.0 collective-permute-done.2
  15.7 0.0 collective-permute-done.3
  15.7 0.0 copy-start.3
  15.7 1.2 %more_sums.2 = (f32[4096,128]{1,0:T(8,128)S(1)}, bf16[1024,128]{1,0:T(8,128)(2,1)S(1)}, f32[8,128]{1,0:T(8,128)S(1)}) custom-call(f32[24,128]{1,0:T(8,128)S(1)} %copy-done.2, bf16[1,528,128]{2,1,0:T(8,128)(2,1)S(1)} %bitcast.15, bf16[1,528,128]{2,1,0:T(8,128)(2,1)S(1)} %bitcast.17, f32[4096,128]{1,0:T(8,128)S(1)} %get-tuple-element.24.refs_3_), custom_call_target="tpu_custom_call" | custom-call | flops 2 | tf_op jit(solution)/shard_map/more_sums/pallas_call | solution.py:442
  16.9 1.4 %collective-permute-start.5 = (bf16[528,128]{1,0:T(8,128)(2,1)S(1)}, bf16[528,128]{1,0:T(8,128)(2,1)S(1)}, u32[]{:S(2)}, u32[]{:S(2)}) collective-permute-start(bf16[528,128]{1,0:T(8,128)(2,1)S(1)} %collective-permute-done.2), channel_id=1, source_target_pairs={{0,4},{4,0},{8,12},{12,8},{1,5},{5,1},{9,13},{13,9},{2,6},{6,2},{1... | collective-permute-start | bytes 405512 | tf_op jit(solution)/shard_map/ppermute | solution.py:394
  18.3 0.1 collective-permute-done.1
  18.4 1.9 %collective-permute-start.6 = (bf16[528,128]{1,0:T(8,128)(2,1)S(1)}, bf16[528,128]{1,0:T(8,128)(2,1)S(1)}, u32[]{:S(2)}, u32[]{:S(2)}) collective-permute-start(bf16[528,128]{1,0:T(8,128)(2,1)S(1)} %collective-permute-done.1), channel_id=1, source_target_pairs={{0,2},{2,0},{1,3},{3,1},{4,6},{6,4},{5,7},{7,5},{8,10},{10,8},{9,1... | collective-permute-start | bytes 405512 | tf_op jit(solution)/shard_map/ppermute | solution.py:394
  20.4 0.0 collective-permute-done.4
  20.4 1.7 %more_sums.3 = (f32[4096,128]{1,0:T(8,128)S(1)}, bf16[1024,128]{1,0:T(8,128)(2,1)S(1)}, f32[8,128]{1,0:T(8,128)S(1)}) custom-call(f32[24,128]{1,0:T(8,128)S(1)} %copy-done.2, bf16[1,528,128]{2,1,0:T(8,128)(2,1)S(1)} %bitcast.13, bf16[1,528,128]{2,1,0:T(8,128)(2,1)S(1)} %bitcast.19, bf16[1,528,128]{2,1,0:T(8,128)(2,1)S(1)} %bitcast.21, ...), custom_call_target="tpu_custom_call" | custom-call | flops 3 | tf_op jit(solution)/shard_map/more_sums/pallas_call | solution.py:442
  22.0 0.0 collective-permute-done.5
  22.1 1.4 %collective-permute-done.6 = bf16[528,128]{1,0:T(8,128)(2,1)S(1)} collective-permute-done((bf16[528,128]{1,0:T(8,128)(2,1)S(1)}, bf16[528,128]{1,0:T(8,128)(2,1)S(1)}, u32[]{:S(2)}, u32[]{:S(2)}) %collective-permute-start.6) | collective-permute-done | bytes 135200 | tf_op jit(solution)/shard_map/ppermute | solution.py:394
  23.5 0.0 copy-done.1
  23.5 0.0 copy-done.3
  23.5 3.9 %table_and_rows.1 = (bf16[4096,128]{1,0:T(8,128)(2,1)}, bf16[512,128]{1,0:T(8,128)(2,1)}) custom-call(f32[24,128]{1,0:T(8,128)S(1)} %copy-done.3, f32[4096,128]{1,0:T(8,128)S(1)} %get-tuple-element.28.refs_1_, f32[4096,128]{1,0:T(8,128)S(1)} %get-tuple-element.29.refs_2_, s16[512,128]{1,0:T(8,128)(2,1)S(1)} %get-tuple-element.30.refs_3_, ...), custom_call_target="tpu_custom_call" | custom-call | tf_op jit(solution)/shard_map/table_and_rows/pallas_call | solution.py:481
  (3 shorter events, 0.0 us)
Async XLA Ops:
  2.6 10.8 %collective-permute-start = (bf16[528,128]{1,0:T(8,128)(2,1)}, bf16[528,128]{1,0:T(8,128)(2,1)S(1)}, u32[]{:S(2)}, u32[]{:S(2)}) collective-permute-start(bf16[528,128]{1,0:T(8,128)(2,1)} %get-tuple-element.21), channel_id=1, source_target_pairs={{0,8},{4,12},{8,0},{12,4},{1,9},{5,13},{9,1},{13,5},{2,10},{6,14},... | collective-permute-start | bytes 405512 | tf_op jit(solution)/shard_map/ppermute | solution.py:394
  6.6 9.0 %collective-permute-start.2 = (bf16[528,128]{1,0:T(8,128)(2,1)}, bf16[528,128]{1,0:T(8,128)(2,1)S(1)}, u32[]{:S(2)}, u32[]{:S(2)}) collective-permute-start(bf16[528,128]{1,0:T(8,128)(2,1)} %get-tuple-element.21), channel_id=1, source_target_pairs={{0,2},{2,0},{1,3},{3,1},{4,6},{6,4},{5,7},{7,5},{8,10},{10,8},{9,1... | collective-permute-start | bytes 405512 | tf_op jit(solution)/shard_map/ppermute | solution.py:394
  8.1 7.5 %collective-permute-start.3 = (bf16[528,128]{1,0:T(8,128)(2,1)}, bf16[528,128]{1,0:T(8,128)(2,1)S(1)}, u32[]{:S(2)}, u32[]{:S(2)}) collective-permute-start(bf16[528,128]{1,0:T(8,128)(2,1)} %get-tuple-element.21), channel_id=1, source_target_pairs={{0,4},{4,0},{8,12},{12,8},{1,5},{5,1},{9,13},{13,9},{2,6},{6,2},{1... | collective-permute-start | bytes 405512 | tf_op jit(solution)/shard_map/ppermute | solution.py:394
  9.7 0.9 %copy-start = (bf16[528,128]{1,0:T(8,128)(2,1)S(1)}, bf16[528,128]{1,0:T(8,128)(2,1)}, u32[]{:S(2)}) copy-start(bf16[528,128]{1,0:T(8,128)(2,1)} %get-tuple-element.21) | copy-start | bytes 405508
  10.6 0.7 %copy-start.2 = (f32[24,128]{1,0:T(8,128)S(1)}, f32[24,128]{1,0:T(8,128)}, u32[]{:S(2)}) copy-start(f32[24,128]{1,0:T(8,128)} %get-tuple-element.20.refs_0_) | copy-start | bytes 36868
  13.4 5.0 %collective-permute-start.1 = (bf16[528,128]{1,0:T(8,128)(2,1)S(1)}, bf16[528,128]{1,0:T(8,128)(2,1)S(1)}, u32[]{:S(2)}, u32[]{:S(2)}) collective-permute-start(bf16[528,128]{1,0:T(8,128)(2,1)S(1)} %collective-permute-done), channel_id=1, source_target_pairs={{0,4},{4,0},{8,12},{12,8},{1,5},{5,1},{9,13},{13,9},{2,6},{6,2},{1... | collective-permute-start | bytes 405512 | tf_op jit(solution)/shard_map/ppermute | solution.py:394
  14.2 6.2 %collective-permute-start.4 = (bf16[528,128]{1,0:T(8,128)(2,1)S(1)}, bf16[528,128]{1,0:T(8,128)(2,1)S(1)}, u32[]{:S(2)}, u32[]{:S(2)}) collective-permute-start(bf16[528,128]{1,0:T(8,128)(2,1)S(1)} %collective-permute-done), channel_id=1, source_target_pairs={{0,2},{2,0},{1,3},{3,1},{4,6},{6,4},{5,7},{7,5},{8,10},{10,8},{9,1... | collective-permute-start | bytes 405512 | tf_op jit(solution)/shard_map/ppermute | solution.py:394
  15.7 7.8 %copy-start.1 = (bf16[528,128]{1,0:T(8,128)(2,1)S(1)}, bf16[528,128]{1,0:T(8,128)(2,1)}, u32[]{:S(2)}) copy-start(bf16[528,128]{1,0:T(8,128)(2,1)} %get-tuple-element.21) | copy-start | bytes 405508
  15.7 7.8 %copy-start.3 = (f32[24,128]{1,0:T(8,128)S(1)}, f32[24,128]{1,0:T(8,128)}, u32[]{:S(2)}) copy-start(f32[24,128]{1,0:T(8,128)} %get-tuple-element.20.refs_0_) | copy-start | bytes 36868
  16.9 5.2 %collective-permute-start.5 = (bf16[528,128]{1,0:T(8,128)(2,1)S(1)}, bf16[528,128]{1,0:T(8,128)(2,1)S(1)}, u32[]{:S(2)}, u32[]{:S(2)}) collective-permute-start(bf16[528,128]{1,0:T(8,128)(2,1)S(1)} %collective-permute-done.2), channel_id=1, source_target_pairs={{0,4},{4,0},{8,12},{12,8},{1,5},{5,1},{9,13},{13,9},{2,6},{6,2},{1... | collective-permute-start | bytes 405512 | tf_op jit(solution)/shard_map/ppermute | solution.py:394
  18.4 5.0 %collective-permute-start.6 = (bf16[528,128]{1,0:T(8,128)(2,1)S(1)}, bf16[528,128]{1,0:T(8,128)(2,1)S(1)}, u32[]{:S(2)}, u32[]{:S(2)}) collective-permute-start(bf16[528,128]{1,0:T(8,128)(2,1)S(1)} %collective-permute-done.1), channel_id=1, source_target_pairs={{0,2},{2,0},{1,3},{3,1},{4,6},{6,4},{5,7},{7,5},{8,10},{10,8},{9,1... | collective-permute-start | bytes 405512 | tf_op jit(solution)/shard_map/ppermute | solution.py:394

commit v22 on v21

--- a/solution.py
+++ b/solution.py
@@ -359,8 +359,8 @@
             start = jnp.where(start > 0, start, first_start)
             value = value * fall * root(z, inner.astype(F32) + first - start)
         table_ref[part, :] = value.astype(BF16)
-        if (b + 1) * LATE_BLOCK % z.window == 0:
-            send(table_ref, table_out, slice((b + 1) * LATE_BLOCK - z.window, (b + 1) * LATE_BLOCK))
+
+    send(table_ref, table_out, slice(0, z.slots))
 
     place = own_ref[0 : z.chunks, :]
     start = jnp.concatenate([runs.start_row(place[r : r + 1]) for r in range(z.chunks)], axis=0)
@@ -490,7 +490,7 @@
             pltpu.VMEM((late_count, 2 * z.chunks, LANES), F32),
             pltpu.VMEM((slots, width), BF16),
             pltpu.VMEM((rows, width), BF16),
-            pltpu.SemaphoreType.DMA((1 + slots // z.window,)),
+            pltpu.SemaphoreType.DMA((2,)),
         ],
         compiler_params=grant,
         name="table_and_rows",

time: 27.7 us -> 27.6 us (level)
  no operation moved by 1% of the time
where the time goes in v22:
time: 27.6 us; the launch traced here: 27.4 us
  starting transfers between devices  12.7 us (46%)
  Pallas kernels  10.3 us (37%)
  waiting for transfers between devices  2.06 us (7%)
  local copies, waits for them, and re-layouts  1.66 us (6%)
  between operations  0.69 us (2%)
    ppermute x7, starting transfers between devices, swap(): lax.ppermute(block, axis, [(i, i ^ distance) for i in range(lax.axis_size...  12.7 us
    pallas_call x3, Pallas kernels, sums(): pl.pallas_call(functools.partial(early_kernel, z, form, len(before)), out...  4.44 us
    pallas_call x1, Pallas kernels, on_device(): pl.pallas_call(functools.partial(late_kernel, z, earlier, form, len(late)...  3.9 us
    ppermute x7, waiting for transfers between devices, swap(): lax.ppermute(block, axis, [(i, i ^ distance) for i in range(lax.axis_size...  2.06 us
    pallas_call x1, Pallas kernels, on_device(): pl.pallas_call(functools.partial(send_kernel, z), out_shape=(shape((block...  1.96 us
    unnamed x8, local copies, waits for them, and re-layouts  1.66 us
  transfers between devices with their start and end apart: 7, of which 3 were waited for; matrix products, arithmetic and copies ran while one was open for 0% of the time, Pallas kernels for 16%

profile of v22, /device:TPU:0, one launch (start us, length us, event | category | flops | bytes accessed | tf_op | source)
XLA Modules:
  0.0 27.4 jit_solution(3640051496558106873)
XLA Ops:
  0.6 2.0 %weigh.1 = (bf16[528,128]{1,0:T(8,128)(2,1)}, f32[24,128]{1,0:T(8,128)}) custom-call(s32[1]{0:T(128)} %bitcast.me_ref, f32[4]{0:T(128)} %rate_ref.1, bf16[512,128]{1,0:T(8,128)(2,1)} %events_ref.1, f32[4,128]{1,0:T(4,128)} %bitcast.28, s32[4,128]{1,0:T(4,128)} %bitcast.29, s32[4,128]{1,0:T(4,128)} %bitcast.30, s32[32,128]{1,0:T(8,128)} %bitcast.27), custom_call_target="tpu_custom_call" | custom-call | tf_op jit(solution)/shard_map/weigh/pallas_call | solution.py:417
  2.6 4.0 %collective-permute-start = (bf16[528,128]{1,0:T(8,128)(2,1)}, bf16[528,128]{1,0:T(8,128)(2,1)S(1)}, u32[]{:S(2)}, u32[]{:S(2)}) collective-permute-start(bf16[528,128]{1,0:T(8,128)(2,1)} %get-tuple-element.21), channel_id=1, source_target_pairs={{0,8},{4,12},{8,0},{12,4},{1,9},{5,13},{9,1},{13,5},{2,10},{6,14},... | collective-permute-start | bytes 405512 | tf_op jit(solution)/shard_map/ppermute | solution.py:394
  6.6 1.5 %collective-permute-start.2 = (bf16[528,128]{1,0:T(8,128)(2,1)}, bf16[528,128]{1,0:T(8,128)(2,1)S(1)}, u32[]{:S(2)}, u32[]{:S(2)}) collective-permute-start(bf16[528,128]{1,0:T(8,128)(2,1)} %get-tuple-element.21), channel_id=1, source_target_pairs={{0,2},{2,0},{1,3},{3,1},{4,6},{6,4},{5,7},{7,5},{8,10},{10,8},{9,1... | collective-permute-start | bytes 405512 | tf_op jit(solution)/shard_map/ppermute | solution.py:394
  8.1 1.6 %collective-permute-start.3 = (bf16[528,128]{1,0:T(8,128)(2,1)}, bf16[528,128]{1,0:T(8,128)(2,1)S(1)}, u32[]{:S(2)}, u32[]{:S(2)}) collective-permute-start(bf16[528,128]{1,0:T(8,128)(2,1)} %get-tuple-element.21), channel_id=1, source_target_pairs={{0,4},{4,0},{8,12},{12,8},{1,5},{5,1},{9,13},{13,9},{2,6},{6,2},{1... | collective-permute-start | bytes 405512 | tf_op jit(solution)/shard_map/ppermute | solution.py:394
  9.7 0.9 %copy-done = bf16[528,128]{1,0:T(8,128)(2,1)S(1)} copy-done((bf16[528,128]{1,0:T(8,128)(2,1)S(1)}, bf16[528,128]{1,0:T(8,128)(2,1)}, u32[]{:S(2)}) %copy-start) | copy-done | bytes 135192
  10.6 0.7 %copy-done.2 = f32[24,128]{1,0:T(8,128)S(1)} copy-done((f32[24,128]{1,0:T(8,128)S(1)}, f32[24,128]{1,0:T(8,128)}, u32[]{:S(2)}) %copy-start.2) | copy-done | bytes 12312
  11.4 1.6 %first_sums.1 = (f32[4096,128]{1,0:T(8,128)S(1)}, f32[4096,128]{1,0:T(8,128)S(1)}, bf16[1024,128]{1,0:T(8,128)(2,1)S(1)}, f32[8,128]{1,0:T(8,128)S(1)}, s16[512,...) custom-call(f32[24,128]{1,0:T(8,128)S(1)} %copy-done.2, bf16[1,528,128]{2,1,0:T(8,128)(2,1)S(1)} %bitcast.23), custom_call_target="tpu_custom_call" | custom-call | flops 1 | tf_op jit(solution)/shard_map/first_sums/pallas_call | solution.py:442
  12.9 0.5 %collective-permute-done = bf16[528,128]{1,0:T(8,128)(2,1)S(1)} collective-permute-done((bf16[528,128]{1,0:T(8,128)(2,1)}, bf16[528,128]{1,0:T(8,128)(2,1)S(1)}, u32[]{:S(2)}, u32[]{:S(2)}) %collective-permute-start) | collective-permute-done | bytes 135200 | tf_op jit(solution)/shard_map/ppermute | solution.py:394
  13.4 0.8 %collective-permute-start.1 = (bf16[528,128]{1,0:T(8,128)(2,1)S(1)}, bf16[528,128]{1,0:T(8,128)(2,1)S(1)}, u32[]{:S(2)}, u32[]{:S(2)}) collective-permute-start(bf16[528,128]{1,0:T(8,128)(2,1)S(1)} %collective-permute-done), channel_id=1, source_target_pairs={{0,4},{4,0},{8,12},{12,8},{1,5},{5,1},{9,13},{13,9},{2,6},{6,2},{1... | collective-permute-start | bytes 405512 | tf_op jit(solution)/shard_map/ppermute | solution.py:394
  14.2 1.4 %collective-permute-start.4 = (bf16[528,128]{1,0:T(8,128)(2,1)S(1)}, bf16[528,128]{1,0:T(8,128)(2,1)S(1)}, u32[]{:S(2)}, u32[]{:S(2)}) collective-permute-start(bf16[528,128]{1,0:T(8,128)(2,1)S(1)} %collective-permute-done), channel_id=1, source_target_pairs={{0,2},{2,0},{1,3},{3,1},{4,6},{6,4},{5,7},{7,5},{8,10},{10,8},{9,1... | collective-permute-start | bytes 405512 | tf_op jit(solution)/shard_map/ppermute | solution.py:394
  15.6 0.0 collective-permute-done.2
  15.7 0.0 collective-permute-done.3
  15.7 0.0 copy-start.3
  15.7 1.2 %more_sums.2 = (f32[4096,128]{1,0:T(8,128)S(1)}, bf16[1024,128]{1,0:T(8,128)(2,1)S(1)}, f32[8,128]{1,0:T(8,128)S(1)}) custom-call(f32[24,128]{1,0:T(8,128)S(1)} %copy-done.2, bf16[1,528,128]{2,1,0:T(8,128)(2,1)S(1)} %bitcast.15, bf16[1,528,128]{2,1,0:T(8,128)(2,1)S(1)} %bitcast.17, f32[4096,128]{1,0:T(8,128)S(1)} %get-tuple-element.24.refs_3_), custom_call_target="tpu_custom_call" | custom-call | flops 2 | tf_op jit(solution)/shard_map/more_sums/pallas_call | solution.py:442
  16.9 1.4 %collective-permute-start.5 = (bf16[528,128]{1,0:T(8,128)(2,1)S(1)}, bf16[528,128]{1,0:T(8,128)(2,1)S(1)}, u32[]{:S(2)}, u32[]{:S(2)}) collective-permute-start(bf16[528,128]{1,0:T(8,128)(2,1)S(1)} %collective-permute-done.2), channel_id=1, source_target_pairs={{0,4},{4,0},{8,12},{12,8},{1,5},{5,1},{9,13},{13,9},{2,6},{6,2},{1... | collective-permute-start | bytes 405512 | tf_op jit(solution)/shard_map/ppermute | solution.py:394
  18.3 0.1 collective-permute-done.1
  18.4 1.9 %collective-permute-start.6 = (bf16[528,128]{1,0:T(8,128)(2,1)S(1)}, bf16[528,128]{1,0:T(8,128)(2,1)S(1)}, u32[]{:S(2)}, u32[]{:S(2)}) collective-permute-start(bf16[528,128]{1,0:T(8,128)(2,1)S(1)} %collective-permute-done.1), channel_id=1, source_target_pairs={{0,2},{2,0},{1,3},{3,1},{4,6},{6,4},{5,7},{7,5},{8,10},{10,8},{9,1... | collective-permute-start | bytes 405512 | tf_op jit(solution)/shard_map/ppermute | solution.py:394
  20.4 0.0 collective-permute-done.4
  20.4 1.7 %more_sums.3 = (f32[4096,128]{1,0:T(8,128)S(1)}, bf16[1024,128]{1,0:T(8,128)(2,1)S(1)}, f32[8,128]{1,0:T(8,128)S(1)}) custom-call(f32[24,128]{1,0:T(8,128)S(1)} %copy-done.2, bf16[1,528,128]{2,1,0:T(8,128)(2,1)S(1)} %bitcast.13, bf16[1,528,128]{2,1,0:T(8,128)(2,1)S(1)} %bitcast.19, bf16[1,528,128]{2,1,0:T(8,128)(2,1)S(1)} %bitcast.21, ...), custom_call_target="tpu_custom_call" | custom-call | flops 3 | tf_op jit(solution)/shard_map/more_sums/pallas_call | solution.py:442
  22.0 0.0 collective-permute-done.5
  22.1 1.4 %collective-permute-done.6 = bf16[528,128]{1,0:T(8,128)(2,1)S(1)} collective-permute-done((bf16[528,128]{1,0:T(8,128)(2,1)S(1)}, bf16[528,128]{1,0:T(8,128)(2,1)S(1)}, u32[]{:S(2)}, u32[]{:S(2)}) %collective-permute-start.6) | collective-permute-done | bytes 135200 | tf_op jit(solution)/shard_map/ppermute | solution.py:394
  23.5 0.0 copy-done.1
  23.5 0.0 copy-done.3
  23.5 3.9 %table_and_rows.1 = (bf16[4096,128]{1,0:T(8,128)(2,1)}, bf16[512,128]{1,0:T(8,128)(2,1)}) custom-call(f32[24,128]{1,0:T(8,128)S(1)} %copy-done.3, f32[4096,128]{1,0:T(8,128)S(1)} %get-tuple-element.28.refs_1_, f32[4096,128]{1,0:T(8,128)S(1)} %get-tuple-element.29.refs_2_, s16[512,128]{1,0:T(8,128)(2,1)S(1)} %get-tuple-element.30.refs_3_, ...), custom_call_target="tpu_custom_call" | custom-call | tf_op jit(solution)/shard_map/table_and_rows/pallas_call | solution.py:481
  (3 shorter events, 0.0 us)
Async XLA Ops:
  2.6 10.8 %collective-permute-start = (bf16[528,128]{1,0:T(8,128)(2,1)}, bf16[528,128]{1,0:T(8,128)(2,1)S(1)}, u32[]{:S(2)}, u32[]{:S(2)}) collective-permute-start(bf16[528,128]{1,0:T(8,128)(2,1)} %get-tuple-element.21), channel_id=1, source_target_pairs={{0,8},{4,12},{8,0},{12,4},{1,9},{5,13},{9,1},{13,5},{2,10},{6,14},... | collective-permute-start | bytes 405512 | tf_op jit(solution)/shard_map/ppermute | solution.py:394
  6.6 9.0 %collective-permute-start.2 = (bf16[528,128]{1,0:T(8,128)(2,1)}, bf16[528,128]{1,0:T(8,128)(2,1)S(1)}, u32[]{:S(2)}, u32[]{:S(2)}) collective-permute-start(bf16[528,128]{1,0:T(8,128)(2,1)} %get-tuple-element.21), channel_id=1, source_target_pairs={{0,2},{2,0},{1,3},{3,1},{4,6},{6,4},{5,7},{7,5},{8,10},{10,8},{9,1... | collective-permute-start | bytes 405512 | tf_op jit(solution)/shard_map/ppermute | solution.py:394
  8.1 7.5 %collective-permute-start.3 = (bf16[528,128]{1,0:T(8,128)(2,1)}, bf16[528,128]{1,0:T(8,128)(2,1)S(1)}, u32[]{:S(2)}, u32[]{:S(2)}) collective-permute-start(bf16[528,128]{1,0:T(8,128)(2,1)} %get-tuple-element.21), channel_id=1, source_target_pairs={{0,4},{4,0},{8,12},{12,8},{1,5},{5,1},{9,13},{13,9},{2,6},{6,2},{1... | collective-permute-start | bytes 405512 | tf_op jit(solution)/shard_map/ppermute | solution.py:394
  9.7 0.9 %copy-start = (bf16[528,128]{1,0:T(8,128)(2,1)S(1)}, bf16[528,128]{1,0:T(8,128)(2,1)}, u32[]{:S(2)}) copy-start(bf16[528,128]{1,0:T(8,128)(2,1)} %get-tuple-element.21) | copy-start | bytes 405508
  10.6 0.7 %copy-start.2 = (f32[24,128]{1,0:T(8,128)S(1)}, f32[24,128]{1,0:T(8,128)}, u32[]{:S(2)}) copy-start(f32[24,128]{1,0:T(8,128)} %get-tuple-element.20.refs_0_) | copy-start | bytes 36868
  13.4 5.0 %collective-permute-start.1 = (bf16[528,128]{1,0:T(8,128)(2,1)S(1)}, bf16[528,128]{1,0:T(8,128)(2,1)S(1)}, u32[]{:S(2)}, u32[]{:S(2)}) collective-permute-start(bf16[528,128]{1,0:T(8,128)(2,1)S(1)} %collective-permute-done), channel_id=1, source_target_pairs={{0,4},{4,0},{8,12},{12,8},{1,5},{5,1},{9,13},{13,9},{2,6},{6,2},{1... | collective-permute-start | bytes 405512 | tf_op jit(solution)/shard_map/ppermute | solution.py:394
  14.2 6.2 %collective-permute-start.4 = (bf16[528,128]{1,0:T(8,128)(2,1)S(1)}, bf16[528,128]{1,0:T(8,128)(2,1)S(1)}, u32[]{:S(2)}, u32[]{:S(2)}) collective-permute-start(bf16[528,128]{1,0:T(8,128)(2,1)S(1)} %collective-permute-done), channel_id=1, source_target_pairs={{0,2},{2,0},{1,3},{3,1},{4,6},{6,4},{5,7},{7,5},{8,10},{10,8},{9,1... | collective-permute-start | bytes 405512 | tf_op jit(solution)/shard_map/ppermute | solution.py:394
  15.7 7.8 %copy-start.1 = (bf16[528,128]{1,0:T(8,128)(2,1)S(1)}, bf16[528,128]{1,0:T(8,128)(2,1)}, u32[]{:S(2)}) copy-start(bf16[528,128]{1,0:T(8,128)(2,1)} %get-tuple-element.21) | copy-start | bytes 405508
  15.7 7.8 %copy-start.3 = (f32[24,128]{1,0:T(8,128)S(1)}, f32[24,128]{1,0:T(8,128)}, u32[]{:S(2)}) copy-start(f32[24,128]{1,0:T(8,128)} %get-tuple-element.20.refs_0_) | copy-start | bytes 36868
  16.9 5.2 %collective-permute-start.5 = (bf16[528,128]{1,0:T(8,128)(2,1)S(1)}, bf16[528,128]{1,0:T(8,128)(2,1)S(1)}, u32[]{:S(2)}, u32[]{:S(2)}) collective-permute-start(bf16[528,128]{1,0:T(8,128)(2,1)S(1)} %collective-permute-done.2), channel_id=1, source_target_pairs={{0,4},{4,0},{8,12},{12,8},{1,5},{5,1},{9,13},{13,9},{2,6},{6,2},{1... | collective-permute-start | bytes 405512 | tf_op jit(solution)/shard_map/ppermute | solution.py:394
  18.4 5.0 %collective-permute-start.6 = (bf16[528,128]{1,0:T(8,128)(2,1)S(1)}, bf16[528,128]{1,0:T(8,128)(2,1)S(1)}, u32[]{:S(2)}, u32[]{:S(2)}) collective-permute-start(bf16[528,128]{1,0:T(8,128)(2,1)S(1)} %collective-permute-done.1), channel_id=1, source_target_pairs={{0,2},{2,0},{1,3},{3,1},{4,6},{6,4},{5,7},{7,5},{8,10},{10,8},{9,1... | collective-permute-start | bytes 405512 | tf_op jit(solution)/shard_map/ppermute | solution.py:394
